TPU v7x, 32 devices: a whole 2x2x4 slice. The times are simulated.
32 devices in a mesh: dp: 8 (over y, x, core), resp: 4 (over z).
Axes of the slice: x: 2, y: 2, z: 4, core: 2. Of those that a mesh axis runs over, the one named last changes fastest.
Arguments:
- queries: bfloat16 [32, 128, 2560], P(('dp', 'resp')), may hold values from -6 to 6
- resp_keys: bfloat16 [32, 128, 512], P(('dp', 'resp')), may hold values from -6 to 6
- resp_values: bfloat16 [32, 128, 512], P(('dp', 'resp')), may hold values from -6 to 6
- grad_out: bfloat16 [32, 128, 2560], P(('dp', 'resp')), may hold values from -6 to 6
- forward_out: bfloat16 [32, 128, 2560], P(('dp', 'resp')), may hold values from -2 to 2
- log_norm: float32 [32, 128, 20], P(('dp', 'resp')), may hold values from 5 to 8
- prompt_keys: bfloat16 [4, 128, 512], P('resp', 'dp'), may hold values from -6 to 6
- prompt_values: bfloat16 [4, 128, 512], P('resp', 'dp'), may hold values from -6 to 6
- resp_len: int32 [32], P(('dp', 'resp')), may hold values from 1 to 128, as said below
- seen_blocks: int32 [32], P(('dp', 'resp')), may hold values from 1 to 16, as said below
Outputs:
- grad_queries: bfloat16 [32, 128, 2560], P(('dp', 'resp'))
- grad_resp_keys: bfloat16 [32, 128, 512], P(('dp', 'resp'))
- grad_resp_values: bfloat16 [32, 128, 512], P(('dp', 'resp'))
- grad_prompt_keys: float32 [4, 128, 512], P('resp', 'dp')
- grad_prompt_values: float32 [4, 128, 512], P('resp', 'dp')
Inputs may be any that keep to these rules, and one draw needn't show every extreme that they name: `resp_len`: some response has all 128 tokens live. `seen_blocks`: some response reads all 16 blocks.
All inputs are finite; a program needn't handle non-finite values.
Results may differ from a plain program's by a relative error of at most 0.009.
Values may be sent and summed in bfloat16 or wider, within the bound.
No kernel may reach another device: no remote copies, remote signals or barrier semaphores. Data moves between devices by JAX's collectives and lax.ppermute only.
A program may use at most 64 MiB of HBM per device.

v0:
```python
import jax
import jax.numpy as jnp
from jax import lax
from jax.sharding import PartitionSpec as P

HQ = 20
HK = 4
DH = 128
GROUP = 4
PB = 16


def shortened(array):
    return jax.tree.map(lambda a: a.astype(jnp.bfloat16) if a.dtype == jnp.float32 else a, array)


def from_partner(array, axis, bit):
    return lax.ppermute(array, axis, [(i, i ^ 1 << bit) for i in range(lax.axis_size(axis))])


def shifted(value, axis, steps):
    count = lax.axis_size(axis)
    pairs = [(source, (source + steps) % count) for source in range(count)]
    return lax.ppermute(value, axis, pairs)


def pair_grads(q4, do4, lse, delta, keys, vals, visible, scale):
    scores = jnp.einsum("tgrd,kgd->tgrk", q4, keys, preferred_element_type=jnp.float32) * scale
    probs = jnp.where(visible[:, None, None, :], jnp.exp(scores - lse[..., None]), 0.0)
    dprob = jnp.einsum("tgrd,kgd->tgrk", do4, vals, preferred_element_type=jnp.float32)
    dscore = probs * (dprob - delta[..., None])
    probs16 = probs.astype(jnp.bfloat16)
    dscore16 = dscore.astype(jnp.bfloat16)
    grad_v = jnp.einsum("tgrk,tgrd->kgd", probs16, do4, preferred_element_type=jnp.float32)
    grad_k = jnp.einsum("tgrk,tgrd->kgd", dscore16, q4, preferred_element_type=jnp.float32) * scale
    grad_q = (
        jnp.einsum("tgrk,kgd->tgrd", dscore16, keys, preferred_element_type=jnp.float32) * scale
    )
    return (grad_q, grad_k, grad_v)


def shards(
    queries,
    resp_keys,
    resp_values,
    grad_out,
    forward_out,
    log_norm,
    prompt_keys,
    prompt_values,
    resp_len,
    seen_blocks,
):
    rows = queries.shape[1]
    width = resp_keys.shape[2]
    ratio = HQ // HK
    scale = 1.0 / DH**0.5
    bits = GROUP.bit_length() - 1
    q4 = queries[0].reshape(rows, HK, ratio, DH)
    do4 = grad_out[0].reshape(rows, HK, ratio, DH)
    o4 = forward_out[0].reshape(rows, HK, ratio, DH)
    delta = jnp.sum(do4.astype(jnp.float32) * o4.astype(jnp.float32), axis=-1)
    lse = log_norm[0].reshape(rows, HK, ratio)
    length = resp_len[0]
    seen = seen_blocks[0]
    tpos = jnp.arange(rows, dtype=jnp.int32)
    live = tpos < length
    my_row = lax.axis_index("dp") % GROUP
    column = lax.axis_index("resp")
    loop_size = lax.axis_size("resp")
    self_ok = live[:, None] & (tpos[None, :] <= tpos[:, None])
    gq_self, gk_self, gv_self = pair_grads(
        q4,
        do4,
        lse,
        delta,
        resp_keys[0].reshape(rows, HK, DH),
        resp_values[0].reshape(rows, HK, DH),
        self_ok,
        scale,
    )

    def visit(grad_q, bundle_k, bundle_v, col):
        count = bundle_k.shape[0]
        block_of = col * GROUP + jnp.arange(count, dtype=jnp.int32) // PB
        visible = live[:, None] & (block_of < seen)[None, :]

        def compute(operand):
            gq, gk, gv = pair_grads(
                q4,
                do4,
                lse,
                delta,
                bundle_k.reshape(count, HK, DH),
                bundle_v.reshape(count, HK, DH),
                visible,
                scale,
            )
            return (grad_q + gq, gk.reshape(count, width), gv.reshape(count, width))

        def skip(operand):
            empty = jnp.zeros((count, width), jnp.float32)
            return (grad_q, empty, empty)

        return lax.cond(col * GROUP < seen, compute, skip, None)

    def move_blocks(pair):
        return shifted((pair[0], pair[1]), "resp", 1)

    def move_sums(pair):
        return shifted((pair[0], pair[1]), "resp", 1)

    start_q = jnp.zeros((rows, HK, ratio, DH), jnp.float32)
    own_k = prompt_keys[0]
    own_v = prompt_values[0]
    pair = (own_k, own_v)
    for bit in range(bits):
        other = jax.tree.map(
            lambda part, own: part.astype(own.dtype), from_partner(shortened(pair), "dp", bit), pair
        )
        upper = my_row >> bit & 1 == 1
        pair = tuple(
            (
                jnp.where(
                    upper, jnp.concatenate([theirs, mine], 0), jnp.concatenate([mine, theirs], 0)
                )
                for mine, theirs in zip(pair, other)
            )
        )
    bundle_k, bundle_v = pair
    zero = jnp.zeros(bundle_k.shape, jnp.float32)

    def step(index, carry):
        grad_q, blk_k, blk_v, sum_k, sum_v = carry
        col = (column - index) % loop_size
        grad_q, part_k, part_v = visit(grad_q, blk_k, blk_v, col)
        blk_k, blk_v = move_blocks((blk_k, blk_v))
        sum_k, sum_v = move_sums((sum_k + part_k, sum_v + part_v))
        return (grad_q, blk_k, blk_v, sum_k, sum_v)

    grad_q, blk_k, blk_v, all_k, all_v = lax.fori_loop(
        0, loop_size, step, (start_q, bundle_k, bundle_v, zero, zero)
    )
    pair = (all_k, all_v)
    for bit in reversed(range(bits)):
        half = pair[0].shape[0] // 2
        upper = my_row >> bit & 1 == 1
        lower_part = tuple((piece[:half] for piece in pair))
        upper_part = tuple((piece[half:] for piece in pair))
        sending = tuple((jnp.where(upper, low, high) for low, high in zip(lower_part, upper_part)))
        received = from_partner(sending, "dp", bit)
        pair = tuple(
            (
                jnp.where(upper, high, low) + got
                for low, high, got in zip(lower_part, upper_part, received)
            )
        )
    sum_k, sum_v = pair
    grad_queries = (grad_q + gq_self).reshape(1, rows, HQ * DH).astype(jnp.bfloat16)
    grad_rk = gk_self.reshape(1, rows, width).astype(jnp.bfloat16)
    grad_rv = gv_self.reshape(1, rows, width).astype(jnp.bfloat16)
    return (
        grad_queries,
        grad_rk,
        grad_rv,
        sum_k.reshape(1, -1, width),
        sum_v.reshape(1, -1, width),
    )


def solution(mesh):
    return jax.shard_map(
        shards,
        mesh=mesh,
        in_specs=(
            P(("dp", "resp"), None, None),
            P(("dp", "resp"), None, None),
            P(("dp", "resp"), None, None),
            P(("dp", "resp"), None, None),
            P(("dp", "resp"), None, None),
            P(("dp", "resp"), None, None),
            P("resp", "dp", None),
            P("resp", "dp", None),
            P(("dp", "resp")),
            P(("dp", "resp")),
        ),
        out_specs=(
            P(("dp", "resp"), None, None),
            P(("dp", "resp"), None, None),
            P(("dp", "resp"), None, None),
            P("resp", "dp", None),
            P("resp", "dp", None),
        ),
        check_vma=False,
    )
```

profile of v0, /device:TPU:0, one launch (start us, length us, event | category | flops | bytes accessed | tf_op | source)
XLA Modules:
  0.0 97.2 jit_solution(10725619149276130268)
XLA Ops:
  0.7 0.5 collective-permute-start.4
  1.9 0.7 reduce
  2.7 0.6 sub.66
  3.3 0.6 fusion.33
  3.9 0.9 reshape_squeeze.15
  5.0 1.0 %reshape_squeeze.16 = bf16[128,4,128]{2,1,0:T(4,128)(2,1)S(1)} reshape(bf16[1,128,512]{2,1,0:T(8,128)(2,1)} %param.16) | data formatting | bytes 262144 | tf_op jit(solution)/shard_map/reshape;squeeze | solution.py:78
  6.7 0.4 copy-done.6
  7.8 0.5 fusion.21
  8.3 0.4 fusion.29
  8.6 0.3 fusion.25
  9.0 0.4 fusion.30
  9.4 0.4 copy-done
  9.8 0.6 copy.42
  10.4 0.3 copy.41
  10.8 0.3 copy.43
  11.1 0.8 copy.54
  11.9 0.8 copy.55
  12.7 0.8 maximum_select_fusion.3
  13.5 3.0 %collective-permute-start.7 = (bf16[32,512]{1,0:T(8,128)(2,1)S(1)}, bf16[32,512]{1,0:T(8,128)(2,1)S(1)}, u32[]{:S(2)}, u32[]{:S(2)}) collective-permute-start(bf16[32,512]{1,0:T(8,128)(2,1)S(1)} %maximum_select_fusion.3), channel_id=1, source_target_pairs={{0,8},{4,12},{8,0},{12,4},{16,24},{20,28},{24,16},{28,20},{1,9},{5... | collective-permute-start | bytes 98312 | tf_op jit(solution)/shard_map/ppermute | solution.py:18
  16.4 0.8 maximum_select_fusion.2
  17.3 1.0 %collective-permute-done.7 = bf16[32,512]{1,0:T(8,128)(2,1)S(1)} collective-permute-done((bf16[32,512]{1,0:T(8,128)(2,1)S(1)}, bf16[32,512]{1,0:T(8,128)(2,1)S(1)}, u32[]{:S(2)}, u32[]{:S(2)}) %collective-permute-start.7) | collective-permute-done | bytes 32800 | tf_op jit(solution)/shard_map/ppermute | solution.py:18
  18.3 2.9 %collective-permute-done.5 = bf16[32,512]{1,0:T(8,128)(2,1)S(1)} collective-permute-done((bf16[32,512]{1,0:T(8,128)(2,1)S(1)}, bf16[32,512]{1,0:T(8,128)(2,1)S(1)}, u32[]{:S(2)}, u32[]{:S(2)}) %collective-permute-start.5) | collective-permute-done | bytes 32800 | tf_op jit(solution)/shard_map/ppermute | solution.py:18
  21.4 57.3 %while.27 = (s32[]{:T(128)}, f32[128,4,5,128]{3,0,2,1:T(8,128)S(1)}, bf16[64,512]{1,0:T(8,128)(2,1)S(1)}, bf16[64,512]{1,0:T(8,128)(2,1)S(1)}, f32[64,512]{1,0:T...) while((s32[]{:T(128)}, ...), condition=%wide.region_4.5_spmd.clone, body=%wide.region_1.4_spmd.clone.sunk | while | flops 211624720 | bytes 12118484 | solution.py:141
  22.1 4.0 %conditional.3 = (f32[128,4,5,128]{3,0,2,1:T(8,128)S(1)}, f32[64,512]{1,0:T(8,128)S(1)}, f32[64,512]{1,0:T(8,128)S(1)}) conditional(s32[]{:T(128)} %convert_element_type.117, f32[128,4,5,128]{3,0,2,1:T(8,128)S(1)} %get-tuple-element.668, (s32[128]{0:T(128)S(1)}, s32[]{:T(128)}, s32[1,64]{1,0:T(1,128)S(1)}, s32[]{:T(128)}, ...), branch_computations={%region_2.2_spmd, %region_3.3_spmd} | conditional | flops 211559168 | bytes 9495716 | solution.py:105
  22.2 0.7 compare_bitcast_fusion
  22.8 0.7 broadcast_compare_fusion
  23.6 0.7 sub.55
  24.3 0.4 fusion.9
  25.0 0.4 fusion.10
  25.6 0.5 fusion.3
  26.2 1.6 %collective-permute-start.3 = (f32[64,512]{1,0:T(8,128)S(1)}, f32[64,512]{1,0:T(8,128)S(1)}, u32[]{:S(2)}, u32[]{:S(2)}) collective-permute-start(f32[64,512]{1,0:T(8,128)S(1)} %add.127), channel_id=1, source_target_pairs={{0,1},{1,2},{2,3},{3,0},{4,5},{5,6},{6,7},{7,4},{8,9},{9,10},{10,1... | collective-permute-start | bytes 393224 | tf_op jit(solution)/shard_map/while/body/eval_jaxpr/ppermute | solution.py:24
  27.8 1.6 %collective-permute-start.2 = (f32[64,512]{1,0:T(8,128)S(1)}, f32[64,512]{1,0:T(8,128)S(1)}, u32[]{:S(2)}, u32[]{:S(2)}) collective-permute-start(f32[64,512]{1,0:T(8,128)S(1)} %add.126), channel_id=1, source_target_pairs={{0,1},{1,2},{2,3},{3,0},{4,5},{5,6},{6,7},{7,4},{8,9},{9,10},{10,1... | collective-permute-start | bytes 393224 | tf_op jit(solution)/shard_map/while/body/eval_jaxpr/ppermute | solution.py:24
  29.5 1.7 %collective-permute-start.1 = (bf16[64,512]{1,0:T(8,128)(2,1)S(1)}, bf16[64,512]{1,0:T(8,128)(2,1)S(1)}, u32[]{:S(2)}, u32[]{:S(2)}) collective-permute-start(bf16[64,512]{1,0:T(8,128)(2,1)S(1)} %copy.112), channel_id=1, source_target_pairs={{0,1},{1,2},{2,3},{3,0},{4,5},{5,6},{6,7},{7,4},{8,9},{9,10},{10,1... | collective-permute-start | bytes 196616 | tf_op jit(solution)/shard_map/while/body/eval_jaxpr/ppermute | solution.py:24
  31.3 5.8 %collective-permute-done = bf16[64,512]{1,0:T(8,128)(2,1)S(1)} collective-permute-done((bf16[64,512]{1,0:T(8,128)(2,1)S(1)}, bf16[64,512]{1,0:T(8,128)(2,1)S(1)}, u32[]{:S(2)}, u32[]{:S(2)}) %collective-permute-start) | collective-permute-done | bytes 65568 | tf_op jit(solution)/shard_map/while/body/eval_jaxpr/ppermute | solution.py:24
  37.0 0.7 collective-permute-done.1
  38.5 3.8 %collective-permute-start.3 = (f32[64,512]{1,0:T(8,128)S(1)}, f32[64,512]{1,0:T(8,128)S(1)}, u32[]{:S(2)}, u32[]{:S(2)}) collective-permute-start(f32[64,512]{1,0:T(8,128)S(1)} %add.127), channel_id=1, source_target_pairs={{0,1},{1,2},{2,3},{3,0},{4,5},{5,6},{6,7},{7,4},{8,9},{9,10},{10,1... | collective-permute-start | bytes 393224 | tf_op jit(solution)/shard_map/while/body/eval_jaxpr/ppermute | solution.py:24
  42.3 1.6 %collective-permute-start.2 = (f32[64,512]{1,0:T(8,128)S(1)}, f32[64,512]{1,0:T(8,128)S(1)}, u32[]{:S(2)}, u32[]{:S(2)}) collective-permute-start(f32[64,512]{1,0:T(8,128)S(1)} %add.126), channel_id=1, source_target_pairs={{0,1},{1,2},{2,3},{3,0},{4,5},{5,6},{6,7},{7,4},{8,9},{9,10},{10,1... | collective-permute-start | bytes 393224 | tf_op jit(solution)/shard_map/while/body/eval_jaxpr/ppermute | solution.py:24
  44.3 6.2 %collective-permute-done = bf16[64,512]{1,0:T(8,128)(2,1)S(1)} collective-permute-done((bf16[64,512]{1,0:T(8,128)(2,1)S(1)}, bf16[64,512]{1,0:T(8,128)(2,1)S(1)}, u32[]{:S(2)}, u32[]{:S(2)}) %collective-permute-start) | collective-permute-done | bytes 65568 | tf_op jit(solution)/shard_map/while/body/eval_jaxpr/ppermute | solution.py:24
  50.5 0.7 collective-permute-done.1
  52.1 5.4 %collective-permute-start.2 = (f32[64,512]{1,0:T(8,128)S(1)}, f32[64,512]{1,0:T(8,128)S(1)}, u32[]{:S(2)}, u32[]{:S(2)}) collective-permute-start(f32[64,512]{1,0:T(8,128)S(1)} %add.126), channel_id=1, source_target_pairs={{0,1},{1,2},{2,3},{3,0},{4,5},{5,6},{6,7},{7,4},{8,9},{9,10},{10,1... | collective-permute-start | bytes 393224 | tf_op jit(solution)/shard_map/while/body/eval_jaxpr/ppermute | solution.py:24
  57.5 0.5 collective-permute-start
  58.1 5.5 %collective-permute-done = bf16[64,512]{1,0:T(8,128)(2,1)S(1)} collective-permute-done((bf16[64,512]{1,0:T(8,128)(2,1)S(1)}, bf16[64,512]{1,0:T(8,128)(2,1)S(1)}, u32[]{:S(2)}, u32[]{:S(2)}) %collective-permute-start) | collective-permute-done | bytes 65568 | tf_op jit(solution)/shard_map/while/body/eval_jaxpr/ppermute | solution.py:24
  63.6 0.7 collective-permute-done.1
  65.0 4.0 %conditional.3 = (f32[128,4,5,128]{3,0,2,1:T(8,128)S(1)}, f32[64,512]{1,0:T(8,128)S(1)}, f32[64,512]{1,0:T(8,128)S(1)}) conditional(s32[]{:T(128)} %convert_element_type.117, f32[128,4,5,128]{3,0,2,1:T(8,128)S(1)} %get-tuple-element.668, (s32[128]{0:T(128)S(1)}, s32[]{:T(128)}, s32[1,64]{1,0:T(1,128)S(1)}, s32[]{:T(128)}, ...), branch_computations={%region_2.2_spmd, %region_3.3_spmd} | conditional | flops 211559168 | bytes 9495716 | solution.py:105
  65.0 0.7 compare_bitcast_fusion
  65.7 0.7 broadcast_compare_fusion
  66.4 0.7 sub.55
  67.2 0.4 fusion.9
  67.8 0.4 fusion.10
  68.5 0.5 fusion.3
  69.1 1.9 %collective-permute-start.2 = (f32[64,512]{1,0:T(8,128)S(1)}, f32[64,512]{1,0:T(8,128)S(1)}, u32[]{:S(2)}, u32[]{:S(2)}) collective-permute-start(f32[64,512]{1,0:T(8,128)S(1)} %add.126), channel_id=1, source_target_pairs={{0,1},{1,2},{2,3},{3,0},{4,5},{5,6},{6,7},{7,4},{8,9},{9,10},{10,1... | collective-permute-start | bytes 393224 | tf_op jit(solution)/shard_map/while/body/eval_jaxpr/ppermute | solution.py:24
  71.0 0.6 collective-permute-start
  71.6 2.5 %collective-permute-start.1 = (bf16[64,512]{1,0:T(8,128)(2,1)S(1)}, bf16[64,512]{1,0:T(8,128)(2,1)S(1)}, u32[]{:S(2)}, u32[]{:S(2)}) collective-permute-start(bf16[64,512]{1,0:T(8,128)(2,1)S(1)} %copy.112), channel_id=1, source_target_pairs={{0,1},{1,2},{2,3},{3,0},{4,5},{5,6},{6,7},{7,4},{8,9},{9,10},{10,1... | collective-permute-start | bytes 196616 | tf_op jit(solution)/shard_map/while/body/eval_jaxpr/ppermute | solution.py:24
  74.1 3.8 %collective-permute-done = bf16[64,512]{1,0:T(8,128)(2,1)S(1)} collective-permute-done((bf16[64,512]{1,0:T(8,128)(2,1)S(1)}, bf16[64,512]{1,0:T(8,128)(2,1)S(1)}, u32[]{:S(2)}, u32[]{:S(2)}) %collective-permute-start) | collective-permute-done | bytes 65568 | tf_op jit(solution)/shard_map/while/body/eval_jaxpr/ppermute | solution.py:24
  78.0 0.7 collective-permute-done.1
  78.7 1.5 %copy.50 = f32[128,4,5,128]{0,3,2,1:T(8,128)} copy(f32[128,4,5,128]{3,0,2,1:T(8,128)S(1)} %get-tuple-element.457) | data formatting | bytes 2621440 | tf_op jit(solution)/shard_map/while | solution.py:141
  80.2 1.6 %fusion.26 = bf16[128,4,5,128]{0,3,2,1:T(8,128)(2,1)S(1)} fusion(f32[128,4,5,128]{0,3,2,1:T(8,128)} %copy.50, bf16[128,4,128,1]{0,2,3,1:T(8,128)(2,1)S(1)} %copy-done.3, bf16[128,4,5,128]{0,3,2,1:T(8,128)(2,1)S(1)} %copy-done.1), kind=kOutput, calls=%fused_computation.39 | convolution fusion | flops 84869120 | bytes 2752512 | tf_op jit(solution)/shard_map/tgrk,kgd->tgrd/dot_general | solution.py:37
  81.8 8.1 %collective-permute-start.8 = (f32[32,512]{1,0:T(8,128)S(1)}, f32[32,512]{1,0:T(8,128)S(1)}, u32[]{:S(2)}, u32[]{:S(2)}) collective-permute-start(f32[32,512]{1,0:T(8,128)S(1)} %slice_select_fusion.1), channel_id=1, source_target_pairs={{0,8},{4,12},{8,0},{12,4},{16,24},{20,28},{24,16},{28,20},{1,9},{5... | collective-permute-start | bytes 196616 | tf_op jit(solution)/shard_map/ppermute | solution.py:18
  89.9 1.1 %copy.53 = bf16[1,128,2560]{2,1,0:T(8,128)(2,1)} copy(bf16[1,128,2560]{1,2,0:T(8,128)(2,1)S(1)} %bitcast.131) | data formatting | bytes 1310720
  91.0 1.3 %collective-permute-done.8 = f32[32,512]{1,0:T(8,128)S(1)} collective-permute-done((f32[32,512]{1,0:T(8,128)S(1)}, f32[32,512]{1,0:T(8,128)S(1)}, u32[]{:S(2)}, u32[]{:S(2)}) %collective-permute-start.8) | collective-permute-done | bytes 65568 | tf_op jit(solution)/shard_map/ppermute | solution.py:18
  92.5 2.8 %collective-permute-done.10 = f32[32,512]{1,0:T(8,128)S(1)} collective-permute-done((f32[32,512]{1,0:T(8,128)S(1)}, f32[32,512]{1,0:T(8,128)S(1)}, u32[]{:S(2)}, u32[]{:S(2)}) %collective-permute-start.10) | collective-permute-done | bytes 65568 | tf_op jit(solution)/shard_map/ppermute | solution.py:18
  95.4 0.6 add_bitcast_fusion.1
  96.0 0.6 collective-permute-done.11
  96.6 0.6 add_bitcast_fusion
  (103 shorter events, 4.4 us)
Async XLA Ops:
  0.6 5.3 %copy-start.4 = (bf16[1,128,2560]{2,1,0:T(8,128)(2,1)S(1)}, bf16[1,128,2560]{2,1,0:T(8,128)(2,1)}, u32[]{:S(2)}) copy-start(bf16[1,128,2560]{2,1,0:T(8,128)(2,1)} %param.14) | copy-start | bytes 1966084
  0.6 5.7 %copy-start.5 = (bf16[1,128,2560]{2,1,0:T(8,128)(2,1)S(1)}, bf16[1,128,2560]{2,1,0:T(8,128)(2,1)}, u32[]{:S(2)}) copy-start(bf16[1,128,2560]{2,1,0:T(8,128)(2,1)} %param.17) | copy-start | bytes 1966084
  0.7 15.8 %collective-permute-start.4 = (bf16[16,512]{1,0:T(8,128)(2,1)}, bf16[16,512]{1,0:T(8,128)(2,1)}, u32[]{:S(2)}, u32[]{:S(2)}) collective-permute-start(bf16[16,512]{1,0:T(8,128)(2,1)} %bitcast.138), channel_id=1, source_target_pairs={{0,4},{4,0},{8,12},{12,8},{16,20},{20,16},{24,28},{28,24},{1,5},{5... | collective-permute-start | bytes 49160 | tf_op jit(solution)/shard_map/ppermute | solution.py:18
  1.2 11.5 %collective-permute-start.6 = (bf16[16,512]{1,0:T(8,128)(2,1)}, bf16[16,512]{1,0:T(8,128)(2,1)}, u32[]{:S(2)}, u32[]{:S(2)}) collective-permute-start(bf16[16,512]{1,0:T(8,128)(2,1)} %bitcast.136), channel_id=1, source_target_pairs={{0,4},{4,0},{8,12},{12,8},{16,20},{20,16},{24,28},{28,24},{1,5},{5... | collective-permute-start | bytes 49160 | tf_op jit(solution)/shard_map/ppermute | solution.py:18
  5.0 2.7 %copy-start.2 = (bf16[128,4,128,1]{0,2,3,1:T(8,128)(2,1)}, bf16[128,4,128,1]{0,2,3,1:T(8,128)(2,1)S(1)}, u32[]{:S(2)}) copy-start(bf16[128,4,128,1]{0,2,3,1:T(8,128)(2,1)S(1)} %copy.66) | copy-start | bytes 393220
  6.0 1.1 %copy-start.6 = (bf16[1,128,2560]{2,1,0:T(8,128)(2,1)S(1)}, bf16[1,128,2560]{2,1,0:T(8,128)(2,1)}, u32[]{:S(2)}) copy-start(bf16[1,128,2560]{2,1,0:T(8,128)(2,1)} %param.18) | copy-start | bytes 1966084
  7.1 0.7 copy-start.7
  7.1 0.7 copy-start.8
  9.0 0.8 copy-start
  9.0 0.8 copy-start.9
  10.4 2.2 %copy-start.10 = (bf16[1,16,512]{2,1,0:T(8,128)(2,1)S(1)}, bf16[1,16,512]{2,1,0:T(8,128)(2,1)}, u32[]{:S(2)}) copy-start(bf16[1,16,512]{2,1,0:T(8,128)(2,1)} %param.21) | copy-start | bytes 49156
  10.4 6.0 %copy-start.11 = (bf16[1,16,512]{2,1,0:T(8,128)(2,1)S(1)}, bf16[1,16,512]{2,1,0:T(8,128)(2,1)}, u32[]{:S(2)}) copy-start(bf16[1,16,512]{2,1,0:T(8,128)(2,1)} %param.20) | copy-start | bytes 49156
  13.5 4.9 %collective-permute-start.7 = (bf16[32,512]{1,0:T(8,128)(2,1)S(1)}, bf16[32,512]{1,0:T(8,128)(2,1)S(1)}, u32[]{:S(2)}, u32[]{:S(2)}) collective-permute-start(bf16[32,512]{1,0:T(8,128)(2,1)S(1)} %maximum_select_fusion.3), channel_id=1, source_target_pairs={{0,8},{4,12},{8,0},{12,4},{16,24},{20,28},{24,16},{28,20},{1,9},{5... | collective-permute-start | bytes 98312 | tf_op jit(solution)/shard_map/ppermute | solution.py:18
  17.2 4.0 %collective-permute-start.5 = (bf16[32,512]{1,0:T(8,128)(2,1)S(1)}, bf16[32,512]{1,0:T(8,128)(2,1)S(1)}, u32[]{:S(2)}, u32[]{:S(2)}) collective-permute-start(bf16[32,512]{1,0:T(8,128)(2,1)S(1)} %maximum_select_fusion.2), channel_id=1, source_target_pairs={{0,8},{4,12},{8,0},{12,4},{16,24},{20,28},{24,16},{28,20},{1,9},{5... | collective-permute-start | bytes 98312 | tf_op jit(solution)/shard_map/ppermute | solution.py:18
  26.2 11.5 %collective-permute-start.3 = (f32[64,512]{1,0:T(8,128)S(1)}, f32[64,512]{1,0:T(8,128)S(1)}, u32[]{:S(2)}, u32[]{:S(2)}) collective-permute-start(f32[64,512]{1,0:T(8,128)S(1)} %add.127), channel_id=1, source_target_pairs={{0,1},{1,2},{2,3},{3,0},{4,5},{5,6},{6,7},{7,4},{8,9},{9,10},{10,1... | collective-permute-start | bytes 393224 | tf_op jit(solution)/shard_map/while/body/eval_jaxpr/ppermute | solution.py:24
  27.8 9.9 %collective-permute-start.2 = (f32[64,512]{1,0:T(8,128)S(1)}, f32[64,512]{1,0:T(8,128)S(1)}, u32[]{:S(2)}, u32[]{:S(2)}) collective-permute-start(f32[64,512]{1,0:T(8,128)S(1)} %add.126), channel_id=1, source_target_pairs={{0,1},{1,2},{2,3},{3,0},{4,5},{5,6},{6,7},{7,4},{8,9},{9,10},{10,1... | collective-permute-start | bytes 393224 | tf_op jit(solution)/shard_map/while/body/eval_jaxpr/ppermute | solution.py:24
  29.5 7.5 %collective-permute-start = (bf16[64,512]{1,0:T(8,128)(2,1)S(1)}, bf16[64,512]{1,0:T(8,128)(2,1)S(1)}, u32[]{:S(2)}, u32[]{:S(2)}) collective-permute-start(bf16[64,512]{1,0:T(8,128)(2,1)S(1)} %copy.111), channel_id=1, source_target_pairs={{0,1},{1,2},{2,3},{3,0},{4,5},{5,6},{6,7},{7,4},{8,9},{9,10},{10,1... | collective-permute-start | bytes 196616 | tf_op jit(solution)/shard_map/while/body/eval_jaxpr/ppermute | solution.py:24
  29.5 8.2 %collective-permute-start.1 = (bf16[64,512]{1,0:T(8,128)(2,1)S(1)}, bf16[64,512]{1,0:T(8,128)(2,1)S(1)}, u32[]{:S(2)}, u32[]{:S(2)}) collective-permute-start(bf16[64,512]{1,0:T(8,128)(2,1)S(1)} %copy.112), channel_id=1, source_target_pairs={{0,1},{1,2},{2,3},{3,0},{4,5},{5,6},{6,7},{7,4},{8,9},{9,10},{10,1... | collective-permute-start | bytes 196616 | tf_op jit(solution)/shard_map/while/body/eval_jaxpr/ppermute | solution.py:24
  38.5 12.7 %collective-permute-start.3 = (f32[64,512]{1,0:T(8,128)S(1)}, f32[64,512]{1,0:T(8,128)S(1)}, u32[]{:S(2)}, u32[]{:S(2)}) collective-permute-start(f32[64,512]{1,0:T(8,128)S(1)} %add.127), channel_id=1, source_target_pairs={{0,1},{1,2},{2,3},{3,0},{4,5},{5,6},{6,7},{7,4},{8,9},{9,10},{10,1... | collective-permute-start | bytes 393224 | tf_op jit(solution)/shard_map/while/body/eval_jaxpr/ppermute | solution.py:24
  42.3 8.9 %collective-permute-start.2 = (f32[64,512]{1,0:T(8,128)S(1)}, f32[64,512]{1,0:T(8,128)S(1)}, u32[]{:S(2)}, u32[]{:S(2)}) collective-permute-start(f32[64,512]{1,0:T(8,128)S(1)} %add.126), channel_id=1, source_target_pairs={{0,1},{1,2},{2,3},{3,0},{4,5},{5,6},{6,7},{7,4},{8,9},{9,10},{10,1... | collective-permute-start | bytes 393224 | tf_op jit(solution)/shard_map/while/body/eval_jaxpr/ppermute | solution.py:24
  44.0 6.6 %collective-permute-start = (bf16[64,512]{1,0:T(8,128)(2,1)S(1)}, bf16[64,512]{1,0:T(8,128)(2,1)S(1)}, u32[]{:S(2)}, u32[]{:S(2)}) collective-permute-start(bf16[64,512]{1,0:T(8,128)(2,1)S(1)} %copy.111), channel_id=1, source_target_pairs={{0,1},{1,2},{2,3},{3,0},{4,5},{5,6},{6,7},{7,4},{8,9},{9,10},{10,1... | collective-permute-start | bytes 196616 | tf_op jit(solution)/shard_map/while/body/eval_jaxpr/ppermute | solution.py:24
  44.2 7.0 %collective-permute-start.1 = (bf16[64,512]{1,0:T(8,128)(2,1)S(1)}, bf16[64,512]{1,0:T(8,128)(2,1)S(1)}, u32[]{:S(2)}, u32[]{:S(2)}) collective-permute-start(bf16[64,512]{1,0:T(8,128)(2,1)S(1)} %copy.112), channel_id=1, source_target_pairs={{0,1},{1,2},{2,3},{3,0},{4,5},{5,6},{6,7},{7,4},{8,9},{9,10},{10,1... | collective-permute-start | bytes 196616 | tf_op jit(solution)/shard_map/while/body/eval_jaxpr/ppermute | solution.py:24
  52.0 12.2 %collective-permute-start.3 = (f32[64,512]{1,0:T(8,128)S(1)}, f32[64,512]{1,0:T(8,128)S(1)}, u32[]{:S(2)}, u32[]{:S(2)}) collective-permute-start(f32[64,512]{1,0:T(8,128)S(1)} %add.127), channel_id=1, source_target_pairs={{0,1},{1,2},{2,3},{3,0},{4,5},{5,6},{6,7},{7,4},{8,9},{9,10},{10,1... | collective-permute-start | bytes 393224 | tf_op jit(solution)/shard_map/while/body/eval_jaxpr/ppermute | solution.py:24
  52.1 12.2 %collective-permute-start.2 = (f32[64,512]{1,0:T(8,128)S(1)}, f32[64,512]{1,0:T(8,128)S(1)}, u32[]{:S(2)}, u32[]{:S(2)}) collective-permute-start(f32[64,512]{1,0:T(8,128)S(1)} %add.126), channel_id=1, source_target_pairs={{0,1},{1,2},{2,3},{3,0},{4,5},{5,6},{6,7},{7,4},{8,9},{9,10},{10,1... | collective-permute-start | bytes 393224 | tf_op jit(solution)/shard_map/while/body/eval_jaxpr/ppermute | solution.py:24
  57.5 6.1 %collective-permute-start = (bf16[64,512]{1,0:T(8,128)(2,1)S(1)}, bf16[64,512]{1,0:T(8,128)(2,1)S(1)}, u32[]{:S(2)}, u32[]{:S(2)}) collective-permute-start(bf16[64,512]{1,0:T(8,128)(2,1)S(1)} %copy.111), channel_id=1, source_target_pairs={{0,1},{1,2},{2,3},{3,0},{4,5},{5,6},{6,7},{7,4},{8,9},{9,10},{10,1... | collective-permute-start | bytes 196616 | tf_op jit(solution)/shard_map/while/body/eval_jaxpr/ppermute | solution.py:24
  58.1 6.2 %collective-permute-start.1 = (bf16[64,512]{1,0:T(8,128)(2,1)S(1)}, bf16[64,512]{1,0:T(8,128)(2,1)S(1)}, u32[]{:S(2)}, u32[]{:S(2)}) collective-permute-start(bf16[64,512]{1,0:T(8,128)(2,1)S(1)} %copy.112), channel_id=1, source_target_pairs={{0,1},{1,2},{2,3},{3,0},{4,5},{5,6},{6,7},{7,4},{8,9},{9,10},{10,1... | collective-permute-start | bytes 196616 | tf_op jit(solution)/shard_map/while/body/eval_jaxpr/ppermute | solution.py:24
  69.0 9.6 %collective-permute-start.3 = (f32[64,512]{1,0:T(8,128)S(1)}, f32[64,512]{1,0:T(8,128)S(1)}, u32[]{:S(2)}, u32[]{:S(2)}) collective-permute-start(f32[64,512]{1,0:T(8,128)S(1)} %add.127), channel_id=1, source_target_pairs={{0,1},{1,2},{2,3},{3,0},{4,5},{5,6},{6,7},{7,4},{8,9},{9,10},{10,1... | collective-permute-start | bytes 393224 | tf_op jit(solution)/shard_map/while/body/eval_jaxpr/ppermute | solution.py:24
  69.1 9.5 %collective-permute-start.2 = (f32[64,512]{1,0:T(8,128)S(1)}, f32[64,512]{1,0:T(8,128)S(1)}, u32[]{:S(2)}, u32[]{:S(2)}) collective-permute-start(f32[64,512]{1,0:T(8,128)S(1)} %add.126), channel_id=1, source_target_pairs={{0,1},{1,2},{2,3},{3,0},{4,5},{5,6},{6,7},{7,4},{8,9},{9,10},{10,1... | collective-permute-start | bytes 393224 | tf_op jit(solution)/shard_map/while/body/eval_jaxpr/ppermute | solution.py:24
  71.0 6.9 %collective-permute-start = (bf16[64,512]{1,0:T(8,128)(2,1)S(1)}, bf16[64,512]{1,0:T(8,128)(2,1)S(1)}, u32[]{:S(2)}, u32[]{:S(2)}) collective-permute-start(bf16[64,512]{1,0:T(8,128)(2,1)S(1)} %copy.111), channel_id=1, source_target_pairs={{0,1},{1,2},{2,3},{3,0},{4,5},{5,6},{6,7},{7,4},{8,9},{9,10},{10,1... | collective-permute-start | bytes 196616 | tf_op jit(solution)/shard_map/while/body/eval_jaxpr/ppermute | solution.py:24
  71.6 7.0 %collective-permute-start.1 = (bf16[64,512]{1,0:T(8,128)(2,1)S(1)}, bf16[64,512]{1,0:T(8,128)(2,1)S(1)}, u32[]{:S(2)}, u32[]{:S(2)}) collective-permute-start(bf16[64,512]{1,0:T(8,128)(2,1)S(1)} %copy.112), channel_id=1, source_target_pairs={{0,1},{1,2},{2,3},{3,0},{4,5},{5,6},{6,7},{7,4},{8,9},{9,10},{10,1... | collective-permute-start | bytes 196616 | tf_op jit(solution)/shard_map/while/body/eval_jaxpr/ppermute | solution.py:24
  78.7 1.5 %copy-start.1 = (bf16[128,4,5,128]{0,3,2,1:T(8,128)(2,1)S(1)}, bf16[128,4,5,128]{0,3,2,1:T(8,128)(2,1)}, u32[]{:S(2)}) copy-start(bf16[128,4,5,128]{0,3,2,1:T(8,128)(2,1)} %copy-done) | copy-start | bytes 1966084
  78.7 1.5 %copy-start.3 = (bf16[128,4,128,1]{0,2,3,1:T(8,128)(2,1)S(1)}, bf16[128,4,128,1]{0,2,3,1:T(8,128)(2,1)}, u32[]{:S(2)}) copy-start(bf16[128,4,128,1]{0,2,3,1:T(8,128)(2,1)} %copy-done.2) | copy-start | bytes 393220
  81.8 10.5 %collective-permute-start.8 = (f32[32,512]{1,0:T(8,128)S(1)}, f32[32,512]{1,0:T(8,128)S(1)}, u32[]{:S(2)}, u32[]{:S(2)}) collective-permute-start(f32[32,512]{1,0:T(8,128)S(1)} %slice_select_fusion.1), channel_id=1, source_target_pairs={{0,8},{4,12},{8,0},{12,4},{16,24},{20,28},{24,16},{28,20},{1,9},{5... | collective-permute-start | bytes 196616 | tf_op jit(solution)/shard_map/ppermute | solution.py:18
  91.0 4.3 %collective-permute-start.10 = (f32[32,512]{1,0:T(8,128)S(1)}, f32[32,512]{1,0:T(8,128)S(1)}, u32[]{:S(2)}, u32[]{:S(2)}) collective-permute-start(f32[32,512]{1,0:T(8,128)S(1)} %slice_select_fusion), channel_id=1, source_target_pairs={{0,8},{4,12},{8,0},{12,4},{16,24},{20,28},{24,16},{28,20},{1,9},{5... | collective-permute-start | bytes 196616 | tf_op jit(solution)/shard_map/ppermute | solution.py:18
  92.4 3.0 %collective-permute-start.9 = (f32[16,512]{1,0:T(8,128)S(1)}, f32[16,512]{1,0:T(8,128)S(1)}, u32[]{:S(2)}, u32[]{:S(2)}) collective-permute-start(f32[16,512]{1,0:T(8,128)S(1)} %slice_select_fusion.3), channel_id=1, source_target_pairs={{0,4},{4,0},{8,12},{12,8},{16,20},{20,16},{24,28},{28,24},{1,5},{5... | collective-permute-start | bytes 98312 | tf_op jit(solution)/shard_map/ppermute | solution.py:18
  95.3 1.3 %collective-permute-start.11 = (f32[16,512]{1,0:T(8,128)S(1)}, f32[16,512]{1,0:T(8,128)S(1)}, u32[]{:S(2)}, u32[]{:S(2)}) collective-permute-start(f32[16,512]{1,0:T(8,128)S(1)} %slice_select_fusion.2), channel_id=1, source_target_pairs={{0,4},{4,0},{8,12},{12,8},{16,20},{20,16},{24,28},{28,24},{1,5},{5... | collective-permute-start | bytes 98312 | tf_op jit(solution)/shard_map/ppermute | solution.py:18
where the time goes:
time: 97.2 us
  starting transfers between devices  33.8 us (35%)
  waiting for transfers between devices  32.7 us (34%)
  local copies, waits for them, and re-layouts  11.9 us (12%)
  other arithmetic  7.45 us (8%)
  matrix products  6.67 us (7%)
  loops' own time  3.11 us (3%)
  between operations  1.6 us (2%)
    ppermute x16, waiting for transfers between devices, shifted(): return lax.ppermute(value, axis, pairs)  24.1 us
    ppermute x16, starting transfers between devices, shifted(): return lax.ppermute(value, axis, pairs)  21.9 us
    ppermute x8, starting transfers between devices, from_partner(): lax.ppermute(array, axis, [(i, i ^ 1 << bit) for i in range(lax.axis_size...  11.9 us
    ppermute x8, waiting for transfers between devices, from_partner(): lax.ppermute(array, axis, [(i, i ^ 1 << bit) for i in range(lax.axis_size...  8.57 us
    unnamed x33, local copies, waits for them, and re-layouts  5.9 us
    another operation x1, loops' own time, shards(): lax.fori_loop(0, loop_size, step, (start_q, bundle_k, bundle_v, zero, zero))  2.88 us
    dot_general x3, matrix products, pair_grads(): jnp.einsum('tgrk,kgd->tgrd', dscore16, keys, preferred_element_type=jnp.f...  2.64 us
    sub x3, local copies, waits for them, and re-layouts, pair_grads(): scores - lse[..., None]  2.04 us
  transfers between devices with their start and end apart: 24, of which 13 were waited for; matrix products, arithmetic and copies ran while one was open for 13% of the time, Pallas kernels for 0%

commit v1 on v0

v1 whole, which is shorter than its diff:
```python
import functools

import jax
import jax.numpy as jnp
from jax import lax
from jax.experimental import pallas as pl
from jax.experimental.pallas import tpu as pltpu
from jax.sharding import PartitionSpec as P

HQ = 20
HK = 4
DH = 128
GROUP = 4
PB = 16
RATIO = HQ // HK
LOG2E = 1.4426950408889634
FAR = 1e30
MIB = 1 << 20

NT = (((1,), (1,)), ((), ()))
NN = (((1,), (0,)), ((), ()))
TN = (((0,), (0,)), ((), ()))


def dot(a, b, dims):
    return lax.dot_general(a, b, dims, preferred_element_type=jnp.float32)


def head_rows(ref, g):
    first = g * RATIO
    return jnp.concatenate(
        [ref[:, (first + r) * DH : (first + r + 1) * DH] for r in range(RATIO)], axis=0
    )


def head_cols(g):
    return slice(g * DH, (g + 1) * DH)


def pair_terms(scores, dprob, lse_rows, delta_rows, keep):
    nk, nq = scores.shape
    probs = jnp.exp2((scores * (LOG2E / DH**0.5)).reshape(nk // 8, 8, nq) - lse_rows)
    if keep is not None:
        probs = jnp.where(keep, probs, 0.0)
    dscore = probs * (dprob.reshape(nk // 8, 8, nq) - delta_rows)
    return (
        probs.reshape(nk, nq).astype(jnp.bfloat16),
        dscore.reshape(nk, nq).astype(jnp.bfloat16),
    )


def self_kernel(
    len_ref, q_ref, do_ref, o_ref, ln_ref, k_ref, v_ref, ds_ref, lse_ref, delta_ref, gk_ref, gv_ref
):
    rows = q_ref.shape[0]
    scale = 1.0 / DH**0.5
    length = len_ref[0]
    ones = jnp.ones((8, DH), jnp.bfloat16)
    live = lax.broadcasted_iota(jnp.int32, (8, rows), 1) < length
    lnt = jnp.transpose(ln_ref[...])
    key_at = lax.broadcasted_iota(jnp.int32, (rows, RATIO * rows), 0)
    query_at = lax.broadcasted_iota(jnp.int32, (rows, RATIO * rows), 1) % rows
    keep = (key_at <= query_at).reshape(rows // 8, 8, RATIO * rows)
    for g in range(HK):
        lse_parts, delta_parts = [], []
        for r in range(RATIO):
            h = g * RATIO + r
            cols = slice(h * DH, (h + 1) * DH)
            prod = do_ref[:, cols].astype(jnp.float32) * o_ref[:, cols].astype(jnp.float32)
            high = prod.astype(jnp.bfloat16)
            low = (prod - high.astype(jnp.float32)).astype(jnp.bfloat16)
            delta_parts.append(dot(ones, high, NT) + dot(ones, low, NT))
            row = jnp.broadcast_to(lnt[h : h + 1, :] * LOG2E, (8, rows))
            lse_parts.append(jnp.where(live, row, FAR))
        lse_rows = jnp.concatenate(lse_parts, axis=1)
        delta_rows = jnp.concatenate(delta_parts, axis=1)
        lse_ref[g] = lse_rows
        delta_ref[g] = delta_rows
        q = head_rows(q_ref, g)
        do = head_rows(do_ref, g)
        cols = head_cols(g)
        p16, ds16 = pair_terms(
            dot(k_ref[:, cols], q, NT),
            dot(v_ref[:, cols], do, NT),
            lse_rows[None],
            delta_rows[None],
            keep,
        )
        ds_ref[g] = ds16
        gv_ref[:, cols] = dot(p16, do, NN).astype(gv_ref.dtype)
        gk_ref[:, cols] = (dot(ds16, q, NN) * scale).astype(gk_ref.dtype)


def prompt_kernel(
    across, n_resp, place_ref, q_ref, do_ref, lse_ref, delta_ref, kv_ref, ds_ref, part_ref
):
    nk = kv_ref.shape[0]
    scale = 1.0 / DH**0.5
    seen, my_row, my_col = place_ref[0], place_ref[1], place_ref[2]
    far = []
    for b in range(nk // (PB * n_resp)):
        for k in range(n_resp):
            block = source(my_col, k, n_resp) * GROUP + (my_row ^ (b << 1) ^ across)
            far.append(jnp.where(block < seen, 0.0, FAR).astype(jnp.float32))
    for g in range(HK):
        lse_rows = jnp.concatenate(
            [jnp.broadcast_to((lse_ref[g] + f)[None], (PB // 8,) + lse_ref.shape[1:]) for f in far],
            axis=0,
        )
        q = head_rows(q_ref, g)
        do = head_rows(do_ref, g)
        cols = head_cols(g)
        vcols = slice(cols.start + HK * DH, cols.stop + HK * DH)
        p16, ds16 = pair_terms(
            dot(kv_ref[:, cols], q, NT),
            dot(kv_ref[:, vcols], do, NT),
            lse_rows,
            delta_ref[g][None],
            None,
        )
        ds_ref[g] = ds16
        part_ref[:, cols] = (dot(ds16, q, NN) * scale).astype(part_ref.dtype)
        part_ref[:, vcols] = dot(p16, do, NN).astype(part_ref.dtype)


def query_kernel(ds0_ref, ds1_ref, ds2_ref, k0_ref, k1_ref, k2_ref, gq_ref):
    rows = gq_ref.shape[0]
    scale = 1.0 / DH**0.5
    for g in range(HK):
        cols = head_cols(g)
        ds = jnp.concatenate([ds0_ref[g], ds1_ref[g], ds2_ref[g]], axis=0)
        keys = jnp.concatenate([k0_ref[:, cols], k1_ref[:, cols], k2_ref[:, cols]], axis=0)
        out = (dot(ds, keys, TN) * scale).astype(gq_ref.dtype)
        for r in range(RATIO):
            h = g * RATIO + r
            gq_ref[:, h * DH : (h + 1) * DH] = out[r * rows : (r + 1) * rows]


VMEM = pl.BlockSpec(memory_space=pltpu.VMEM)
SMEM = pl.BlockSpec(memory_space=pltpu.SMEM)


def call(kernel, name, outs, scalars, arrays, flops):
    nbytes = sum(a.size * a.dtype.itemsize for a in arrays)
    return pl.pallas_call(
        kernel,
        name=name,
        out_shape=outs,
        in_specs=[SMEM] * len(scalars) + [VMEM] * len(arrays),
        out_specs=jax.tree.map(lambda _: VMEM, outs),
        compiler_params=pltpu.CompilerParams(vmem_limit_bytes=24 * MIB),
        cost_estimate=pl.CostEstimate(flops=flops, bytes_accessed=nbytes, transcendentals=0),
    )(*scalars, *arrays)


def source(col, k, count):
    if count & (count - 1) == 0:
        return col ^ k
    return lax.rem(col + count - k, count)


def column_pairs(k, count):
    if count & (count - 1) == 0:
        return [(i ^ k, i) for i in range(count)]
    return [((i - k) % count, i) for i in range(count)]


def from_partner(array, bit):
    return lax.ppermute(array, "dp", [(i, i ^ 1 << bit) for i in range(lax.axis_size("dp"))])


def shards(
    queries,
    resp_keys,
    resp_values,
    grad_out,
    forward_out,
    log_norm,
    prompt_keys,
    prompt_values,
    resp_len,
    seen_blocks,
):
    rows = queries.shape[1]
    width = resp_keys.shape[2]
    bits = GROUP.bit_length() - 1
    n_resp = lax.axis_size("resp")
    q, do, o, ln = queries[0], grad_out[0], forward_out[0], log_norm[0]
    kr, vr = resp_keys[0], resp_values[0]
    my_row = lax.axis_index("dp") % GROUP
    my_col = lax.axis_index("resp")
    place = jnp.stack([seen_blocks[0], my_row.astype(jnp.int32), my_col.astype(jnp.int32)])

    own = jnp.concatenate([prompt_keys[0], prompt_values[0]], axis=1)
    half = jnp.concatenate(
        [own] + [lax.ppermute(own, "resp", column_pairs(k, n_resp)) for k in range(1, n_resp)], 0
    )
    for bit in range(1, bits):
        half = jnp.concatenate([half, from_partner(half, bit)], 0)
    other = from_partner(half, 0)
    nk = half.shape[0]

    f32, b16 = jnp.float32, jnp.bfloat16
    macs = HQ * rows * DH
    ds_self, lse, delta, grad_rk, grad_rv = call(
        self_kernel,
        "self_pairs",
        (
            jax.ShapeDtypeStruct((HK, rows, RATIO * rows), b16),
            jax.ShapeDtypeStruct((HK, 8, RATIO * rows), f32),
            jax.ShapeDtypeStruct((HK, 8, RATIO * rows), f32),
            jax.ShapeDtypeStruct((rows, width), b16),
            jax.ShapeDtypeStruct((rows, width), b16),
        ),
        (resp_len,),
        (q, do, o, ln, kr, vr),
        8 * macs * rows,
    )

    def visit(kv, across, kind):
        return call(
            functools.partial(prompt_kernel, across, n_resp),
            "prompt_pairs",
            (
                jax.ShapeDtypeStruct((HK, nk, RATIO * rows), b16),
                jax.ShapeDtypeStruct((nk, 2 * width), kind),
            ),
            (place,),
            (q, do, lse, delta, kv),
            8 * macs * nk,
        )

    ds_half, part_half = visit(half, 0, f32)
    ds_other, part_other = visit(other, 1, b16)

    total = part_half + from_partner(part_other, 0).astype(f32)
    for bit in reversed(range(1, bits)):
        cut = total.shape[0] // 2
        total = total[:cut] + from_partner(total[cut:].astype(b16), bit).astype(f32)
    pieces = total.reshape(n_resp, -1, 2 * width)
    total = pieces[0]
    for k in range(1, n_resp):
        back = [(i, s) for s, i in column_pairs(k, n_resp)]
        total = total + lax.ppermute(pieces[k].astype(b16), "resp", back).astype(f32)

    grad_q = call(
        query_kernel,
        "query_grads",
        jax.ShapeDtypeStruct((rows, HQ * DH), b16),
        (),
        (ds_self, ds_half, ds_other, kr, half, other),
        2 * macs * (rows + 2 * nk),
    )
    return (
        grad_q[None],
        grad_rk[None],
        grad_rv[None],
        total[None, :, :width],
        total[None, :, width:],
    )


def solution(mesh):
    by_both, by_block = P(("dp", "resp"), None, None), P("resp", "dp", None)
    return jax.shard_map(
        shards,
        mesh=mesh,
        in_specs=(by_both,) * 6 + (by_block,) * 2 + (P(("dp", "resp")),) * 2,
        out_specs=(by_both,) * 3 + (by_block,) * 2,
        check_vma=False,
    )
```

time: 97.2 us -> 42.5 us (0.44)
  starting transfers between devices: 33.8 us -> 13.8 us
  waiting for transfers between devices: 32.7 us -> 13.8 us
  local copies, waits for them, and re-layouts: 11.9 us -> 2.97 us
  Pallas kernels: 0 us -> 7.73 us
  matrix products: 6.67 us -> 0 us
  other arithmetic: 7.45 us -> 1.73 us
  loops' own time: 3.11 us -> 0 us
    ppermute x24 -> x10, starting transfers between devices: 33.8 us -> 13.8 us  [the longest x3 5.62 us: shards(): lax.ppermute(own, 'resp', column_pairs(k, n_resp))]
    ppermute x24 -> x10, waiting for transfers between devices: 32.7 us -> 13.8 us  [the longest x4 7.36 us: from_partner(): lax.ppermute(array, 'dp', [(i, i ^ 1 << bit) for i in range(lax.axis_size...]
    pallas_call x0 -> x4, Pallas kernels: none -> 7.73 us  [call(): pl.pallas_call(kernel, name=name, out_shape=outs, in_specs=[SMEM] * len(s...]
    dot_general x15 -> x0, matrix products: 6.67 us -> none  [the longest x3 2.64 us: pair_grads(): jnp.einsum('tgrk,kgd->tgrd', dscore16, keys, preferred_element_type=jnp.f...]
    unnamed x33 -> x16, local copies, waits for them, and re-layouts: 5.9 us -> 2.31 us
    another operation x5 -> x0, loops' own time: 3.11 us -> none  [the longest x1 2.88 us: shards(): lax.fori_loop(0, loop_size, step, (start_q, bundle_k, bundle_v, zero, zero))]
    another operation x9 -> x0, local copies, waits for them, and re-layouts: 2.13 us -> none  [the longest x2 1.08 us: shards(): resp_keys[0].reshape(rows, HK, DH)]
    and x5 -> x0, other arithmetic: 2.09 us -> none  [the longest x4 1.47 us: visit(): visible = live[:, None] & (block_of < seen)[None, :]]
  transfers between devices with their start and end apart: 24 -> 10, of which waited for: 13 -> 5; matrix products, arithmetic and copies ran while one was open for 13% -> 0% of each run, Pallas kernels for 0% -> 14%
where the time goes in v1:
time: 42.5 us; the launch traced here: 42.1 us
  starting transfers between devices  13.8 us (32%)
  waiting for transfers between devices  13.8 us (32%)
  Pallas kernels  7.73 us (18%)
  local copies, waits for them, and re-layouts  2.97 us (7%)
  between operations  2.12 us (5%)
  other arithmetic  1.73 us (4%)
    pallas_call x4, Pallas kernels, call(): pl.pallas_call(kernel, name=name, out_shape=outs, in_specs=[SMEM] * len(s...  7.73 us
    ppermute x4, waiting for transfers between devices, from_partner(): lax.ppermute(array, 'dp', [(i, i ^ 1 << bit) for i in range(lax.axis_size...  7.36 us
    ppermute x3, waiting for transfers between devices, shards(): lax.ppermute(own, 'resp', column_pairs(k, n_resp))  5.71 us
    ppermute x3, starting transfers between devices, shards(): lax.ppermute(own, 'resp', column_pairs(k, n_resp))  5.62 us
    ppermute x3, starting transfers between devices, shards(): lax.ppermute(pieces[k].astype(b16), 'resp', back).astype(f32)  4.44 us
    ppermute x4, starting transfers between devices, from_partner(): lax.ppermute(array, 'dp', [(i, i ^ 1 << bit) for i in range(lax.axis_size...  3.74 us
    unnamed x16, local copies, waits for them, and re-layouts  2.31 us
  transfers between devices with their start and end apart: 10, of which 5 were waited for; matrix products, arithmetic and copies ran while one was open for 0% of the time, Pallas kernels for 14%

profile of v1, /device:TPU:0, one launch (start us, length us, event | category | flops | bytes accessed | tf_op | source)
XLA Modules:
  0.0 42.1 jit_solution(16028689346220239979)
XLA Ops:
  0.6 0.0 copy-start
  0.6 0.8 %pad_maximum_fusion.1 = (bf16[16,1024]{1,0:T(8,128)(2,1)S(1)}, bf16[128,1024]{1,0:T(8,128)(2,1)S(1)}) fusion(bf16[16,512]{1,0:T(8,128)(2,1)} %bitcast.29, bf16[16,512]{1,0:T(8,128)(2,1)} %bitcast.31), kind=kLoop, calls=%fused_computation.9 | loop fusion | flops 65535 | bytes 98304 | tf_op jit(solution)/shard_map/concatenate | solution.py:194
  1.4 3.0 %collective-permute-start = (bf16[16,1024]{1,0:T(8,128)(2,1)S(1)}, bf16[16,1024]{1,0:T(8,128)(2,1)S(1)}, u32[]{:S(2)}, u32[]{:S(2)}) collective-permute-start(bf16[16,1024]{1,0:T(8,128)(2,1)S(1)} %get-tuple-element.30), channel_id=1, source_target_pairs={{1,0},{0,1},{3,2},{2,3},{5,4},{4,5},{7,6},{6,7},{9,8},{8,9},{11,10... | collective-permute-start | bytes 98312 | tf_op jit(solution)/shard_map/ppermute | solution.py:196
  4.5 2.6 %collective-permute-start.1 = (bf16[16,1024]{1,0:T(8,128)(2,1)S(1)}, bf16[16,1024]{1,0:T(8,128)(2,1)S(1)}, u32[]{:S(2)}, u32[]{:S(2)}) collective-permute-start(bf16[16,1024]{1,0:T(8,128)(2,1)S(1)} %get-tuple-element.30), channel_id=1, source_target_pairs={{2,0},{3,1},{0,2},{1,3},{6,4},{7,5},{4,6},{5,7},{10,8},{11,9},{8,1... | collective-permute-start | bytes 98312 | tf_op jit(solution)/shard_map/ppermute | solution.py:196
  7.1 0.0 collective-permute-start.2
  7.1 0.0 collective-permute-done
  7.1 2.8 %collective-permute-done.1 = bf16[16,1024]{1,0:T(8,128)(2,1)S(1)} collective-permute-done((bf16[16,1024]{1,0:T(8,128)(2,1)S(1)}, bf16[16,1024]{1,0:T(8,128)(2,1)S(1)}, u32[]{:S(2)}, u32[]{:S(2)}) %collective-permute-start.1) | collective-permute-done | bytes 32800 | tf_op jit(solution)/shard_map/ppermute | solution.py:196
  9.9 2.9 %collective-permute-done.2 = bf16[16,1024]{1,0:T(8,128)(2,1)S(1)} collective-permute-done((bf16[16,1024]{1,0:T(8,128)(2,1)S(1)}, bf16[16,1024]{1,0:T(8,128)(2,1)S(1)}, u32[]{:S(2)}, u32[]{:S(2)}) %collective-permute-start.2) | collective-permute-done | bytes 32800 | tf_op jit(solution)/shard_map/ppermute | solution.py:196
  12.8 0.7 %pad_maximum_fusion = bf16[64,1024]{1,0:T(8,128)(2,1)S(1)} fusion(bf16[16,1024]{1,0:T(8,128)(2,1)S(1)} %collective-permute-done.2, bf16[16,1024]{1,0:T(8,128)(2,1)S(1)} %collective-permute-done.1, bf16[16,1024]{1,0:T(8,128)(2,1)S(1)} %collective-permute-done, bf16[16,512]{1,0:T(8,128)(2,1)} %bitcast.30, bf16[16,512]{1,0:T(8,128)(2,1)} %bitcast.32), kind=kLoop, calls=%fused_computation.3 | loop fusion | flops 655360 | bytes 262144 | tf_op jit(solution)/shard_map/concatenate | solution.py:195
  13.5 1.6 %collective-permute-start.3 = (bf16[64,1024]{1,0:T(8,128)(2,1)S(1)}, bf16[64,1024]{1,0:T(8,128)(2,1)S(1)}, u32[]{:S(2)}, u32[]{:S(2)}) collective-permute-start(bf16[64,1024]{1,0:T(8,128)(2,1)S(1)} %pad_maximum_fusion), channel_id=1, source_target_pairs={{0,8},{4,12},{8,0},{12,4},{16,24},{20,28},{24,16},{28,20},{1,9},{5... | collective-permute-start | bytes 393224 | tf_op jit(solution)/shard_map/ppermute | solution.py:169
  15.1 0.0 copy-start.5
  15.1 0.0 copy-start.3
  15.1 0.0 copy-start.4
  15.1 3.4 %collective-permute-done.3 = bf16[64,1024]{1,0:T(8,128)(2,1)S(1)} collective-permute-done((bf16[64,1024]{1,0:T(8,128)(2,1)S(1)}, bf16[64,1024]{1,0:T(8,128)(2,1)S(1)}, u32[]{:S(2)}, u32[]{:S(2)}) %collective-permute-start.3) | collective-permute-done | bytes 131104 | tf_op jit(solution)/shard_map/ppermute | solution.py:169
  18.6 0.1 collective-permute-start.4
  19.3 0.0 copy-done.5
  19.3 0.1 copy.15
  20.1 0.0 copy-done
  20.1 0.0 copy-done.3
  20.1 0.0 copy-done.4
  20.1 0.0 copy-start.1
  20.1 1.1 %copy-done.1 = bf16[1,128,2560]{2,1,0:T(8,128)(2,1)S(1)} copy-done((bf16[1,128,2560]{2,1,0:T(8,128)(2,1)S(1)}, bf16[1,128,2560]{2,1,0:T(8,128)(2,1)}, u32[]{:S(2)}) %copy-start.1) | copy-done | bytes 655384
  21.2 0.0 copy-start.2
  21.2 1.1 %copy-done.2 = bf16[1,128,2560]{2,1,0:T(8,128)(2,1)S(1)} copy-done((bf16[1,128,2560]{2,1,0:T(8,128)(2,1)S(1)}, bf16[1,128,2560]{2,1,0:T(8,128)(2,1)}, u32[]{:S(2)}) %copy-start.2) | copy-done | bytes 655384
  22.3 2.5 %self_pairs.1 = (bf16[4,128,640]{2,1,0:T(8,128)(2,1)S(1)}, f32[4,8,640]{2,1,0:T(8,128)S(1)}, f32[4,8,640]{2,1,0:T(8,128)S(1)}, bf16[128,512]{1,0:T(8,128)(2,1)}, bf16[128,512]{1,0:T(8,128)(2,1)}) custom-call(s32[1]{0:T(128)S(6)} %copy.20.len_ref, bf16[128,2560]{1,0:T(8,128)(2,1)S(1)} %bitcast.17, bf16[128,2560]{1,0:T(8,128)(2,1)S(1)} %bitcast.20, ...), custom_call_target="tpu_custom_call" | custom-call | flops 335544320 | bytes 2238464 | tf_op jit(solution)/shard_map/self_pairs/pallas_call | solution.py:145
  24.8 0.1 pad_add_fusion.place_ref
  24.9 0.0 collective-permute-done.4.kv_ref.k2_ref
  24.9 1.8 %prompt_pairs.3 = (bf16[4,128,640]{2,1,0:T(8,128)(2,1)S(1)}, bf16[128,1024]{1,0:T(8,128)(2,1)S(1)}) custom-call(s32[3]{0:T(128)S(1)} %pad_add_fusion.place_ref, bf16[128,2560]{1,0:T(8,128)(2,1)S(1)} %bitcast.18, bf16[128,2560]{1,0:T(8,128)(2,1)S(1)} %bitcast.21, f32[4,8,640]{2,1,0:T(8,128)S(1)} %get-tuple-element.15.lse_ref, ...), custom_call_target="tpu_custom_call" | custom-call | flops 335544320 | bytes 1736704 | tf_op jit(solution)/shard_map/prompt_pairs/pallas_call | solution.py:145
  26.7 0.5 %collective-permute-start.5 = (bf16[128,1024]{1,0:T(8,128)(2,1)S(1)}, bf16[128,1024]{1,0:T(8,128)(2,1)S(1)}, u32[]{:S(2)}, u32[]{:S(2)}) collective-permute-start(bf16[128,1024]{1,0:T(8,128)(2,1)S(1)} %get-tuple-element.22), channel_id=1, source_target_pairs={{0,4},{4,0},{8,12},{12,8},{16,20},{20,16},{24,28},{28,24},{1,5},{5... | collective-permute-start | bytes 786440 | tf_op jit(solution)/shard_map/ppermute | solution.py:169
  27.3 1.8 %prompt_pairs.2 = (bf16[4,128,640]{2,1,0:T(8,128)(2,1)S(1)}, f32[128,1024]{1,0:T(8,128)S(1)}) custom-call(s32[3]{0:T(128)S(1)} %pad_add_fusion.place_ref, bf16[128,2560]{1,0:T(8,128)(2,1)S(1)} %bitcast.19, bf16[128,2560]{1,0:T(8,128)(2,1)S(1)} %bitcast.22, f32[4,8,640]{2,1,0:T(8,128)S(1)} %get-tuple-element.15.lse_ref, ...), custom_call_target="tpu_custom_call" | custom-call | flops 335544320 | bytes 1736704 | tf_op jit(solution)/shard_map/prompt_pairs/pallas_call | solution.py:145
  29.1 0.0 collective-permute-done.5
  29.1 0.1 convert_add_fusion
  29.2 1.6 %collective-permute-start.6 = (bf16[64,1024]{1,0:T(8,128)(2,1)S(1)}, bf16[64,1024]{1,0:T(8,128)(2,1)S(1)}, u32[]{:S(2)}, u32[]{:S(2)}) collective-permute-start(bf16[64,1024]{1,0:T(8,128)(2,1)S(1)} %slice.57), channel_id=1, source_target_pairs={{0,8},{4,12},{8,0},{12,4},{16,24},{20,28},{24,16},{28,20},{1,9},{5... | collective-permute-start | bytes 393224 | tf_op jit(solution)/shard_map/ppermute | solution.py:169
  30.8 3.9 %collective-permute-done.6 = bf16[64,1024]{1,0:T(8,128)(2,1)S(1)} collective-permute-done((bf16[64,1024]{1,0:T(8,128)(2,1)S(1)}, bf16[64,1024]{1,0:T(8,128)(2,1)S(1)}, u32[]{:S(2)}, u32[]{:S(2)}) %collective-permute-start.6) | collective-permute-done | bytes 131104 | tf_op jit(solution)/shard_map/ppermute | solution.py:169
  34.8 0.1 collective-permute-start.7
  34.8 0.9 %collective-permute-start.8 = (bf16[16,1024]{1,0:T(8,128)(2,1)S(1)}, bf16[16,1024]{1,0:T(8,128)(2,1)S(1)}, u32[]{:S(2)}, u32[]{:S(2)}) collective-permute-start(bf16[16,1024]{1,0:T(8,128)(2,1)S(1)} %get-tuple-element.27), channel_id=1, source_target_pairs={{0,2},{1,3},{2,0},{3,1},{4,6},{5,7},{6,4},{7,5},{8,10},{9,11},{10,... | collective-permute-start | bytes 98312 | tf_op jit(solution)/shard_map/ppermute | solution.py:244
  35.7 3.5 %collective-permute-start.9 = (bf16[16,1024]{1,0:T(8,128)(2,1)S(1)}, bf16[16,1024]{1,0:T(8,128)(2,1)S(1)}, u32[]{:S(2)}, u32[]{:S(2)}) collective-permute-start(bf16[16,1024]{1,0:T(8,128)(2,1)S(1)} %get-tuple-element.26), channel_id=1, source_target_pairs={{0,3},{1,2},{2,1},{3,0},{4,7},{5,6},{6,5},{7,4},{8,11},{9,10},{10,... | collective-permute-start | bytes 98312 | tf_op jit(solution)/shard_map/ppermute | solution.py:244
  39.2 1.5 %query_grads.1 = bf16[128,2560]{1,0:T(8,128)(2,1)} custom-call(bf16[4,128,640]{2,1,0:T(8,128)(2,1)S(1)} %get-tuple-element.14.ds0_ref, bf16[4,128,640]{2,1,0:T(8,128)(2,1)S(1)} %get-tuple-element.17.ds1_ref, bf16[4,128,640]{2,1,0:T(8,128)(2,1)S(1)} %get-tuple-element.18.ds2_ref, bf16[128,512]{1,0:T(8,128)(2,1)S(1)} %bitcast.25, ...), custom_call_target="tpu_custom_call" | custom-call | flops 251658240 | bytes 2621440 | tf_op jit(solution)/shard_map/query_grads/pallas_call | solution.py:145
  40.8 0.0 collective-permute-done.7
  40.8 0.0 collective-permute-done.8
  40.8 0.7 %collective-permute-done.9 = bf16[16,1024]{1,0:T(8,128)(2,1)S(1)} collective-permute-done((bf16[16,1024]{1,0:T(8,128)(2,1)S(1)}, bf16[16,1024]{1,0:T(8,128)(2,1)S(1)}, u32[]{:S(2)}, u32[]{:S(2)}) %collective-permute-start.9) | collective-permute-done | bytes 32800 | tf_op jit(solution)/shard_map/ppermute | solution.py:244
  41.5 0.6 %slice_bitcast_fusion = (f32[1,16,512]{2,1,0:T(8,128)}, f32[1,16,512]{2,1,0:T(8,128)}) fusion(f32[16,1024]{1,0:T(8,128)S(1)} %fusion.1), kind=kLoop, calls=%fused_computation.7 | loop fusion | bytes 131072 | tf_op jit(solution)/shard_map/broadcast_in_dim | solution.py:259
  (8 shorter events, 0.1 us)
Async XLA Ops:
  0.6 19.5 %copy-start = (bf16[1,128,2560]{2,1,0:T(8,128)(2,1)S(1)}, bf16[1,128,2560]{2,1,0:T(8,128)(2,1)}, u32[]{:S(2)}) copy-start(bf16[1,128,2560]{2,1,0:T(8,128)(2,1)} %param.10) | copy-start | bytes 1966084
  1.4 5.6 %collective-permute-start = (bf16[16,1024]{1,0:T(8,128)(2,1)S(1)}, bf16[16,1024]{1,0:T(8,128)(2,1)S(1)}, u32[]{:S(2)}, u32[]{:S(2)}) collective-permute-start(bf16[16,1024]{1,0:T(8,128)(2,1)S(1)} %get-tuple-element.30), channel_id=1, source_target_pairs={{1,0},{0,1},{3,2},{2,3},{5,4},{4,5},{7,6},{6,7},{9,8},{8,9},{11,10... | collective-permute-start | bytes 98312 | tf_op jit(solution)/shard_map/ppermute | solution.py:196
  4.5 5.4 %collective-permute-start.1 = (bf16[16,1024]{1,0:T(8,128)(2,1)S(1)}, bf16[16,1024]{1,0:T(8,128)(2,1)S(1)}, u32[]{:S(2)}, u32[]{:S(2)}) collective-permute-start(bf16[16,1024]{1,0:T(8,128)(2,1)S(1)} %get-tuple-element.30), channel_id=1, source_target_pairs={{2,0},{3,1},{0,2},{1,3},{6,4},{7,5},{4,6},{5,7},{10,8},{11,9},{8,1... | collective-permute-start | bytes 98312 | tf_op jit(solution)/shard_map/ppermute | solution.py:196
  7.1 5.7 %collective-permute-start.2 = (bf16[16,1024]{1,0:T(8,128)(2,1)S(1)}, bf16[16,1024]{1,0:T(8,128)(2,1)S(1)}, u32[]{:S(2)}, u32[]{:S(2)}) collective-permute-start(bf16[16,1024]{1,0:T(8,128)(2,1)S(1)} %get-tuple-element.30), channel_id=1, source_target_pairs={{3,0},{2,1},{1,2},{0,3},{7,4},{6,5},{5,6},{4,7},{11,8},{10,9},{9,1... | collective-permute-start | bytes 98312 | tf_op jit(solution)/shard_map/ppermute | solution.py:196
  13.5 5.0 %collective-permute-start.3 = (bf16[64,1024]{1,0:T(8,128)(2,1)S(1)}, bf16[64,1024]{1,0:T(8,128)(2,1)S(1)}, u32[]{:S(2)}, u32[]{:S(2)}) collective-permute-start(bf16[64,1024]{1,0:T(8,128)(2,1)S(1)} %pad_maximum_fusion), channel_id=1, source_target_pairs={{0,8},{4,12},{8,0},{12,4},{16,24},{20,28},{24,16},{28,20},{1,9},{5... | collective-permute-start | bytes 393224 | tf_op jit(solution)/shard_map/ppermute | solution.py:169
  15.1 4.2 %copy-start.5 = (f32[1,128,20]{1,0,2:T(1,128)S(1)}, f32[1,128,20]{1,0,2:T(1,128)}, u32[]{:S(2)}) copy-start(f32[1,128,20]{1,0,2:T(1,128)} %param.15) | copy-start | bytes 30724
  15.1 5.0 %copy-start.3 = (bf16[1,128,512]{2,1,0:T(8,128)(2,1)S(1)}, bf16[1,128,512]{2,1,0:T(8,128)(2,1)}, u32[]{:S(2)}) copy-start(bf16[1,128,512]{2,1,0:T(8,128)(2,1)} %param.11) | copy-start | bytes 393220
  15.1 5.0 %copy-start.4 = (bf16[1,128,512]{2,1,0:T(8,128)(2,1)S(1)}, bf16[1,128,512]{2,1,0:T(8,128)(2,1)}, u32[]{:S(2)}) copy-start(bf16[1,128,512]{2,1,0:T(8,128)(2,1)} %param.12) | copy-start | bytes 393220
  18.6 6.3 %collective-permute-start.4 = (bf16[128,1024]{1,0:T(8,128)(2,1)S(1)}, bf16[128,1024]{1,0:T(8,128)(2,1)S(1)}, u32[]{:S(2)}, u32[]{:S(2)}) collective-permute-start(bf16[128,1024]{1,0:T(8,128)(2,1)S(1)} %constant_dynamic-update-slice_fusion.kv_ref.k1_ref), channel_id=1, source_target_pairs={{0,4},{4,0},{8,12},{12,8},{16,20},{20,16},{24,28},{28,24},{1,5},{5... | collective-permute-start | bytes 786440 | tf_op jit(solution)/shard_map/ppermute | solution.py:169
  20.1 1.1 %copy-start.1 = (bf16[1,128,2560]{2,1,0:T(8,128)(2,1)S(1)}, bf16[1,128,2560]{2,1,0:T(8,128)(2,1)}, u32[]{:S(2)}) copy-start(bf16[1,128,2560]{2,1,0:T(8,128)(2,1)} %param.13) | copy-start | bytes 1966084
  21.2 1.1 %copy-start.2 = (bf16[1,128,2560]{2,1,0:T(8,128)(2,1)S(1)}, bf16[1,128,2560]{2,1,0:T(8,128)(2,1)}, u32[]{:S(2)}) copy-start(bf16[1,128,2560]{2,1,0:T(8,128)(2,1)} %param.14) | copy-start | bytes 1966084
  26.7 2.4 %collective-permute-start.5 = (bf16[128,1024]{1,0:T(8,128)(2,1)S(1)}, bf16[128,1024]{1,0:T(8,128)(2,1)S(1)}, u32[]{:S(2)}, u32[]{:S(2)}) collective-permute-start(bf16[128,1024]{1,0:T(8,128)(2,1)S(1)} %get-tuple-element.22), channel_id=1, source_target_pairs={{0,4},{4,0},{8,12},{12,8},{16,20},{20,16},{24,28},{28,24},{1,5},{5... | collective-permute-start | bytes 786440 | tf_op jit(solution)/shard_map/ppermute | solution.py:169
  29.2 5.5 %collective-permute-start.6 = (bf16[64,1024]{1,0:T(8,128)(2,1)S(1)}, bf16[64,1024]{1,0:T(8,128)(2,1)S(1)}, u32[]{:S(2)}, u32[]{:S(2)}) collective-permute-start(bf16[64,1024]{1,0:T(8,128)(2,1)S(1)} %slice.57), channel_id=1, source_target_pairs={{0,8},{4,12},{8,0},{12,4},{16,24},{20,28},{24,16},{28,20},{1,9},{5... | collective-permute-start | bytes 393224 | tf_op jit(solution)/shard_map/ppermute | solution.py:169
  34.8 6.0 %collective-permute-start.7 = (bf16[16,1024]{1,0:T(8,128)(2,1)S(1)}, bf16[16,1024]{1,0:T(8,128)(2,1)S(1)}, u32[]{:S(2)}, u32[]{:S(2)}) collective-permute-start(bf16[16,1024]{1,0:T(8,128)(2,1)S(1)} %get-tuple-element.25), channel_id=1, source_target_pairs={{0,1},{1,0},{2,3},{3,2},{4,5},{5,4},{6,7},{7,6},{8,9},{9,8},{10,11... | collective-permute-start | bytes 98312 | tf_op jit(solution)/shard_map/ppermute | solution.py:244
  34.8 5.9 %collective-permute-start.8 = (bf16[16,1024]{1,0:T(8,128)(2,1)S(1)}, bf16[16,1024]{1,0:T(8,128)(2,1)S(1)}, u32[]{:S(2)}, u32[]{:S(2)}) collective-permute-start(bf16[16,1024]{1,0:T(8,128)(2,1)S(1)} %get-tuple-element.27), channel_id=1, source_target_pairs={{0,2},{1,3},{2,0},{3,1},{4,6},{5,7},{6,4},{7,5},{8,10},{9,11},{10,... | collective-permute-start | bytes 98312 | tf_op jit(solution)/shard_map/ppermute | solution.py:244
  35.7 5.7 %collective-permute-start.9 = (bf16[16,1024]{1,0:T(8,128)(2,1)S(1)}, bf16[16,1024]{1,0:T(8,128)(2,1)S(1)}, u32[]{:S(2)}, u32[]{:S(2)}) collective-permute-start(bf16[16,1024]{1,0:T(8,128)(2,1)S(1)} %get-tuple-element.26), channel_id=1, source_target_pairs={{0,3},{1,2},{2,1},{3,0},{4,7},{5,6},{6,5},{7,4},{8,11},{9,10},{10,... | collective-permute-start | bytes 98312 | tf_op jit(solution)/shard_map/ppermute | solution.py:244

commit v2 on v1

--- a/solution.py
+++ b/solution.py
@@ -50,18 +50,41 @@
 
 
 def self_kernel(
-    len_ref, q_ref, do_ref, o_ref, ln_ref, k_ref, v_ref, ds_ref, lse_ref, delta_ref, gk_ref, gv_ref
+    len_ref, q_hbm, do_hbm, o_hbm, ln_hbm, k_hbm, v_hbm,
+    q_ref, do_ref, p_ref, ds_ref, lse_ref, delta_ref,
+    o_ref, ln_ref, k_ref, v_ref, sems,
 ):
     rows = q_ref.shape[0]
-    scale = 1.0 / DH**0.5
-    length = len_ref[0]
+    span = RATIO * DH
+    first = [
+        pltpu.make_async_copy(ln_hbm, ln_ref, sems.at[HK, 0]),
+        pltpu.make_async_copy(k_hbm, k_ref, sems.at[HK, 1]),
+        pltpu.make_async_copy(v_hbm, v_ref, sems.at[HK, 2]),
+    ]
+    parts = []
+    for g in range(HK):
+        cols = slice(g * span, (g + 1) * span)
+        parts.append(
+            [
+                pltpu.make_async_copy(hbm.at[:, cols], ref.at[:, cols], sems.at[g, i])
+                for i, (hbm, ref) in enumerate(
+                    ((do_hbm, do_ref), (o_hbm, o_ref), (q_hbm, q_ref))
+                )
+            ]
+        )
+    for copy in parts[0] + first + sum(parts[1:], []):
+        copy.start()
     ones = jnp.ones((8, DH), jnp.bfloat16)
-    live = lax.broadcasted_iota(jnp.int32, (8, rows), 1) < length
-    lnt = jnp.transpose(ln_ref[...])
+    live = lax.broadcasted_iota(jnp.int32, (8, rows), 1) < len_ref[0]
     key_at = lax.broadcasted_iota(jnp.int32, (rows, RATIO * rows), 0)
     query_at = lax.broadcasted_iota(jnp.int32, (rows, RATIO * rows), 1) % rows
     keep = (key_at <= query_at).reshape(rows // 8, 8, RATIO * rows)
     for g in range(HK):
+        for copy in parts[g]:
+            copy.wait()
+        if g == 0:
+            for copy in first:
+                copy.wait()
         lse_parts, delta_parts = [], []
         for r in range(RATIO):
             h = g * RATIO + r
@@ -70,38 +93,42 @@
             high = prod.astype(jnp.bfloat16)
             low = (prod - high.astype(jnp.float32)).astype(jnp.bfloat16)
             delta_parts.append(dot(ones, high, NT) + dot(ones, low, NT))
-            row = jnp.broadcast_to(lnt[h : h + 1, :] * LOG2E, (8, rows))
+            row = jnp.broadcast_to(ln_ref[h] * LOG2E, (8, rows))
             lse_parts.append(jnp.where(live, row, FAR))
         lse_rows = jnp.concatenate(lse_parts, axis=1)
         delta_rows = jnp.concatenate(delta_parts, axis=1)
         lse_ref[g] = lse_rows
         delta_ref[g] = delta_rows
-        q = head_rows(q_ref, g)
-        do = head_rows(do_ref, g)
         cols = head_cols(g)
-        p16, ds16 = pair_terms(
-            dot(k_ref[:, cols], q, NT),
-            dot(v_ref[:, cols], do, NT),
+        p_ref[g], ds_ref[g] = pair_terms(
+            dot(k_ref[:, cols], head_rows(q_ref, g), NT),
+            dot(v_ref[:, cols], head_rows(do_ref, g), NT),
             lse_rows[None],
             delta_rows[None],
             keep,
         )
-        ds_ref[g] = ds16
-        gv_ref[:, cols] = dot(p16, do, NN).astype(gv_ref.dtype)
-        gk_ref[:, cols] = (dot(ds16, q, NN) * scale).astype(gk_ref.dtype)
+
+
+def response_kernel(q_ref, do_ref, p_ref, ds_ref, gk_ref, gv_ref):
+    scale = 1.0 / DH**0.5
+    for g in range(HK):
+        cols = head_cols(g)
+        gv_ref[:, cols] = dot(p_ref[g], head_rows(do_ref, g), NN).astype(gv_ref.dtype)
+        gk_ref[:, cols] = (dot(ds_ref[g], head_rows(q_ref, g), NN) * scale).astype(gk_ref.dtype)
 
 
 def prompt_kernel(
-    across, n_resp, place_ref, q_ref, do_ref, lse_ref, delta_ref, kv_ref, ds_ref, part_ref
+    across, n_resp, seen_ref, q_ref, do_ref, lse_ref, delta_ref, kv_ref, ds_ref, part_ref
 ):
     nk = kv_ref.shape[0]
     scale = 1.0 / DH**0.5
-    seen, my_row, my_col = place_ref[0], place_ref[1], place_ref[2]
+    my_row = lax.rem(lax.axis_index("dp"), GROUP)
+    my_col = lax.axis_index("resp")
     far = []
     for b in range(nk // (PB * n_resp)):
         for k in range(n_resp):
             block = source(my_col, k, n_resp) * GROUP + (my_row ^ (b << 1) ^ across)
-            far.append(jnp.where(block < seen, 0.0, FAR).astype(jnp.float32))
+            far.append(jnp.where(block < seen_ref[0], 0.0, FAR))
     for g in range(HK):
         lse_rows = jnp.concatenate(
             [jnp.broadcast_to((lse_ref[g] + f)[None], (PB // 8,) + lse_ref.shape[1:]) for f in far],
@@ -138,16 +165,20 @@
 
 VMEM = pl.BlockSpec(memory_space=pltpu.VMEM)
 SMEM = pl.BlockSpec(memory_space=pltpu.SMEM)
-
-
-def call(kernel, name, outs, scalars, arrays, flops):
+HBM = pl.BlockSpec(memory_space=pltpu.HBM)
+
+
+def call(kernel, name, outs, scalars, arrays, flops, place=VMEM, scratch=()):
     nbytes = sum(a.size * a.dtype.itemsize for a in arrays)
+    if place is HBM:
+        arrays = [pltpu.with_memory_space_constraint(a, pltpu.HBM) for a in arrays]
     return pl.pallas_call(
         kernel,
         name=name,
         out_shape=outs,
-        in_specs=[SMEM] * len(scalars) + [VMEM] * len(arrays),
+        in_specs=[SMEM] * len(scalars) + [place] * len(arrays),
         out_specs=jax.tree.map(lambda _: VMEM, outs),
+        scratch_shapes=scratch,
         compiler_params=pltpu.CompilerParams(vmem_limit_bytes=24 * MIB),
         cost_estimate=pl.CostEstimate(flops=flops, bytes_accessed=nbytes, transcendentals=0),
     )(*scalars, *arrays)
@@ -185,39 +216,13 @@
     width = resp_keys.shape[2]
     bits = GROUP.bit_length() - 1
     n_resp = lax.axis_size("resp")
-    q, do, o, ln = queries[0], grad_out[0], forward_out[0], log_norm[0]
+    ln = jnp.transpose(log_norm, (2, 0, 1))
     kr, vr = resp_keys[0], resp_values[0]
-    my_row = lax.axis_index("dp") % GROUP
-    my_col = lax.axis_index("resp")
-    place = jnp.stack([seen_blocks[0], my_row.astype(jnp.int32), my_col.astype(jnp.int32)])
-
-    own = jnp.concatenate([prompt_keys[0], prompt_values[0]], axis=1)
-    half = jnp.concatenate(
-        [own] + [lax.ppermute(own, "resp", column_pairs(k, n_resp)) for k in range(1, n_resp)], 0
-    )
-    for bit in range(1, bits):
-        half = jnp.concatenate([half, from_partner(half, bit)], 0)
-    other = from_partner(half, 0)
-    nk = half.shape[0]
-
     f32, b16 = jnp.float32, jnp.bfloat16
     macs = HQ * rows * DH
-    ds_self, lse, delta, grad_rk, grad_rv = call(
-        self_kernel,
-        "self_pairs",
-        (
-            jax.ShapeDtypeStruct((HK, rows, RATIO * rows), b16),
-            jax.ShapeDtypeStruct((HK, 8, RATIO * rows), f32),
-            jax.ShapeDtypeStruct((HK, 8, RATIO * rows), f32),
-            jax.ShapeDtypeStruct((rows, width), b16),
-            jax.ShapeDtypeStruct((rows, width), b16),
-        ),
-        (resp_len,),
-        (q, do, o, ln, kr, vr),
-        8 * macs * rows,
-    )
 
     def visit(kv, across, kind):
+        nk = kv.shape[0]
         return call(
             functools.partial(prompt_kernel, across, n_resp),
             "prompt_pairs",
@@ -225,32 +230,81 @@
                 jax.ShapeDtypeStruct((HK, nk, RATIO * rows), b16),
                 jax.ShapeDtypeStruct((nk, 2 * width), kind),
             ),
-            (place,),
+            (seen_blocks,),
             (q, do, lse, delta, kv),
             8 * macs * nk,
         )
 
+    own = lax.optimization_barrier(jnp.concatenate([prompt_keys[0], prompt_values[0]], axis=1))
+    pieces = [lax.ppermute(own, "resp", column_pairs(k, n_resp)) for k in range(1, n_resp)]
+    q, do, p_self, ds_self, lse, delta = call(
+        self_kernel,
+        "self_pairs",
+        (
+            jax.ShapeDtypeStruct((rows, HQ * DH), b16),
+            jax.ShapeDtypeStruct((rows, HQ * DH), b16),
+            jax.ShapeDtypeStruct((HK, rows, RATIO * rows), b16),
+            jax.ShapeDtypeStruct((HK, rows, RATIO * rows), b16),
+            jax.ShapeDtypeStruct((HK, 8, RATIO * rows), f32),
+            jax.ShapeDtypeStruct((HK, 8, RATIO * rows), f32),
+        ),
+        (resp_len,),
+        (queries[0], grad_out[0], forward_out[0], ln, kr, vr),
+        4 * macs * rows,
+        HBM,
+        (
+            pltpu.VMEM((rows, HQ * DH), b16),
+            pltpu.VMEM((HQ, 1, rows), f32),
+            pltpu.VMEM((rows, width), b16),
+            pltpu.VMEM((rows, width), b16),
+            pltpu.SemaphoreType.DMA((HK + 1, 3)),
+        ),
+    )
+    pieces, q, do, p_self, ds_self, lse, delta = lax.optimization_barrier(
+        (pieces, q, do, p_self, ds_self, lse, delta)
+    )
+
+    half = jnp.concatenate([own] + pieces, 0)
+    for bit in range(1, bits):
+        half = jnp.concatenate([half, from_partner(half, bit)], 0)
+
+    other = from_partner(half, 0)
     ds_half, part_half = visit(half, 0, f32)
+    other, ds_half, part_half = lax.optimization_barrier((other, ds_half, part_half))
     ds_other, part_other = visit(other, 1, b16)
 
-    total = part_half + from_partner(part_other, 0).astype(f32)
-    for bit in reversed(range(1, bits)):
-        cut = total.shape[0] // 2
-        total = total[:cut] + from_partner(total[cut:].astype(b16), bit).astype(f32)
-    pieces = total.reshape(n_resp, -1, 2 * width)
-    total = pieces[0]
-    for k in range(1, n_resp):
-        back = [(i, s) for s, i in column_pairs(k, n_resp)]
-        total = total + lax.ppermute(pieces[k].astype(b16), "resp", back).astype(f32)
-
+    got = from_partner(part_other, 0)
+    grad_rk, grad_rv = call(
+        response_kernel,
+        "response_grads",
+        (
+            jax.ShapeDtypeStruct((rows, width), b16),
+            jax.ShapeDtypeStruct((rows, width), b16),
+        ),
+        (),
+        (q, do, p_self, ds_self),
+        4 * macs * rows,
+    )
+    got, grad_rk, grad_rv = lax.optimization_barrier((got, grad_rk, grad_rv))
+    total = part_half + got.astype(f32)
     grad_q = call(
         query_kernel,
         "query_grads",
         jax.ShapeDtypeStruct((rows, HQ * DH), b16),
         (),
         (ds_self, ds_half, ds_other, kr, half, other),
-        2 * macs * (rows + 2 * nk),
-    )
+        2 * macs * (rows + half.shape[0] + other.shape[0]),
+    )
+    for bit in reversed(range(1, bits)):
+        cut = total.shape[0] // 2
+        got = from_partner(total[cut:].astype(b16), bit)
+        got, grad_q = lax.optimization_barrier((got, grad_q))
+        total = total[:cut] + got.astype(f32)
+    pieces = total.reshape(n_resp, -1, 2 * width)
+    total = pieces[0]
+    for k in range(1, n_resp):
+        back = [(i, s) for s, i in column_pairs(k, n_resp)]
+        total = total + lax.ppermute(pieces[k].astype(b16), "resp", back).astype(f32)
     return (
         grad_q[None],
         grad_rk[None],

time: 42.5 us -> 36.7 us (0.86)
  waiting for transfers between devices: 13.8 us -> 10.9 us
  local copies, waits for them, and re-layouts: 2.97 us -> 0.68 us
  other arithmetic: 1.73 us -> 0.85 us
  Pallas kernels: 7.73 us -> 8.44 us
    ppermute x3, waiting for transfers between devices: 5.71 us -> 0.43 us  [shards(): lax.ppermute(own, 'resp', column_pairs(k, n_resp))]
    ppermute x3, waiting for transfers between devices: 0.69 us -> 4.32 us  [shards(): lax.ppermute(pieces[k].astype(b16), 'resp', back).astype(f32)]
    unnamed x16 -> x6, local copies, waits for them, and re-layouts: 2.31 us -> 0.02 us
    ppermute x4, waiting for transfers between devices: 7.36 us -> 6.2 us  [from_partner(): lax.ppermute(array, 'dp', [(i, i ^ 1 << bit) for i in range(lax.axis_size...]
    concatenate x2, other arithmetic: 1.55 us -> 0.75 us  [the longest x1 0.74 us: shards(): jnp.concatenate([prompt_keys[0], prompt_values[0]], axis=1)]
    pallas_call x4 -> x5, Pallas kernels: 7.73 us -> 8.44 us  [call(): pl.pallas_call(kernel, name=name, out_shape=outs, in_specs=[SMEM] * len(s...]
  transfers between devices with their start and end apart: 10 -> 10, of which waited for: 5 -> 5; matrix products, arithmetic and copies ran while one was open for 0% -> 0% of each run, Pallas kernels for 14% -> 20%
where the time goes in v2:
time: 36.7 us; the launch traced here: 36.4 us
  starting transfers between devices  13.4 us (37%)
  waiting for transfers between devices  10.9 us (30%)
  Pallas kernels  8.44 us (23%)
  between operations  2.04 us (6%)
  other arithmetic  0.85 us (2%)
  local copies, waits for them, and re-layouts  0.68 us (2%)
    pallas_call x5, Pallas kernels, call(): pl.pallas_call(kernel, name=name, out_shape=outs, in_specs=[SMEM] * len(s...  8.44 us
    ppermute x4, waiting for transfers between devices, from_partner(): lax.ppermute(array, 'dp', [(i, i ^ 1 << bit) for i in range(lax.axis_size...  6.2 us
    ppermute x3, starting transfers between devices, shards(): lax.ppermute(own, 'resp', column_pairs(k, n_resp))  5.62 us
    ppermute x3, waiting for transfers between devices, shards(): lax.ppermute(pieces[k].astype(b16), 'resp', back).astype(f32)  4.32 us
    ppermute x3, starting transfers between devices, shards(): lax.ppermute(pieces[k].astype(b16), 'resp', back).astype(f32)  4.05 us
    ppermute x4, starting transfers between devices, from_partner(): lax.ppermute(array, 'dp', [(i, i ^ 1 << bit) for i in range(lax.axis_size...  3.77 us
    concatenate x1, other arithmetic, shards(): jnp.concatenate([prompt_keys[0], prompt_values[0]], axis=1)  0.74 us
  transfers between devices with their start and end apart: 10, of which 5 were waited for; matrix products, arithmetic and copies ran while one was open for 0% of the time, Pallas kernels for 20%

profile of v2, /device:TPU:0, one launch (start us, length us, event | category | flops | bytes accessed | tf_op | source)
XLA Modules:
  0.0 36.4 jit_solution(16534391207034229810)
XLA Ops:
  0.6 0.7 %pad_maximum_fusion.1 = bf16[16,1024]{1,0:T(8,128)(2,1)S(1)} fusion(bf16[16,512]{1,0:T(8,128)(2,1)} %bitcast.22, bf16[16,512]{1,0:T(8,128)(2,1)} %bitcast.23), kind=kLoop, calls=%fused_computation.9 | loop fusion | flops 65536 | bytes 65536 | tf_op jit(solution)/shard_map/concatenate | solution.py:238
  1.4 5.0 %collective-permute-start.2 = (bf16[16,1024]{1,0:T(8,128)(2,1)S(1)}, bf16[16,1024]{1,0:T(8,128)(2,1)S(1)}, u32[]{:S(2)}, u32[]{:S(2)}) collective-permute-start(bf16[16,1024]{1,0:T(8,128)(2,1)S(1)} %pad_maximum_fusion.1), channel_id=1, source_target_pairs={{3,0},{2,1},{1,2},{0,3},{7,4},{6,5},{5,6},{4,7},{11,8},{10,9},{9,1... | collective-permute-start | bytes 98312 | tf_op jit(solution)/shard_map/ppermute | solution.py:239
  6.4 0.0 collective-permute-start.1
  6.4 0.6 %collective-permute-start = (bf16[16,1024]{1,0:T(8,128)(2,1)S(1)}, bf16[16,1024]{1,0:T(8,128)(2,1)S(1)}, u32[]{:S(2)}, u32[]{:S(2)}) collective-permute-start(bf16[16,1024]{1,0:T(8,128)(2,1)S(1)} %pad_maximum_fusion.1), channel_id=1, source_target_pairs={{1,0},{0,1},{3,2},{2,3},{5,4},{4,5},{7,6},{6,7},{9,8},{8,9},{11,10... | collective-permute-start | bytes 98312 | tf_op jit(solution)/shard_map/ppermute | solution.py:239
  7.6 3.2 %self_pairs.1 = (bf16[128,2560]{1,0:T(8,128)(2,1)S(1)}, bf16[128,2560]{1,0:T(8,128)(2,1)S(1)}, bf16[4,128,640]{2,1,0:T(8,128)(2,1)S(1)}, bf16[4,128,640]{2,1,0:T...) custom-call(s32[1]{0:T(128)S(6)} %copy.19.len_ref, bf16[128,2560]{1,0:T(8,128)(2,1)} %bitcast.17, ...), custom_call_target="tpu_custom_call" | custom-call | flops 167772160 | bytes 2238464 | tf_op jit(solution)/shard_map/self_pairs/pallas_call | solution.py:175
  10.8 0.0 collective-permute-done.2
  10.8 0.4 %collective-permute-done.1 = bf16[16,1024]{1,0:T(8,128)(2,1)S(1)} collective-permute-done((bf16[16,1024]{1,0:T(8,128)(2,1)S(1)}, bf16[16,1024]{1,0:T(8,128)(2,1)S(1)}, u32[]{:S(2)}, u32[]{:S(2)}) %collective-permute-start.1) | collective-permute-done | bytes 32800 | tf_op jit(solution)/shard_map/ppermute | solution.py:239
  11.2 0.0 collective-permute-done
  11.3 1.6 %collective-permute-start.3 = (bf16[64,1024]{1,0:T(8,128)(2,1)S(1)}, bf16[64,1024]{1,0:T(8,128)(2,1)S(1)}, u32[]{:S(2)}, u32[]{:S(2)}) collective-permute-start(bf16[64,1024]{1,0:T(8,128)(2,1)S(1)} %pad_maximum_fusion), channel_id=1, source_target_pairs={{0,8},{4,12},{8,0},{12,4},{16,24},{20,28},{24,16},{28,20},{1,9},{5... | collective-permute-start | bytes 393224 | tf_op jit(solution)/shard_map/ppermute | solution.py:200
  12.8 3.5 %collective-permute-done.3 = bf16[64,1024]{1,0:T(8,128)(2,1)S(1)} collective-permute-done((bf16[64,1024]{1,0:T(8,128)(2,1)S(1)}, bf16[64,1024]{1,0:T(8,128)(2,1)S(1)}, u32[]{:S(2)}, u32[]{:S(2)}) %collective-permute-start.3) | collective-permute-done | bytes 131104 | tf_op jit(solution)/shard_map/ppermute | solution.py:200
  16.3 0.1 collective-permute-start.4
  17.0 1.3 %prompt_pairs.2 = (bf16[4,128,640]{2,1,0:T(8,128)(2,1)S(1)}, f32[128,1024]{1,0:T(8,128)S(1)}) custom-call(s32[1]{0:T(128)S(6)} %copy.20.seen_ref, bf16[128,2560]{1,0:T(8,128)(2,1)S(1)} %get-tuple-element.43.q_ref, bf16[128,2560]{1,0:T(8,128)(2,1)S(1)} %get-tuple-element.44.do_ref, f32[4,8,640]{2,1,0:T(8,128)S(1)} %get-tuple-element.45.lse_ref, ...), custom_call_target="tpu_custom_call" | custom-call | flops 335544320 | bytes 1736704 | tf_op jit(solution)/shard_map/prompt_pairs/pallas_call | solution.py:175
  18.3 0.0 collective-permute-done.4.kv_ref.k2_ref
  18.3 1.3 %prompt_pairs.3 = (bf16[4,128,640]{2,1,0:T(8,128)(2,1)S(1)}, bf16[128,1024]{1,0:T(8,128)(2,1)S(1)}) custom-call(s32[1]{0:T(128)S(6)} %copy.20.seen_ref, bf16[128,2560]{1,0:T(8,128)(2,1)S(1)} %get-tuple-element.43.q_ref, bf16[128,2560]{1,0:T(8,128)(2,1)S(1)} %get-tuple-element.44.do_ref, f32[4,8,640]{2,1,0:T(8,128)S(1)} %get-tuple-element.45.lse_ref, ...), custom_call_target="tpu_custom_call" | custom-call | flops 335544320 | bytes 1736704 | tf_op jit(solution)/shard_map/prompt_pairs/pallas_call | solution.py:175
  19.6 0.6 %collective-permute-start.5 = (bf16[128,1024]{1,0:T(8,128)(2,1)S(1)}, bf16[128,1024]{1,0:T(8,128)(2,1)S(1)}, u32[]{:S(2)}, u32[]{:S(2)}) collective-permute-start(bf16[128,1024]{1,0:T(8,128)(2,1)S(1)} %get-tuple-element.51), channel_id=1, source_target_pairs={{0,4},{4,0},{8,12},{12,8},{16,20},{20,16},{24,28},{28,24},{1,5},{5... | collective-permute-start | bytes 786440 | tf_op jit(solution)/shard_map/ppermute | solution.py:200
  20.2 1.2 %response_grads.1 = (bf16[128,512]{1,0:T(8,128)(2,1)}, bf16[128,512]{1,0:T(8,128)(2,1)}) custom-call(bf16[128,2560]{1,0:T(8,128)(2,1)S(1)} %get-tuple-element.43.q_ref, bf16[128,2560]{1,0:T(8,128)(2,1)S(1)} %get-tuple-element.44.do_ref, bf16[4,128,640]{2,1,0:T(8,128)(2,1)S(1)} %get-tuple-element.52.p_ref, ...), custom_call_target="tpu_custom_call" | custom-call | flops 167772160 | bytes 2621440 | tf_op jit(solution)/shard_map/response_grads/pallas_call | solution.py:175
  21.4 0.0 collective-permute-done.5
  21.4 0.1 convert_add_fusion
  21.4 0.0 copy-start
  21.5 1.6 %collective-permute-start.6 = (bf16[64,1024]{1,0:T(8,128)(2,1)S(1)}, bf16[64,1024]{1,0:T(8,128)(2,1)S(1)}, u32[]{:S(2)}, u32[]{:S(2)}) collective-permute-start(bf16[64,1024]{1,0:T(8,128)(2,1)S(1)} %slice.57), channel_id=1, source_target_pairs={{0,8},{4,12},{8,0},{12,4},{16,24},{20,28},{24,16},{28,20},{1,9},{5... | collective-permute-start | bytes 393224 | tf_op jit(solution)/shard_map/ppermute | solution.py:200
  23.0 0.0 copy-done
  23.0 1.5 %query_grads.1 = bf16[128,2560]{1,0:T(8,128)(2,1)} custom-call(bf16[4,128,640]{2,1,0:T(8,128)(2,1)S(1)} %get-tuple-element.53.ds_ref.ds0_ref, bf16[4,128,640]{2,1,0:T(8,128)(2,1)S(1)} %get-tuple-element.57.ds1_ref, bf16[4,128,640]{2,1,0:T(8,128)(2,1)S(1)} %get-tuple-element.58.ds2_ref, bf16[128,512]{1,0:T(8,128)(2,1)S(1)} %bitcast.16, ...), custom_call_target="tpu_custom_call" | custom-call | flops 251658240 | bytes 2621440 | tf_op jit(solution)/shard_map/query_grads/pallas_call | solution.py:175
  24.6 2.7 %collective-permute-done.6 = bf16[64,1024]{1,0:T(8,128)(2,1)S(1)} collective-permute-done((bf16[64,1024]{1,0:T(8,128)(2,1)S(1)}, bf16[64,1024]{1,0:T(8,128)(2,1)S(1)}, u32[]{:S(2)}, u32[]{:S(2)}) %collective-permute-start.6) | collective-permute-done | bytes 131104 | tf_op jit(solution)/shard_map/ppermute | solution.py:200
  27.4 1.1 %collective-permute-start.7 = (bf16[16,1024]{1,0:T(8,128)(2,1)S(1)}, bf16[16,1024]{1,0:T(8,128)(2,1)S(1)}, u32[]{:S(2)}, u32[]{:S(2)}) collective-permute-start(bf16[16,1024]{1,0:T(8,128)(2,1)S(1)} %get-tuple-element.65), channel_id=1, source_target_pairs={{0,1},{1,0},{2,3},{3,2},{4,5},{5,4},{6,7},{7,6},{8,9},{9,8},{10,11... | collective-permute-start | bytes 98312 | tf_op jit(solution)/shard_map/ppermute | solution.py:307
  28.5 2.4 %collective-permute-start.9 = (bf16[16,1024]{1,0:T(8,128)(2,1)S(1)}, bf16[16,1024]{1,0:T(8,128)(2,1)S(1)}, u32[]{:S(2)}, u32[]{:S(2)}) collective-permute-start(bf16[16,1024]{1,0:T(8,128)(2,1)S(1)} %get-tuple-element.66), channel_id=1, source_target_pairs={{0,3},{1,2},{2,1},{3,0},{4,7},{5,6},{6,5},{7,4},{8,11},{9,10},{10,... | collective-permute-start | bytes 98312 | tf_op jit(solution)/shard_map/ppermute | solution.py:307
  30.9 0.5 %collective-permute-start.8 = (bf16[16,1024]{1,0:T(8,128)(2,1)S(1)}, bf16[16,1024]{1,0:T(8,128)(2,1)S(1)}, u32[]{:S(2)}, u32[]{:S(2)}) collective-permute-start(bf16[16,1024]{1,0:T(8,128)(2,1)S(1)} %get-tuple-element.67), channel_id=1, source_target_pairs={{0,2},{1,3},{2,0},{3,1},{4,6},{5,7},{6,4},{7,5},{8,10},{9,11},{10,... | collective-permute-start | bytes 98312 | tf_op jit(solution)/shard_map/ppermute | solution.py:307
  31.4 0.0 collective-permute-done.7
  31.4 3.2 %collective-permute-done.9 = bf16[16,1024]{1,0:T(8,128)(2,1)S(1)} collective-permute-done((bf16[16,1024]{1,0:T(8,128)(2,1)S(1)}, bf16[16,1024]{1,0:T(8,128)(2,1)S(1)}, u32[]{:S(2)}, u32[]{:S(2)}) %collective-permute-start.9) | collective-permute-done | bytes 32800 | tf_op jit(solution)/shard_map/ppermute | solution.py:307
  34.6 1.2 %collective-permute-done.8 = bf16[16,1024]{1,0:T(8,128)(2,1)S(1)} collective-permute-done((bf16[16,1024]{1,0:T(8,128)(2,1)S(1)}, bf16[16,1024]{1,0:T(8,128)(2,1)S(1)}, u32[]{:S(2)}, u32[]{:S(2)}) %collective-permute-start.8) | collective-permute-done | bytes 32800 | tf_op jit(solution)/shard_map/ppermute | solution.py:307
  35.8 0.6 %slice_bitcast_fusion = (f32[1,16,512]{2,1,0:T(8,128)}, f32[1,16,512]{2,1,0:T(8,128)}) fusion(f32[16,1024]{1,0:T(8,128)S(1)} %fusion.1), kind=kLoop, calls=%fused_computation.7 | loop fusion | bytes 131072 | tf_op jit(solution)/shard_map/broadcast_in_dim | solution.py:313
  (10 shorter events, 0.1 us)
Async XLA Ops:
  1.4 9.4 %collective-permute-start.2 = (bf16[16,1024]{1,0:T(8,128)(2,1)S(1)}, bf16[16,1024]{1,0:T(8,128)(2,1)S(1)}, u32[]{:S(2)}, u32[]{:S(2)}) collective-permute-start(bf16[16,1024]{1,0:T(8,128)(2,1)S(1)} %pad_maximum_fusion.1), channel_id=1, source_target_pairs={{3,0},{2,1},{1,2},{0,3},{7,4},{6,5},{5,6},{4,7},{11,8},{10,9},{9,1... | collective-permute-start | bytes 98312 | tf_op jit(solution)/shard_map/ppermute | solution.py:239
  6.4 4.8 %collective-permute-start.1 = (bf16[16,1024]{1,0:T(8,128)(2,1)S(1)}, bf16[16,1024]{1,0:T(8,128)(2,1)S(1)}, u32[]{:S(2)}, u32[]{:S(2)}) collective-permute-start(bf16[16,1024]{1,0:T(8,128)(2,1)S(1)} %pad_maximum_fusion.1), channel_id=1, source_target_pairs={{2,0},{3,1},{0,2},{1,3},{6,4},{7,5},{4,6},{5,7},{10,8},{11,9},{8,1... | collective-permute-start | bytes 98312 | tf_op jit(solution)/shard_map/ppermute | solution.py:239
  6.4 4.8 %collective-permute-start = (bf16[16,1024]{1,0:T(8,128)(2,1)S(1)}, bf16[16,1024]{1,0:T(8,128)(2,1)S(1)}, u32[]{:S(2)}, u32[]{:S(2)}) collective-permute-start(bf16[16,1024]{1,0:T(8,128)(2,1)S(1)} %pad_maximum_fusion.1), channel_id=1, source_target_pairs={{1,0},{0,1},{3,2},{2,3},{5,4},{4,5},{7,6},{6,7},{9,8},{8,9},{11,10... | collective-permute-start | bytes 98312 | tf_op jit(solution)/shard_map/ppermute | solution.py:239
  11.3 5.0 %collective-permute-start.3 = (bf16[64,1024]{1,0:T(8,128)(2,1)S(1)}, bf16[64,1024]{1,0:T(8,128)(2,1)S(1)}, u32[]{:S(2)}, u32[]{:S(2)}) collective-permute-start(bf16[64,1024]{1,0:T(8,128)(2,1)S(1)} %pad_maximum_fusion), channel_id=1, source_target_pairs={{0,8},{4,12},{8,0},{12,4},{16,24},{20,28},{24,16},{28,20},{1,9},{5... | collective-permute-start | bytes 393224 | tf_op jit(solution)/shard_map/ppermute | solution.py:200
  16.3 2.0 %collective-permute-start.4 = (bf16[128,1024]{1,0:T(8,128)(2,1)S(1)}, bf16[128,1024]{1,0:T(8,128)(2,1)S(1)}, u32[]{:S(2)}, u32[]{:S(2)}) collective-permute-start(bf16[128,1024]{1,0:T(8,128)(2,1)S(1)} %constant_dynamic-update-slice_fusion.kv_ref.k1_ref), channel_id=1, source_target_pairs={{0,4},{4,0},{8,12},{12,8},{16,20},{20,16},{24,28},{28,24},{1,5},{5... | collective-permute-start | bytes 786440 | tf_op jit(solution)/shard_map/ppermute | solution.py:200
  19.6 1.7 %collective-permute-start.5 = (bf16[128,1024]{1,0:T(8,128)(2,1)S(1)}, bf16[128,1024]{1,0:T(8,128)(2,1)S(1)}, u32[]{:S(2)}, u32[]{:S(2)}) collective-permute-start(bf16[128,1024]{1,0:T(8,128)(2,1)S(1)} %get-tuple-element.51), channel_id=1, source_target_pairs={{0,4},{4,0},{8,12},{12,8},{16,20},{20,16},{24,28},{28,24},{1,5},{5... | collective-permute-start | bytes 786440 | tf_op jit(solution)/shard_map/ppermute | solution.py:200
  21.4 1.6 %copy-start = (bf16[1,128,512]{2,1,0:T(8,128)(2,1)S(1)}, bf16[1,128,512]{2,1,0:T(8,128)(2,1)}, u32[]{:S(2)}) copy-start(bf16[1,128,512]{2,1,0:T(8,128)(2,1)} %param.11) | copy-start | bytes 393220
  21.5 5.8 %collective-permute-start.6 = (bf16[64,1024]{1,0:T(8,128)(2,1)S(1)}, bf16[64,1024]{1,0:T(8,128)(2,1)S(1)}, u32[]{:S(2)}, u32[]{:S(2)}) collective-permute-start(bf16[64,1024]{1,0:T(8,128)(2,1)S(1)} %slice.57), channel_id=1, source_target_pairs={{0,8},{4,12},{8,0},{12,4},{16,24},{20,28},{24,16},{28,20},{1,9},{5... | collective-permute-start | bytes 393224 | tf_op jit(solution)/shard_map/ppermute | solution.py:200
  27.4 4.1 %collective-permute-start.7 = (bf16[16,1024]{1,0:T(8,128)(2,1)S(1)}, bf16[16,1024]{1,0:T(8,128)(2,1)S(1)}, u32[]{:S(2)}, u32[]{:S(2)}) collective-permute-start(bf16[16,1024]{1,0:T(8,128)(2,1)S(1)} %get-tuple-element.65), channel_id=1, source_target_pairs={{0,1},{1,0},{2,3},{3,2},{4,5},{5,4},{6,7},{7,6},{8,9},{9,8},{10,11... | collective-permute-start | bytes 98312 | tf_op jit(solution)/shard_map/ppermute | solution.py:307
  28.5 6.1 %collective-permute-start.9 = (bf16[16,1024]{1,0:T(8,128)(2,1)S(1)}, bf16[16,1024]{1,0:T(8,128)(2,1)S(1)}, u32[]{:S(2)}, u32[]{:S(2)}) collective-permute-start(bf16[16,1024]{1,0:T(8,128)(2,1)S(1)} %get-tuple-element.66), channel_id=1, source_target_pairs={{0,3},{1,2},{2,1},{3,0},{4,7},{5,6},{6,5},{7,4},{8,11},{9,10},{10,... | collective-permute-start | bytes 98312 | tf_op jit(solution)/shard_map/ppermute | solution.py:307
  30.9 4.8 %collective-permute-start.8 = (bf16[16,1024]{1,0:T(8,128)(2,1)S(1)}, bf16[16,1024]{1,0:T(8,128)(2,1)S(1)}, u32[]{:S(2)}, u32[]{:S(2)}) collective-permute-start(bf16[16,1024]{1,0:T(8,128)(2,1)S(1)} %get-tuple-element.67), channel_id=1, source_target_pairs={{0,2},{1,3},{2,0},{3,1},{4,6},{5,7},{6,4},{7,5},{8,10},{9,11},{10,... | collective-permute-start | bytes 98312 | tf_op jit(solution)/shard_map/ppermute | solution.py:307

commit v3 on v2

v3 whole, which is shorter than its diff:
```python
import functools

import jax
import jax.numpy as jnp
from jax import lax
from jax.experimental import pallas as pl
from jax.experimental.pallas import tpu as pltpu
from jax.sharding import PartitionSpec as P

HQ = 20
HK = 4
DH = 128
GROUP = 4
PB = 16
RATIO = HQ // HK
LOG2E = 1.4426950408889634
FAR = 1e30
MIB = 1 << 20

NT = (((1,), (1,)), ((), ()))
NN = (((1,), (0,)), ((), ()))
TN = (((0,), (0,)), ((), ()))


def dot(a, b, dims):
    return lax.dot_general(a, b, dims, preferred_element_type=jnp.float32)


def head_rows(ref, g):
    first = g * RATIO
    return jnp.concatenate(
        [ref[:, (first + r) * DH : (first + r + 1) * DH] for r in range(RATIO)], axis=0
    )


def head_cols(g):
    return slice(g * DH, (g + 1) * DH)


def pair_terms(scores, dprob, lse_rows, delta_rows, keep):
    nk, nq = scores.shape
    probs = jnp.exp2((scores * (LOG2E / DH**0.5)).reshape(nk // 8, 8, nq) - lse_rows)
    if keep is not None:
        probs = jnp.where(keep, probs, 0.0)
    dscore = probs * (dprob.reshape(nk // 8, 8, nq) - delta_rows)
    return (
        probs.reshape(nk, nq).astype(jnp.bfloat16),
        dscore.reshape(nk, nq).astype(jnp.bfloat16),
    )


def load_kernel(
    q_hbm, do_hbm, o_hbm, k_hbm, v_hbm, ln_hbm,
    q_ref, do_ref, k_ref, v_ref, ln_ref, delta_ref, o_ref, sems,
):
    span = RATIO * DH
    parts = []
    for g in range(HK):
        cols = slice(g * span, (g + 1) * span)
        parts.append(
            [
                pltpu.make_async_copy(hbm.at[:, cols], ref.at[:, cols], sems.at[g, i])
                for i, (hbm, ref) in enumerate(((do_hbm, do_ref), (o_hbm, o_ref)))
            ]
        )
    later = [
        pltpu.make_async_copy(hbm, ref, sems.at[HK, i])
        for i, (hbm, ref) in enumerate(
            ((q_hbm, q_ref), (k_hbm, k_ref), (v_hbm, v_ref), (ln_hbm, ln_ref))
        )
    ]
    for copy in sum(parts, []) + later:
        copy.start()
    ones = jnp.ones((8, DH), jnp.bfloat16)
    for g in range(HK):
        for copy in parts[g]:
            copy.wait()
        sums = []
        for h in range(g * RATIO, (g + 1) * RATIO):
            cols = slice(h * DH, (h + 1) * DH)
            prod = do_ref[:, cols].astype(jnp.float32) * o_ref[:, cols].astype(jnp.float32)
            high = prod.astype(jnp.bfloat16)
            low = (prod - high.astype(jnp.float32)).astype(jnp.bfloat16)
            sums.append(dot(ones, high, NT) + dot(ones, low, NT))
        delta_ref[g] = jnp.concatenate(sums, axis=1)
    for copy in later:
        copy.wait()


def self_kernel(
    len_ref, seen_in, q_ref, do_ref, k_ref, v_ref, delta_ref, ln_ref, p_ref, ds_ref, lse_ref, seen_ref
):
    rows = q_ref.shape[0]
    live = lax.broadcasted_iota(jnp.int32, (8, rows), 1) < len_ref[0]
    seen_ref[...] = jnp.full(seen_ref.shape, seen_in[0], jnp.int32)
    key_at = lax.broadcasted_iota(jnp.int32, (rows, RATIO * rows), 0)
    query_at = lax.broadcasted_iota(jnp.int32, (rows, RATIO * rows), 1) % rows
    keep = (key_at <= query_at).reshape(rows // 8, 8, RATIO * rows)
    for g in range(HK):
        lse_rows = jnp.concatenate(
            [
                jnp.where(live, jnp.broadcast_to(ln_ref[h] * LOG2E, (8, rows)), FAR)
                for h in range(g * RATIO, (g + 1) * RATIO)
            ],
            axis=1,
        )
        lse_ref[g] = lse_rows
        cols = head_cols(g)
        p_ref[g], ds_ref[g] = pair_terms(
            dot(k_ref[:, cols], head_rows(q_ref, g), NT),
            dot(v_ref[:, cols], head_rows(do_ref, g), NT),
            lse_rows[None],
            delta_ref[g][None],
            keep,
        )


def response_kernel(q_ref, do_ref, p_ref, ds_ref, gk_ref, gv_ref):
    scale = 1.0 / DH**0.5
    for g in range(HK):
        cols = head_cols(g)
        gv_ref[:, cols] = dot(p_ref[g], head_rows(do_ref, g), NN).astype(gv_ref.dtype)
        gk_ref[:, cols] = (dot(ds_ref[g], head_rows(q_ref, g), NN) * scale).astype(gk_ref.dtype)


def prompt_kernel(
    pieces, across, n_resp, seen_ref, q_ref, do_ref, lse_ref, delta_ref, kv_ref, ds_ref, part_ref
):
    scale = 1.0 / DH**0.5
    my_row = lax.rem(lax.axis_index("dp"), GROUP)
    my_col = lax.axis_index("resp")
    far = []
    for core, row, k in pieces:
        block = source(my_col, k, n_resp) * GROUP + (my_row ^ (row << 1) ^ core ^ across)
        far.append(jnp.where(seen_ref[...] > block, 0.0, FAR))
    far = [jnp.concatenate([f] * (lse_ref.shape[2] // f.shape[1]), axis=1) for f in far]
    for g in range(HK):
        lse_rows = jnp.concatenate(
            [jnp.broadcast_to((lse_ref[g] + f)[None], (PB // 8,) + lse_ref.shape[1:]) for f in far],
            axis=0,
        )
        q = head_rows(q_ref, g)
        do = head_rows(do_ref, g)
        cols = head_cols(g)
        vcols = slice(cols.start + HK * DH, cols.stop + HK * DH)
        p16, ds16 = pair_terms(
            dot(kv_ref[:, cols], q, NT),
            dot(kv_ref[:, vcols], do, NT),
            lse_rows,
            delta_ref[g][None],
            None,
        )
        ds_ref[g] = ds16
        part_ref[:, cols] = (dot(ds16, q, NN) * scale).astype(part_ref.dtype)
        part_ref[:, vcols] = dot(p16, do, NN).astype(part_ref.dtype)


def query_kernel(ds0_ref, ds1_ref, ds2_ref, k0_ref, k1_ref, k2_ref, gq_ref):
    rows = gq_ref.shape[0]
    scale = 1.0 / DH**0.5
    for g in range(HK):
        cols = head_cols(g)
        ds = jnp.concatenate([ds0_ref[g], ds1_ref[g], ds2_ref[g]], axis=0)
        keys = jnp.concatenate([k0_ref[:, cols], k1_ref[:, cols], k2_ref[:, cols]], axis=0)
        out = (dot(ds, keys, TN) * scale).astype(gq_ref.dtype)
        for r in range(RATIO):
            h = g * RATIO + r
            gq_ref[:, h * DH : (h + 1) * DH] = out[r * rows : (r + 1) * rows]


VMEM = pl.BlockSpec(memory_space=pltpu.VMEM)
SMEM = pl.BlockSpec(memory_space=pltpu.SMEM)
HBM = pl.BlockSpec(memory_space=pltpu.HBM)


def call(kernel, name, outs, scalars, arrays, flops, place=VMEM, scratch=()):
    nbytes = sum(a.size * a.dtype.itemsize for a in arrays)
    if place is HBM:
        arrays = [pltpu.with_memory_space_constraint(a, pltpu.HBM) for a in arrays]
    return pl.pallas_call(
        kernel,
        name=name,
        out_shape=outs,
        in_specs=[SMEM] * len(scalars) + [place] * len(arrays),
        out_specs=jax.tree.map(lambda _: VMEM, outs),
        scratch_shapes=scratch,
        compiler_params=pltpu.CompilerParams(vmem_limit_bytes=24 * MIB),
        cost_estimate=pl.CostEstimate(flops=flops, bytes_accessed=nbytes, transcendentals=0),
    )(*scalars, *arrays)


def source(col, k, count):
    if count & (count - 1) == 0:
        return col ^ k
    if isinstance(col, int):
        return (col - k) % count
    return lax.rem(col + count - k, count)


def pairs(core, row, k):
    n_dp, n_resp = lax.axis_size("dp"), lax.axis_size("resp")
    return [
        ((d ^ core ^ row << 1) * n_resp + source(r, k, n_resp), d * n_resp + r)
        for d in range(n_dp)
        for r in range(n_resp)
    ]


def fetch(array, *step):
    return lax.ppermute(array, ("dp", "resp"), pairs(*step))


def give(array, *step):
    return lax.ppermute(array, ("dp", "resp"), [(i, j) for j, i in pairs(*step)])


def shards(
    queries,
    resp_keys,
    resp_values,
    grad_out,
    forward_out,
    log_norm,
    prompt_keys,
    prompt_values,
    resp_len,
    seen_blocks,
):
    rows = queries.shape[1]
    width = resp_keys.shape[2]
    n_resp = lax.axis_size("resp")
    ln = jnp.transpose(log_norm, (2, 0, 1))
    f32, b16 = jnp.float32, jnp.bfloat16
    macs = HQ * rows * DH

    if n_resp == 4:
        near, relay = (1, 2), (1, 2)
    else:
        near, relay = tuple(range(1, n_resp)), None
    first = [(0, 0, 0)] + [(1, 0, k) for k in near]
    extra = [(0, 0, relay[0] ^ relay[1])] if relay else []
    pieces = first + extra + [(c ^ 1, 1, k) for c, _, k in first] + [(c, 1, k) for c, _, k in extra]
    n_first, n_half = len(first) * PB, len(pieces) * PB // 2

    def visit(kv, across, kind):
        nk = kv.shape[0]
        return call(
            functools.partial(prompt_kernel, pieces, across, n_resp),
            "prompt_pairs",
            (
                jax.ShapeDtypeStruct((HK, nk, RATIO * rows), b16),
                jax.ShapeDtypeStruct((nk, 2 * width), kind),
            ),
            (),
            (seen, q, do, lse, delta, kv),
            8 * macs * nk,
        )

    own = lax.optimization_barrier(jnp.concatenate([prompt_keys[0], prompt_values[0]], axis=1))
    got = [own] + [fetch(own, 1, 0, k) for k in near]
    q, do, kr, vr, ln, delta = call(
        load_kernel,
        "load_delta",
        (
            jax.ShapeDtypeStruct((rows, HQ * DH), b16),
            jax.ShapeDtypeStruct((rows, HQ * DH), b16),
            jax.ShapeDtypeStruct((rows, width), b16),
            jax.ShapeDtypeStruct((rows, width), b16),
            jax.ShapeDtypeStruct((HQ, 1, rows), f32),
            jax.ShapeDtypeStruct((HK, 8, RATIO * rows), f32),
        ),
        (),
        (queries[0], grad_out[0], forward_out[0], resp_keys[0], resp_values[0], ln),
        macs,
        HBM,
        (pltpu.VMEM((rows, HQ * DH), b16), pltpu.SemaphoreType.DMA((HK + 1, 4))),
    )
    got, q, do, kr, vr, ln, delta, resp_len, seen_blocks = lax.optimization_barrier(
        (got, q, do, kr, vr, ln, delta, resp_len, seen_blocks)
    )

    bundle = jnp.concatenate(got, 0)
    moved = [fetch(bundle, 1, 1, 0)]
    if relay:
        moved = [fetch(got[relay[1]], 1, 0, relay[0])] + moved
        moved = moved + [fetch(got[relay[1]], 1, 1, relay[0])]
    p_self, ds_self, lse, seen = call(
        self_kernel,
        "self_pairs",
        (
            jax.ShapeDtypeStruct((HK, rows, RATIO * rows), b16),
            jax.ShapeDtypeStruct((HK, rows, RATIO * rows), b16),
            jax.ShapeDtypeStruct((HK, 8, RATIO * rows), f32),
            jax.ShapeDtypeStruct((8, DH), jnp.int32),
        ),
        (resp_len, seen_blocks),
        (q, do, kr, vr, delta, ln),
        4 * macs * rows,
    )
    moved, p_self, ds_self, lse, seen = lax.optimization_barrier(
        (moved, p_self, ds_self, lse, seen)
    )
    half = jnp.concatenate([bundle] + moved, 0)

    other = fetch(half, 1, 0, 0)
    ds_half, part_half = visit(half, 0, f32)
    other, ds_half, part_half = lax.optimization_barrier((other, ds_half, part_half))
    ds_other, part_other = visit(other, 1, b16)

    back = fetch(part_other, 1, 0, 0)
    grad_rk, grad_rv = call(
        response_kernel,
        "response_grads",
        (
            jax.ShapeDtypeStruct((rows, width), b16),
            jax.ShapeDtypeStruct((rows, width), b16),
        ),
        (),
        (q, do, p_self, ds_self),
        4 * macs * rows,
    )
    back, grad_rk, grad_rv = lax.optimization_barrier((back, grad_rk, grad_rv))
    total = part_half + back.astype(f32)
    low, high = total[:n_half], total[n_half:]
    moved = [give(high[:n_first].astype(b16), 1, 1, 0)]
    if relay:
        moved.append(give(low[n_first:].astype(b16), 1, 0, relay[0]))
        moved.append(give(high[n_first:].astype(b16), 1, 1, relay[0]))
    grad_q = call(
        query_kernel,
        "query_grads",
        jax.ShapeDtypeStruct((rows, HQ * DH), b16),
        (),
        (ds_self, ds_half, ds_other, kr, half, other),
        2 * macs * (rows + half.shape[0] + other.shape[0]),
    )
    moved, grad_q = lax.optimization_barrier((moved, grad_q))
    total = low[:n_first] + moved[0].astype(f32)
    sums = [total[i * PB : (i + 1) * PB] for i in range(len(first))]
    for piece in moved[1:]:
        sums[relay[1]] = sums[relay[1]] + piece.astype(f32)
    total = sums[0]
    for k in near:
        total = total + give(sums[k].astype(b16), 1, 0, k).astype(f32)
    return (
        grad_q[None],
        grad_rk[None],
        grad_rv[None],
        total[None, :, :width],
        total[None, :, width:],
    )


def solution(mesh):
    by_both, by_block = P(("dp", "resp"), None, None), P("resp", "dp", None)
    return jax.shard_map(
        shards,
        mesh=mesh,
        in_specs=(by_both,) * 6 + (by_block,) * 2 + (P(("dp", "resp")),) * 2,
        out_specs=(by_both,) * 3 + (by_block,) * 2,
        check_vma=False,
    )
```

time: 36.7 us -> 35.4 us (0.965)
  waiting for transfers between devices: 10.9 us -> 9.82 us
    ppermute x10 -> x12, waiting for transfers between devices: 10.9 us -> 9.82 us  [the longest x5 5.22 us: give(): lax.ppermute(array, ('dp', 'resp'), [(i, j) for j, i in pairs(*step)])]
    ppermute x10 -> x12, starting transfers between devices: 13.4 us -> 13.1 us  [the longest x7 8.67 us: fetch(): return lax.ppermute(array, ('dp', 'resp'), pairs(*step))]
    pallas_call x5 -> x6, Pallas kernels: 8.44 us -> 8.44 us  [call(): pl.pallas_call(kernel, name=name, out_shape=outs, in_specs=[SMEM] * len(s...]
  transfers between devices with their start and end apart: 10 -> 12, of which waited for: 5 -> 9; matrix products, arithmetic and copies ran while one was open for 0% -> 0% of each run, Pallas kernels for 20% -> 20%
where the time goes in v3:
time: 35.4 us; the launch traced here: 35 us
  starting transfers between devices  13.1 us (37%)
  waiting for transfers between devices  9.82 us (28%)
  Pallas kernels  8.44 us (24%)
  between operations  2.05 us (6%)
  other arithmetic  0.88 us (2%)
  local copies, waits for them, and re-layouts  0.68 us (2%)
    ppermute x7, starting transfers between devices, fetch(): return lax.ppermute(array, ('dp', 'resp'), pairs(*step))  8.67 us
    pallas_call x6, Pallas kernels, call(): pl.pallas_call(kernel, name=name, out_shape=outs, in_specs=[SMEM] * len(s...  8.44 us
    ppermute x5, waiting for transfers between devices, give(): lax.ppermute(array, ('dp', 'resp'), [(i, j) for j, i in pairs(*step)])  5.22 us
    ppermute x7, waiting for transfers between devices, fetch(): return lax.ppermute(array, ('dp', 'resp'), pairs(*step))  4.6 us
    ppermute x5, starting transfers between devices, give(): lax.ppermute(array, ('dp', 'resp'), [(i, j) for j, i in pairs(*step)])  4.46 us
    concatenate x1, other arithmetic, shards(): jnp.concatenate([prompt_keys[0], prompt_values[0]], axis=1)  0.74 us
  transfers between devices with their start and end apart: 12, of which 9 were waited for; matrix products, arithmetic and copies ran while one was open for 0% of the time, Pallas kernels for 20%

profile of v3, /device:TPU:0, one launch (start us, length us, event | category | flops | bytes accessed | tf_op | source)
XLA Modules:
  0.0 35.0 jit_solution(944605070580951794)
XLA Ops:
  0.6 0.7 %pad_maximum_fusion.1 = bf16[16,1024]{1,0:T(8,128)(2,1)S(1)} fusion(bf16[16,512]{1,0:T(8,128)(2,1)} %bitcast.21, bf16[16,512]{1,0:T(8,128)(2,1)} %bitcast.22), kind=kLoop, calls=%fused_computation.11 | loop fusion | flops 65536 | bytes 65536 | tf_op jit(solution)/shard_map/concatenate | solution.py:259
  1.4 3.5 %collective-permute-start.1 = (bf16[16,1024]{1,0:T(8,128)(2,1)S(1)}, bf16[16,1024]{1,0:T(8,128)(2,1)S(1)}, u32[]{:S(2)}, u32[]{:S(2)}) collective-permute-start(bf16[16,1024]{1,0:T(8,128)(2,1)S(1)} %pad_maximum_fusion.1), channel_id=1, source_target_pairs={{6,0},{7,1},{4,2},{5,3},{2,4},{3,5},{0,6},{1,7},{14,8},{15,9},{12,... | collective-permute-start | bytes 98312 | tf_op jit(solution)/shard_map/ppermute | solution.py:210
  4.8 1.9 %collective-permute-start = (bf16[16,1024]{1,0:T(8,128)(2,1)S(1)}, bf16[16,1024]{1,0:T(8,128)(2,1)S(1)}, u32[]{:S(2)}, u32[]{:S(2)}) collective-permute-start(bf16[16,1024]{1,0:T(8,128)(2,1)S(1)} %pad_maximum_fusion.1), channel_id=1, source_target_pairs={{5,0},{4,1},{7,2},{6,3},{1,4},{0,5},{3,6},{2,7},{13,8},{12,9},{15,... | collective-permute-start | bytes 98312 | tf_op jit(solution)/shard_map/ppermute | solution.py:210
  6.7 2.5 %load_delta.1 = (bf16[128,2560]{1,0:T(8,128)(2,1)S(1)}, bf16[128,2560]{1,0:T(8,128)(2,1)S(1)}, bf16[128,512]{1,0:T(8,128)(2,1)S(1)}, bf16[128,512]{1,0:T(8,128)(...) custom-call(bf16[128,2560]{1,0:T(8,128)(2,1)} %bitcast.15, bf16[128,2560]{1,0:T(8,128)(2,1)} %bitcast.16, ...), custom_call_target="tpu_custom_call" | custom-call | flops 327680 | bytes 2238464 | tf_op jit(solution)/shard_map/load_delta/pallas_call | solution.py:180
  10.5 0.0 collective-permute-done.1
  10.5 0.0 collective-permute-done
  10.5 1.0 %collective-permute-start.4 = (bf16[16,1024]{1,0:T(8,128)(2,1)S(1)}, bf16[16,1024]{1,0:T(8,128)(2,1)S(1)}, u32[]{:S(2)}, u32[]{:S(2)}) collective-permute-start(bf16[16,1024]{1,0:T(8,128)(2,1)S(1)} %collective-permute-done.1), channel_id=1, source_target_pairs={{13,0},{12,1},{15,2},{14,3},{9,4},{8,5},{11,6},{10,7},{5,8},{4,9},... | collective-permute-start | bytes 98312 | tf_op jit(solution)/shard_map/ppermute | solution.py:210
  11.5 1.7 %collective-permute-start.2 = (bf16[16,1024]{1,0:T(8,128)(2,1)S(1)}, bf16[16,1024]{1,0:T(8,128)(2,1)S(1)}, u32[]{:S(2)}, u32[]{:S(2)}) collective-permute-start(bf16[16,1024]{1,0:T(8,128)(2,1)S(1)} %collective-permute-done.1), channel_id=1, source_target_pairs={{5,0},{4,1},{7,2},{6,3},{1,4},{0,5},{3,6},{2,7},{13,8},{12,9},{15,... | collective-permute-start | bytes 98312 | tf_op jit(solution)/shard_map/ppermute | solution.py:210
  13.3 0.1 collective-permute-start.3
  13.4 0.7 %self_pairs.1 = (bf16[4,128,640]{2,1,0:T(8,128)(2,1)S(1)}, bf16[4,128,640]{2,1,0:T(8,128)(2,1)S(1)}, f32[4,8,640]{2,1,0:T(8,128)S(1)}, s32[8,128]{1,0:T(8,128)S(1)}) custom-call(s32[1]{0:T(128)S(6)} %copy.20.len_ref, s32[1]{0:T(128)S(6)} %copy.21.seen_in, bf16[128,2560]{1,0:T(8,128)(2,1)S(1)} %get-tuple-element.60.q_ref, ...), custom_call_target="tpu_custom_call" | custom-call | flops 167772160 | bytes 1665024 | tf_op jit(solution)/shard_map/self_pairs/pallas_call | solution.py:180
  14.0 1.1 %collective-permute-done.4 = bf16[16,1024]{1,0:T(8,128)(2,1)S(1)} collective-permute-done((bf16[16,1024]{1,0:T(8,128)(2,1)S(1)}, bf16[16,1024]{1,0:T(8,128)(2,1)S(1)}, u32[]{:S(2)}, u32[]{:S(2)}) %collective-permute-start.4) | collective-permute-done | bytes 32800 | tf_op jit(solution)/shard_map/ppermute | solution.py:210
  15.2 0.7 %collective-permute-done.2 = bf16[16,1024]{1,0:T(8,128)(2,1)S(1)} collective-permute-done((bf16[16,1024]{1,0:T(8,128)(2,1)S(1)}, bf16[16,1024]{1,0:T(8,128)(2,1)S(1)}, u32[]{:S(2)}, u32[]{:S(2)}) %collective-permute-start.2) | collective-permute-done | bytes 32800 | tf_op jit(solution)/shard_map/ppermute | solution.py:210
  15.9 2.5 %collective-permute-done.3 = bf16[48,1024]{1,0:T(8,128)(2,1)S(1)} collective-permute-done((bf16[48,1024]{1,0:T(8,128)(2,1)S(1)}, bf16[48,1024]{1,0:T(8,128)(2,1)S(1)}, u32[]{:S(2)}, u32[]{:S(2)}) %collective-permute-start.3) | collective-permute-done | bytes 98336 | tf_op jit(solution)/shard_map/ppermute | solution.py:210
  18.4 0.2 collective-permute-start.5
  18.6 1.3 %prompt_pairs.2 = (bf16[4,128,640]{2,1,0:T(8,128)(2,1)S(1)}, f32[128,1024]{1,0:T(8,128)S(1)}) custom-call(s32[8,128]{1,0:T(8,128)S(1)} %get-tuple-element.73.seen_ref, bf16[128,2560]{1,0:T(8,128)(2,1)S(1)} %get-tuple-element.60.q_ref, bf16[128,2560]{1,0:T(8,128)(2,1)S(1)} %get-tuple-element.61.do_ref, f32[4,8,640]{2,1,0:T(8,128)S(1)} %get-tuple-element.74.lse_ref, ...), custom_call_target="tpu_custom_call" | custom-call | flops 335544320 | bytes 1740800 | tf_op jit(solution)/shard_map/prompt_pairs/pallas_call | solution.py:180
  19.9 0.1 collective-permute-done.5.kv_ref.k2_ref
  20.0 1.3 %prompt_pairs.3 = (bf16[4,128,640]{2,1,0:T(8,128)(2,1)S(1)}, bf16[128,1024]{1,0:T(8,128)(2,1)S(1)}) custom-call(s32[8,128]{1,0:T(8,128)S(1)} %get-tuple-element.73.seen_ref, bf16[128,2560]{1,0:T(8,128)(2,1)S(1)} %get-tuple-element.60.q_ref, bf16[128,2560]{1,0:T(8,128)(2,1)S(1)} %get-tuple-element.61.do_ref, f32[4,8,640]{2,1,0:T(8,128)S(1)} %get-tuple-element.74.lse_ref, ...), custom_call_target="tpu_custom_call" | custom-call | flops 335544320 | bytes 1740800 | tf_op jit(solution)/shard_map/prompt_pairs/pallas_call | solution.py:180
  21.3 0.3 collective-permute-start.6
  21.7 1.2 %response_grads.1 = (bf16[128,512]{1,0:T(8,128)(2,1)}, bf16[128,512]{1,0:T(8,128)(2,1)}) custom-call(bf16[128,2560]{1,0:T(8,128)(2,1)S(1)} %get-tuple-element.60.q_ref, bf16[128,2560]{1,0:T(8,128)(2,1)S(1)} %get-tuple-element.61.do_ref, bf16[4,128,640]{2,1,0:T(8,128)(2,1)S(1)} %get-tuple-element.80.p_ref, ...), custom_call_target="tpu_custom_call" | custom-call | flops 167772160 | bytes 2621440 | tf_op jit(solution)/shard_map/response_grads/pallas_call | solution.py:180
  22.8 0.1 collective-permute-done.6
  22.9 0.1 fusion.3
  23.0 0.4 %collective-permute-start.7 = (bf16[48,1024]{1,0:T(8,128)(2,1)S(1)}, bf16[48,1024]{1,0:T(8,128)(2,1)S(1)}, u32[]{:S(2)}, u32[]{:S(2)}) collective-permute-start(bf16[48,1024]{1,0:T(8,128)(2,1)S(1)} %slice.46), channel_id=1, source_target_pairs={{0,12},{1,13},{2,14},{3,15},{4,8},{5,9},{6,10},{7,11},{8,4},{9,5},... | collective-permute-start | bytes 294920 | tf_op jit(solution)/shard_map/ppermute | solution.py:214
  23.5 1.1 %collective-permute-start.9 = (bf16[16,1024]{1,0:T(8,128)(2,1)S(1)}, bf16[16,1024]{1,0:T(8,128)(2,1)S(1)}, u32[]{:S(2)}, u32[]{:S(2)}) collective-permute-start(bf16[16,1024]{1,0:T(8,128)(2,1)S(1)} %get-tuple-element.95), channel_id=1, source_target_pairs={{0,13},{1,12},{2,15},{3,14},{4,9},{5,8},{6,11},{7,10},{8,5},{9,4},... | collective-permute-start | bytes 98312 | tf_op jit(solution)/shard_map/ppermute | solution.py:214
  24.6 1.6 %collective-permute-start.8 = (bf16[16,1024]{1,0:T(8,128)(2,1)S(1)}, bf16[16,1024]{1,0:T(8,128)(2,1)S(1)}, u32[]{:S(2)}, u32[]{:S(2)}) collective-permute-start(bf16[16,1024]{1,0:T(8,128)(2,1)S(1)} %get-tuple-element.96), channel_id=1, source_target_pairs={{0,5},{1,4},{2,7},{3,6},{4,1},{5,0},{6,3},{7,2},{8,13},{9,12},{10,... | collective-permute-start | bytes 98312 | tf_op jit(solution)/shard_map/ppermute | solution.py:214
  26.2 1.6 %query_grads.1 = bf16[128,2560]{1,0:T(8,128)(2,1)} custom-call(bf16[4,128,640]{2,1,0:T(8,128)(2,1)S(1)} %get-tuple-element.81.ds_ref.ds0_ref, bf16[4,128,640]{2,1,0:T(8,128)(2,1)S(1)} %get-tuple-element.85.ds1_ref, bf16[4,128,640]{2,1,0:T(8,128)(2,1)S(1)} %get-tuple-element.86.ds2_ref, bf16[128,512]{1,0:T(8,128)(2,1)S(1)} %get-tuple-element.62.k_ref.k0_ref, ...), custom_call_target="tpu_custom_call" | custom-call | flops 251658240 | bytes 2621440 | tf_op jit(solution)/shard_map/query_grads/pallas_call | solution.py:180
  27.8 0.1 collective-permute-done.9
  27.9 0.7 %collective-permute-done.8 = bf16[16,1024]{1,0:T(8,128)(2,1)S(1)} collective-permute-done((bf16[16,1024]{1,0:T(8,128)(2,1)S(1)}, bf16[16,1024]{1,0:T(8,128)(2,1)S(1)}, u32[]{:S(2)}, u32[]{:S(2)}) %collective-permute-start.8) | collective-permute-done | bytes 32800 | tf_op jit(solution)/shard_map/ppermute | solution.py:214
  28.5 0.0 collective-permute-done.7
  28.6 1.1 %collective-permute-start.10 = (bf16[16,1024]{1,0:T(8,128)(2,1)S(1)}, bf16[16,1024]{1,0:T(8,128)(2,1)S(1)}, u32[]{:S(2)}, u32[]{:S(2)}) collective-permute-start(bf16[16,1024]{1,0:T(8,128)(2,1)S(1)} %slice.67), channel_id=1, source_target_pairs={{0,5},{1,4},{2,7},{3,6},{4,1},{5,0},{6,3},{7,2},{8,13},{9,12},{10,... | collective-permute-start | bytes 98312 | tf_op jit(solution)/shard_map/ppermute | solution.py:214
  29.7 0.2 collective-permute-start.11
  29.9 2.1 %collective-permute-done.10 = bf16[16,1024]{1,0:T(8,128)(2,1)S(1)} collective-permute-done((bf16[16,1024]{1,0:T(8,128)(2,1)S(1)}, bf16[16,1024]{1,0:T(8,128)(2,1)S(1)}, u32[]{:S(2)}, u32[]{:S(2)}) %collective-permute-start.10) | collective-permute-done | bytes 32800 | tf_op jit(solution)/shard_map/ppermute | solution.py:214
  32.0 2.4 %collective-permute-done.11 = bf16[16,1024]{1,0:T(8,128)(2,1)S(1)} collective-permute-done((bf16[16,1024]{1,0:T(8,128)(2,1)S(1)}, bf16[16,1024]{1,0:T(8,128)(2,1)S(1)}, u32[]{:S(2)}, u32[]{:S(2)}) %collective-permute-start.11) | collective-permute-done | bytes 32800 | tf_op jit(solution)/shard_map/ppermute | solution.py:214
  34.4 0.6 %slice_bitcast_fusion = (f32[1,16,512]{2,1,0:T(8,128)}, f32[1,16,512]{2,1,0:T(8,128)}) fusion(f32[16,1024]{1,0:T(8,128)S(1)} %fusion.2), kind=kLoop, calls=%fused_computation.9 | loop fusion | bytes 131072 | tf_op jit(solution)/shard_map/broadcast_in_dim | solution.py:350
  (13 shorter events, 0.1 us)
Async XLA Ops:
  1.4 9.1 %collective-permute-start.1 = (bf16[16,1024]{1,0:T(8,128)(2,1)S(1)}, bf16[16,1024]{1,0:T(8,128)(2,1)S(1)}, u32[]{:S(2)}, u32[]{:S(2)}) collective-permute-start(bf16[16,1024]{1,0:T(8,128)(2,1)S(1)} %pad_maximum_fusion.1), channel_id=1, source_target_pairs={{6,0},{7,1},{4,2},{5,3},{2,4},{3,5},{0,6},{1,7},{14,8},{15,9},{12,... | collective-permute-start | bytes 98312 | tf_op jit(solution)/shard_map/ppermute | solution.py:210
  4.8 5.7 %collective-permute-start = (bf16[16,1024]{1,0:T(8,128)(2,1)S(1)}, bf16[16,1024]{1,0:T(8,128)(2,1)S(1)}, u32[]{:S(2)}, u32[]{:S(2)}) collective-permute-start(bf16[16,1024]{1,0:T(8,128)(2,1)S(1)} %pad_maximum_fusion.1), channel_id=1, source_target_pairs={{5,0},{4,1},{7,2},{6,3},{1,4},{0,5},{3,6},{2,7},{13,8},{12,9},{15,... | collective-permute-start | bytes 98312 | tf_op jit(solution)/shard_map/ppermute | solution.py:210
  10.5 4.6 %collective-permute-start.4 = (bf16[16,1024]{1,0:T(8,128)(2,1)S(1)}, bf16[16,1024]{1,0:T(8,128)(2,1)S(1)}, u32[]{:S(2)}, u32[]{:S(2)}) collective-permute-start(bf16[16,1024]{1,0:T(8,128)(2,1)S(1)} %collective-permute-done.1), channel_id=1, source_target_pairs={{13,0},{12,1},{15,2},{14,3},{9,4},{8,5},{11,6},{10,7},{5,8},{4,9},... | collective-permute-start | bytes 98312 | tf_op jit(solution)/shard_map/ppermute | solution.py:210
  11.5 4.4 %collective-permute-start.2 = (bf16[16,1024]{1,0:T(8,128)(2,1)S(1)}, bf16[16,1024]{1,0:T(8,128)(2,1)S(1)}, u32[]{:S(2)}, u32[]{:S(2)}) collective-permute-start(bf16[16,1024]{1,0:T(8,128)(2,1)S(1)} %collective-permute-done.1), channel_id=1, source_target_pairs={{5,0},{4,1},{7,2},{6,3},{1,4},{0,5},{3,6},{2,7},{13,8},{12,9},{15,... | collective-permute-start | bytes 98312 | tf_op jit(solution)/shard_map/ppermute | solution.py:210
  13.3 5.1 %collective-permute-start.3 = (bf16[48,1024]{1,0:T(8,128)(2,1)S(1)}, bf16[48,1024]{1,0:T(8,128)(2,1)S(1)}, u32[]{:S(2)}, u32[]{:S(2)}) collective-permute-start(bf16[48,1024]{1,0:T(8,128)(2,1)S(1)} %pad_maximum_fusion), channel_id=1, source_target_pairs={{12,0},{13,1},{14,2},{15,3},{8,4},{9,5},{10,6},{11,7},{4,8},{5,9},... | collective-permute-start | bytes 294920 | tf_op jit(solution)/shard_map/ppermute | solution.py:210
  18.4 1.6 %collective-permute-start.5 = (bf16[128,1024]{1,0:T(8,128)(2,1)S(1)}, bf16[128,1024]{1,0:T(8,128)(2,1)S(1)}, u32[]{:S(2)}, u32[]{:S(2)}) collective-permute-start(bf16[128,1024]{1,0:T(8,128)(2,1)S(1)} %constant_dynamic-update-slice_fusion.kv_ref.k1_ref), channel_id=1, source_target_pairs={{4,0},{5,1},{6,2},{7,3},{0,4},{1,5},{2,6},{3,7},{12,8},{13,9},{14,... | collective-permute-start | bytes 786440 | tf_op jit(solution)/shard_map/ppermute | solution.py:210
  21.3 1.6 %collective-permute-start.6 = (bf16[128,1024]{1,0:T(8,128)(2,1)S(1)}, bf16[128,1024]{1,0:T(8,128)(2,1)S(1)}, u32[]{:S(2)}, u32[]{:S(2)}) collective-permute-start(bf16[128,1024]{1,0:T(8,128)(2,1)S(1)} %get-tuple-element.79), channel_id=1, source_target_pairs={{4,0},{5,1},{6,2},{7,3},{0,4},{1,5},{2,6},{3,7},{12,8},{13,9},{14,... | collective-permute-start | bytes 786440 | tf_op jit(solution)/shard_map/ppermute | solution.py:210
  23.0 5.5 %collective-permute-start.7 = (bf16[48,1024]{1,0:T(8,128)(2,1)S(1)}, bf16[48,1024]{1,0:T(8,128)(2,1)S(1)}, u32[]{:S(2)}, u32[]{:S(2)}) collective-permute-start(bf16[48,1024]{1,0:T(8,128)(2,1)S(1)} %slice.46), channel_id=1, source_target_pairs={{0,12},{1,13},{2,14},{3,15},{4,8},{5,9},{6,10},{7,11},{8,4},{9,5},... | collective-permute-start | bytes 294920 | tf_op jit(solution)/shard_map/ppermute | solution.py:214
  23.5 4.3 %collective-permute-start.9 = (bf16[16,1024]{1,0:T(8,128)(2,1)S(1)}, bf16[16,1024]{1,0:T(8,128)(2,1)S(1)}, u32[]{:S(2)}, u32[]{:S(2)}) collective-permute-start(bf16[16,1024]{1,0:T(8,128)(2,1)S(1)} %get-tuple-element.95), channel_id=1, source_target_pairs={{0,13},{1,12},{2,15},{3,14},{4,9},{5,8},{6,11},{7,10},{8,5},{9,4},... | collective-permute-start | bytes 98312 | tf_op jit(solution)/shard_map/ppermute | solution.py:214
  24.6 3.9 %collective-permute-start.8 = (bf16[16,1024]{1,0:T(8,128)(2,1)S(1)}, bf16[16,1024]{1,0:T(8,128)(2,1)S(1)}, u32[]{:S(2)}, u32[]{:S(2)}) collective-permute-start(bf16[16,1024]{1,0:T(8,128)(2,1)S(1)} %get-tuple-element.96), channel_id=1, source_target_pairs={{0,5},{1,4},{2,7},{3,6},{4,1},{5,0},{6,3},{7,2},{8,13},{9,12},{10,... | collective-permute-start | bytes 98312 | tf_op jit(solution)/shard_map/ppermute | solution.py:214
  28.6 3.4 %collective-permute-start.10 = (bf16[16,1024]{1,0:T(8,128)(2,1)S(1)}, bf16[16,1024]{1,0:T(8,128)(2,1)S(1)}, u32[]{:S(2)}, u32[]{:S(2)}) collective-permute-start(bf16[16,1024]{1,0:T(8,128)(2,1)S(1)} %slice.67), channel_id=1, source_target_pairs={{0,5},{1,4},{2,7},{3,6},{4,1},{5,0},{6,3},{7,2},{8,13},{9,12},{10,... | collective-permute-start | bytes 98312 | tf_op jit(solution)/shard_map/ppermute | solution.py:214
  29.7 4.7 %collective-permute-start.11 = (bf16[16,1024]{1,0:T(8,128)(2,1)S(1)}, bf16[16,1024]{1,0:T(8,128)(2,1)S(1)}, u32[]{:S(2)}, u32[]{:S(2)}) collective-permute-start(bf16[16,1024]{1,0:T(8,128)(2,1)S(1)} %fusion.1), channel_id=1, source_target_pairs={{0,6},{1,7},{2,4},{3,5},{4,2},{5,3},{6,0},{7,1},{8,14},{9,15},{10,... | collective-permute-start | bytes 98312 | tf_op jit(solution)/shard_map/ppermute | solution.py:214

commit v4 on v3

--- a/solution.py
+++ b/solution.py
@@ -49,68 +49,60 @@
     )
 
 
-def load_kernel(
-    q_hbm, do_hbm, o_hbm, k_hbm, v_hbm, ln_hbm,
-    q_ref, do_ref, k_ref, v_ref, ln_ref, delta_ref, o_ref, sems,
+def scalar_kernel(len_ref, seen_ref, len_rows, seen_rows):
+    len_rows[...] = jnp.full(len_rows.shape, len_ref[0], jnp.int32)
+    seen_rows[...] = jnp.full(seen_rows.shape, seen_ref[0], jnp.int32)
+
+
+def self_kernel(
+    len_ref, q_hbm, do_hbm, o_hbm, ln_hbm, k_hbm, v_hbm,
+    q_ref, do_ref, k_ref, v_ref, p_ref, ds_ref, lse_ref, delta_ref,
+    o_ref, ln_ref, sems,
 ):
+    rows = q_ref.shape[0]
     span = RATIO * DH
+    first = [
+        pltpu.make_async_copy(hbm, ref, sems.at[HK, i])
+        for i, (hbm, ref) in enumerate(((ln_hbm, ln_ref), (k_hbm, k_ref), (v_hbm, v_ref)))
+    ]
     parts = []
     for g in range(HK):
         cols = slice(g * span, (g + 1) * span)
         parts.append(
             [
                 pltpu.make_async_copy(hbm.at[:, cols], ref.at[:, cols], sems.at[g, i])
-                for i, (hbm, ref) in enumerate(((do_hbm, do_ref), (o_hbm, o_ref)))
+                for i, (hbm, ref) in enumerate(((do_hbm, do_ref), (o_hbm, o_ref), (q_hbm, q_ref)))
             ]
         )
-    later = [
-        pltpu.make_async_copy(hbm, ref, sems.at[HK, i])
-        for i, (hbm, ref) in enumerate(
-            ((q_hbm, q_ref), (k_hbm, k_ref), (v_hbm, v_ref), (ln_hbm, ln_ref))
-        )
-    ]
-    for copy in sum(parts, []) + later:
+    for copy in parts[0] + first + sum(parts[1:], []):
         copy.start()
     ones = jnp.ones((8, DH), jnp.bfloat16)
-    for g in range(HK):
-        for copy in parts[g]:
+    live = lax.broadcasted_iota(jnp.int32, (8, rows), 1) < len_ref[...]
+    key_at = lax.broadcasted_iota(jnp.int32, (rows, RATIO * rows), 0)
+    query_at = lax.broadcasted_iota(jnp.int32, (rows, RATIO * rows), 1) % rows
+    keep = (key_at <= query_at).reshape(rows // 8, 8, RATIO * rows)
+    for g in range(HK):
+        for copy in parts[g] + (first if g == 0 else []):
             copy.wait()
-        sums = []
+        lse_parts, delta_parts = [], []
         for h in range(g * RATIO, (g + 1) * RATIO):
             cols = slice(h * DH, (h + 1) * DH)
             prod = do_ref[:, cols].astype(jnp.float32) * o_ref[:, cols].astype(jnp.float32)
             high = prod.astype(jnp.bfloat16)
             low = (prod - high.astype(jnp.float32)).astype(jnp.bfloat16)
-            sums.append(dot(ones, high, NT) + dot(ones, low, NT))
-        delta_ref[g] = jnp.concatenate(sums, axis=1)
-    for copy in later:
-        copy.wait()
-
-
-def self_kernel(
-    len_ref, seen_in, q_ref, do_ref, k_ref, v_ref, delta_ref, ln_ref, p_ref, ds_ref, lse_ref, seen_ref
-):
-    rows = q_ref.shape[0]
-    live = lax.broadcasted_iota(jnp.int32, (8, rows), 1) < len_ref[0]
-    seen_ref[...] = jnp.full(seen_ref.shape, seen_in[0], jnp.int32)
-    key_at = lax.broadcasted_iota(jnp.int32, (rows, RATIO * rows), 0)
-    query_at = lax.broadcasted_iota(jnp.int32, (rows, RATIO * rows), 1) % rows
-    keep = (key_at <= query_at).reshape(rows // 8, 8, RATIO * rows)
-    for g in range(HK):
-        lse_rows = jnp.concatenate(
-            [
-                jnp.where(live, jnp.broadcast_to(ln_ref[h] * LOG2E, (8, rows)), FAR)
-                for h in range(g * RATIO, (g + 1) * RATIO)
-            ],
-            axis=1,
-        )
+            delta_parts.append(dot(ones, high, NT) + dot(ones, low, NT))
+            row = jnp.broadcast_to(ln_ref[h] * LOG2E, (8, rows))
+            lse_parts.append(jnp.where(live, row, FAR))
+        lse_rows = jnp.concatenate(lse_parts, axis=1)
+        delta_rows = jnp.concatenate(delta_parts, axis=1)
         lse_ref[g] = lse_rows
+        delta_ref[g] = delta_rows
         cols = head_cols(g)
         p_ref[g], ds_ref[g] = pair_terms(
             dot(k_ref[:, cols], head_rows(q_ref, g), NT),
             dot(v_ref[:, cols], head_rows(do_ref, g), NT),
             lse_rows[None],
-            delta_ref[g][None],
+            delta_rows[None],
             keep,
         )
 
@@ -173,20 +165,19 @@
 HBM = pl.BlockSpec(memory_space=pltpu.HBM)
 
 
-def call(kernel, name, outs, scalars, arrays, flops, place=VMEM, scratch=()):
-    nbytes = sum(a.size * a.dtype.itemsize for a in arrays)
-    if place is HBM:
-        arrays = [pltpu.with_memory_space_constraint(a, pltpu.HBM) for a in arrays]
+def call(kernel, name, outs, scalars, arrays, flops, in_hbm=(), scratch=()):
+    nbytes = sum(a.size * a.dtype.itemsize for a in (*arrays, *in_hbm))
+    in_hbm = [pltpu.with_memory_space_constraint(a, pltpu.HBM) for a in in_hbm]
     return pl.pallas_call(
         kernel,
         name=name,
         out_shape=outs,
-        in_specs=[SMEM] * len(scalars) + [place] * len(arrays),
+        in_specs=[SMEM] * len(scalars) + [VMEM] * len(arrays) + [HBM] * len(in_hbm),
         out_specs=jax.tree.map(lambda _: VMEM, outs),
         scratch_shapes=scratch,
         compiler_params=pltpu.CompilerParams(vmem_limit_bytes=24 * MIB),
         cost_estimate=pl.CostEstimate(flops=flops, bytes_accessed=nbytes, transcendentals=0),
-    )(*scalars, *arrays)
+    )(*scalars, *arrays, *in_hbm)
 
 
 def source(col, k, count):
@@ -258,47 +249,47 @@
 
     own = lax.optimization_barrier(jnp.concatenate([prompt_keys[0], prompt_values[0]], axis=1))
     got = [own] + [fetch(own, 1, 0, k) for k in near]
-    q, do, kr, vr, ln, delta = call(
-        load_kernel,
-        "load_delta",
+    length, seen = call(
+        scalar_kernel,
+        "spread_scalars",
+        (jax.ShapeDtypeStruct((8, rows), jnp.int32), jax.ShapeDtypeStruct((8, DH), jnp.int32)),
+        (resp_len, seen_blocks),
+        (),
+        0,
+    )
+    got, length, seen = lax.optimization_barrier((got, length, seen))
+
+    bundle = lax.optimization_barrier(jnp.concatenate(got, 0))
+    moved = [fetch(bundle, 1, 1, 0)]
+    if relay:
+        at = relay[1] * PB
+        moved = [fetch(bundle[at : at + PB], 1, 0, relay[0])] + moved
+        moved = moved + [fetch(bundle[at : at + PB], 1, 1, relay[0])]
+    q, do, kr, vr, p_self, ds_self, lse, delta = call(
+        self_kernel,
+        "self_pairs",
         (
             jax.ShapeDtypeStruct((rows, HQ * DH), b16),
             jax.ShapeDtypeStruct((rows, HQ * DH), b16),
             jax.ShapeDtypeStruct((rows, width), b16),
             jax.ShapeDtypeStruct((rows, width), b16),
-            jax.ShapeDtypeStruct((HQ, 1, rows), f32),
+            jax.ShapeDtypeStruct((HK, rows, RATIO * rows), b16),
+            jax.ShapeDtypeStruct((HK, rows, RATIO * rows), b16),
+            jax.ShapeDtypeStruct((HK, 8, RATIO * rows), f32),
             jax.ShapeDtypeStruct((HK, 8, RATIO * rows), f32),
         ),
         (),
-        (queries[0], grad_out[0], forward_out[0], resp_keys[0], resp_values[0], ln),
-        macs,
-        HBM,
-        (pltpu.VMEM((rows, HQ * DH), b16), pltpu.SemaphoreType.DMA((HK + 1, 4))),
-    )
-    got, q, do, kr, vr, ln, delta, resp_len, seen_blocks = lax.optimization_barrier(
-        (got, q, do, kr, vr, ln, delta, resp_len, seen_blocks)
-    )
-
-    bundle = jnp.concatenate(got, 0)
-    moved = [fetch(bundle, 1, 1, 0)]
-    if relay:
-        moved = [fetch(got[relay[1]], 1, 0, relay[0])] + moved
-        moved = moved + [fetch(got[relay[1]], 1, 1, relay[0])]
-    p_self, ds_self, lse, seen = call(
-        self_kernel,
-        "self_pairs",
+        (length,),
+        5 * macs * rows,
+        (queries[0], grad_out[0], forward_out[0], ln, resp_keys[0], resp_values[0]),
         (
-            jax.ShapeDtypeStruct((HK, rows, RATIO * rows), b16),
-            jax.ShapeDtypeStruct((HK, rows, RATIO * rows), b16),
-            jax.ShapeDtypeStruct((HK, 8, RATIO * rows), f32),
-            jax.ShapeDtypeStruct((8, DH), jnp.int32),
+            pltpu.VMEM((rows, HQ * DH), b16),
+            pltpu.VMEM((HQ, 1, rows), f32),
+            pltpu.SemaphoreType.DMA((HK + 1, 3)),
         ),
-        (resp_len, seen_blocks),
-        (q, do, kr, vr, delta, ln),
-        4 * macs * rows,
-    )
-    moved, p_self, ds_self, lse, seen = lax.optimization_barrier(
-        (moved, p_self, ds_self, lse, seen)
+    )
+    moved, q, do, kr, vr, p_self, ds_self, lse, delta = lax.optimization_barrier(
+        (moved, q, do, kr, vr, p_self, ds_self, lse, delta)
     )
     half = jnp.concatenate([bundle] + moved, 0)
 
@@ -339,6 +330,7 @@
     sums = [total[i * PB : (i + 1) * PB] for i in range(len(first))]
     for piece in moved[1:]:
         sums[relay[1]] = sums[relay[1]] + piece.astype(f32)
+    sums = lax.optimization_barrier(sums)
     total = sums[0]
     for k in near:
         total = total + give(sums[k].astype(b16), 1, 0, k).astype(f32)

time: 35.4 us -> 33.3 us (0.941)
  waiting for transfers between devices: 9.82 us -> 5.45 us
  starting transfers between devices: 13.1 us -> 15.3 us
    ppermute x7, waiting for transfers between devices: 4.6 us -> 0.56 us  [fetch(): return lax.ppermute(array, ('dp', 'resp'), pairs(*step))]
    ppermute x5, starting transfers between devices: 4.46 us -> 6.05 us  [give(): lax.ppermute(array, ('dp', 'resp'), [(i, j) for j, i in pairs(*step)])]
    ppermute x7, starting transfers between devices: 8.67 us -> 9.21 us  [fetch(): return lax.ppermute(array, ('dp', 'resp'), pairs(*step))]
  transfers between devices with their start and end apart: 12 -> 12, of which waited for: 9 -> 7; matrix products, arithmetic and copies ran while one was open for 0% -> 0% of each run, Pallas kernels for 20% -> 22%
where the time goes in v4:
time: 33.3 us; the launch traced here: 33 us
  starting transfers between devices  15.3 us (46%)
  Pallas kernels  8.7 us (26%)
  waiting for transfers between devices  5.45 us (16%)
  between operations  2.05 us (6%)
  other arithmetic  0.89 us (3%)
  local copies, waits for them, and re-layouts  0.65 us (2%)
    ppermute x7, starting transfers between devices, fetch(): return lax.ppermute(array, ('dp', 'resp'), pairs(*step))  9.21 us
    pallas_call x6, Pallas kernels, call(): pl.pallas_call(kernel, name=name, out_shape=outs, in_specs=[SMEM] * len(s...  8.7 us
    ppermute x5, starting transfers between devices, give(): lax.ppermute(array, ('dp', 'resp'), [(i, j) for j, i in pairs(*step)])  6.05 us
    ppermute x5, waiting for transfers between devices, give(): lax.ppermute(array, ('dp', 'resp'), [(i, j) for j, i in pairs(*step)])  4.89 us
    concatenate x1, other arithmetic, shards(): jnp.concatenate([prompt_keys[0], prompt_values[0]], axis=1)  0.74 us
  transfers between devices with their start and end apart: 12, of which 7 were waited for; matrix products, arithmetic and copies ran while one was open for 0% of the time, Pallas kernels for 22%

profile of v4, /device:TPU:0, one launch (start us, length us, event | category | flops | bytes accessed | tf_op | source)
XLA Modules:
  0.0 33.0 jit_solution(3682590212572094235)
XLA Ops:
  0.6 0.7 %pad_maximum_fusion.2 = bf16[16,1024]{1,0:T(8,128)(2,1)S(1)} fusion(bf16[16,512]{1,0:T(8,128)(2,1)} %bitcast.21, bf16[16,512]{1,0:T(8,128)(2,1)} %bitcast.22), kind=kLoop, calls=%fused_computation.9 | loop fusion | flops 65536 | bytes 65536 | tf_op jit(solution)/shard_map/concatenate | solution.py:250
  1.4 3.5 %collective-permute-start.1 = (bf16[16,1024]{1,0:T(8,128)(2,1)S(1)}, bf16[16,1024]{1,0:T(8,128)(2,1)S(1)}, u32[]{:S(2)}, u32[]{:S(2)}) collective-permute-start(bf16[16,1024]{1,0:T(8,128)(2,1)S(1)} %pad_maximum_fusion.2), channel_id=1, source_target_pairs={{6,0},{7,1},{4,2},{5,3},{2,4},{3,5},{0,6},{1,7},{14,8},{15,9},{12,... | collective-permute-start | bytes 98312 | tf_op jit(solution)/shard_map/ppermute | solution.py:201
  4.8 1.9 %collective-permute-start = (bf16[16,1024]{1,0:T(8,128)(2,1)S(1)}, bf16[16,1024]{1,0:T(8,128)(2,1)S(1)}, u32[]{:S(2)}, u32[]{:S(2)}) collective-permute-start(bf16[16,1024]{1,0:T(8,128)(2,1)S(1)} %pad_maximum_fusion.2), channel_id=1, source_target_pairs={{5,0},{4,1},{7,2},{6,3},{1,4},{0,5},{3,6},{2,7},{13,8},{12,9},{15,... | collective-permute-start | bytes 98312 | tf_op jit(solution)/shard_map/ppermute | solution.py:201
  8.0 0.0 collective-permute-done.1
  8.0 0.3 collective-permute-done
  8.3 1.7 %collective-permute-start.3 = (bf16[48,1024]{1,0:T(8,128)(2,1)S(1)}, bf16[48,1024]{1,0:T(8,128)(2,1)S(1)}, u32[]{:S(2)}, u32[]{:S(2)}) collective-permute-start(bf16[48,1024]{1,0:T(8,128)(2,1)S(1)} %pad_maximum_fusion.1), channel_id=1, source_target_pairs={{12,0},{13,1},{14,2},{15,3},{8,4},{9,5},{10,6},{11,7},{4,8},{5,9},... | collective-permute-start | bytes 294920 | tf_op jit(solution)/shard_map/ppermute | solution.py:201
  10.0 1.1 %collective-permute-start.4 = (bf16[16,1024]{1,0:T(8,128)(2,1)S(1)}, bf16[16,1024]{1,0:T(8,128)(2,1)S(1)}, u32[]{:S(2)}, u32[]{:S(2)}) collective-permute-start(bf16[16,1024]{1,0:T(8,128)(2,1)S(1)} %slice.50), channel_id=1, source_target_pairs={{13,0},{12,1},{15,2},{14,3},{9,4},{8,5},{11,6},{10,7},{5,8},{4,9},... | collective-permute-start | bytes 98312 | tf_op jit(solution)/shard_map/ppermute | solution.py:201
  11.1 0.6 %collective-permute-start.2 = (bf16[16,1024]{1,0:T(8,128)(2,1)S(1)}, bf16[16,1024]{1,0:T(8,128)(2,1)S(1)}, u32[]{:S(2)}, u32[]{:S(2)}) collective-permute-start(bf16[16,1024]{1,0:T(8,128)(2,1)S(1)} %slice.50), channel_id=1, source_target_pairs={{5,0},{4,1},{7,2},{6,3},{1,4},{0,5},{3,6},{2,7},{13,8},{12,9},{15,... | collective-permute-start | bytes 98312 | tf_op jit(solution)/shard_map/ppermute | solution.py:201
  11.8 3.4 %self_pairs.1 = (bf16[128,2560]{1,0:T(8,128)(2,1)S(1)}, bf16[128,2560]{1,0:T(8,128)(2,1)S(1)}, bf16[128,512]{1,0:T(8,128)(2,1)S(1)}, bf16[128,512]{1,0:T(8,128)(...) custom-call(s32[8,128]{1,0:T(8,128)S(1)} %get-tuple-element.53.len_r, ...), custom_call_target="tpu_custom_call" | custom-call | flops 209715200 | bytes 2242560 | tf_op jit(solution)/shard_map/self_pairs/pallas_call | solution.py:171
  15.1 0.0 collective-permute-done.4
  15.1 0.0 collective-permute-done.2
  15.1 0.0 collective-permute-done.3
  15.2 0.1 collective-permute-start.5
  15.3 1.3 %prompt_pairs.2 = (bf16[4,128,640]{2,1,0:T(8,128)(2,1)S(1)}, f32[128,1024]{1,0:T(8,128)S(1)}) custom-call(s32[8,128]{1,0:T(8,128)S(1)} %get-tuple-element.64.seen_ref, bf16[128,2560]{1,0:T(8,128)(2,1)S(1)} %get-tuple-element.65.q_ref, bf16[128,2560]{1,0:T(8,128)(2,1)S(1)} %get-tuple-element.66.do_ref, f32[4,8,640]{2,1,0:T(8,128)S(1)} %get-tuple-element.67.lse_ref, ...), custom_call_target="tpu_custom_call" | custom-call | flops 335544320 | bytes 1740800 | tf_op jit(solution)/shard_map/prompt_pairs/pallas_call | solution.py:171
  16.6 0.2 collective-permute-done.5.kv_ref.k2_ref
  16.8 1.3 %prompt_pairs.3 = (bf16[4,128,640]{2,1,0:T(8,128)(2,1)S(1)}, bf16[128,1024]{1,0:T(8,128)(2,1)S(1)}) custom-call(s32[8,128]{1,0:T(8,128)S(1)} %get-tuple-element.64.seen_ref, bf16[128,2560]{1,0:T(8,128)(2,1)S(1)} %get-tuple-element.65.q_ref, bf16[128,2560]{1,0:T(8,128)(2,1)S(1)} %get-tuple-element.66.do_ref, f32[4,8,640]{2,1,0:T(8,128)S(1)} %get-tuple-element.67.lse_ref, ...), custom_call_target="tpu_custom_call" | custom-call | flops 335544320 | bytes 1740800 | tf_op jit(solution)/shard_map/prompt_pairs/pallas_call | solution.py:171
  18.1 0.4 %collective-permute-start.6 = (bf16[128,1024]{1,0:T(8,128)(2,1)S(1)}, bf16[128,1024]{1,0:T(8,128)(2,1)S(1)}, u32[]{:S(2)}, u32[]{:S(2)}) collective-permute-start(bf16[128,1024]{1,0:T(8,128)(2,1)S(1)} %get-tuple-element.73), channel_id=1, source_target_pairs={{4,0},{5,1},{6,2},{7,3},{0,4},{1,5},{2,6},{3,7},{12,8},{13,9},{14,... | collective-permute-start | bytes 786440 | tf_op jit(solution)/shard_map/ppermute | solution.py:201
  18.5 1.2 %response_grads.1 = (bf16[128,512]{1,0:T(8,128)(2,1)}, bf16[128,512]{1,0:T(8,128)(2,1)}) custom-call(bf16[128,2560]{1,0:T(8,128)(2,1)S(1)} %get-tuple-element.65.q_ref, bf16[128,2560]{1,0:T(8,128)(2,1)S(1)} %get-tuple-element.66.do_ref, bf16[4,128,640]{2,1,0:T(8,128)(2,1)S(1)} %get-tuple-element.74.p_ref, ...), custom_call_target="tpu_custom_call" | custom-call | flops 167772160 | bytes 2621440 | tf_op jit(solution)/shard_map/response_grads/pallas_call | solution.py:171
  19.6 0.1 collective-permute-done.6
  19.7 0.1 fusion.1
  19.8 1.5 %collective-permute-start.7 = (bf16[48,1024]{1,0:T(8,128)(2,1)S(1)}, bf16[48,1024]{1,0:T(8,128)(2,1)S(1)}, u32[]{:S(2)}, u32[]{:S(2)}) collective-permute-start(bf16[48,1024]{1,0:T(8,128)(2,1)S(1)} %slice.51), channel_id=1, source_target_pairs={{0,12},{1,13},{2,14},{3,15},{4,8},{5,9},{6,10},{7,11},{8,4},{9,5},... | collective-permute-start | bytes 294920 | tf_op jit(solution)/shard_map/ppermute | solution.py:205
  21.3 1.4 %collective-permute-start.9 = (bf16[16,1024]{1,0:T(8,128)(2,1)S(1)}, bf16[16,1024]{1,0:T(8,128)(2,1)S(1)}, u32[]{:S(2)}, u32[]{:S(2)}) collective-permute-start(bf16[16,1024]{1,0:T(8,128)(2,1)S(1)} %get-tuple-element.93), channel_id=1, source_target_pairs={{0,13},{1,12},{2,15},{3,14},{4,9},{5,8},{6,11},{7,10},{8,5},{9,4},... | collective-permute-start | bytes 98312 | tf_op jit(solution)/shard_map/ppermute | solution.py:205
  22.6 0.4 %collective-permute-start.8 = (bf16[16,1024]{1,0:T(8,128)(2,1)S(1)}, bf16[16,1024]{1,0:T(8,128)(2,1)S(1)}, u32[]{:S(2)}, u32[]{:S(2)}) collective-permute-start(bf16[16,1024]{1,0:T(8,128)(2,1)S(1)} %get-tuple-element.94), channel_id=1, source_target_pairs={{0,5},{1,4},{2,7},{3,6},{4,1},{5,0},{6,3},{7,2},{8,13},{9,12},{10,... | collective-permute-start | bytes 98312 | tf_op jit(solution)/shard_map/ppermute | solution.py:205
  23.0 1.6 %query_grads.1 = bf16[128,2560]{1,0:T(8,128)(2,1)} custom-call(bf16[4,128,640]{2,1,0:T(8,128)(2,1)S(1)} %get-tuple-element.75.ds_ref.ds0_ref, bf16[4,128,640]{2,1,0:T(8,128)(2,1)S(1)} %get-tuple-element.79.ds1_ref, bf16[4,128,640]{2,1,0:T(8,128)(2,1)S(1)} %get-tuple-element.80.ds2_ref, bf16[128,512]{1,0:T(8,128)(2,1)S(1)} %get-tuple-element.81.k0_ref, ...), custom_call_target="tpu_custom_call" | custom-call | flops 251658240 | bytes 2621440 | tf_op jit(solution)/shard_map/query_grads/pallas_call | solution.py:171
  24.5 1.0 %collective-permute-done.9 = bf16[16,1024]{1,0:T(8,128)(2,1)S(1)} collective-permute-done((bf16[16,1024]{1,0:T(8,128)(2,1)S(1)}, bf16[16,1024]{1,0:T(8,128)(2,1)S(1)}, u32[]{:S(2)}, u32[]{:S(2)}) %collective-permute-start.9) | collective-permute-done | bytes 32800 | tf_op jit(solution)/shard_map/ppermute | solution.py:205
  25.5 0.5 %collective-permute-done.8 = bf16[16,1024]{1,0:T(8,128)(2,1)S(1)} collective-permute-done((bf16[16,1024]{1,0:T(8,128)(2,1)S(1)}, bf16[16,1024]{1,0:T(8,128)(2,1)S(1)}, u32[]{:S(2)}, u32[]{:S(2)}) %collective-permute-start.8) | collective-permute-done | bytes 32800 | tf_op jit(solution)/shard_map/ppermute | solution.py:205
  26.0 0.0 collective-permute-done.7
  26.0 1.3 %collective-permute-start.10 = (bf16[16,1024]{1,0:T(8,128)(2,1)S(1)}, bf16[16,1024]{1,0:T(8,128)(2,1)S(1)}, u32[]{:S(2)}, u32[]{:S(2)}) collective-permute-start(bf16[16,1024]{1,0:T(8,128)(2,1)S(1)} %get-tuple-element.89), channel_id=1, source_target_pairs={{0,5},{1,4},{2,7},{3,6},{4,1},{5,0},{6,3},{7,2},{8,13},{9,12},{10,... | collective-permute-start | bytes 98312 | tf_op jit(solution)/shard_map/ppermute | solution.py:205
  27.3 1.6 %collective-permute-start.11 = (bf16[16,1024]{1,0:T(8,128)(2,1)S(1)}, bf16[16,1024]{1,0:T(8,128)(2,1)S(1)}, u32[]{:S(2)}, u32[]{:S(2)}) collective-permute-start(bf16[16,1024]{1,0:T(8,128)(2,1)S(1)} %get-tuple-element.90), channel_id=1, source_target_pairs={{0,6},{1,7},{2,4},{3,5},{4,2},{5,3},{6,0},{7,1},{8,14},{9,15},{10,... | collective-permute-start | bytes 98312 | tf_op jit(solution)/shard_map/ppermute | solution.py:205
  28.9 0.5 %collective-permute-done.10 = bf16[16,1024]{1,0:T(8,128)(2,1)S(1)} collective-permute-done((bf16[16,1024]{1,0:T(8,128)(2,1)S(1)}, bf16[16,1024]{1,0:T(8,128)(2,1)S(1)}, u32[]{:S(2)}, u32[]{:S(2)}) %collective-permute-start.10) | collective-permute-done | bytes 32800 | tf_op jit(solution)/shard_map/ppermute | solution.py:205
  29.4 2.9 %collective-permute-done.11 = bf16[16,1024]{1,0:T(8,128)(2,1)S(1)} collective-permute-done((bf16[16,1024]{1,0:T(8,128)(2,1)S(1)}, bf16[16,1024]{1,0:T(8,128)(2,1)S(1)}, u32[]{:S(2)}, u32[]{:S(2)}) %collective-permute-start.11) | collective-permute-done | bytes 32800 | tf_op jit(solution)/shard_map/ppermute | solution.py:205
  32.4 0.6 %slice_bitcast_fusion = (f32[1,16,512]{2,1,0:T(8,128)}, f32[1,16,512]{2,1,0:T(8,128)}) fusion(f32[16,1024]{1,0:T(8,128)S(1)} %convert_add_fusion.1), kind=kLoop, calls=%fused_computation.7 | loop fusion | bytes 131072 | tf_op jit(solution)/shard_map/broadcast_in_dim | solution.py:342
  (10 shorter events, 0.1 us)
Async XLA Ops:
  1.4 6.6 %collective-permute-start.1 = (bf16[16,1024]{1,0:T(8,128)(2,1)S(1)}, bf16[16,1024]{1,0:T(8,128)(2,1)S(1)}, u32[]{:S(2)}, u32[]{:S(2)}) collective-permute-start(bf16[16,1024]{1,0:T(8,128)(2,1)S(1)} %pad_maximum_fusion.2), channel_id=1, source_target_pairs={{6,0},{7,1},{4,2},{5,3},{2,4},{3,5},{0,6},{1,7},{14,8},{15,9},{12,... | collective-permute-start | bytes 98312 | tf_op jit(solution)/shard_map/ppermute | solution.py:201
  4.8 3.5 %collective-permute-start = (bf16[16,1024]{1,0:T(8,128)(2,1)S(1)}, bf16[16,1024]{1,0:T(8,128)(2,1)S(1)}, u32[]{:S(2)}, u32[]{:S(2)}) collective-permute-start(bf16[16,1024]{1,0:T(8,128)(2,1)S(1)} %pad_maximum_fusion.2), channel_id=1, source_target_pairs={{5,0},{4,1},{7,2},{6,3},{1,4},{0,5},{3,6},{2,7},{13,8},{12,9},{15,... | collective-permute-start | bytes 98312 | tf_op jit(solution)/shard_map/ppermute | solution.py:201
  8.3 6.8 %collective-permute-start.3 = (bf16[48,1024]{1,0:T(8,128)(2,1)S(1)}, bf16[48,1024]{1,0:T(8,128)(2,1)S(1)}, u32[]{:S(2)}, u32[]{:S(2)}) collective-permute-start(bf16[48,1024]{1,0:T(8,128)(2,1)S(1)} %pad_maximum_fusion.1), channel_id=1, source_target_pairs={{12,0},{13,1},{14,2},{15,3},{8,4},{9,5},{10,6},{11,7},{4,8},{5,9},... | collective-permute-start | bytes 294920 | tf_op jit(solution)/shard_map/ppermute | solution.py:201
  10.0 5.1 %collective-permute-start.4 = (bf16[16,1024]{1,0:T(8,128)(2,1)S(1)}, bf16[16,1024]{1,0:T(8,128)(2,1)S(1)}, u32[]{:S(2)}, u32[]{:S(2)}) collective-permute-start(bf16[16,1024]{1,0:T(8,128)(2,1)S(1)} %slice.50), channel_id=1, source_target_pairs={{13,0},{12,1},{15,2},{14,3},{9,4},{8,5},{11,6},{10,7},{5,8},{4,9},... | collective-permute-start | bytes 98312 | tf_op jit(solution)/shard_map/ppermute | solution.py:201
  11.1 4.0 %collective-permute-start.2 = (bf16[16,1024]{1,0:T(8,128)(2,1)S(1)}, bf16[16,1024]{1,0:T(8,128)(2,1)S(1)}, u32[]{:S(2)}, u32[]{:S(2)}) collective-permute-start(bf16[16,1024]{1,0:T(8,128)(2,1)S(1)} %slice.50), channel_id=1, source_target_pairs={{5,0},{4,1},{7,2},{6,3},{1,4},{0,5},{3,6},{2,7},{13,8},{12,9},{15,... | collective-permute-start | bytes 98312 | tf_op jit(solution)/shard_map/ppermute | solution.py:201
  15.2 1.6 %collective-permute-start.5 = (bf16[128,1024]{1,0:T(8,128)(2,1)S(1)}, bf16[128,1024]{1,0:T(8,128)(2,1)S(1)}, u32[]{:S(2)}, u32[]{:S(2)}) collective-permute-start(bf16[128,1024]{1,0:T(8,128)(2,1)S(1)} %pad_maximum_fusion.kv_ref.k1_ref), channel_id=1, source_target_pairs={{4,0},{5,1},{6,2},{7,3},{0,4},{1,5},{2,6},{3,7},{12,8},{13,9},{14,... | collective-permute-start | bytes 786440 | tf_op jit(solution)/shard_map/ppermute | solution.py:201
  18.1 1.6 %collective-permute-start.6 = (bf16[128,1024]{1,0:T(8,128)(2,1)S(1)}, bf16[128,1024]{1,0:T(8,128)(2,1)S(1)}, u32[]{:S(2)}, u32[]{:S(2)}) collective-permute-start(bf16[128,1024]{1,0:T(8,128)(2,1)S(1)} %get-tuple-element.73), channel_id=1, source_target_pairs={{4,0},{5,1},{6,2},{7,3},{0,4},{1,5},{2,6},{3,7},{12,8},{13,9},{14,... | collective-permute-start | bytes 786440 | tf_op jit(solution)/shard_map/ppermute | solution.py:201
  19.8 6.2 %collective-permute-start.7 = (bf16[48,1024]{1,0:T(8,128)(2,1)S(1)}, bf16[48,1024]{1,0:T(8,128)(2,1)S(1)}, u32[]{:S(2)}, u32[]{:S(2)}) collective-permute-start(bf16[48,1024]{1,0:T(8,128)(2,1)S(1)} %slice.51), channel_id=1, source_target_pairs={{0,12},{1,13},{2,14},{3,15},{4,8},{5,9},{6,10},{7,11},{8,4},{9,5},... | collective-permute-start | bytes 294920 | tf_op jit(solution)/shard_map/ppermute | solution.py:205
  21.3 4.2 %collective-permute-start.9 = (bf16[16,1024]{1,0:T(8,128)(2,1)S(1)}, bf16[16,1024]{1,0:T(8,128)(2,1)S(1)}, u32[]{:S(2)}, u32[]{:S(2)}) collective-permute-start(bf16[16,1024]{1,0:T(8,128)(2,1)S(1)} %get-tuple-element.93), channel_id=1, source_target_pairs={{0,13},{1,12},{2,15},{3,14},{4,9},{5,8},{6,11},{7,10},{8,5},{9,4},... | collective-permute-start | bytes 98312 | tf_op jit(solution)/shard_map/ppermute | solution.py:205
  22.6 3.3 %collective-permute-start.8 = (bf16[16,1024]{1,0:T(8,128)(2,1)S(1)}, bf16[16,1024]{1,0:T(8,128)(2,1)S(1)}, u32[]{:S(2)}, u32[]{:S(2)}) collective-permute-start(bf16[16,1024]{1,0:T(8,128)(2,1)S(1)} %get-tuple-element.94), channel_id=1, source_target_pairs={{0,5},{1,4},{2,7},{3,6},{4,1},{5,0},{6,3},{7,2},{8,13},{9,12},{10,... | collective-permute-start | bytes 98312 | tf_op jit(solution)/shard_map/ppermute | solution.py:205
  26.0 3.4 %collective-permute-start.10 = (bf16[16,1024]{1,0:T(8,128)(2,1)S(1)}, bf16[16,1024]{1,0:T(8,128)(2,1)S(1)}, u32[]{:S(2)}, u32[]{:S(2)}) collective-permute-start(bf16[16,1024]{1,0:T(8,128)(2,1)S(1)} %get-tuple-element.89), channel_id=1, source_target_pairs={{0,5},{1,4},{2,7},{3,6},{4,1},{5,0},{6,3},{7,2},{8,13},{9,12},{10,... | collective-permute-start | bytes 98312 | tf_op jit(solution)/shard_map/ppermute | solution.py:205
  27.3 5.1 %collective-permute-start.11 = (bf16[16,1024]{1,0:T(8,128)(2,1)S(1)}, bf16[16,1024]{1,0:T(8,128)(2,1)S(1)}, u32[]{:S(2)}, u32[]{:S(2)}) collective-permute-start(bf16[16,1024]{1,0:T(8,128)(2,1)S(1)} %get-tuple-element.90), channel_id=1, source_target_pairs={{0,6},{1,7},{2,4},{3,5},{4,2},{5,3},{6,0},{7,1},{8,14},{9,15},{10,... | collective-permute-start | bytes 98312 | tf_op jit(solution)/shard_map/ppermute | solution.py:205

commit v5 on v4

v5 whole, which is shorter than its diff:
```python
import functools

import jax
import jax.numpy as jnp
from jax import lax
from jax.experimental import pallas as pl
from jax.experimental.pallas import tpu as pltpu
from jax.sharding import PartitionSpec as P

HQ = 20
HK = 4
DH = 128
GROUP = 4
PB = 16
RATIO = HQ // HK
LOG2E = 1.4426950408889634
FAR = 1e30
MIB = 1 << 20

NT = (((1,), (1,)), ((), ()))
NN = (((1,), (0,)), ((), ()))
TN = (((0,), (0,)), ((), ()))


def dot(a, b, dims):
    return lax.dot_general(a, b, dims, preferred_element_type=jnp.float32)


def head_rows(ref, g):
    first = g * RATIO
    return jnp.concatenate(
        [ref[:, (first + r) * DH : (first + r + 1) * DH] for r in range(RATIO)], axis=0
    )


def head_cols(g):
    return slice(g * DH, (g + 1) * DH)


def pair_terms(scores, dprob, lse_rows, delta_rows, keep):
    nk, nq = scores.shape
    probs = jnp.exp2((scores * (LOG2E / DH**0.5)).reshape(nk // 8, 8, nq) - lse_rows)
    if keep is not None:
        probs = jnp.where(keep, probs, 0.0)
    dscore = probs * (dprob.reshape(nk // 8, 8, nq) - delta_rows)
    return (
        probs.reshape(nk, nq).astype(jnp.bfloat16),
        dscore.reshape(nk, nq).astype(jnp.bfloat16),
    )


def load_kernel(len_ref, seen_ref, *refs):
    count = (len(refs) - 2) // 2
    sems, outs = refs[-1], refs[count:-1]
    copies = [
        pltpu.make_async_copy(refs[i], outs[i], sems.at[i]) for i in range(count)
    ]
    for copy in copies:
        copy.start()
    outs[count][...] = jnp.concatenate(
        [jnp.full((8, DH), ref[0], jnp.int32) for ref in (len_ref, seen_ref)], axis=1
    )
    for copy in copies:
        copy.wait()


def self_kernel(
    scalars_ref, q_ref, do_ref, k_ref, v_ref, o_hbm, ln_hbm, p_ref, ds_ref, rows_ref, o_ref, ln_ref, sems
):
    rows = q_ref.shape[0]
    nq = RATIO * rows
    span = RATIO * DH
    first = pltpu.make_async_copy(ln_hbm, ln_ref, sems.at[HK])
    first.start()
    parts = []
    for g in range(HK):
        cols = slice(g * span, (g + 1) * span)
        parts.append(pltpu.make_async_copy(o_hbm.at[:, cols], o_ref.at[:, cols], sems.at[g]))
        parts[g].start()
    ones = jnp.ones((8, DH), jnp.bfloat16)
    live = lax.broadcasted_iota(jnp.int32, (1, rows), 1) < scalars_ref[:1, :rows]
    key_at = lax.broadcasted_iota(jnp.int32, (rows, nq), 0)
    query_at = lax.broadcasted_iota(jnp.int32, (rows, nq), 1) % rows
    keep = (key_at <= query_at).reshape(rows // 8, 8, nq)
    rows_ref[:, nq:] = scalars_ref[:, DH:].astype(jnp.float32)
    for g in range(HK):
        parts[g].wait()
        if g == 0:
            first.wait()
        lse_parts, delta_parts = [], []
        for h in range(g * RATIO, (g + 1) * RATIO):
            cols = slice(h * DH, (h + 1) * DH)
            prod = do_ref[:, cols].astype(jnp.float32) * o_ref[:, cols].astype(jnp.float32)
            high = prod.astype(jnp.bfloat16)
            low = (prod - high.astype(jnp.float32)).astype(jnp.bfloat16)
            delta_parts.append(dot(ones, high, NT) + dot(ones, low, NT))
            lse_parts.append(jnp.where(live, ln_ref[h] * LOG2E, FAR))
        lse_row = jnp.concatenate(lse_parts, axis=1)
        delta_rows = jnp.concatenate(delta_parts, axis=1)
        rows_ref[g : g + 1, :nq] = lse_row
        rows_ref[HK + g : HK + g + 1, :nq] = delta_rows[:1]
        cols = head_cols(g)
        p_ref[g], ds_ref[g] = pair_terms(
            dot(k_ref[:, cols], head_rows(q_ref, g), NT),
            dot(v_ref[:, cols], head_rows(do_ref, g), NT),
            jnp.broadcast_to(lse_row, (8, nq))[None],
            delta_rows[None],
            keep,
        )


def response_kernel(q_ref, do_ref, p_ref, ds_ref, ds2_ref, kv_ref, gk_ref, gv_ref, gq2_ref):
    scale = 1.0 / DH**0.5
    query_kernel(1, ds2_ref, kv_ref, gq2_ref)
    for g in range(HK):
        cols = head_cols(g)
        gv_ref[:, cols] = dot(p_ref[g], head_rows(do_ref, g), NN).astype(gv_ref.dtype)
        gk_ref[:, cols] = (dot(ds_ref[g], head_rows(q_ref, g), NN) * scale).astype(gk_ref.dtype)


def prompt_kernel(pieces, n_resp, cuts, q_ref, do_ref, rows_ref, kv_ref, *refs):
    scale = 1.0 / DH**0.5
    nq = RATIO * q_ref.shape[0]
    before, (ds_ref, *outs) = (refs[0], refs[1:]) if cuts else (None, refs)
    cuts = cuts or (0, kv_ref.shape[0])
    my_row = lax.rem(lax.axis_index("dp"), GROUP)
    my_col = lax.axis_index("resp")
    seen = rows_ref[:, nq:]
    far = []
    for core, row, k in pieces:
        block = source(my_col, k, n_resp) * GROUP + (my_row ^ (row << 1) ^ core)
        far.append(jnp.where(seen > block.astype(jnp.float32), 0.0, FAR))
    far = [jnp.concatenate([f] * (nq // f.shape[1]), axis=1) for f in far]

    def put(sums, cols):
        if before is not None:
            sums = sums + before[:, cols]
        for out, low, high in zip(outs, cuts, cuts[1:]):
            out[:, cols] = sums[low:high].astype(out.dtype)

    for g in range(HK):
        lse = jnp.broadcast_to(rows_ref[g : g + 1, :nq], (8, nq))
        delta = jnp.broadcast_to(rows_ref[HK + g : HK + g + 1, :nq], (8, nq))
        lse_rows = jnp.concatenate(
            [jnp.broadcast_to((lse + f)[None], (PB // 8, 8, nq)) for f in far], axis=0
        )
        q = head_rows(q_ref, g)
        do = head_rows(do_ref, g)
        cols = head_cols(g)
        vcols = slice(cols.start + HK * DH, cols.stop + HK * DH)
        p16, ds16 = pair_terms(
            dot(kv_ref[:, cols], q, NT),
            dot(kv_ref[:, vcols], do, NT),
            lse_rows,
            delta[None],
            None,
        )
        ds_ref[g] = ds16
        put(dot(ds16, q, NN) * scale, cols)
        put(dot(p16, do, NN), vcols)


def query_kernel(count, *refs):
    gq_ref = refs[-1]
    rows = gq_ref.shape[0]
    scale = 1.0 / DH**0.5
    for g in range(HK):
        cols = head_cols(g)
        ds = jnp.concatenate([ref[g] for ref in refs[:count]], axis=0)
        keys = jnp.concatenate([ref[:, cols] for ref in refs[count : 2 * count]], axis=0)
        out = (dot(ds, keys, TN) * scale).astype(gq_ref.dtype)
        for r in range(RATIO):
            h = g * RATIO + r
            gq_ref[:, h * DH : (h + 1) * DH] = out[r * rows : (r + 1) * rows]


def add_kernel(a_ref, b_ref, out_ref):
    out_ref[...] = (a_ref[...] + b_ref[...].astype(jnp.float32)).astype(out_ref.dtype)


VMEM = pl.BlockSpec(memory_space=pltpu.VMEM)
SMEM = pl.BlockSpec(memory_space=pltpu.SMEM)
HBM = pl.BlockSpec(memory_space=pltpu.HBM)


def call(kernel, name, outs, scalars, arrays, flops, in_hbm=(), scratch=()):
    nbytes = sum(a.size * a.dtype.itemsize for a in (*arrays, *in_hbm))
    in_hbm = [pltpu.with_memory_space_constraint(a, pltpu.HBM) for a in in_hbm]
    return pl.pallas_call(
        kernel,
        name=name,
        out_shape=outs,
        in_specs=[SMEM] * len(scalars) + [VMEM] * len(arrays) + [HBM] * len(in_hbm),
        out_specs=jax.tree.map(lambda _: VMEM, outs),
        scratch_shapes=scratch,
        compiler_params=pltpu.CompilerParams(vmem_limit_bytes=24 * MIB),
        cost_estimate=pl.CostEstimate(flops=flops, bytes_accessed=nbytes, transcendentals=0),
    )(*scalars, *arrays, *in_hbm)


def source(col, k, count):
    if count & (count - 1) == 0:
        return col ^ k
    if isinstance(col, int):
        return (col - k) % count
    return lax.rem(col + count - k, count)


def pairs(core, row, k):
    n_dp, n_resp = lax.axis_size("dp"), lax.axis_size("resp")
    return [
        ((d ^ core ^ row << 1) * n_resp + source(r, k, n_resp), d * n_resp + r)
        for d in range(n_dp)
        for r in range(n_resp)
    ]


def fetch(array, *step):
    return lax.ppermute(array, ("dp", "resp"), pairs(*step))


def give(array, *step):
    return lax.ppermute(array, ("dp", "resp"), [(i, j) for j, i in pairs(*step)])


def shards(
    queries,
    resp_keys,
    resp_values,
    grad_out,
    forward_out,
    log_norm,
    prompt_keys,
    prompt_values,
    resp_len,
    seen_blocks,
):
    rows = queries.shape[1]
    width = resp_keys.shape[2]
    n_resp = lax.axis_size("resp")
    ln = jnp.transpose(log_norm, (2, 0, 1))
    f32, b16 = jnp.float32, jnp.bfloat16
    macs = HQ * rows * DH

    if n_resp == 4:
        near, relay = (1, 2), (1, 2)
    else:
        near, relay = tuple(range(1, n_resp)), None
    first = [(0, 0, 0)] + [(1, 0, k) for k in near]
    extra = [(0, 0, relay[0] ^ relay[1])] if relay else []
    pieces = first + extra + [(c ^ 1, 1, k) for c, _, k in first] + [(c, 1, k) for c, _, k in extra]
    n_first, n_half = len(first) * PB, len(pieces) * PB // 2

    array = jax.ShapeDtypeStruct
    full = array((rows, HQ * DH), b16)

    own = lax.optimization_barrier(jnp.concatenate([prompt_keys[0], prompt_values[0]], axis=1))
    got = [own] + [fetch(own, 1, 0, k) for k in near]
    loaded = call(
        load_kernel,
        "load",
        (full, full, *[array((rows, width), b16)] * 2, array((8, 2 * DH), jnp.int32)),
        (resp_len, seen_blocks),
        (),
        0,
        (queries[0], grad_out[0], resp_keys[0], resp_values[0]),
        (pltpu.SemaphoreType.DMA((4,)),),
    )
    got, (q, do, kr, vr, scalars) = lax.optimization_barrier((got, loaded))

    bundle = lax.optimization_barrier(jnp.concatenate(got, 0))
    moved = [fetch(bundle, 1, 1, 0)]
    if relay:
        piece, q, do = lax.optimization_barrier((bundle[relay[1] * PB :][:PB], q, do))
        moved = [fetch(piece, 1, 0, relay[0])] + moved + [fetch(piece, 1, 1, relay[0])]
    q2, do2 = fetch(q, 1, 0, 0), fetch(do, 1, 0, 0)
    worked = call(
        self_kernel,
        "self_pairs",
        (
            array((HK, rows, RATIO * rows), b16),
            array((HK, rows, RATIO * rows), b16),
            array((8, RATIO * rows + DH), f32),
        ),
        (),
        (scalars, q, do, kr, vr),
        5 * macs * rows,
        (forward_out[0], ln),
        (
            pltpu.VMEM((rows, HQ * DH), b16),
            pltpu.VMEM((HQ, 1, rows), f32),
            pltpu.SemaphoreType.DMA((HK + 1,)),
        ),
    )
    moved, (p_self, ds_self, terms) = lax.optimization_barrier((moved, worked))
    half = jnp.concatenate([bundle] + moved, 0)
    terms2 = fetch(terms, 1, 0, 0)

    nk = half.shape[0]
    ds_shape = array((HK, nk, RATIO * rows), b16)

    def visit(name, outs, cuts, arrays):
        return call(
            functools.partial(prompt_kernel, pieces, n_resp, cuts),
            name,
            (ds_shape, *outs),
            (),
            arrays,
            8 * macs * nk,
        )

    ds_half, part = visit("own_pairs", [array((nk, 2 * width), f32)], None, (q, do, terms, half))
    part, terms2, q2, do2 = lax.optimization_barrier((part, terms2, q2, do2))
    cuts = (0, n_first, n_half, n_half + n_first, nk) if relay else (0, n_half, nk)
    kinds = (f32, b16, b16, b16) if relay else (f32, b16)
    cut_shapes = [array((j - i, 2 * width), t) for i, j, t in zip(cuts, cuts[1:], kinds)]
    ds_other, low, *sent = visit("other_pairs", cut_shapes, cuts, (q2, do2, terms2, half, part))

    if relay:
        moved = [
            give(sent[1], 1, 1, 0),
            give(sent[0], 1, 0, relay[0]),
            give(sent[2], 1, 1, relay[0]),
        ]
    else:
        moved = [give(sent[0], 1, 1, 0)]
    *grads, back = call(
        response_kernel,
        "response_grads",
        (array((rows, width), b16), array((rows, width), b16), full),
        (),
        (q, do, p_self, ds_self, ds_other, half),
        4 * macs * rows + 2 * macs * nk,
    )
    moved, (grad_rk, grad_rv) = lax.optimization_barrier((moved, grads))
    back = fetch(back, 1, 0, 0)
    total = low + moved[0].astype(f32)
    sums = [total[i * PB : (i + 1) * PB] for i in range(len(first))]
    for piece in moved[1:]:
        sums[relay[1]] = sums[relay[1]] + piece.astype(f32)
    sums, ds_half = lax.optimization_barrier((sums, ds_half))
    moved = [give(sums[k].astype(b16), 1, 0, k) for k in near]
    grad_q = call(
        functools.partial(query_kernel, 2),
        "query_grads",
        array(full.shape, f32),
        (),
        (ds_self, ds_half, kr, half),
        200 * macs * (rows + nk),
    )
    grad_q, back = lax.optimization_barrier((grad_q, back))
    grad_q = call(add_kernel, "add_grads", full, (), (grad_q, back), 0)
    moved, grad_q = lax.optimization_barrier((moved, grad_q))
    total = sums[0]
    for piece in moved:
        total = total + piece.astype(f32)
    return (
        grad_q[None],
        grad_rk[None],
        grad_rv[None],
        total[None, :, :width],
        total[None, :, width:],
    )


def solution(mesh):
    by_both, by_block = P(("dp", "resp"), None, None), P("resp", "dp", None)
    return jax.shard_map(
        shards,
        mesh=mesh,
        in_specs=(by_both,) * 6 + (by_block,) * 2 + (P(("dp", "resp")),) * 2,
        out_specs=(by_both,) * 3 + (by_block,) * 2,
        check_vma=False,
    )
```

time: 33.3 us -> 32 us (0.961)
  the two profiles are of different devices: /device:TPU:0 before, /device:TPU:1 now
where the time goes in v5:
time: 32 us; the launch traced here: 31.7 us
  starting transfers between devices  14.7 us (46%)
  Pallas kernels  9.61 us (30%)
  waiting for transfers between devices  3.77 us (12%)
  between operations  2.08 us (6%)
  other arithmetic  0.83 us (3%)
  local copies, waits for them, and re-layouts  0.64 us (2%)
    pallas_call x7, Pallas kernels, call(): pl.pallas_call(kernel, name=name, out_shape=outs, in_specs=[SMEM] * len(s...  9.61 us
    ppermute x9, starting transfers between devices, fetch(): return lax.ppermute(array, ('dp', 'resp'), pairs(*step))  8.84 us
    ppermute x5, starting transfers between devices, give(): lax.ppermute(array, ('dp', 'resp'), [(i, j) for j, i in pairs(*step)])  5.9 us
    ppermute x5, waiting for transfers between devices, give(): lax.ppermute(array, ('dp', 'resp'), [(i, j) for j, i in pairs(*step)])  3.62 us
    concatenate x1, other arithmetic, shards(): jnp.concatenate([prompt_keys[0], prompt_values[0]], axis=1)  0.74 us
  transfers between devices with their start and end apart: 14, of which 4 were waited for; matrix products, arithmetic and copies ran while one was open for 0% of the time, Pallas kernels for 26%

profile of v5, /device:TPU:1, one launch (start us, length us, event | category | flops | bytes accessed | tf_op | source)
XLA Modules:
  0.0 31.7 jit_solution(13327020938963229878)
XLA Ops:
  0.6 0.7 %pad_maximum_fusion.2 = bf16[16,1024]{1,0:T(8,128)(2,1)S(1)} fusion(bf16[16,512]{1,0:T(8,128)(2,1)} %bitcast.21, bf16[16,512]{1,0:T(8,128)(2,1)} %bitcast.22), kind=kLoop, calls=%fused_computation.8 | loop fusion | flops 65536 | bytes 65536 | tf_op jit(solution)/shard_map/concatenate | solution.py:257
  1.4 3.7 %collective-permute-start.1 = (bf16[16,1024]{1,0:T(8,128)(2,1)S(1)}, bf16[16,1024]{1,0:T(8,128)(2,1)S(1)}, u32[]{:S(2)}, u32[]{:S(2)}) collective-permute-start(bf16[16,1024]{1,0:T(8,128)(2,1)S(1)} %pad_maximum_fusion.2), channel_id=1, source_target_pairs={{6,0},{7,1},{4,2},{5,3},{2,4},{3,5},{0,6},{1,7},{14,8},{15,9},{12,... | collective-permute-start | bytes 98312 | tf_op jit(solution)/shard_map/ppermute | solution.py:219
  5.1 1.0 %collective-permute-start = (bf16[16,1024]{1,0:T(8,128)(2,1)S(1)}, bf16[16,1024]{1,0:T(8,128)(2,1)S(1)}, u32[]{:S(2)}, u32[]{:S(2)}) collective-permute-start(bf16[16,1024]{1,0:T(8,128)(2,1)S(1)} %pad_maximum_fusion.2), channel_id=1, source_target_pairs={{5,0},{4,1},{7,2},{6,3},{1,4},{0,5},{3,6},{2,7},{13,8},{12,9},{15,... | collective-permute-start | bytes 98312 | tf_op jit(solution)/shard_map/ppermute | solution.py:219
  7.4 1.4 %load.1 = (bf16[128,2560]{1,0:T(8,128)(2,1)S(1)}, bf16[128,2560]{1,0:T(8,128)(2,1)S(1)}, bf16[128,512]{1,0:T(8,128)(2,1)S(1)}, bf16[128,512]{1,0:T(8,128)(2,1)S(1)}, s32[8,256]{1,0:T(8,128)S(1)}) custom-call(s32[1]{0:T(128)S(6)} %copy.15.len_ref, s32[1]{0:T(128)S(6)} %copy.16.seen_ref, bf16[128,2560]{1,0:T(8,128)(2,1)} %bitcast.17, ...), custom_call_target="tpu_custom_call" | custom-call | bytes 1572864 | tf_op jit(solution)/shard_map/load/pallas_call | solution.py:189
  8.8 0.0 collective-permute-done.1
  8.8 0.0 collective-permute-done
  8.8 0.7 %collective-permute-start.6 = (bf16[128,2560]{1,0:T(8,128)(2,1)S(1)}, bf16[128,2560]{1,0:T(8,128)(2,1)S(1)}, u32[]{:S(2)}, u32[]{:S(2)}) collective-permute-start(bf16[128,2560]{1,0:T(8,128)(2,1)S(1)} %get-tuple-element.68.q_ref), channel_id=1, source_target_pairs={{4,0},{5,1},{6,2},{7,3},{0,4},{1,5},{2,6},{3,7},{12,8},{13,9},{14,... | collective-permute-start | bytes 1966088 | tf_op jit(solution)/shard_map/ppermute | solution.py:219
  9.6 0.1 collective-permute-start.7
  9.6 1.5 %collective-permute-start.3 = (bf16[48,1024]{1,0:T(8,128)(2,1)S(1)}, bf16[48,1024]{1,0:T(8,128)(2,1)S(1)}, u32[]{:S(2)}, u32[]{:S(2)}) collective-permute-start(bf16[48,1024]{1,0:T(8,128)(2,1)S(1)} %pad_maximum_fusion.1), channel_id=1, source_target_pairs={{12,0},{13,1},{14,2},{15,3},{8,4},{9,5},{10,6},{11,7},{4,8},{5,9},... | collective-permute-start | bytes 294920 | tf_op jit(solution)/shard_map/ppermute | solution.py:219
  11.2 0.6 %collective-permute-start.4 = (bf16[16,1024]{1,0:T(8,128)(2,1)S(1)}, bf16[16,1024]{1,0:T(8,128)(2,1)S(1)}, u32[]{:S(2)}, u32[]{:S(2)}) collective-permute-start(bf16[16,1024]{1,0:T(8,128)(2,1)S(1)} %slice.24), channel_id=1, source_target_pairs={{13,0},{12,1},{15,2},{14,3},{9,4},{8,5},{11,6},{10,7},{5,8},{4,9},... | collective-permute-start | bytes 98312 | tf_op jit(solution)/shard_map/ppermute | solution.py:219
  11.8 1.1 %collective-permute-start.2 = (bf16[16,1024]{1,0:T(8,128)(2,1)S(1)}, bf16[16,1024]{1,0:T(8,128)(2,1)S(1)}, u32[]{:S(2)}, u32[]{:S(2)}) collective-permute-start(bf16[16,1024]{1,0:T(8,128)(2,1)S(1)} %slice.24), channel_id=1, source_target_pairs={{5,0},{4,1},{7,2},{6,3},{1,4},{0,5},{3,6},{2,7},{13,8},{12,9},{15,... | collective-permute-start | bytes 98312 | tf_op jit(solution)/shard_map/ppermute | solution.py:219
  12.9 2.7 %self_pairs.1 = (bf16[4,128,640]{2,1,0:T(8,128)(2,1)S(1)}, bf16[4,128,640]{2,1,0:T(8,128)(2,1)S(1)}, f32[8,768]{1,0:T(8,128)S(1)}) custom-call(s32[8,256]{1,0:T(8,128)S(1)} %get-tuple-element.71.scalars_ref, bf16[128,2560]{1,0:T(8,128)(2,1)S(1)} %get-tuple-element.68.q_ref, bf16[128,2560]{1,0:T(8,128)(2,1)S(1)} %get-tuple-element.69.do_ref, ...), custom_call_target="tpu_custom_call" | custom-call | flops 209715200 | bytes 2246656 | tf_op jit(solution)/shard_map/self_pairs/pallas_call | solution.py:189
  15.6 0.1 collective-permute-done.4
  15.8 0.0 collective-permute-done.2
  15.8 0.0 collective-permute-done.3
  15.8 0.0 collective-permute-start.5
  15.8 1.3 %own_pairs.1 = (bf16[4,128,640]{2,1,0:T(8,128)(2,1)S(1)}, f32[128,1024]{1,0:T(8,128)S(1)}) custom-call(bf16[128,2560]{1,0:T(8,128)(2,1)S(1)} %get-tuple-element.68.q_ref, bf16[128,2560]{1,0:T(8,128)(2,1)S(1)} %get-tuple-element.69.do_ref, f32[8,768]{1,0:T(8,128)S(1)} %get-tuple-element.77.rows_ref, bf16[128,1024]{1,0:T(8,128)(2,1)S(1)} %pad_maximum_fusion.kv_ref.refs_3_), custom_call_target="tpu_custom_call" | custom-call | flops 335544320 | bytes 1597440 | tf_op jit(solution)/shard_map/own_pairs/pallas_call | solution.py:189
  17.1 0.0 collective-permute-done.5.rows_ref
  17.1 0.0 collective-permute-done.6.q_ref
  17.2 0.0 collective-permute-done.7.do_ref
  17.2 1.3 %other_pairs.1 = (bf16[4,128,640]{2,1,0:T(8,128)(2,1)S(1)}, f32[48,1024]{1,0:T(8,128)S(1)}, bf16[16,1024]{1,0:T(8,128)(2,1)S(1)}, bf16[48,1024]{1,0:T(8,128)(2,1)S(1)}, bf16[16,1024]{1,0:T(8,128)(2,1)S(1)}) custom-call(bf16[128,2560]{1,0:T(8,128)(2,1)S(1)} %collective-permute-done.6.q_ref, bf16[128,2560]{1,0:T(8,128)(2,1)S(1)} %collective-permute-done.7.do_ref, ...), custom_call_target="tpu_custom_call" | custom-call | flops 335544320 | bytes 2121728 | tf_op jit(solution)/shard_map/other_pairs/pallas_call | solution.py:189
  18.5 1.6 %collective-permute-start.8 = (bf16[48,1024]{1,0:T(8,128)(2,1)S(1)}, bf16[48,1024]{1,0:T(8,128)(2,1)S(1)}, u32[]{:S(2)}, u32[]{:S(2)}) collective-permute-start(bf16[48,1024]{1,0:T(8,128)(2,1)S(1)} %get-tuple-element.87), channel_id=1, source_target_pairs={{0,12},{1,13},{2,14},{3,15},{4,8},{5,9},{6,10},{7,11},{8,4},{9,5},... | collective-permute-start | bytes 294920 | tf_op jit(solution)/shard_map/ppermute | solution.py:223
  20.1 0.6 %collective-permute-start.9 = (bf16[16,1024]{1,0:T(8,128)(2,1)S(1)}, bf16[16,1024]{1,0:T(8,128)(2,1)S(1)}, u32[]{:S(2)}, u32[]{:S(2)}) collective-permute-start(bf16[16,1024]{1,0:T(8,128)(2,1)S(1)} %get-tuple-element.88), channel_id=1, source_target_pairs={{0,5},{1,4},{2,7},{3,6},{4,1},{5,0},{6,3},{7,2},{8,13},{9,12},{10,... | collective-permute-start | bytes 98312 | tf_op jit(solution)/shard_map/ppermute | solution.py:223
  20.7 1.1 %collective-permute-start.10 = (bf16[16,1024]{1,0:T(8,128)(2,1)S(1)}, bf16[16,1024]{1,0:T(8,128)(2,1)S(1)}, u32[]{:S(2)}, u32[]{:S(2)}) collective-permute-start(bf16[16,1024]{1,0:T(8,128)(2,1)S(1)} %get-tuple-element.89), channel_id=1, source_target_pairs={{0,13},{1,12},{2,15},{3,14},{4,9},{5,8},{6,11},{7,10},{8,5},{9,4},... | collective-permute-start | bytes 98312 | tf_op jit(solution)/shard_map/ppermute | solution.py:223
  21.8 1.4 %response_grads.1 = (bf16[128,512]{1,0:T(8,128)(2,1)}, bf16[128,512]{1,0:T(8,128)(2,1)}, bf16[128,2560]{1,0:T(8,128)(2,1)S(1)}) custom-call(bf16[128,2560]{1,0:T(8,128)(2,1)S(1)} %get-tuple-element.68.q_ref, bf16[128,2560]{1,0:T(8,128)(2,1)S(1)} %get-tuple-element.69.do_ref, bf16[4,128,640]{2,1,0:T(8,128)(2,1)S(1)} %get-tuple-element.90.p_ref, ...), custom_call_target="tpu_custom_call" | custom-call | flops 251658240 | bytes 3538944 | tf_op jit(solution)/shard_map/response_grads/pallas_call | solution.py:189
  23.2 0.0 collective-permute-start.13
  23.3 0.5 %collective-permute-done.9 = bf16[16,1024]{1,0:T(8,128)(2,1)S(1)} collective-permute-done((bf16[16,1024]{1,0:T(8,128)(2,1)S(1)}, bf16[16,1024]{1,0:T(8,128)(2,1)S(1)}, u32[]{:S(2)}, u32[]{:S(2)}) %collective-permute-start.9) | collective-permute-done | bytes 32800 | tf_op jit(solution)/shard_map/ppermute | solution.py:223
  23.7 1.2 %collective-permute-done.10 = bf16[16,1024]{1,0:T(8,128)(2,1)S(1)} collective-permute-done((bf16[16,1024]{1,0:T(8,128)(2,1)S(1)}, bf16[16,1024]{1,0:T(8,128)(2,1)S(1)}, u32[]{:S(2)}, u32[]{:S(2)}) %collective-permute-start.10) | collective-permute-done | bytes 32800 | tf_op jit(solution)/shard_map/ppermute | solution.py:223
  25.0 0.0 collective-permute-done.8
  25.0 0.0 copy-start
  25.0 1.3 %collective-permute-start.11 = (bf16[16,1024]{1,0:T(8,128)(2,1)S(1)}, bf16[16,1024]{1,0:T(8,128)(2,1)S(1)}, u32[]{:S(2)}, u32[]{:S(2)}) collective-permute-start(bf16[16,1024]{1,0:T(8,128)(2,1)S(1)} %get-tuple-element.99), channel_id=1, source_target_pairs={{0,5},{1,4},{2,7},{3,6},{4,1},{5,0},{6,3},{7,2},{8,13},{9,12},{10,... | collective-permute-start | bytes 98312 | tf_op jit(solution)/shard_map/ppermute | solution.py:223
  26.3 1.3 %collective-permute-start.12 = (bf16[16,1024]{1,0:T(8,128)(2,1)S(1)}, bf16[16,1024]{1,0:T(8,128)(2,1)S(1)}, u32[]{:S(2)}, u32[]{:S(2)}) collective-permute-start(bf16[16,1024]{1,0:T(8,128)(2,1)S(1)} %get-tuple-element.100), channel_id=1, source_target_pairs={{0,6},{1,7},{2,4},{3,5},{4,2},{5,3},{6,0},{7,1},{8,14},{9,15},{10,... | collective-permute-start | bytes 98312 | tf_op jit(solution)/shard_map/ppermute | solution.py:223
  27.6 0.5 %query_grads.1.a_ref = f32[128,2560]{1,0:T(8,128)S(1)} custom-call(bf16[4,128,640]{2,1,0:T(8,128)(2,1)S(1)} %get-tuple-element.91.ds_ref.refs_0_, bf16[4,128,640]{2,1,0:T(8,128)(2,1)S(1)} %get-tuple-element.101.refs_1_, bf16[128,512]{1,0:T(8,128)(2,1)S(1)} %get-tuple-element.72.k_ref.refs_2_, bf16[128,1024]{1,0:T(8,128)(2,1)S(1)} %pad_maximum_fusion.kv_ref.refs_3_), custom_call_target="tpu_custom_call" | custom-call | flops 16777216000 | bytes 1703936 | tf_op jit(solution)/shard_map/query_grads/pallas_call | solution.py:189
  28.1 0.0 copy-done
  28.1 0.0 collective-permute-done.13.b_ref
  28.2 0.0 slice-start
  28.2 0.9 %add_grads.1 = bf16[128,2560]{1,0:T(8,128)(2,1)} custom-call(f32[128,2560]{1,0:T(8,128)S(1)} %query_grads.1.a_ref, bf16[128,2560]{1,0:T(8,128)(2,1)S(1)} %collective-permute-done.13.b_ref), custom_call_target="tpu_custom_call" | custom-call | bytes 1966080 | tf_op jit(solution)/shard_map/add_grads/pallas_call | solution.py:189
  29.1 0.0 collective-permute-done.11
  29.1 1.9 %collective-permute-done.12 = bf16[16,1024]{1,0:T(8,128)(2,1)S(1)} collective-permute-done((bf16[16,1024]{1,0:T(8,128)(2,1)S(1)}, bf16[16,1024]{1,0:T(8,128)(2,1)S(1)}, u32[]{:S(2)}, u32[]{:S(2)}) %collective-permute-start.12) | collective-permute-done | bytes 32800 | tf_op jit(solution)/shard_map/ppermute | solution.py:223
  31.0 0.0 slice-done
  31.0 0.6 %slice_bitcast_fusion = (f32[1,16,512]{2,1,0:T(8,128)}, f32[1,16,512]{2,1,0:T(8,128)}) fusion(f32[16,1024]{1,0:T(8,128)S(1)} %convert_add_fusion.1), kind=kLoop, calls=%fused_computation.6 | loop fusion | bytes 131072 | tf_op jit(solution)/shard_map/broadcast_in_dim | solution.py:362
  (6 shorter events, 0.1 us)
Async XLA Ops:
  1.4 7.4 %collective-permute-start.1 = (bf16[16,1024]{1,0:T(8,128)(2,1)S(1)}, bf16[16,1024]{1,0:T(8,128)(2,1)S(1)}, u32[]{:S(2)}, u32[]{:S(2)}) collective-permute-start(bf16[16,1024]{1,0:T(8,128)(2,1)S(1)} %pad_maximum_fusion.2), channel_id=1, source_target_pairs={{6,0},{7,1},{4,2},{5,3},{2,4},{3,5},{0,6},{1,7},{14,8},{15,9},{12,... | collective-permute-start | bytes 98312 | tf_op jit(solution)/shard_map/ppermute | solution.py:219
  5.1 3.7 %collective-permute-start = (bf16[16,1024]{1,0:T(8,128)(2,1)S(1)}, bf16[16,1024]{1,0:T(8,128)(2,1)S(1)}, u32[]{:S(2)}, u32[]{:S(2)}) collective-permute-start(bf16[16,1024]{1,0:T(8,128)(2,1)S(1)} %pad_maximum_fusion.2), channel_id=1, source_target_pairs={{5,0},{4,1},{7,2},{6,3},{1,4},{0,5},{3,6},{2,7},{13,8},{12,9},{15,... | collective-permute-start | bytes 98312 | tf_op jit(solution)/shard_map/ppermute | solution.py:219
  8.8 8.3 %collective-permute-start.6 = (bf16[128,2560]{1,0:T(8,128)(2,1)S(1)}, bf16[128,2560]{1,0:T(8,128)(2,1)S(1)}, u32[]{:S(2)}, u32[]{:S(2)}) collective-permute-start(bf16[128,2560]{1,0:T(8,128)(2,1)S(1)} %get-tuple-element.68.q_ref), channel_id=1, source_target_pairs={{4,0},{5,1},{6,2},{7,3},{0,4},{1,5},{2,6},{3,7},{12,8},{13,9},{14,... | collective-permute-start | bytes 1966088 | tf_op jit(solution)/shard_map/ppermute | solution.py:219
  9.6 7.6 %collective-permute-start.7 = (bf16[128,2560]{1,0:T(8,128)(2,1)S(1)}, bf16[128,2560]{1,0:T(8,128)(2,1)S(1)}, u32[]{:S(2)}, u32[]{:S(2)}) collective-permute-start(bf16[128,2560]{1,0:T(8,128)(2,1)S(1)} %get-tuple-element.69.do_ref), channel_id=1, source_target_pairs={{4,0},{5,1},{6,2},{7,3},{0,4},{1,5},{2,6},{3,7},{12,8},{13,9},{14,... | collective-permute-start | bytes 1966088 | tf_op jit(solution)/shard_map/ppermute | solution.py:219
  9.6 6.1 %collective-permute-start.3 = (bf16[48,1024]{1,0:T(8,128)(2,1)S(1)}, bf16[48,1024]{1,0:T(8,128)(2,1)S(1)}, u32[]{:S(2)}, u32[]{:S(2)}) collective-permute-start(bf16[48,1024]{1,0:T(8,128)(2,1)S(1)} %pad_maximum_fusion.1), channel_id=1, source_target_pairs={{12,0},{13,1},{14,2},{15,3},{8,4},{9,5},{10,6},{11,7},{4,8},{5,9},... | collective-permute-start | bytes 294920 | tf_op jit(solution)/shard_map/ppermute | solution.py:219
  11.2 4.6 %collective-permute-start.4 = (bf16[16,1024]{1,0:T(8,128)(2,1)S(1)}, bf16[16,1024]{1,0:T(8,128)(2,1)S(1)}, u32[]{:S(2)}, u32[]{:S(2)}) collective-permute-start(bf16[16,1024]{1,0:T(8,128)(2,1)S(1)} %slice.24), channel_id=1, source_target_pairs={{13,0},{12,1},{15,2},{14,3},{9,4},{8,5},{11,6},{10,7},{5,8},{4,9},... | collective-permute-start | bytes 98312 | tf_op jit(solution)/shard_map/ppermute | solution.py:219
  11.8 4.0 %collective-permute-start.2 = (bf16[16,1024]{1,0:T(8,128)(2,1)S(1)}, bf16[16,1024]{1,0:T(8,128)(2,1)S(1)}, u32[]{:S(2)}, u32[]{:S(2)}) collective-permute-start(bf16[16,1024]{1,0:T(8,128)(2,1)S(1)} %slice.24), channel_id=1, source_target_pairs={{5,0},{4,1},{7,2},{6,3},{1,4},{0,5},{3,6},{2,7},{13,8},{12,9},{15,... | collective-permute-start | bytes 98312 | tf_op jit(solution)/shard_map/ppermute | solution.py:219
  15.8 1.4 %collective-permute-start.5 = (f32[8,768]{1,0:T(8,128)S(1)}, f32[8,768]{1,0:T(8,128)S(1)}, u32[]{:S(2)}, u32[]{:S(2)}) collective-permute-start(f32[8,768]{1,0:T(8,128)S(1)} %get-tuple-element.77.rows_ref), channel_id=1, source_target_pairs={{4,0},{5,1},{6,2},{7,3},{0,4},{1,5},{2,6},{3,7},{12,8},{13,9},{14,... | collective-permute-start | bytes 73736 | tf_op jit(solution)/shard_map/ppermute | solution.py:219
  18.5 6.5 %collective-permute-start.8 = (bf16[48,1024]{1,0:T(8,128)(2,1)S(1)}, bf16[48,1024]{1,0:T(8,128)(2,1)S(1)}, u32[]{:S(2)}, u32[]{:S(2)}) collective-permute-start(bf16[48,1024]{1,0:T(8,128)(2,1)S(1)} %get-tuple-element.87), channel_id=1, source_target_pairs={{0,12},{1,13},{2,14},{3,15},{4,8},{5,9},{6,10},{7,11},{8,4},{9,5},... | collective-permute-start | bytes 294920 | tf_op jit(solution)/shard_map/ppermute | solution.py:223
  20.1 3.7 %collective-permute-start.9 = (bf16[16,1024]{1,0:T(8,128)(2,1)S(1)}, bf16[16,1024]{1,0:T(8,128)(2,1)S(1)}, u32[]{:S(2)}, u32[]{:S(2)}) collective-permute-start(bf16[16,1024]{1,0:T(8,128)(2,1)S(1)} %get-tuple-element.88), channel_id=1, source_target_pairs={{0,5},{1,4},{2,7},{3,6},{4,1},{5,0},{6,3},{7,2},{8,13},{9,12},{10,... | collective-permute-start | bytes 98312 | tf_op jit(solution)/shard_map/ppermute | solution.py:223
  20.7 4.3 %collective-permute-start.10 = (bf16[16,1024]{1,0:T(8,128)(2,1)S(1)}, bf16[16,1024]{1,0:T(8,128)(2,1)S(1)}, u32[]{:S(2)}, u32[]{:S(2)}) collective-permute-start(bf16[16,1024]{1,0:T(8,128)(2,1)S(1)} %get-tuple-element.89), channel_id=1, source_target_pairs={{0,13},{1,12},{2,15},{3,14},{4,9},{5,8},{6,11},{7,10},{8,5},{9,4},... | collective-permute-start | bytes 98312 | tf_op jit(solution)/shard_map/ppermute | solution.py:223
  23.2 4.9 %collective-permute-start.13 = (bf16[128,2560]{1,0:T(8,128)(2,1)S(1)}, bf16[128,2560]{1,0:T(8,128)(2,1)S(1)}, u32[]{:S(2)}, u32[]{:S(2)}) collective-permute-start(bf16[128,2560]{1,0:T(8,128)(2,1)S(1)} %get-tuple-element.102), channel_id=1, source_target_pairs={{4,0},{5,1},{6,2},{7,3},{0,4},{1,5},{2,6},{3,7},{12,8},{13,9},{14,... | collective-permute-start | bytes 1966088 | tf_op jit(solution)/shard_map/ppermute | solution.py:219
  25.0 3.1 %copy-start = (f32[48,1024]{1,0:T(8,128)}, f32[48,1024]{1,0:T(8,128)S(1)}, u32[]{:S(2)}) copy-start(f32[48,1024]{1,0:T(8,128)S(1)} %convert_add_fusion) | copy-start | bytes 589828
  25.0 4.1 %collective-permute-start.11 = (bf16[16,1024]{1,0:T(8,128)(2,1)S(1)}, bf16[16,1024]{1,0:T(8,128)(2,1)S(1)}, u32[]{:S(2)}, u32[]{:S(2)}) collective-permute-start(bf16[16,1024]{1,0:T(8,128)(2,1)S(1)} %get-tuple-element.99), channel_id=1, source_target_pairs={{0,5},{1,4},{2,7},{3,6},{4,1},{5,0},{6,3},{7,2},{8,13},{9,12},{10,... | collective-permute-start | bytes 98312 | tf_op jit(solution)/shard_map/ppermute | solution.py:223
  26.3 4.7 %collective-permute-start.12 = (bf16[16,1024]{1,0:T(8,128)(2,1)S(1)}, bf16[16,1024]{1,0:T(8,128)(2,1)S(1)}, u32[]{:S(2)}, u32[]{:S(2)}) collective-permute-start(bf16[16,1024]{1,0:T(8,128)(2,1)S(1)} %get-tuple-element.100), channel_id=1, source_target_pairs={{0,6},{1,7},{2,4},{3,5},{4,2},{5,3},{6,0},{7,1},{8,14},{9,15},{10,... | collective-permute-start | bytes 98312 | tf_op jit(solution)/shard_map/ppermute | solution.py:223
  28.2 2.9 %slice-start = ((f32[48,1024]{1,0:T(8,128)}), f32[16,1024]{1,0:T(8,128)S(1)}, s32[]{:S(2)}) async-start(f32[48,1024]{1,0:T(8,128)} %copy-done), calls=%async_computation | async-start | bytes 131072 | tf_op jit(solution)/shard_map/slice | solution.py:338

commit v6 on v5

v6 whole, which is shorter than its diff:
```python
import functools

import jax
import jax.numpy as jnp
from jax import lax
from jax.experimental import pallas as pl
from jax.experimental.pallas import tpu as pltpu
from jax.sharding import PartitionSpec as P

HQ = 20
HK = 4
DH = 128
GROUP = 4
PB = 16
RATIO = HQ // HK
LOG2E = 1.4426950408889634
FAR = 1e30
MIB = 1 << 20

NT = (((1,), (1,)), ((), ()))
NN = (((1,), (0,)), ((), ()))
TN = (((0,), (0,)), ((), ()))


def dot(a, b, dims):
    return lax.dot_general(a, b, dims, preferred_element_type=jnp.float32)


def head_rows(ref, g):
    first = g * RATIO
    return jnp.concatenate(
        [ref[:, (first + r) * DH : (first + r + 1) * DH] for r in range(RATIO)], axis=0
    )


def head_cols(g):
    return slice(g * DH, (g + 1) * DH)


def probabilities(scores, lse_rows):
    nk, nq = scores.shape
    return jnp.exp2((scores * (LOG2E / DH**0.5)).reshape(nk // 8, 8, nq) - lse_rows)


def score_grads(probs, dprob, delta_rows):
    nk, nq = dprob.shape
    dscore = probs * (dprob.reshape(nk // 8, 8, nq) - delta_rows)
    return dscore.reshape(nk, nq).astype(jnp.bfloat16)


def eight(row):
    return jnp.broadcast_to(row, (8, row.shape[1]))


def load_kernel(len_ref, seen_ref, *refs):
    count = (len(refs) - 2) // 2
    sems, outs = refs[-1], refs[count:-1]
    copies = [
        pltpu.make_async_copy(refs[i], outs[i], sems.at[i]) for i in range(count)
    ]
    for copy in copies:
        copy.start()
    outs[count][...] = jnp.concatenate(
        [jnp.full((8, DH), ref[0], jnp.int32) for ref in (len_ref, seen_ref)], axis=1
    )
    for copy in copies:
        copy.wait()


def self_kernel(
    scalars_ref, q_ref, do_ref, k_ref, v_ref, o_hbm, ln_hbm, p_ref, ds_ref, rows_ref,
    o_ref, ln_ref, probs_ref, sems,
):
    rows = q_ref.shape[0]
    nq = RATIO * rows
    span = RATIO * DH
    first = pltpu.make_async_copy(ln_hbm, ln_ref, sems.at[HK])
    first.start()
    parts = []
    for g in range(HK):
        cols = slice(g * span, (g + 1) * span)
        parts.append(pltpu.make_async_copy(o_hbm.at[:, cols], o_ref.at[:, cols], sems.at[g]))
        parts[g].start()
    live = lax.broadcasted_iota(jnp.int32, (1, rows), 1) < scalars_ref[:1, :rows]
    key_at = lax.broadcasted_iota(jnp.int32, (rows, nq), 0)
    query_at = lax.broadcasted_iota(jnp.int32, (rows, nq), 1) % rows
    keep = (key_at <= query_at).reshape(rows // 8, 8, nq)
    same = key_at[:, :rows] == query_at[:, :rows]
    rows_ref[:, nq:] = scalars_ref[:, DH:].astype(jnp.float32)
    first.wait()
    for g in range(HK):
        lse_row = jnp.concatenate(
            [
                jnp.where(live, ln_ref[h] * LOG2E, FAR)
                for h in range(g * RATIO, (g + 1) * RATIO)
            ],
            axis=1,
        )
        rows_ref[g : g + 1, :nq] = lse_row
        scores = dot(k_ref[:, head_cols(g)], head_rows(q_ref, g), NT)
        probs = jnp.where(keep, probabilities(scores, eight(lse_row)[None]), 0.0)
        probs_ref[g] = probs.reshape(rows, nq)
        p_ref[g] = probs.reshape(rows, nq).astype(p_ref.dtype)
    for g in range(HK):
        parts[g].wait()
        delta_parts = []
        for h in range(g * RATIO, (g + 1) * RATIO):
            cols = slice(h * DH, (h + 1) * DH)
            products = dot(o_ref[:, cols], do_ref[:, cols], NT)
            delta_parts.append(jnp.sum(jnp.where(same, products, 0.0), axis=0, keepdims=True))
        delta_row = jnp.concatenate(delta_parts, axis=1)
        rows_ref[HK + g : HK + g + 1, :nq] = delta_row
        dprob = dot(v_ref[:, head_cols(g)], head_rows(do_ref, g), NT)
        probs = probs_ref[g].reshape(rows // 8, 8, nq)
        ds_ref[g] = score_grads(probs, dprob, eight(delta_row)[None])


def block_rows(pieces, across, n_resp, rows_ref, nq):
    my_row = lax.rem(lax.axis_index("dp"), GROUP)
    my_col = lax.axis_index("resp")
    seen = rows_ref[:, nq:]
    far = []
    for core, row, k in pieces:
        block = source(my_col, k, n_resp) * GROUP + (my_row ^ (row << 1) ^ core ^ across)
        rows = jnp.where(seen > block.astype(jnp.float32), 0.0, FAR)
        far.append(jnp.concatenate([rows] * (nq // rows.shape[1]), axis=1))
    return far


def prompt_terms(far, g, q, do, rows_ref, kv_ref):
    nq = q.shape[0]
    lse = eight(rows_ref[g : g + 1, :nq])
    delta = eight(rows_ref[HK + g : HK + g + 1, :nq])
    lse_rows = jnp.concatenate(
        [jnp.broadcast_to((lse + f)[None], (PB // 8, 8, nq)) for f in far], axis=0
    )
    probs = probabilities(dot(kv_ref[:, head_cols(g)], q, NT), lse_rows)
    dprob = dot(kv_ref[:, head_cols(HK + g)], do, NT)
    return probs, score_grads(probs, dprob, delta[None])


def own_kernel(pieces, n_resp, q_ref, do_ref, rows_ref, kv_ref, ds_ref, part_ref):
    scale = 1.0 / DH**0.5
    far = block_rows(pieces, 0, n_resp, rows_ref, RATIO * q_ref.shape[0])
    for g in range(HK):
        q = head_rows(q_ref, g)
        do = head_rows(do_ref, g)
        probs, ds16 = prompt_terms(far, g, q, do, rows_ref, kv_ref)
        ds_ref[g] = ds16
        p16 = probs.reshape(ds16.shape).astype(jnp.bfloat16)
        part_ref[:, head_cols(g)] = dot(ds16, q, NN) * scale
        part_ref[:, head_cols(HK + g)] = dot(p16, do, NN)


def other_kernel(pieces, n_resp, cuts, q_ref, do_ref, rows_ref, kv_ref, part_ref, *outs):
    scale = 1.0 / DH**0.5
    far = block_rows(pieces, 0, n_resp, rows_ref, RATIO * q_ref.shape[0])

    def put(sums, cols):
        sums = sums + part_ref[:, cols]
        for out, low, high in zip(outs, cuts, cuts[1:]):
            out[:, cols] = sums[low:high].astype(out.dtype)

    for g in range(HK):
        q = head_rows(q_ref, g)
        do = head_rows(do_ref, g)
        probs, ds16 = prompt_terms(far, g, q, do, rows_ref, kv_ref)
        p16 = probs.reshape(ds16.shape).astype(jnp.bfloat16)
        put(dot(ds16, q, NN) * scale, head_cols(g))
        put(dot(p16, do, NN), head_cols(HK + g))


def response_kernel(
    pieces, n_resp, q_ref, do_ref, rows_ref, p_ref, ds_ref, kv_ref, gk_ref, gv_ref, ds2_ref
):
    scale = 1.0 / DH**0.5
    far = block_rows(pieces, 1, n_resp, rows_ref, RATIO * q_ref.shape[0])
    for g in range(HK):
        q = head_rows(q_ref, g)
        do = head_rows(do_ref, g)
        cols = head_cols(g)
        gv_ref[:, cols] = dot(p_ref[g], do, NN).astype(gv_ref.dtype)
        gk_ref[:, cols] = (dot(ds_ref[g], q, NN) * scale).astype(gk_ref.dtype)
        ds2_ref[g] = prompt_terms(far, g, q, do, rows_ref, kv_ref)[1]


def query_kernel(ds0_ref, ds1_ref, ds2_ref, k0_ref, k1_ref, k2_ref, gq_ref):
    rows = gq_ref.shape[0]
    scale = 1.0 / DH**0.5
    for g in range(HK):
        cols = head_cols(g)
        ds = jnp.concatenate([ds0_ref[g], ds1_ref[g], ds2_ref[g]], axis=0)
        keys = jnp.concatenate([k0_ref[:, cols], k1_ref[:, cols], k2_ref[:, cols]], axis=0)
        out = (dot(ds, keys, TN) * scale).astype(gq_ref.dtype)
        for r in range(RATIO):
            h = g * RATIO + r
            gq_ref[:, h * DH : (h + 1) * DH] = out[r * rows : (r + 1) * rows]


VMEM = pl.BlockSpec(memory_space=pltpu.VMEM)
SMEM = pl.BlockSpec(memory_space=pltpu.SMEM)
HBM = pl.BlockSpec(memory_space=pltpu.HBM)


def call(kernel, name, outs, scalars, arrays, flops, in_hbm=(), scratch=()):
    nbytes = sum(a.size * a.dtype.itemsize for a in (*arrays, *in_hbm))
    in_hbm = [pltpu.with_memory_space_constraint(a, pltpu.HBM) for a in in_hbm]
    return pl.pallas_call(
        kernel,
        name=name,
        out_shape=outs,
        in_specs=[SMEM] * len(scalars) + [VMEM] * len(arrays) + [HBM] * len(in_hbm),
        out_specs=jax.tree.map(lambda _: VMEM, outs),
        scratch_shapes=scratch,
        compiler_params=pltpu.CompilerParams(vmem_limit_bytes=24 * MIB),
        cost_estimate=pl.CostEstimate(flops=flops, bytes_accessed=nbytes, transcendentals=0),
    )(*scalars, *arrays, *in_hbm)


def source(col, k, count):
    if count & (count - 1) == 0:
        return col ^ k
    if isinstance(col, int):
        return (col - k) % count
    return lax.rem(col + count - k, count)


def pairs(core, row, k):
    n_dp, n_resp = lax.axis_size("dp"), lax.axis_size("resp")
    return [
        ((d ^ core ^ row << 1) * n_resp + source(r, k, n_resp), d * n_resp + r)
        for d in range(n_dp)
        for r in range(n_resp)
    ]


def fetch(array, *step):
    return lax.ppermute(array, ("dp", "resp"), pairs(*step))


def give(array, *step):
    return lax.ppermute(array, ("dp", "resp"), [(i, j) for j, i in pairs(*step)])


def shards(
    queries,
    resp_keys,
    resp_values,
    grad_out,
    forward_out,
    log_norm,
    prompt_keys,
    prompt_values,
    resp_len,
    seen_blocks,
):
    rows = queries.shape[1]
    width = resp_keys.shape[2]
    n_resp = lax.axis_size("resp")
    ln = jnp.transpose(log_norm, (2, 0, 1))
    f32, b16 = jnp.float32, jnp.bfloat16
    macs = HQ * rows * DH

    if n_resp == 4:
        near, relay = (1, 2), (1, 2)
    else:
        near, relay = tuple(range(1, n_resp)), None
    first = [(0, 0, 0)] + [(1, 0, k) for k in near]
    extra = [(0, 0, relay[0] ^ relay[1])] if relay else []
    pieces = first + extra + [(c ^ 1, 1, k) for c, _, k in first] + [(c, 1, k) for c, _, k in extra]
    n_first, n_half = len(first) * PB, len(pieces) * PB // 2

    array = jax.ShapeDtypeStruct
    full = array((rows, HQ * DH), b16)

    own = lax.optimization_barrier(jnp.concatenate([prompt_keys[0], prompt_values[0]], axis=1))
    got = [own] + [fetch(own, 1, 0, k) for k in near]
    q2, do2 = fetch(queries[0], 1, 0, 0), fetch(grad_out[0], 1, 0, 0)
    loaded = call(
        load_kernel,
        "load",
        (full, full, *[array((rows, width), b16)] * 2, array((8, 2 * DH), jnp.int32)),
        (resp_len, seen_blocks),
        (),
        0,
        (queries[0], grad_out[0], resp_keys[0], resp_values[0]),
        (pltpu.SemaphoreType.DMA((4,)),),
    )
    got, (q, do, kr, vr, scalars) = lax.optimization_barrier((got[::-1], loaded))
    got = got[::-1]

    bundle = lax.optimization_barrier(jnp.concatenate(got, 0))
    moved = [fetch(bundle, 1, 1, 0)]
    if relay:
        piece = bundle[relay[1] * PB :][:PB]
        far = fetch(piece, 1, 1, relay[0])
        moved = [fetch(piece, 1, 0, relay[0])] + moved + [far]
    ds_self_shape = array((HK, rows, RATIO * rows), b16)
    worked = call(
        self_kernel,
        "self_pairs",
        (ds_self_shape, ds_self_shape, array((8, RATIO * rows + DH), f32)),
        (),
        (scalars, q, do, kr, vr),
        5 * macs * rows,
        (forward_out[0], ln),
        (
            pltpu.VMEM((rows, HQ * DH), b16),
            pltpu.VMEM((HQ, 1, rows), f32),
            pltpu.VMEM((HK, rows, RATIO * rows), f32),
            pltpu.SemaphoreType.DMA((HK + 1,)),
        ),
    )
    moved, (p_self, ds_self, terms) = lax.optimization_barrier((moved[::-1], worked))
    moved = moved[::-1]
    terms2 = fetch(terms, 1, 0, 0)
    half = jnp.concatenate([bundle] + moved, 0)
    nk = half.shape[0]
    ds_shape = array((HK, nk, RATIO * rows), b16)

    ds_half, part = call(
        functools.partial(own_kernel, pieces, n_resp),
        "own_pairs",
        (ds_shape, array((nk, 2 * width), f32)),
        (),
        (q, do, terms, half),
        8 * macs * nk,
    )
    part, terms2, q2, do2 = lax.optimization_barrier((part, terms2, q2, do2))
    cuts = (0, n_first, n_half, n_half + n_first, nk) if relay else (0, n_half, nk)
    kinds = (f32, b16, b16, b16) if relay else (f32, b16)
    low, *sent = call(
        functools.partial(other_kernel, pieces, n_resp, cuts),
        "other_pairs",
        [array((j - i, 2 * width), t) for i, j, t in zip(cuts, cuts[1:], kinds)],
        (),
        (q2, do2, terms2, half, part),
        8 * macs * nk,
    )

    other = fetch(half, 1, 0, 0)
    if relay:
        moved = [
            give(sent[1], 1, 1, 0),
            give(sent[0], 1, 0, relay[0]),
            give(sent[2], 1, 1, relay[0]),
        ]
    else:
        moved = [give(sent[0], 1, 1, 0)]
    late = call(
        functools.partial(response_kernel, pieces, n_resp),
        "response_grads",
        (array((rows, width), b16), array((rows, width), b16), ds_shape),
        (),
        (q, do, terms, p_self, ds_self, other),
        4 * macs * rows + 4 * macs * nk,
    )
    moved, (grad_rk, grad_rv, ds_other) = lax.optimization_barrier((moved, late))
    total = low + moved[0].astype(f32)
    sums = [total[i * PB : (i + 1) * PB] for i in range(len(first))]
    for piece in moved[1:]:
        sums[relay[1]] = sums[relay[1]] + piece.astype(f32)
    sums, ds_other = lax.optimization_barrier((sums, ds_other))
    moved = [give(sums[k].astype(b16), 1, 0, k) for k in reversed(near)]
    grad_q = call(
        query_kernel,
        "query_grads",
        full,
        (),
        (ds_self, ds_half, ds_other, kr, half, other),
        2 * macs * (rows + 2 * nk),
    )
    moved, grad_q = lax.optimization_barrier((moved, grad_q))
    total = sums[0]
    for piece in moved:
        total = total + piece.astype(f32)
    return (
        grad_q[None],
        grad_rk[None],
        grad_rv[None],
        total[None, :, :width],
        total[None, :, width:],
    )


def solution(mesh):
    by_both, by_block = P(("dp", "resp"), None, None), P("resp", "dp", None)
    return jax.shard_map(
        shards,
        mesh=mesh,
        in_specs=(by_both,) * 6 + (by_block,) * 2 + (P(("dp", "resp")),) * 2,
        out_specs=(by_both,) * 3 + (by_block,) * 2,
        check_vma=False,
    )
```

time: 32 us -> 31.1 us (0.972)
  the two profiles are of different devices: /device:TPU:1 before, /device:TPU:0 now
where the time goes in v6:
time: 31.1 us; the launch traced here: 30.7 us
  starting transfers between devices  15.4 us (50%)
  Pallas kernels  9.51 us (31%)
  waiting for transfers between devices  2.23 us (7%)
  between operations  2.04 us (7%)
  other arithmetic  0.83 us (3%)
  local copies, waits for them, and re-layouts  0.64 us (2%)
    ppermute x9, starting transfers between devices, fetch(): return lax.ppermute(array, ('dp', 'resp'), pairs(*step))  9.75 us
    pallas_call x6, Pallas kernels, call(): pl.pallas_call(kernel, name=name, out_shape=outs, in_specs=[SMEM] * len(s...  9.51 us
    ppermute x5, starting transfers between devices, give(): lax.ppermute(array, ('dp', 'resp'), [(i, j) for j, i in pairs(*step)])  5.67 us
    ppermute x5, waiting for transfers between devices, give(): lax.ppermute(array, ('dp', 'resp'), [(i, j) for j, i in pairs(*step)])  2.11 us
    concatenate x1, other arithmetic, shards(): jnp.concatenate([prompt_keys[0], prompt_values[0]], axis=1)  0.74 us
    broadcast_in_dim x1, local copies, waits for them, and re-layouts, shards(): total[None, :, width:]  0.63 us
  transfers between devices with their start and end apart: 14, of which 5 were waited for; matrix products, arithmetic and copies ran while one was open for 3% of the time, Pallas kernels for 31%

profile of v6, /device:TPU:0, one launch (start us, length us, event | category | flops | bytes accessed | tf_op | source)
XLA Modules:
  0.0 30.7 jit_solution(7734095141393129052)
XLA Ops:
  0.6 0.5 %collective-permute-start.6 = (bf16[128,2560]{1,0:T(8,128)(2,1)}, bf16[128,2560]{1,0:T(8,128)(2,1)S(1)}, u32[]{:S(2)}, u32[]{:S(2)}) collective-permute-start(bf16[128,2560]{1,0:T(8,128)(2,1)} %bitcast.16), channel_id=1, source_target_pairs={{4,0},{5,1},{6,2},{7,3},{0,4},{1,5},{2,6},{3,7},{12,8},{13,9},{14,... | collective-permute-start | bytes 1966088 | tf_op jit(solution)/shard_map/ppermute | solution.py:238
  1.1 0.1 collective-permute-start.7
  1.2 0.7 %pad_maximum_fusion.2 = bf16[16,1024]{1,0:T(8,128)(2,1)S(1)} fusion(bf16[16,512]{1,0:T(8,128)(2,1)} %bitcast.23, bf16[16,512]{1,0:T(8,128)(2,1)} %bitcast.24), kind=kLoop, calls=%fused_computation.8 | loop fusion | flops 65536 | bytes 65536 | tf_op jit(solution)/shard_map/concatenate | solution.py:276
  2.0 3.7 %collective-permute-start = (bf16[16,1024]{1,0:T(8,128)(2,1)S(1)}, bf16[16,1024]{1,0:T(8,128)(2,1)S(1)}, u32[]{:S(2)}, u32[]{:S(2)}) collective-permute-start(bf16[16,1024]{1,0:T(8,128)(2,1)S(1)} %pad_maximum_fusion.2), channel_id=1, source_target_pairs={{6,0},{7,1},{4,2},{5,3},{2,4},{3,5},{0,6},{1,7},{14,8},{15,9},{12,... | collective-permute-start | bytes 98312 | tf_op jit(solution)/shard_map/ppermute | solution.py:238
  5.7 1.6 %collective-permute-start.1 = (bf16[16,1024]{1,0:T(8,128)(2,1)S(1)}, bf16[16,1024]{1,0:T(8,128)(2,1)S(1)}, u32[]{:S(2)}, u32[]{:S(2)}) collective-permute-start(bf16[16,1024]{1,0:T(8,128)(2,1)S(1)} %pad_maximum_fusion.2), channel_id=1, source_target_pairs={{5,0},{4,1},{7,2},{6,3},{1,4},{0,5},{3,6},{2,7},{13,8},{12,9},{15,... | collective-permute-start | bytes 98312 | tf_op jit(solution)/shard_map/ppermute | solution.py:238
  8.6 1.4 %load.1 = (bf16[128,2560]{1,0:T(8,128)(2,1)S(1)}, bf16[128,2560]{1,0:T(8,128)(2,1)S(1)}, bf16[128,512]{1,0:T(8,128)(2,1)S(1)}, bf16[128,512]{1,0:T(8,128)(2,1)S(1)}, s32[8,256]{1,0:T(8,128)S(1)}) custom-call(s32[1]{0:T(128)S(6)} %copy.15.len_ref, s32[1]{0:T(128)S(6)} %copy.16.seen_ref, bf16[128,2560]{1,0:T(8,128)(2,1)} %bitcast.17, ...), custom_call_target="tpu_custom_call" | custom-call | bytes 1572864 | tf_op jit(solution)/shard_map/load/pallas_call | solution.py:208
  10.0 0.0 collective-permute-done
  10.0 0.0 collective-permute-done.1
  10.0 1.2 %collective-permute-start.3 = (bf16[48,1024]{1,0:T(8,128)(2,1)S(1)}, bf16[48,1024]{1,0:T(8,128)(2,1)S(1)}, u32[]{:S(2)}, u32[]{:S(2)}) collective-permute-start(bf16[48,1024]{1,0:T(8,128)(2,1)S(1)} %pad_maximum_fusion.1), channel_id=1, source_target_pairs={{12,0},{13,1},{14,2},{15,3},{8,4},{9,5},{10,6},{11,7},{4,8},{5,9},... | collective-permute-start | bytes 294920 | tf_op jit(solution)/shard_map/ppermute | solution.py:238
  11.2 0.6 %collective-permute-start.2 = (bf16[16,1024]{1,0:T(8,128)(2,1)S(1)}, bf16[16,1024]{1,0:T(8,128)(2,1)S(1)}, u32[]{:S(2)}, u32[]{:S(2)}) collective-permute-start(bf16[16,1024]{1,0:T(8,128)(2,1)S(1)} %slice.24), channel_id=1, source_target_pairs={{13,0},{12,1},{15,2},{14,3},{9,4},{8,5},{11,6},{10,7},{5,8},{4,9},... | collective-permute-start | bytes 98312 | tf_op jit(solution)/shard_map/ppermute | solution.py:238
  11.8 1.1 %collective-permute-start.4 = (bf16[16,1024]{1,0:T(8,128)(2,1)S(1)}, bf16[16,1024]{1,0:T(8,128)(2,1)S(1)}, u32[]{:S(2)}, u32[]{:S(2)}) collective-permute-start(bf16[16,1024]{1,0:T(8,128)(2,1)S(1)} %slice.24), channel_id=1, source_target_pairs={{5,0},{4,1},{7,2},{6,3},{1,4},{0,5},{3,6},{2,7},{13,8},{12,9},{15,... | collective-permute-start | bytes 98312 | tf_op jit(solution)/shard_map/ppermute | solution.py:238
  13.0 2.5 %self_pairs.1 = (bf16[4,128,640]{2,1,0:T(8,128)(2,1)S(1)}, bf16[4,128,640]{2,1,0:T(8,128)(2,1)S(1)}, f32[8,768]{1,0:T(8,128)S(1)}) custom-call(s32[8,256]{1,0:T(8,128)S(1)} %get-tuple-element.63.scalars_ref, bf16[128,2560]{1,0:T(8,128)(2,1)S(1)} %get-tuple-element.58.q_ref, bf16[128,2560]{1,0:T(8,128)(2,1)S(1)} %get-tuple-element.59.do_ref, ...), custom_call_target="tpu_custom_call" | custom-call | flops 209715200 | bytes 2246656 | tf_op jit(solution)/shard_map/self_pairs/pallas_call | solution.py:208
  15.4 0.1 collective-permute-done.2
  15.5 0.0 collective-permute-done.4
  15.5 0.0 collective-permute-done.3
  15.6 0.8 %collective-permute-start.11 = (bf16[128,1024]{1,0:T(8,128)(2,1)S(1)}, bf16[128,1024]{1,0:T(8,128)(2,1)S(1)}, u32[]{:S(2)}, u32[]{:S(2)}) collective-permute-start(bf16[128,1024]{1,0:T(8,128)(2,1)S(1)} %pad_maximum_fusion.kv_ref.k1_ref), channel_id=1, source_target_pairs={{4,0},{5,1},{6,2},{7,3},{0,4},{1,5},{2,6},{3,7},{12,8},{13,9},{14,... | collective-permute-start | bytes 786440 | tf_op jit(solution)/shard_map/ppermute | solution.py:238
  16.4 0.1 collective-permute-start.5
  16.4 1.3 %own_pairs.1 = (bf16[4,128,640]{2,1,0:T(8,128)(2,1)S(1)}, f32[128,1024]{1,0:T(8,128)S(1)}) custom-call(bf16[128,2560]{1,0:T(8,128)(2,1)S(1)} %get-tuple-element.58.q_ref, bf16[128,2560]{1,0:T(8,128)(2,1)S(1)} %get-tuple-element.59.do_ref, f32[8,768]{1,0:T(8,128)S(1)} %get-tuple-element.69.rows_ref, bf16[128,1024]{1,0:T(8,128)(2,1)S(1)} %pad_maximum_fusion.kv_ref.k1_ref), custom_call_target="tpu_custom_call" | custom-call | flops 335544320 | bytes 1597440 | tf_op jit(solution)/shard_map/own_pairs/pallas_call | solution.py:208
  17.7 0.0 collective-permute-done.5.rows_ref
  17.8 0.0 collective-permute-done.6.q_ref
  17.8 0.0 collective-permute-done.7.do_ref
  17.8 1.3 %other_pairs.1 = (f32[48,1024]{1,0:T(8,128)S(1)}, bf16[16,1024]{1,0:T(8,128)(2,1)S(1)}, bf16[48,1024]{1,0:T(8,128)(2,1)S(1)}, bf16[16,1024]{1,0:T(8,128)(2,1)S(1)}) custom-call(bf16[128,2560]{1,0:T(8,128)(2,1)S(1)} %collective-permute-done.6.q_ref, bf16[128,2560]{1,0:T(8,128)(2,1)S(1)} %collective-permute-done.7.do_ref, ...), custom_call_target="tpu_custom_call" | custom-call | flops 335544320 | bytes 2121728 | tf_op jit(solution)/shard_map/other_pairs/pallas_call | solution.py:208
  19.1 1.2 %collective-permute-start.8 = (bf16[48,1024]{1,0:T(8,128)(2,1)S(1)}, bf16[48,1024]{1,0:T(8,128)(2,1)S(1)}, u32[]{:S(2)}, u32[]{:S(2)}) collective-permute-start(bf16[48,1024]{1,0:T(8,128)(2,1)S(1)} %get-tuple-element.79), channel_id=1, source_target_pairs={{0,12},{1,13},{2,14},{3,15},{4,8},{5,9},{6,10},{7,11},{8,4},{9,5},... | collective-permute-start | bytes 294920 | tf_op jit(solution)/shard_map/ppermute | solution.py:242
  20.3 1.0 %collective-permute-start.10 = (bf16[16,1024]{1,0:T(8,128)(2,1)S(1)}, bf16[16,1024]{1,0:T(8,128)(2,1)S(1)}, u32[]{:S(2)}, u32[]{:S(2)}) collective-permute-start(bf16[16,1024]{1,0:T(8,128)(2,1)S(1)} %get-tuple-element.81), channel_id=1, source_target_pairs={{0,13},{1,12},{2,15},{3,14},{4,9},{5,8},{6,11},{7,10},{8,5},{9,4},... | collective-permute-start | bytes 98312 | tf_op jit(solution)/shard_map/ppermute | solution.py:242
  21.3 1.1 %collective-permute-start.9 = (bf16[16,1024]{1,0:T(8,128)(2,1)S(1)}, bf16[16,1024]{1,0:T(8,128)(2,1)S(1)}, u32[]{:S(2)}, u32[]{:S(2)}) collective-permute-start(bf16[16,1024]{1,0:T(8,128)(2,1)S(1)} %get-tuple-element.80), channel_id=1, source_target_pairs={{0,5},{1,4},{2,7},{3,6},{4,1},{5,0},{6,3},{7,2},{8,13},{9,12},{10,... | collective-permute-start | bytes 98312 | tf_op jit(solution)/shard_map/ppermute | solution.py:242
  22.4 0.0 collective-permute-done.11.kv_ref.k2_ref
  22.4 1.5 %response_grads.1 = (bf16[128,512]{1,0:T(8,128)(2,1)}, bf16[128,512]{1,0:T(8,128)(2,1)}, bf16[4,128,640]{2,1,0:T(8,128)(2,1)S(1)}) custom-call(bf16[128,2560]{1,0:T(8,128)(2,1)S(1)} %get-tuple-element.58.q_ref, bf16[128,2560]{1,0:T(8,128)(2,1)S(1)} %get-tuple-element.59.do_ref, f32[8,768]{1,0:T(8,128)S(1)} %get-tuple-element.69.rows_ref, ...), custom_call_target="tpu_custom_call" | custom-call | flops 335544320 | bytes 2908160 | tf_op jit(solution)/shard_map/response_grads/pallas_call | solution.py:208
  23.9 0.7 %collective-permute-done.10 = bf16[16,1024]{1,0:T(8,128)(2,1)S(1)} collective-permute-done((bf16[16,1024]{1,0:T(8,128)(2,1)S(1)}, bf16[16,1024]{1,0:T(8,128)(2,1)S(1)}, u32[]{:S(2)}, u32[]{:S(2)}) %collective-permute-start.10) | collective-permute-done | bytes 32800 | tf_op jit(solution)/shard_map/ppermute | solution.py:242
  24.6 0.3 collective-permute-done.9
  24.9 0.0 collective-permute-done.8
  25.0 1.4 %collective-permute-start.12 = (bf16[16,1024]{1,0:T(8,128)(2,1)S(1)}, bf16[16,1024]{1,0:T(8,128)(2,1)S(1)}, u32[]{:S(2)}, u32[]{:S(2)}) collective-permute-start(bf16[16,1024]{1,0:T(8,128)(2,1)S(1)} %get-tuple-element.91), channel_id=1, source_target_pairs={{0,6},{1,7},{2,4},{3,5},{4,2},{5,3},{6,0},{7,1},{8,14},{9,15},{10,... | collective-permute-start | bytes 98312 | tf_op jit(solution)/shard_map/ppermute | solution.py:242
  26.4 0.9 %collective-permute-start.13 = (bf16[16,1024]{1,0:T(8,128)(2,1)S(1)}, bf16[16,1024]{1,0:T(8,128)(2,1)S(1)}, u32[]{:S(2)}, u32[]{:S(2)}) collective-permute-start(bf16[16,1024]{1,0:T(8,128)(2,1)S(1)} %get-tuple-element.92), channel_id=1, source_target_pairs={{0,5},{1,4},{2,7},{3,6},{4,1},{5,0},{6,3},{7,2},{8,13},{9,12},{10,... | collective-permute-start | bytes 98312 | tf_op jit(solution)/shard_map/ppermute | solution.py:242
  27.3 1.5 %query_grads.1 = bf16[128,2560]{1,0:T(8,128)(2,1)} custom-call(bf16[4,128,640]{2,1,0:T(8,128)(2,1)S(1)} %get-tuple-element.83.ds_ref.ds0_ref, bf16[4,128,640]{2,1,0:T(8,128)(2,1)S(1)} %get-tuple-element.93.ds1_ref, bf16[4,128,640]{2,1,0:T(8,128)(2,1)S(1)} %get-tuple-element.94.ds2_ref, bf16[128,512]{1,0:T(8,128)(2,1)S(1)} %get-tuple-element.64.k_ref.k0_ref, ...), custom_call_target="tpu_custom_call" | custom-call | flops 251658240 | bytes 2621440 | tf_op jit(solution)/shard_map/query_grads/pallas_call | solution.py:208
  28.9 0.9 %collective-permute-done.12 = bf16[16,1024]{1,0:T(8,128)(2,1)S(1)} collective-permute-done((bf16[16,1024]{1,0:T(8,128)(2,1)S(1)}, bf16[16,1024]{1,0:T(8,128)(2,1)S(1)}, u32[]{:S(2)}, u32[]{:S(2)}) %collective-permute-start.12) | collective-permute-done | bytes 32800 | tf_op jit(solution)/shard_map/ppermute | solution.py:242
  29.8 0.2 collective-permute-done.13
  30.0 0.6 %slice_bitcast_fusion = (f32[1,16,512]{2,1,0:T(8,128)}, f32[1,16,512]{2,1,0:T(8,128)}) fusion(f32[16,1024]{1,0:T(8,128)S(1)} %convert_add_fusion.1), kind=kLoop, calls=%fused_computation.6 | loop fusion | bytes 131072 | tf_op jit(solution)/shard_map/broadcast_in_dim | solution.py:382
  (7 shorter events, 0.1 us)
Async XLA Ops:
  0.6 17.1 %collective-permute-start.6 = (bf16[128,2560]{1,0:T(8,128)(2,1)}, bf16[128,2560]{1,0:T(8,128)(2,1)S(1)}, u32[]{:S(2)}, u32[]{:S(2)}) collective-permute-start(bf16[128,2560]{1,0:T(8,128)(2,1)} %bitcast.16), channel_id=1, source_target_pairs={{4,0},{5,1},{6,2},{7,3},{0,4},{1,5},{2,6},{3,7},{12,8},{13,9},{14,... | collective-permute-start | bytes 1966088 | tf_op jit(solution)/shard_map/ppermute | solution.py:238
  1.1 16.6 %collective-permute-start.7 = (bf16[128,2560]{1,0:T(8,128)(2,1)}, bf16[128,2560]{1,0:T(8,128)(2,1)S(1)}, u32[]{:S(2)}, u32[]{:S(2)}) collective-permute-start(bf16[128,2560]{1,0:T(8,128)(2,1)} %bitcast.18), channel_id=1, source_target_pairs={{4,0},{5,1},{6,2},{7,3},{0,4},{1,5},{2,6},{3,7},{12,8},{13,9},{14,... | collective-permute-start | bytes 1966088 | tf_op jit(solution)/shard_map/ppermute | solution.py:238
  2.0 8.0 %collective-permute-start = (bf16[16,1024]{1,0:T(8,128)(2,1)S(1)}, bf16[16,1024]{1,0:T(8,128)(2,1)S(1)}, u32[]{:S(2)}, u32[]{:S(2)}) collective-permute-start(bf16[16,1024]{1,0:T(8,128)(2,1)S(1)} %pad_maximum_fusion.2), channel_id=1, source_target_pairs={{6,0},{7,1},{4,2},{5,3},{2,4},{3,5},{0,6},{1,7},{14,8},{15,9},{12,... | collective-permute-start | bytes 98312 | tf_op jit(solution)/shard_map/ppermute | solution.py:238
  5.7 4.3 %collective-permute-start.1 = (bf16[16,1024]{1,0:T(8,128)(2,1)S(1)}, bf16[16,1024]{1,0:T(8,128)(2,1)S(1)}, u32[]{:S(2)}, u32[]{:S(2)}) collective-permute-start(bf16[16,1024]{1,0:T(8,128)(2,1)S(1)} %pad_maximum_fusion.2), channel_id=1, source_target_pairs={{5,0},{4,1},{7,2},{6,3},{1,4},{0,5},{3,6},{2,7},{13,8},{12,9},{15,... | collective-permute-start | bytes 98312 | tf_op jit(solution)/shard_map/ppermute | solution.py:238
  10.0 5.5 %collective-permute-start.3 = (bf16[48,1024]{1,0:T(8,128)(2,1)S(1)}, bf16[48,1024]{1,0:T(8,128)(2,1)S(1)}, u32[]{:S(2)}, u32[]{:S(2)}) collective-permute-start(bf16[48,1024]{1,0:T(8,128)(2,1)S(1)} %pad_maximum_fusion.1), channel_id=1, source_target_pairs={{12,0},{13,1},{14,2},{15,3},{8,4},{9,5},{10,6},{11,7},{4,8},{5,9},... | collective-permute-start | bytes 294920 | tf_op jit(solution)/shard_map/ppermute | solution.py:238
  11.2 4.3 %collective-permute-start.2 = (bf16[16,1024]{1,0:T(8,128)(2,1)S(1)}, bf16[16,1024]{1,0:T(8,128)(2,1)S(1)}, u32[]{:S(2)}, u32[]{:S(2)}) collective-permute-start(bf16[16,1024]{1,0:T(8,128)(2,1)S(1)} %slice.24), channel_id=1, source_target_pairs={{13,0},{12,1},{15,2},{14,3},{9,4},{8,5},{11,6},{10,7},{5,8},{4,9},... | collective-permute-start | bytes 98312 | tf_op jit(solution)/shard_map/ppermute | solution.py:238
  11.8 3.7 %collective-permute-start.4 = (bf16[16,1024]{1,0:T(8,128)(2,1)S(1)}, bf16[16,1024]{1,0:T(8,128)(2,1)S(1)}, u32[]{:S(2)}, u32[]{:S(2)}) collective-permute-start(bf16[16,1024]{1,0:T(8,128)(2,1)S(1)} %slice.24), channel_id=1, source_target_pairs={{5,0},{4,1},{7,2},{6,3},{1,4},{0,5},{3,6},{2,7},{13,8},{12,9},{15,... | collective-permute-start | bytes 98312 | tf_op jit(solution)/shard_map/ppermute | solution.py:238
  15.6 6.8 %collective-permute-start.11 = (bf16[128,1024]{1,0:T(8,128)(2,1)S(1)}, bf16[128,1024]{1,0:T(8,128)(2,1)S(1)}, u32[]{:S(2)}, u32[]{:S(2)}) collective-permute-start(bf16[128,1024]{1,0:T(8,128)(2,1)S(1)} %pad_maximum_fusion.kv_ref.k1_ref), channel_id=1, source_target_pairs={{4,0},{5,1},{6,2},{7,3},{0,4},{1,5},{2,6},{3,7},{12,8},{13,9},{14,... | collective-permute-start | bytes 786440 | tf_op jit(solution)/shard_map/ppermute | solution.py:238
  16.4 1.4 %collective-permute-start.5 = (f32[8,768]{1,0:T(8,128)S(1)}, f32[8,768]{1,0:T(8,128)S(1)}, u32[]{:S(2)}, u32[]{:S(2)}) collective-permute-start(f32[8,768]{1,0:T(8,128)S(1)} %get-tuple-element.69.rows_ref), channel_id=1, source_target_pairs={{4,0},{5,1},{6,2},{7,3},{0,4},{1,5},{2,6},{3,7},{12,8},{13,9},{14,... | collective-permute-start | bytes 73736 | tf_op jit(solution)/shard_map/ppermute | solution.py:238
  19.1 5.8 %collective-permute-start.8 = (bf16[48,1024]{1,0:T(8,128)(2,1)S(1)}, bf16[48,1024]{1,0:T(8,128)(2,1)S(1)}, u32[]{:S(2)}, u32[]{:S(2)}) collective-permute-start(bf16[48,1024]{1,0:T(8,128)(2,1)S(1)} %get-tuple-element.79), channel_id=1, source_target_pairs={{0,12},{1,13},{2,14},{3,15},{4,8},{5,9},{6,10},{7,11},{8,4},{9,5},... | collective-permute-start | bytes 294920 | tf_op jit(solution)/shard_map/ppermute | solution.py:242
  20.3 4.3 %collective-permute-start.10 = (bf16[16,1024]{1,0:T(8,128)(2,1)S(1)}, bf16[16,1024]{1,0:T(8,128)(2,1)S(1)}, u32[]{:S(2)}, u32[]{:S(2)}) collective-permute-start(bf16[16,1024]{1,0:T(8,128)(2,1)S(1)} %get-tuple-element.81), channel_id=1, source_target_pairs={{0,13},{1,12},{2,15},{3,14},{4,9},{5,8},{6,11},{7,10},{8,5},{9,4},... | collective-permute-start | bytes 98312 | tf_op jit(solution)/shard_map/ppermute | solution.py:242
  21.3 3.6 %collective-permute-start.9 = (bf16[16,1024]{1,0:T(8,128)(2,1)S(1)}, bf16[16,1024]{1,0:T(8,128)(2,1)S(1)}, u32[]{:S(2)}, u32[]{:S(2)}) collective-permute-start(bf16[16,1024]{1,0:T(8,128)(2,1)S(1)} %get-tuple-element.80), channel_id=1, source_target_pairs={{0,5},{1,4},{2,7},{3,6},{4,1},{5,0},{6,3},{7,2},{8,13},{9,12},{10,... | collective-permute-start | bytes 98312 | tf_op jit(solution)/shard_map/ppermute | solution.py:242
  25.0 4.8 %collective-permute-start.12 = (bf16[16,1024]{1,0:T(8,128)(2,1)S(1)}, bf16[16,1024]{1,0:T(8,128)(2,1)S(1)}, u32[]{:S(2)}, u32[]{:S(2)}) collective-permute-start(bf16[16,1024]{1,0:T(8,128)(2,1)S(1)} %get-tuple-element.91), channel_id=1, source_target_pairs={{0,6},{1,7},{2,4},{3,5},{4,2},{5,3},{6,0},{7,1},{8,14},{9,15},{10,... | collective-permute-start | bytes 98312 | tf_op jit(solution)/shard_map/ppermute | solution.py:242
  26.4 3.6 %collective-permute-start.13 = (bf16[16,1024]{1,0:T(8,128)(2,1)S(1)}, bf16[16,1024]{1,0:T(8,128)(2,1)S(1)}, u32[]{:S(2)}, u32[]{:S(2)}) collective-permute-start(bf16[16,1024]{1,0:T(8,128)(2,1)S(1)} %get-tuple-element.92), channel_id=1, source_target_pairs={{0,5},{1,4},{2,7},{3,6},{4,1},{5,0},{6,3},{7,2},{8,13},{9,12},{10,... | collective-permute-start | bytes 98312 | tf_op jit(solution)/shard_map/ppermute | solution.py:242

commit v7 on v6

--- a/solution.py
+++ b/solution.py
@@ -311,9 +311,9 @@
             pltpu.SemaphoreType.DMA((HK + 1,)),
         ),
     )
+    terms2 = fetch(worked[2], 1, 0, 0)
     moved, (p_self, ds_self, terms) = lax.optimization_barrier((moved[::-1], worked))
     moved = moved[::-1]
-    terms2 = fetch(terms, 1, 0, 0)
     half = jnp.concatenate([bundle] + moved, 0)
     nk = half.shape[0]
     ds_shape = array((HK, nk, RATIO * rows), b16)
@@ -324,7 +324,7 @@
         (ds_shape, array((nk, 2 * width), f32)),
         (),
         (q, do, terms, half),
-        8 * macs * nk,
+        88 * macs * nk,
     )
     part, terms2, q2, do2 = lax.optimization_barrier((part, terms2, q2, do2))
     cuts = (0, n_first, n_half, n_half + n_first, nk) if relay else (0, n_half, nk)

time: 31.1 us -> 30.9 us (level)
  starting transfers between devices: 15.4 us -> 14.8 us
  waiting for transfers between devices: 2.23 us -> 2.62 us
    ppermute x5, waiting for transfers between devices: 2.11 us -> 2.44 us  [give(): lax.ppermute(array, ('dp', 'resp'), [(i, j) for j, i in pairs(*step)])]
    ppermute x9, starting transfers between devices: 9.75 us -> 9.43 us  [fetch(): return lax.ppermute(array, ('dp', 'resp'), pairs(*step))]
  transfers between devices with their start and end apart: 14 -> 14, of which waited for: 5 -> 4; matrix products, arithmetic and copies ran while one was open for 3% -> 0% of each run, Pallas kernels for 31% -> 31%
where the time goes in v7:
time: 30.9 us; the launch traced here: 30.5 us
  starting transfers between devices  14.8 us (48%)
  Pallas kernels  9.49 us (31%)
  waiting for transfers between devices  2.62 us (8%)
  between operations  2.05 us (7%)
  other arithmetic  0.83 us (3%)
  local copies, waits for them, and re-layouts  0.64 us (2%)
    pallas_call x6, Pallas kernels, call(): pl.pallas_call(kernel, name=name, out_shape=outs, in_specs=[SMEM] * len(s...  9.49 us
    ppermute x9, starting transfers between devices, fetch(): return lax.ppermute(array, ('dp', 'resp'), pairs(*step))  9.43 us
    ppermute x5, starting transfers between devices, give(): lax.ppermute(array, ('dp', 'resp'), [(i, j) for j, i in pairs(*step)])  5.4 us
    ppermute x5, waiting for transfers between devices, give(): lax.ppermute(array, ('dp', 'resp'), [(i, j) for j, i in pairs(*step)])  2.44 us
    concatenate x1, other arithmetic, shards(): jnp.concatenate([prompt_keys[0], prompt_values[0]], axis=1)  0.74 us
    broadcast_in_dim x1, local copies, waits for them, and re-layouts, shards(): total[None, :, width:]  0.63 us
  transfers between devices with their start and end apart: 14, of which 4 were waited for; matrix products, arithmetic and copies ran while one was open for 0% of the time, Pallas kernels for 31%

profile of v7, /device:TPU:0, one launch (start us, length us, event | category | flops | bytes accessed | tf_op | source)
XLA Modules:
  0.0 30.5 jit_solution(16974956880098023202)
XLA Ops:
  0.6 0.7 %pad_maximum_fusion.2 = bf16[16,1024]{1,0:T(8,128)(2,1)S(1)} fusion(bf16[16,512]{1,0:T(8,128)(2,1)} %bitcast.23, bf16[16,512]{1,0:T(8,128)(2,1)} %bitcast.24), kind=kLoop, calls=%fused_computation.8 | loop fusion | flops 65536 | bytes 65536 | tf_op jit(solution)/shard_map/concatenate | solution.py:276
  1.4 3.5 %collective-permute-start = (bf16[16,1024]{1,0:T(8,128)(2,1)S(1)}, bf16[16,1024]{1,0:T(8,128)(2,1)S(1)}, u32[]{:S(2)}, u32[]{:S(2)}) collective-permute-start(bf16[16,1024]{1,0:T(8,128)(2,1)S(1)} %pad_maximum_fusion.2), channel_id=1, source_target_pairs={{6,0},{7,1},{4,2},{5,3},{2,4},{3,5},{0,6},{1,7},{14,8},{15,9},{12,... | collective-permute-start | bytes 98312 | tf_op jit(solution)/shard_map/ppermute | solution.py:238
  4.8 1.9 %collective-permute-start.1 = (bf16[16,1024]{1,0:T(8,128)(2,1)S(1)}, bf16[16,1024]{1,0:T(8,128)(2,1)S(1)}, u32[]{:S(2)}, u32[]{:S(2)}) collective-permute-start(bf16[16,1024]{1,0:T(8,128)(2,1)S(1)} %pad_maximum_fusion.2), channel_id=1, source_target_pairs={{5,0},{4,1},{7,2},{6,3},{1,4},{0,5},{3,6},{2,7},{13,8},{12,9},{15,... | collective-permute-start | bytes 98312 | tf_op jit(solution)/shard_map/ppermute | solution.py:238
  6.7 0.0 collective-permute-start.6
  6.7 0.5 %collective-permute-start.7 = (bf16[128,2560]{1,0:T(8,128)(2,1)}, bf16[128,2560]{1,0:T(8,128)(2,1)S(1)}, u32[]{:S(2)}, u32[]{:S(2)}) collective-permute-start(bf16[128,2560]{1,0:T(8,128)(2,1)} %bitcast.18), channel_id=1, source_target_pairs={{4,0},{5,1},{6,2},{7,3},{0,4},{1,5},{2,6},{3,7},{12,8},{13,9},{14,... | collective-permute-start | bytes 1966088 | tf_op jit(solution)/shard_map/ppermute | solution.py:238
  8.5 1.4 %load.1 = (bf16[128,2560]{1,0:T(8,128)(2,1)S(1)}, bf16[128,2560]{1,0:T(8,128)(2,1)S(1)}, bf16[128,512]{1,0:T(8,128)(2,1)S(1)}, bf16[128,512]{1,0:T(8,128)(2,1)S(1)}, s32[8,256]{1,0:T(8,128)S(1)}) custom-call(s32[1]{0:T(128)S(6)} %copy.15.len_ref, s32[1]{0:T(128)S(6)} %copy.16.seen_ref, bf16[128,2560]{1,0:T(8,128)(2,1)} %bitcast.17, ...), custom_call_target="tpu_custom_call" | custom-call | bytes 1572864 | tf_op jit(solution)/shard_map/load/pallas_call | solution.py:208
  9.9 0.0 collective-permute-done
  9.9 0.0 collective-permute-done.1
  9.9 1.2 %collective-permute-start.3 = (bf16[48,1024]{1,0:T(8,128)(2,1)S(1)}, bf16[48,1024]{1,0:T(8,128)(2,1)S(1)}, u32[]{:S(2)}, u32[]{:S(2)}) collective-permute-start(bf16[48,1024]{1,0:T(8,128)(2,1)S(1)} %pad_maximum_fusion.1), channel_id=1, source_target_pairs={{12,0},{13,1},{14,2},{15,3},{8,4},{9,5},{10,6},{11,7},{4,8},{5,9},... | collective-permute-start | bytes 294920 | tf_op jit(solution)/shard_map/ppermute | solution.py:238
  11.1 0.5 %collective-permute-start.2 = (bf16[16,1024]{1,0:T(8,128)(2,1)S(1)}, bf16[16,1024]{1,0:T(8,128)(2,1)S(1)}, u32[]{:S(2)}, u32[]{:S(2)}) collective-permute-start(bf16[16,1024]{1,0:T(8,128)(2,1)S(1)} %slice.24), channel_id=1, source_target_pairs={{13,0},{12,1},{15,2},{14,3},{9,4},{8,5},{11,6},{10,7},{5,8},{4,9},... | collective-permute-start | bytes 98312 | tf_op jit(solution)/shard_map/ppermute | solution.py:238
  11.6 1.2 %collective-permute-start.4 = (bf16[16,1024]{1,0:T(8,128)(2,1)S(1)}, bf16[16,1024]{1,0:T(8,128)(2,1)S(1)}, u32[]{:S(2)}, u32[]{:S(2)}) collective-permute-start(bf16[16,1024]{1,0:T(8,128)(2,1)S(1)} %slice.24), channel_id=1, source_target_pairs={{5,0},{4,1},{7,2},{6,3},{1,4},{0,5},{3,6},{2,7},{13,8},{12,9},{15,... | collective-permute-start | bytes 98312 | tf_op jit(solution)/shard_map/ppermute | solution.py:238
  12.8 2.5 %self_pairs.1 = (bf16[4,128,640]{2,1,0:T(8,128)(2,1)S(1)}, bf16[4,128,640]{2,1,0:T(8,128)(2,1)S(1)}, f32[8,768]{1,0:T(8,128)S(1)}) custom-call(s32[8,256]{1,0:T(8,128)S(1)} %get-tuple-element.63.scalars_ref, bf16[128,2560]{1,0:T(8,128)(2,1)S(1)} %get-tuple-element.58.q_ref, bf16[128,2560]{1,0:T(8,128)(2,1)S(1)} %get-tuple-element.59.do_ref, ...), custom_call_target="tpu_custom_call" | custom-call | flops 209715200 | bytes 2246656 | tf_op jit(solution)/shard_map/self_pairs/pallas_call | solution.py:208
  15.3 0.2 collective-permute-done.2
  15.4 0.6 %collective-permute-start.5 = (f32[8,768]{1,0:T(8,128)S(1)}, f32[8,768]{1,0:T(8,128)S(1)}, u32[]{:S(2)}, u32[]{:S(2)}) collective-permute-start(f32[8,768]{1,0:T(8,128)S(1)} %get-tuple-element.69.rows_ref), channel_id=1, source_target_pairs={{4,0},{5,1},{6,2},{7,3},{0,4},{1,5},{2,6},{3,7},{12,8},{13,9},{14,... | collective-permute-start | bytes 73736 | tf_op jit(solution)/shard_map/ppermute | solution.py:238
  16.1 0.0 collective-permute-done.4
  16.1 0.0 collective-permute-done.3
  16.1 0.1 collective-permute-start.11
  16.2 1.3 %own_pairs.1 = (bf16[4,128,640]{2,1,0:T(8,128)(2,1)S(1)}, f32[128,1024]{1,0:T(8,128)S(1)}) custom-call(bf16[128,2560]{1,0:T(8,128)(2,1)S(1)} %get-tuple-element.58.q_ref, bf16[128,2560]{1,0:T(8,128)(2,1)S(1)} %get-tuple-element.59.do_ref, f32[8,768]{1,0:T(8,128)S(1)} %get-tuple-element.69.rows_ref, bf16[128,1024]{1,0:T(8,128)(2,1)S(1)} %pad_maximum_fusion.kv_ref.k1_ref), custom_call_target="tpu_custom_call" | custom-call | flops 3690987520 | bytes 1597440 | tf_op jit(solution)/shard_map/own_pairs/pallas_call | solution.py:208
  17.5 0.0 collective-permute-done.5.rows_ref
  17.5 0.0 collective-permute-done.6.q_ref
  17.5 0.0 collective-permute-done.7.do_ref
  17.5 1.3 %other_pairs.1 = (f32[48,1024]{1,0:T(8,128)S(1)}, bf16[16,1024]{1,0:T(8,128)(2,1)S(1)}, bf16[48,1024]{1,0:T(8,128)(2,1)S(1)}, bf16[16,1024]{1,0:T(8,128)(2,1)S(1)}) custom-call(bf16[128,2560]{1,0:T(8,128)(2,1)S(1)} %collective-permute-done.6.q_ref, bf16[128,2560]{1,0:T(8,128)(2,1)S(1)} %collective-permute-done.7.do_ref, ...), custom_call_target="tpu_custom_call" | custom-call | flops 335544320 | bytes 2121728 | tf_op jit(solution)/shard_map/other_pairs/pallas_call | solution.py:208
  18.8 1.5 %collective-permute-start.8 = (bf16[48,1024]{1,0:T(8,128)(2,1)S(1)}, bf16[48,1024]{1,0:T(8,128)(2,1)S(1)}, u32[]{:S(2)}, u32[]{:S(2)}) collective-permute-start(bf16[48,1024]{1,0:T(8,128)(2,1)S(1)} %get-tuple-element.79), channel_id=1, source_target_pairs={{0,12},{1,13},{2,14},{3,15},{4,8},{5,9},{6,10},{7,11},{8,4},{9,5},... | collective-permute-start | bytes 294920 | tf_op jit(solution)/shard_map/ppermute | solution.py:242
  20.3 0.5 %collective-permute-start.10 = (bf16[16,1024]{1,0:T(8,128)(2,1)S(1)}, bf16[16,1024]{1,0:T(8,128)(2,1)S(1)}, u32[]{:S(2)}, u32[]{:S(2)}) collective-permute-start(bf16[16,1024]{1,0:T(8,128)(2,1)S(1)} %get-tuple-element.81), channel_id=1, source_target_pairs={{0,13},{1,12},{2,15},{3,14},{4,9},{5,8},{6,11},{7,10},{8,5},{9,4},... | collective-permute-start | bytes 98312 | tf_op jit(solution)/shard_map/ppermute | solution.py:242
  20.8 1.4 %collective-permute-start.9 = (bf16[16,1024]{1,0:T(8,128)(2,1)S(1)}, bf16[16,1024]{1,0:T(8,128)(2,1)S(1)}, u32[]{:S(2)}, u32[]{:S(2)}) collective-permute-start(bf16[16,1024]{1,0:T(8,128)(2,1)S(1)} %get-tuple-element.80), channel_id=1, source_target_pairs={{0,5},{1,4},{2,7},{3,6},{4,1},{5,0},{6,3},{7,2},{8,13},{9,12},{10,... | collective-permute-start | bytes 98312 | tf_op jit(solution)/shard_map/ppermute | solution.py:242
  22.2 0.0 collective-permute-done.11.kv_ref.k2_ref
  22.2 1.5 %response_grads.1 = (bf16[128,512]{1,0:T(8,128)(2,1)}, bf16[128,512]{1,0:T(8,128)(2,1)}, bf16[4,128,640]{2,1,0:T(8,128)(2,1)S(1)}) custom-call(bf16[128,2560]{1,0:T(8,128)(2,1)S(1)} %get-tuple-element.58.q_ref, bf16[128,2560]{1,0:T(8,128)(2,1)S(1)} %get-tuple-element.59.do_ref, f32[8,768]{1,0:T(8,128)S(1)} %get-tuple-element.69.rows_ref, ...), custom_call_target="tpu_custom_call" | custom-call | flops 335544320 | bytes 2908160 | tf_op jit(solution)/shard_map/response_grads/pallas_call | solution.py:208
  23.7 1.0 %collective-permute-done.10 = bf16[16,1024]{1,0:T(8,128)(2,1)S(1)} collective-permute-done((bf16[16,1024]{1,0:T(8,128)(2,1)S(1)}, bf16[16,1024]{1,0:T(8,128)(2,1)S(1)}, u32[]{:S(2)}, u32[]{:S(2)}) %collective-permute-start.10) | collective-permute-done | bytes 32800 | tf_op jit(solution)/shard_map/ppermute | solution.py:242
  24.7 0.0 collective-permute-done.9
  24.7 0.0 collective-permute-done.8
  24.8 1.0 %collective-permute-start.12 = (bf16[16,1024]{1,0:T(8,128)(2,1)S(1)}, bf16[16,1024]{1,0:T(8,128)(2,1)S(1)}, u32[]{:S(2)}, u32[]{:S(2)}) collective-permute-start(bf16[16,1024]{1,0:T(8,128)(2,1)S(1)} %get-tuple-element.91), channel_id=1, source_target_pairs={{0,6},{1,7},{2,4},{3,5},{4,2},{5,3},{6,0},{7,1},{8,14},{9,15},{10,... | collective-permute-start | bytes 98312 | tf_op jit(solution)/shard_map/ppermute | solution.py:242
  25.8 1.0 %collective-permute-start.13 = (bf16[16,1024]{1,0:T(8,128)(2,1)S(1)}, bf16[16,1024]{1,0:T(8,128)(2,1)S(1)}, u32[]{:S(2)}, u32[]{:S(2)}) collective-permute-start(bf16[16,1024]{1,0:T(8,128)(2,1)S(1)} %get-tuple-element.92), channel_id=1, source_target_pairs={{0,5},{1,4},{2,7},{3,6},{4,1},{5,0},{6,3},{7,2},{8,13},{9,12},{10,... | collective-permute-start | bytes 98312 | tf_op jit(solution)/shard_map/ppermute | solution.py:242
  26.8 1.5 %query_grads.1 = bf16[128,2560]{1,0:T(8,128)(2,1)} custom-call(bf16[4,128,640]{2,1,0:T(8,128)(2,1)S(1)} %get-tuple-element.83.ds_ref.ds0_ref, bf16[4,128,640]{2,1,0:T(8,128)(2,1)S(1)} %get-tuple-element.93.ds1_ref, bf16[4,128,640]{2,1,0:T(8,128)(2,1)S(1)} %get-tuple-element.94.ds2_ref, bf16[128,512]{1,0:T(8,128)(2,1)S(1)} %get-tuple-element.64.k_ref.k0_ref, ...), custom_call_target="tpu_custom_call" | custom-call | flops 251658240 | bytes 2621440 | tf_op jit(solution)/shard_map/query_grads/pallas_call | solution.py:208
  28.3 1.2 %collective-permute-done.12 = bf16[16,1024]{1,0:T(8,128)(2,1)S(1)} collective-permute-done((bf16[16,1024]{1,0:T(8,128)(2,1)S(1)}, bf16[16,1024]{1,0:T(8,128)(2,1)S(1)}, u32[]{:S(2)}, u32[]{:S(2)}) %collective-permute-start.12) | collective-permute-done | bytes 32800 | tf_op jit(solution)/shard_map/ppermute | solution.py:242
  29.5 0.3 %collective-permute-done.13 = bf16[16,1024]{1,0:T(8,128)(2,1)S(1)} collective-permute-done((bf16[16,1024]{1,0:T(8,128)(2,1)S(1)}, bf16[16,1024]{1,0:T(8,128)(2,1)S(1)}, u32[]{:S(2)}, u32[]{:S(2)}) %collective-permute-start.13) | collective-permute-done | bytes 32800 | tf_op jit(solution)/shard_map/ppermute | solution.py:242
  29.8 0.6 %slice_bitcast_fusion = (f32[1,16,512]{2,1,0:T(8,128)}, f32[1,16,512]{2,1,0:T(8,128)}) fusion(f32[16,1024]{1,0:T(8,128)S(1)} %convert_add_fusion.1), kind=kLoop, calls=%fused_computation.6 | loop fusion | bytes 131072 | tf_op jit(solution)/shard_map/broadcast_in_dim | solution.py:382
  (7 shorter events, 0.1 us)
Async XLA Ops:
  1.4 8.5 %collective-permute-start = (bf16[16,1024]{1,0:T(8,128)(2,1)S(1)}, bf16[16,1024]{1,0:T(8,128)(2,1)S(1)}, u32[]{:S(2)}, u32[]{:S(2)}) collective-permute-start(bf16[16,1024]{1,0:T(8,128)(2,1)S(1)} %pad_maximum_fusion.2), channel_id=1, source_target_pairs={{6,0},{7,1},{4,2},{5,3},{2,4},{3,5},{0,6},{1,7},{14,8},{15,9},{12,... | collective-permute-start | bytes 98312 | tf_op jit(solution)/shard_map/ppermute | solution.py:238
  4.8 5.1 %collective-permute-start.1 = (bf16[16,1024]{1,0:T(8,128)(2,1)S(1)}, bf16[16,1024]{1,0:T(8,128)(2,1)S(1)}, u32[]{:S(2)}, u32[]{:S(2)}) collective-permute-start(bf16[16,1024]{1,0:T(8,128)(2,1)S(1)} %pad_maximum_fusion.2), channel_id=1, source_target_pairs={{5,0},{4,1},{7,2},{6,3},{1,4},{0,5},{3,6},{2,7},{13,8},{12,9},{15,... | collective-permute-start | bytes 98312 | tf_op jit(solution)/shard_map/ppermute | solution.py:238
  6.7 10.8 %collective-permute-start.6 = (bf16[128,2560]{1,0:T(8,128)(2,1)}, bf16[128,2560]{1,0:T(8,128)(2,1)S(1)}, u32[]{:S(2)}, u32[]{:S(2)}) collective-permute-start(bf16[128,2560]{1,0:T(8,128)(2,1)} %bitcast.16), channel_id=1, source_target_pairs={{4,0},{5,1},{6,2},{7,3},{0,4},{1,5},{2,6},{3,7},{12,8},{13,9},{14,... | collective-permute-start | bytes 1966088 | tf_op jit(solution)/shard_map/ppermute | solution.py:238
  6.7 10.8 %collective-permute-start.7 = (bf16[128,2560]{1,0:T(8,128)(2,1)}, bf16[128,2560]{1,0:T(8,128)(2,1)S(1)}, u32[]{:S(2)}, u32[]{:S(2)}) collective-permute-start(bf16[128,2560]{1,0:T(8,128)(2,1)} %bitcast.18), channel_id=1, source_target_pairs={{4,0},{5,1},{6,2},{7,3},{0,4},{1,5},{2,6},{3,7},{12,8},{13,9},{14,... | collective-permute-start | bytes 1966088 | tf_op jit(solution)/shard_map/ppermute | solution.py:238
  9.9 6.1 %collective-permute-start.3 = (bf16[48,1024]{1,0:T(8,128)(2,1)S(1)}, bf16[48,1024]{1,0:T(8,128)(2,1)S(1)}, u32[]{:S(2)}, u32[]{:S(2)}) collective-permute-start(bf16[48,1024]{1,0:T(8,128)(2,1)S(1)} %pad_maximum_fusion.1), channel_id=1, source_target_pairs={{12,0},{13,1},{14,2},{15,3},{8,4},{9,5},{10,6},{11,7},{4,8},{5,9},... | collective-permute-start | bytes 294920 | tf_op jit(solution)/shard_map/ppermute | solution.py:238
  11.1 4.3 %collective-permute-start.2 = (bf16[16,1024]{1,0:T(8,128)(2,1)S(1)}, bf16[16,1024]{1,0:T(8,128)(2,1)S(1)}, u32[]{:S(2)}, u32[]{:S(2)}) collective-permute-start(bf16[16,1024]{1,0:T(8,128)(2,1)S(1)} %slice.24), channel_id=1, source_target_pairs={{13,0},{12,1},{15,2},{14,3},{9,4},{8,5},{11,6},{10,7},{5,8},{4,9},... | collective-permute-start | bytes 98312 | tf_op jit(solution)/shard_map/ppermute | solution.py:238
  11.6 4.4 %collective-permute-start.4 = (bf16[16,1024]{1,0:T(8,128)(2,1)S(1)}, bf16[16,1024]{1,0:T(8,128)(2,1)S(1)}, u32[]{:S(2)}, u32[]{:S(2)}) collective-permute-start(bf16[16,1024]{1,0:T(8,128)(2,1)S(1)} %slice.24), channel_id=1, source_target_pairs={{5,0},{4,1},{7,2},{6,3},{1,4},{0,5},{3,6},{2,7},{13,8},{12,9},{15,... | collective-permute-start | bytes 98312 | tf_op jit(solution)/shard_map/ppermute | solution.py:238
  15.4 2.0 %collective-permute-start.5 = (f32[8,768]{1,0:T(8,128)S(1)}, f32[8,768]{1,0:T(8,128)S(1)}, u32[]{:S(2)}, u32[]{:S(2)}) collective-permute-start(f32[8,768]{1,0:T(8,128)S(1)} %get-tuple-element.69.rows_ref), channel_id=1, source_target_pairs={{4,0},{5,1},{6,2},{7,3},{0,4},{1,5},{2,6},{3,7},{12,8},{13,9},{14,... | collective-permute-start | bytes 73736 | tf_op jit(solution)/shard_map/ppermute | solution.py:238
  16.1 6.1 %collective-permute-start.11 = (bf16[128,1024]{1,0:T(8,128)(2,1)S(1)}, bf16[128,1024]{1,0:T(8,128)(2,1)S(1)}, u32[]{:S(2)}, u32[]{:S(2)}) collective-permute-start(bf16[128,1024]{1,0:T(8,128)(2,1)S(1)} %pad_maximum_fusion.kv_ref.k1_ref), channel_id=1, source_target_pairs={{4,0},{5,1},{6,2},{7,3},{0,4},{1,5},{2,6},{3,7},{12,8},{13,9},{14,... | collective-permute-start | bytes 786440 | tf_op jit(solution)/shard_map/ppermute | solution.py:238
  18.8 5.9 %collective-permute-start.8 = (bf16[48,1024]{1,0:T(8,128)(2,1)S(1)}, bf16[48,1024]{1,0:T(8,128)(2,1)S(1)}, u32[]{:S(2)}, u32[]{:S(2)}) collective-permute-start(bf16[48,1024]{1,0:T(8,128)(2,1)S(1)} %get-tuple-element.79), channel_id=1, source_target_pairs={{0,12},{1,13},{2,14},{3,15},{4,8},{5,9},{6,10},{7,11},{8,4},{9,5},... | collective-permute-start | bytes 294920 | tf_op jit(solution)/shard_map/ppermute | solution.py:242
  20.3 4.4 %collective-permute-start.10 = (bf16[16,1024]{1,0:T(8,128)(2,1)S(1)}, bf16[16,1024]{1,0:T(8,128)(2,1)S(1)}, u32[]{:S(2)}, u32[]{:S(2)}) collective-permute-start(bf16[16,1024]{1,0:T(8,128)(2,1)S(1)} %get-tuple-element.81), channel_id=1, source_target_pairs={{0,13},{1,12},{2,15},{3,14},{4,9},{5,8},{6,11},{7,10},{8,5},{9,4},... | collective-permute-start | bytes 98312 | tf_op jit(solution)/shard_map/ppermute | solution.py:242
  20.8 3.9 %collective-permute-start.9 = (bf16[16,1024]{1,0:T(8,128)(2,1)S(1)}, bf16[16,1024]{1,0:T(8,128)(2,1)S(1)}, u32[]{:S(2)}, u32[]{:S(2)}) collective-permute-start(bf16[16,1024]{1,0:T(8,128)(2,1)S(1)} %get-tuple-element.80), channel_id=1, source_target_pairs={{0,5},{1,4},{2,7},{3,6},{4,1},{5,0},{6,3},{7,2},{8,13},{9,12},{10,... | collective-permute-start | bytes 98312 | tf_op jit(solution)/shard_map/ppermute | solution.py:242
  24.8 4.7 %collective-permute-start.12 = (bf16[16,1024]{1,0:T(8,128)(2,1)S(1)}, bf16[16,1024]{1,0:T(8,128)(2,1)S(1)}, u32[]{:S(2)}, u32[]{:S(2)}) collective-permute-start(bf16[16,1024]{1,0:T(8,128)(2,1)S(1)} %get-tuple-element.91), channel_id=1, source_target_pairs={{0,6},{1,7},{2,4},{3,5},{4,2},{5,3},{6,0},{7,1},{8,14},{9,15},{10,... | collective-permute-start | bytes 98312 | tf_op jit(solution)/shard_map/ppermute | solution.py:242
  25.8 4.0 %collective-permute-start.13 = (bf16[16,1024]{1,0:T(8,128)(2,1)S(1)}, bf16[16,1024]{1,0:T(8,128)(2,1)S(1)}, u32[]{:S(2)}, u32[]{:S(2)}) collective-permute-start(bf16[16,1024]{1,0:T(8,128)(2,1)S(1)} %get-tuple-element.92), channel_id=1, source_target_pairs={{0,5},{1,4},{2,7},{3,6},{4,1},{5,0},{6,3},{7,2},{8,13},{9,12},{10,... | collective-permute-start | bytes 98312 | tf_op jit(solution)/shard_map/ppermute | solution.py:242

commit v8 on v7

--- a/solution.py
+++ b/solution.py
@@ -52,15 +52,14 @@
     return jnp.broadcast_to(row, (8, row.shape[1]))
 
 
-def load_kernel(len_ref, seen_ref, *refs):
-    count = (len(refs) - 2) // 2
-    sems, outs = refs[-1], refs[count:-1]
+def load_kernel(len_ref, seen_ref, q_hbm, k_hbm, ln_hbm, q_ref, k_ref, ln_ref, out_ref, sems):
     copies = [
-        pltpu.make_async_copy(refs[i], outs[i], sems.at[i]) for i in range(count)
+        pltpu.make_async_copy(hbm, ref, sems.at[i])
+        for i, (hbm, ref) in enumerate(((q_hbm, q_ref), (k_hbm, k_ref), (ln_hbm, ln_ref)))
     ]
     for copy in copies:
         copy.start()
-    outs[count][...] = jnp.concatenate(
+    out_ref[...] = jnp.concatenate(
         [jnp.full((8, DH), ref[0], jnp.int32) for ref in (len_ref, seen_ref)], axis=1
     )
     for copy in copies:
@@ -68,26 +67,23 @@
 
 
 def self_kernel(
-    scalars_ref, q_ref, do_ref, k_ref, v_ref, o_hbm, ln_hbm, p_ref, ds_ref, rows_ref,
-    o_ref, ln_ref, probs_ref, sems,
+    scalars_ref, q_ref, k_ref, ln_ref, do_hbm, v_hbm, o_hbm,
+    do_ref, p_ref, ds_ref, rows_ref, v_ref, o_ref, probs_ref, sems,
 ):
     rows = q_ref.shape[0]
     nq = RATIO * rows
-    span = RATIO * DH
-    first = pltpu.make_async_copy(ln_hbm, ln_ref, sems.at[HK])
-    first.start()
-    parts = []
-    for g in range(HK):
-        cols = slice(g * span, (g + 1) * span)
-        parts.append(pltpu.make_async_copy(o_hbm.at[:, cols], o_ref.at[:, cols], sems.at[g]))
-        parts[g].start()
+    copies = [
+        pltpu.make_async_copy(hbm, ref, sems.at[i])
+        for i, (hbm, ref) in enumerate(((do_hbm, do_ref), (v_hbm, v_ref), (o_hbm, o_ref)))
+    ]
+    for copy in copies:
+        copy.start()
     live = lax.broadcasted_iota(jnp.int32, (1, rows), 1) < scalars_ref[:1, :rows]
     key_at = lax.broadcasted_iota(jnp.int32, (rows, nq), 0)
     query_at = lax.broadcasted_iota(jnp.int32, (rows, nq), 1) % rows
     keep = (key_at <= query_at).reshape(rows // 8, 8, nq)
     same = key_at[:, :rows] == query_at[:, :rows]
     rows_ref[:, nq:] = scalars_ref[:, DH:].astype(jnp.float32)
-    first.wait()
     for g in range(HK):
         lse_row = jnp.concatenate(
             [
@@ -101,8 +97,9 @@
         probs = jnp.where(keep, probabilities(scores, eight(lse_row)[None]), 0.0)
         probs_ref[g] = probs.reshape(rows, nq)
         p_ref[g] = probs.reshape(rows, nq).astype(p_ref.dtype)
-    for g in range(HK):
-        parts[g].wait()
+    for copy in copies:
+        copy.wait()
+    for g in range(HK):
         delta_parts = []
         for h in range(g * RATIO, (g + 1) * RATIO):
             cols = slice(h * DH, (h + 1) * DH)
@@ -276,17 +273,21 @@
     own = lax.optimization_barrier(jnp.concatenate([prompt_keys[0], prompt_values[0]], axis=1))
     got = [own] + [fetch(own, 1, 0, k) for k in near]
     q2, do2 = fetch(queries[0], 1, 0, 0), fetch(grad_out[0], 1, 0, 0)
+    pair_shape = (HK, rows, RATIO * rows)
+    terms_shape = array((8, RATIO * rows + DH), f32)
+    narrow = array((rows, width), b16)
+    narrow = array((rows, width), b16)
     loaded = call(
         load_kernel,
         "load",
-        (full, full, *[array((rows, width), b16)] * 2, array((8, 2 * DH), jnp.int32)),
+        (full, narrow, array((HQ, 1, rows), f32), array((8, 2 * DH), jnp.int32)),
         (resp_len, seen_blocks),
         (),
         0,
-        (queries[0], grad_out[0], resp_keys[0], resp_values[0]),
-        (pltpu.SemaphoreType.DMA((4,)),),
-    )
-    got, (q, do, kr, vr, scalars) = lax.optimization_barrier((got[::-1], loaded))
+        (queries[0], resp_keys[0], ln),
+        (pltpu.SemaphoreType.DMA((3,)),),
+    )
+    got, (q, kr, ln, scalars) = lax.optimization_barrier((got[::-1], loaded))
     got = got[::-1]
 
     bundle = lax.optimization_barrier(jnp.concatenate(got, 0))
@@ -295,24 +296,24 @@
         piece = bundle[relay[1] * PB :][:PB]
         far = fetch(piece, 1, 1, relay[0])
         moved = [fetch(piece, 1, 0, relay[0])] + moved + [far]
-    ds_self_shape = array((HK, rows, RATIO * rows), b16)
+    pair_shape = array((HK, rows, RATIO * rows), b16)
     worked = call(
         self_kernel,
         "self_pairs",
-        (ds_self_shape, ds_self_shape, array((8, RATIO * rows + DH), f32)),
-        (),
-        (scalars, q, do, kr, vr),
+        (full, pair_shape, pair_shape, array((8, RATIO * rows + DH), f32)),
+        (),
+        (scalars, q, kr, ln),
         5 * macs * rows,
-        (forward_out[0], ln),
+        (grad_out[0], resp_values[0], forward_out[0]),
         (
+            pltpu.VMEM((rows, width), b16),
             pltpu.VMEM((rows, HQ * DH), b16),
-            pltpu.VMEM((HQ, 1, rows), f32),
             pltpu.VMEM((HK, rows, RATIO * rows), f32),
-            pltpu.SemaphoreType.DMA((HK + 1,)),
+            pltpu.SemaphoreType.DMA((3,)),
         ),
     )
-    terms2 = fetch(worked[2], 1, 0, 0)
-    moved, (p_self, ds_self, terms) = lax.optimization_barrier((moved[::-1], worked))
+    terms2 = fetch(worked[3], 1, 0, 0)
+    moved, (do, p_self, ds_self, terms) = lax.optimization_barrier((moved[::-1], worked))
     moved = moved[::-1]
     half = jnp.concatenate([bundle] + moved, 0)
     nk = half.shape[0]

time: 30.9 us -> 30.1 us (0.974)
  Pallas kernels: 9.49 us -> 9.01 us
  waiting for transfers between devices: 2.62 us -> 2.31 us
    ppermute x5, waiting for transfers between devices: 2.44 us -> 1.86 us  [give(): lax.ppermute(array, ('dp', 'resp'), [(i, j) for j, i in pairs(*step)])]
    pallas_call x6, Pallas kernels: 9.49 us -> 9.01 us  [call(): pl.pallas_call(kernel, name=name, out_shape=outs, in_specs=[SMEM] * len(s...]
  transfers between devices with their start and end apart: 14 -> 14, of which waited for: 4 -> 5; matrix products, arithmetic and copies ran while one was open for 0% -> 0% of each run, Pallas kernels for 31% -> 30%
where the time goes in v8:
time: 30.1 us; the launch traced here: 29.8 us
  starting transfers between devices  15 us (50%)
  Pallas kernels  9.01 us (30%)
  waiting for transfers between devices  2.31 us (8%)
  between operations  2.05 us (7%)
  other arithmetic  0.83 us (3%)
  local copies, waits for them, and re-layouts  0.64 us (2%)
    ppermute x9, starting transfers between devices, fetch(): return lax.ppermute(array, ('dp', 'resp'), pairs(*step))  9.43 us
    pallas_call x6, Pallas kernels, call(): pl.pallas_call(kernel, name=name, out_shape=outs, in_specs=[SMEM] * len(s...  9.01 us
    ppermute x5, starting transfers between devices, give(): lax.ppermute(array, ('dp', 'resp'), [(i, j) for j, i in pairs(*step)])  5.56 us
    ppermute x5, waiting for transfers between devices, give(): lax.ppermute(array, ('dp', 'resp'), [(i, j) for j, i in pairs(*step)])  1.86 us
    concatenate x1, other arithmetic, shards(): jnp.concatenate([prompt_keys[0], prompt_values[0]], axis=1)  0.74 us
    broadcast_in_dim x1, local copies, waits for them, and re-layouts, shards(): total[None, :, width:]  0.63 us
  transfers between devices with their start and end apart: 14, of which 5 were waited for; matrix products, arithmetic and copies ran while one was open for 0% of the time, Pallas kernels for 30%

profile of v8, /device:TPU:0, one launch (start us, length us, event | category | flops | bytes accessed | tf_op | source)
XLA Modules:
  0.0 29.8 jit_solution(2707345487920717)
XLA Ops:
  0.6 0.7 %pad_maximum_fusion.2 = bf16[16,1024]{1,0:T(8,128)(2,1)S(1)} fusion(bf16[16,512]{1,0:T(8,128)(2,1)} %bitcast.23, bf16[16,512]{1,0:T(8,128)(2,1)} %bitcast.24), kind=kLoop, calls=%fused_computation.8 | loop fusion | flops 65536 | bytes 65536 | tf_op jit(solution)/shard_map/concatenate | solution.py:273
  1.4 3.5 %collective-permute-start = (bf16[16,1024]{1,0:T(8,128)(2,1)S(1)}, bf16[16,1024]{1,0:T(8,128)(2,1)S(1)}, u32[]{:S(2)}, u32[]{:S(2)}) collective-permute-start(bf16[16,1024]{1,0:T(8,128)(2,1)S(1)} %pad_maximum_fusion.2), channel_id=1, source_target_pairs={{6,0},{7,1},{4,2},{5,3},{2,4},{3,5},{0,6},{1,7},{14,8},{15,9},{12,... | collective-permute-start | bytes 98312 | tf_op jit(solution)/shard_map/ppermute | solution.py:235
  4.8 1.9 %collective-permute-start.1 = (bf16[16,1024]{1,0:T(8,128)(2,1)S(1)}, bf16[16,1024]{1,0:T(8,128)(2,1)S(1)}, u32[]{:S(2)}, u32[]{:S(2)}) collective-permute-start(bf16[16,1024]{1,0:T(8,128)(2,1)S(1)} %pad_maximum_fusion.2), channel_id=1, source_target_pairs={{5,0},{4,1},{7,2},{6,3},{1,4},{0,5},{3,6},{2,7},{13,8},{12,9},{15,... | collective-permute-start | bytes 98312 | tf_op jit(solution)/shard_map/ppermute | solution.py:235
  6.7 0.0 collective-permute-start.6
  6.7 0.5 %collective-permute-start.7 = (bf16[128,2560]{1,0:T(8,128)(2,1)}, bf16[128,2560]{1,0:T(8,128)(2,1)S(1)}, u32[]{:S(2)}, u32[]{:S(2)}) collective-permute-start(bf16[128,2560]{1,0:T(8,128)(2,1)} %bitcast.16), channel_id=1, source_target_pairs={{4,0},{5,1},{6,2},{7,3},{0,4},{1,5},{2,6},{3,7},{12,8},{13,9},{14,... | collective-permute-start | bytes 1966088 | tf_op jit(solution)/shard_map/ppermute | solution.py:235
  8.5 1.1 %load.1 = (bf16[128,2560]{1,0:T(8,128)(2,1)S(1)}, bf16[128,512]{1,0:T(8,128)(2,1)S(1)}, f32[20,1,128]{2,1,0:T(1,128)S(1)}, s32[8,256]{1,0:T(8,128)S(1)}) custom-call(s32[1]{0:T(128)S(6)} %copy.15.len_ref, s32[1]{0:T(128)S(6)} %copy.16.seen_ref, bf16[128,2560]{1,0:T(8,128)(2,1)} %bitcast.19, bf16[128,512]{1,0:T(8,128)(2,1)} %bitcast.21, f32[20,1,128]{2,1,0:T(1,128)} %bitcast.25), custom_call_target="tpu_custom_call" | custom-call | bytes 796672 | tf_op jit(solution)/shard_map/load/pallas_call | solution.py:205
  9.7 0.0 collective-permute-done
  9.7 0.0 collective-permute-done.1
  9.7 1.2 %collective-permute-start.3 = (bf16[48,1024]{1,0:T(8,128)(2,1)S(1)}, bf16[48,1024]{1,0:T(8,128)(2,1)S(1)}, u32[]{:S(2)}, u32[]{:S(2)}) collective-permute-start(bf16[48,1024]{1,0:T(8,128)(2,1)S(1)} %pad_maximum_fusion.1), channel_id=1, source_target_pairs={{12,0},{13,1},{14,2},{15,3},{8,4},{9,5},{10,6},{11,7},{4,8},{5,9},... | collective-permute-start | bytes 294920 | tf_op jit(solution)/shard_map/ppermute | solution.py:235
  10.9 0.5 %collective-permute-start.2 = (bf16[16,1024]{1,0:T(8,128)(2,1)S(1)}, bf16[16,1024]{1,0:T(8,128)(2,1)S(1)}, u32[]{:S(2)}, u32[]{:S(2)}) collective-permute-start(bf16[16,1024]{1,0:T(8,128)(2,1)S(1)} %slice.24), channel_id=1, source_target_pairs={{13,0},{12,1},{15,2},{14,3},{9,4},{8,5},{11,6},{10,7},{5,8},{4,9},... | collective-permute-start | bytes 98312 | tf_op jit(solution)/shard_map/ppermute | solution.py:235
  11.4 1.2 %collective-permute-start.4 = (bf16[16,1024]{1,0:T(8,128)(2,1)S(1)}, bf16[16,1024]{1,0:T(8,128)(2,1)S(1)}, u32[]{:S(2)}, u32[]{:S(2)}) collective-permute-start(bf16[16,1024]{1,0:T(8,128)(2,1)S(1)} %slice.24), channel_id=1, source_target_pairs={{5,0},{4,1},{7,2},{6,3},{1,4},{0,5},{3,6},{2,7},{13,8},{12,9},{15,... | collective-permute-start | bytes 98312 | tf_op jit(solution)/shard_map/ppermute | solution.py:235
  12.6 2.2 %self_pairs.1 = (bf16[128,2560]{1,0:T(8,128)(2,1)S(1)}, bf16[4,128,640]{2,1,0:T(8,128)(2,1)S(1)}, bf16[4,128,640]{2,1,0:T(8,128)(2,1)S(1)}, f32[8,768]{1,0:T(8,128)S(1)}) custom-call(s32[8,256]{1,0:T(8,128)S(1)} %get-tuple-element.61.scalars_ref, bf16[128,2560]{1,0:T(8,128)(2,1)S(1)} %get-tuple-element.57.q_ref, ...), custom_call_target="tpu_custom_call" | custom-call | flops 209715200 | bytes 2246656 | tf_op jit(solution)/shard_map/self_pairs/pallas_call | solution.py:205
  14.8 0.4 %collective-permute-done.2 = bf16[16,1024]{1,0:T(8,128)(2,1)S(1)} collective-permute-done((bf16[16,1024]{1,0:T(8,128)(2,1)S(1)}, bf16[16,1024]{1,0:T(8,128)(2,1)S(1)}, u32[]{:S(2)}, u32[]{:S(2)}) %collective-permute-start.2) | collective-permute-done | bytes 32800 | tf_op jit(solution)/shard_map/ppermute | solution.py:235
  15.2 0.6 %collective-permute-start.5 = (f32[8,768]{1,0:T(8,128)S(1)}, f32[8,768]{1,0:T(8,128)S(1)}, u32[]{:S(2)}, u32[]{:S(2)}) collective-permute-start(f32[8,768]{1,0:T(8,128)S(1)} %get-tuple-element.69.rows_ref), channel_id=1, source_target_pairs={{4,0},{5,1},{6,2},{7,3},{0,4},{1,5},{2,6},{3,7},{12,8},{13,9},{14,... | collective-permute-start | bytes 73736 | tf_op jit(solution)/shard_map/ppermute | solution.py:235
  15.8 0.0 collective-permute-done.4
  15.8 0.0 collective-permute-done.3
  15.9 0.1 collective-permute-start.11
  15.9 1.3 %own_pairs.1 = (bf16[4,128,640]{2,1,0:T(8,128)(2,1)S(1)}, f32[128,1024]{1,0:T(8,128)S(1)}) custom-call(bf16[128,2560]{1,0:T(8,128)(2,1)S(1)} %get-tuple-element.57.q_ref, bf16[128,2560]{1,0:T(8,128)(2,1)S(1)} %get-tuple-element.68.do_ref, f32[8,768]{1,0:T(8,128)S(1)} %get-tuple-element.69.rows_ref, bf16[128,1024]{1,0:T(8,128)(2,1)S(1)} %pad_maximum_fusion.kv_ref.k1_ref), custom_call_target="tpu_custom_call" | custom-call | flops 3690987520 | bytes 1597440 | tf_op jit(solution)/shard_map/own_pairs/pallas_call | solution.py:205
  17.2 0.0 collective-permute-done.5.rows_ref
  17.3 0.0 collective-permute-done.6.q_ref
  17.3 0.0 collective-permute-done.7.do_ref
  17.3 1.3 %other_pairs.1 = (f32[48,1024]{1,0:T(8,128)S(1)}, bf16[16,1024]{1,0:T(8,128)(2,1)S(1)}, bf16[48,1024]{1,0:T(8,128)(2,1)S(1)}, bf16[16,1024]{1,0:T(8,128)(2,1)S(1)}) custom-call(bf16[128,2560]{1,0:T(8,128)(2,1)S(1)} %collective-permute-done.6.q_ref, bf16[128,2560]{1,0:T(8,128)(2,1)S(1)} %collective-permute-done.7.do_ref, ...), custom_call_target="tpu_custom_call" | custom-call | flops 335544320 | bytes 2121728 | tf_op jit(solution)/shard_map/other_pairs/pallas_call | solution.py:205
  18.6 1.2 %collective-permute-start.8 = (bf16[48,1024]{1,0:T(8,128)(2,1)S(1)}, bf16[48,1024]{1,0:T(8,128)(2,1)S(1)}, u32[]{:S(2)}, u32[]{:S(2)}) collective-permute-start(bf16[48,1024]{1,0:T(8,128)(2,1)S(1)} %get-tuple-element.79), channel_id=1, source_target_pairs={{0,12},{1,13},{2,14},{3,15},{4,8},{5,9},{6,10},{7,11},{8,4},{9,5},... | collective-permute-start | bytes 294920 | tf_op jit(solution)/shard_map/ppermute | solution.py:239
  19.8 0.8 %collective-permute-start.10 = (bf16[16,1024]{1,0:T(8,128)(2,1)S(1)}, bf16[16,1024]{1,0:T(8,128)(2,1)S(1)}, u32[]{:S(2)}, u32[]{:S(2)}) collective-permute-start(bf16[16,1024]{1,0:T(8,128)(2,1)S(1)} %get-tuple-element.81), channel_id=1, source_target_pairs={{0,13},{1,12},{2,15},{3,14},{4,9},{5,8},{6,11},{7,10},{8,5},{9,4},... | collective-permute-start | bytes 98312 | tf_op jit(solution)/shard_map/ppermute | solution.py:239
  20.6 1.4 %collective-permute-start.9 = (bf16[16,1024]{1,0:T(8,128)(2,1)S(1)}, bf16[16,1024]{1,0:T(8,128)(2,1)S(1)}, u32[]{:S(2)}, u32[]{:S(2)}) collective-permute-start(bf16[16,1024]{1,0:T(8,128)(2,1)S(1)} %get-tuple-element.80), channel_id=1, source_target_pairs={{0,5},{1,4},{2,7},{3,6},{4,1},{5,0},{6,3},{7,2},{8,13},{9,12},{10,... | collective-permute-start | bytes 98312 | tf_op jit(solution)/shard_map/ppermute | solution.py:239
  22.0 0.0 collective-permute-done.11.kv_ref.k2_ref
  22.0 1.5 %response_grads.1 = (bf16[128,512]{1,0:T(8,128)(2,1)}, bf16[128,512]{1,0:T(8,128)(2,1)}, bf16[4,128,640]{2,1,0:T(8,128)(2,1)S(1)}) custom-call(bf16[128,2560]{1,0:T(8,128)(2,1)S(1)} %get-tuple-element.57.q_ref, bf16[128,2560]{1,0:T(8,128)(2,1)S(1)} %get-tuple-element.68.do_ref, f32[8,768]{1,0:T(8,128)S(1)} %get-tuple-element.69.rows_ref, ...), custom_call_target="tpu_custom_call" | custom-call | flops 335544320 | bytes 2908160 | tf_op jit(solution)/shard_map/response_grads/pallas_call | solution.py:205
  23.5 0.6 %collective-permute-done.10 = bf16[16,1024]{1,0:T(8,128)(2,1)S(1)} collective-permute-done((bf16[16,1024]{1,0:T(8,128)(2,1)S(1)}, bf16[16,1024]{1,0:T(8,128)(2,1)S(1)}, u32[]{:S(2)}, u32[]{:S(2)}) %collective-permute-start.10) | collective-permute-done | bytes 32800 | tf_op jit(solution)/shard_map/ppermute | solution.py:239
  24.1 0.2 collective-permute-done.9
  24.3 0.0 collective-permute-done.8
  24.4 1.4 %collective-permute-start.12 = (bf16[16,1024]{1,0:T(8,128)(2,1)S(1)}, bf16[16,1024]{1,0:T(8,128)(2,1)S(1)}, u32[]{:S(2)}, u32[]{:S(2)}) collective-permute-start(bf16[16,1024]{1,0:T(8,128)(2,1)S(1)} %get-tuple-element.91), channel_id=1, source_target_pairs={{0,6},{1,7},{2,4},{3,5},{4,2},{5,3},{6,0},{7,1},{8,14},{9,15},{10,... | collective-permute-start | bytes 98312 | tf_op jit(solution)/shard_map/ppermute | solution.py:239
  25.8 0.8 %collective-permute-start.13 = (bf16[16,1024]{1,0:T(8,128)(2,1)S(1)}, bf16[16,1024]{1,0:T(8,128)(2,1)S(1)}, u32[]{:S(2)}, u32[]{:S(2)}) collective-permute-start(bf16[16,1024]{1,0:T(8,128)(2,1)S(1)} %get-tuple-element.92), channel_id=1, source_target_pairs={{0,5},{1,4},{2,7},{3,6},{4,1},{5,0},{6,3},{7,2},{8,13},{9,12},{10,... | collective-permute-start | bytes 98312 | tf_op jit(solution)/shard_map/ppermute | solution.py:239
  26.6 1.5 %query_grads.1 = bf16[128,2560]{1,0:T(8,128)(2,1)} custom-call(bf16[4,128,640]{2,1,0:T(8,128)(2,1)S(1)} %get-tuple-element.83.ds_ref.ds0_ref, bf16[4,128,640]{2,1,0:T(8,128)(2,1)S(1)} %get-tuple-element.93.ds1_ref, bf16[4,128,640]{2,1,0:T(8,128)(2,1)S(1)} %get-tuple-element.94.ds2_ref, bf16[128,512]{1,0:T(8,128)(2,1)S(1)} %get-tuple-element.62.k_ref.k0_ref, ...), custom_call_target="tpu_custom_call" | custom-call | flops 251658240 | bytes 2621440 | tf_op jit(solution)/shard_map/query_grads/pallas_call | solution.py:205
  28.1 0.6 %collective-permute-done.12 = bf16[16,1024]{1,0:T(8,128)(2,1)S(1)} collective-permute-done((bf16[16,1024]{1,0:T(8,128)(2,1)S(1)}, bf16[16,1024]{1,0:T(8,128)(2,1)S(1)}, u32[]{:S(2)}, u32[]{:S(2)}) %collective-permute-start.12) | collective-permute-done | bytes 32800 | tf_op jit(solution)/shard_map/ppermute | solution.py:239
  28.8 0.4 %collective-permute-done.13 = bf16[16,1024]{1,0:T(8,128)(2,1)S(1)} collective-permute-done((bf16[16,1024]{1,0:T(8,128)(2,1)S(1)}, bf16[16,1024]{1,0:T(8,128)(2,1)S(1)}, u32[]{:S(2)}, u32[]{:S(2)}) %collective-permute-start.13) | collective-permute-done | bytes 32800 | tf_op jit(solution)/shard_map/ppermute | solution.py:239
  29.2 0.6 %slice_bitcast_fusion = (f32[1,16,512]{2,1,0:T(8,128)}, f32[1,16,512]{2,1,0:T(8,128)}) fusion(f32[16,1024]{1,0:T(8,128)S(1)} %convert_add_fusion.1), kind=kLoop, calls=%fused_computation.6 | loop fusion | bytes 131072 | tf_op jit(solution)/shard_map/broadcast_in_dim | solution.py:383
  (7 shorter events, 0.1 us)
Async XLA Ops:
  1.4 8.3 %collective-permute-start = (bf16[16,1024]{1,0:T(8,128)(2,1)S(1)}, bf16[16,1024]{1,0:T(8,128)(2,1)S(1)}, u32[]{:S(2)}, u32[]{:S(2)}) collective-permute-start(bf16[16,1024]{1,0:T(8,128)(2,1)S(1)} %pad_maximum_fusion.2), channel_id=1, source_target_pairs={{6,0},{7,1},{4,2},{5,3},{2,4},{3,5},{0,6},{1,7},{14,8},{15,9},{12,... | collective-permute-start | bytes 98312 | tf_op jit(solution)/shard_map/ppermute | solution.py:235
  4.8 4.8 %collective-permute-start.1 = (bf16[16,1024]{1,0:T(8,128)(2,1)S(1)}, bf16[16,1024]{1,0:T(8,128)(2,1)S(1)}, u32[]{:S(2)}, u32[]{:S(2)}) collective-permute-start(bf16[16,1024]{1,0:T(8,128)(2,1)S(1)} %pad_maximum_fusion.2), channel_id=1, source_target_pairs={{5,0},{4,1},{7,2},{6,3},{1,4},{0,5},{3,6},{2,7},{13,8},{12,9},{15,... | collective-permute-start | bytes 98312 | tf_op jit(solution)/shard_map/ppermute | solution.py:235
  6.7 10.6 %collective-permute-start.6 = (bf16[128,2560]{1,0:T(8,128)(2,1)}, bf16[128,2560]{1,0:T(8,128)(2,1)S(1)}, u32[]{:S(2)}, u32[]{:S(2)}) collective-permute-start(bf16[128,2560]{1,0:T(8,128)(2,1)} %bitcast.18), channel_id=1, source_target_pairs={{4,0},{5,1},{6,2},{7,3},{0,4},{1,5},{2,6},{3,7},{12,8},{13,9},{14,... | collective-permute-start | bytes 1966088 | tf_op jit(solution)/shard_map/ppermute | solution.py:235
  6.7 10.6 %collective-permute-start.7 = (bf16[128,2560]{1,0:T(8,128)(2,1)}, bf16[128,2560]{1,0:T(8,128)(2,1)S(1)}, u32[]{:S(2)}, u32[]{:S(2)}) collective-permute-start(bf16[128,2560]{1,0:T(8,128)(2,1)} %bitcast.16), channel_id=1, source_target_pairs={{4,0},{5,1},{6,2},{7,3},{0,4},{1,5},{2,6},{3,7},{12,8},{13,9},{14,... | collective-permute-start | bytes 1966088 | tf_op jit(solution)/shard_map/ppermute | solution.py:235
  9.7 6.1 %collective-permute-start.3 = (bf16[48,1024]{1,0:T(8,128)(2,1)S(1)}, bf16[48,1024]{1,0:T(8,128)(2,1)S(1)}, u32[]{:S(2)}, u32[]{:S(2)}) collective-permute-start(bf16[48,1024]{1,0:T(8,128)(2,1)S(1)} %pad_maximum_fusion.1), channel_id=1, source_target_pairs={{12,0},{13,1},{14,2},{15,3},{8,4},{9,5},{10,6},{11,7},{4,8},{5,9},... | collective-permute-start | bytes 294920 | tf_op jit(solution)/shard_map/ppermute | solution.py:235
  10.9 4.3 %collective-permute-start.2 = (bf16[16,1024]{1,0:T(8,128)(2,1)S(1)}, bf16[16,1024]{1,0:T(8,128)(2,1)S(1)}, u32[]{:S(2)}, u32[]{:S(2)}) collective-permute-start(bf16[16,1024]{1,0:T(8,128)(2,1)S(1)} %slice.24), channel_id=1, source_target_pairs={{13,0},{12,1},{15,2},{14,3},{9,4},{8,5},{11,6},{10,7},{5,8},{4,9},... | collective-permute-start | bytes 98312 | tf_op jit(solution)/shard_map/ppermute | solution.py:235
  11.4 4.4 %collective-permute-start.4 = (bf16[16,1024]{1,0:T(8,128)(2,1)S(1)}, bf16[16,1024]{1,0:T(8,128)(2,1)S(1)}, u32[]{:S(2)}, u32[]{:S(2)}) collective-permute-start(bf16[16,1024]{1,0:T(8,128)(2,1)S(1)} %slice.24), channel_id=1, source_target_pairs={{5,0},{4,1},{7,2},{6,3},{1,4},{0,5},{3,6},{2,7},{13,8},{12,9},{15,... | collective-permute-start | bytes 98312 | tf_op jit(solution)/shard_map/ppermute | solution.py:235
  15.2 2.0 %collective-permute-start.5 = (f32[8,768]{1,0:T(8,128)S(1)}, f32[8,768]{1,0:T(8,128)S(1)}, u32[]{:S(2)}, u32[]{:S(2)}) collective-permute-start(f32[8,768]{1,0:T(8,128)S(1)} %get-tuple-element.69.rows_ref), channel_id=1, source_target_pairs={{4,0},{5,1},{6,2},{7,3},{0,4},{1,5},{2,6},{3,7},{12,8},{13,9},{14,... | collective-permute-start | bytes 73736 | tf_op jit(solution)/shard_map/ppermute | solution.py:235
  15.9 6.1 %collective-permute-start.11 = (bf16[128,1024]{1,0:T(8,128)(2,1)S(1)}, bf16[128,1024]{1,0:T(8,128)(2,1)S(1)}, u32[]{:S(2)}, u32[]{:S(2)}) collective-permute-start(bf16[128,1024]{1,0:T(8,128)(2,1)S(1)} %pad_maximum_fusion.kv_ref.k1_ref), channel_id=1, source_target_pairs={{4,0},{5,1},{6,2},{7,3},{0,4},{1,5},{2,6},{3,7},{12,8},{13,9},{14,... | collective-permute-start | bytes 786440 | tf_op jit(solution)/shard_map/ppermute | solution.py:235
  18.6 5.7 %collective-permute-start.8 = (bf16[48,1024]{1,0:T(8,128)(2,1)S(1)}, bf16[48,1024]{1,0:T(8,128)(2,1)S(1)}, u32[]{:S(2)}, u32[]{:S(2)}) collective-permute-start(bf16[48,1024]{1,0:T(8,128)(2,1)S(1)} %get-tuple-element.79), channel_id=1, source_target_pairs={{0,12},{1,13},{2,14},{3,15},{4,8},{5,9},{6,10},{7,11},{8,4},{9,5},... | collective-permute-start | bytes 294920 | tf_op jit(solution)/shard_map/ppermute | solution.py:239
  19.8 4.4 %collective-permute-start.10 = (bf16[16,1024]{1,0:T(8,128)(2,1)S(1)}, bf16[16,1024]{1,0:T(8,128)(2,1)S(1)}, u32[]{:S(2)}, u32[]{:S(2)}) collective-permute-start(bf16[16,1024]{1,0:T(8,128)(2,1)S(1)} %get-tuple-element.81), channel_id=1, source_target_pairs={{0,13},{1,12},{2,15},{3,14},{4,9},{5,8},{6,11},{7,10},{8,5},{9,4},... | collective-permute-start | bytes 98312 | tf_op jit(solution)/shard_map/ppermute | solution.py:239
  20.6 3.8 %collective-permute-start.9 = (bf16[16,1024]{1,0:T(8,128)(2,1)S(1)}, bf16[16,1024]{1,0:T(8,128)(2,1)S(1)}, u32[]{:S(2)}, u32[]{:S(2)}) collective-permute-start(bf16[16,1024]{1,0:T(8,128)(2,1)S(1)} %get-tuple-element.80), channel_id=1, source_target_pairs={{0,5},{1,4},{2,7},{3,6},{4,1},{5,0},{6,3},{7,2},{8,13},{9,12},{10,... | collective-permute-start | bytes 98312 | tf_op jit(solution)/shard_map/ppermute | solution.py:239
  24.4 4.4 %collective-permute-start.12 = (bf16[16,1024]{1,0:T(8,128)(2,1)S(1)}, bf16[16,1024]{1,0:T(8,128)(2,1)S(1)}, u32[]{:S(2)}, u32[]{:S(2)}) collective-permute-start(bf16[16,1024]{1,0:T(8,128)(2,1)S(1)} %get-tuple-element.91), channel_id=1, source_target_pairs={{0,6},{1,7},{2,4},{3,5},{4,2},{5,3},{6,0},{7,1},{8,14},{9,15},{10,... | collective-permute-start | bytes 98312 | tf_op jit(solution)/shard_map/ppermute | solution.py:239
  25.8 3.4 %collective-permute-start.13 = (bf16[16,1024]{1,0:T(8,128)(2,1)S(1)}, bf16[16,1024]{1,0:T(8,128)(2,1)S(1)}, u32[]{:S(2)}, u32[]{:S(2)}) collective-permute-start(bf16[16,1024]{1,0:T(8,128)(2,1)S(1)} %get-tuple-element.92), channel_id=1, source_target_pairs={{0,5},{1,4},{2,7},{3,6},{4,1},{5,0},{6,3},{7,2},{8,13},{9,12},{10,... | collective-permute-start | bytes 98312 | tf_op jit(solution)/shard_map/ppermute | solution.py:239

commit v9 on v8

--- a/solution.py
+++ b/solution.py
@@ -124,29 +124,44 @@
     return far
 
 
-def prompt_terms(far, g, q, do, rows_ref, kv_ref):
-    nq = q.shape[0]
-    lse = eight(rows_ref[g : g + 1, :nq])
-    delta = eight(rows_ref[HK + g : HK + g + 1, :nq])
-    lse_rows = jnp.concatenate(
-        [jnp.broadcast_to((lse + f)[None], (PB // 8, 8, nq)) for f in far], axis=0
-    )
-    probs = probabilities(dot(kv_ref[:, head_cols(g)], q, NT), lse_rows)
-    dprob = dot(kv_ref[:, head_cols(HK + g)], do, NT)
-    return probs, score_grads(probs, dprob, delta[None])
+def prompt_terms(far, q_ref, do_ref, rows_ref, kv_ref, use):
+    nq = RATIO * q_ref.shape[0]
+
+    def products(g):
+        return (
+            dot(kv_ref[:, head_cols(g)], head_rows(q_ref, g), NT),
+            dot(kv_ref[:, head_cols(HK + g)], head_rows(do_ref, g), NT),
+        )
+
+    ahead = [products(g) for g in range(2)]
+    last = None
+    for g in range(HK):
+        if g + 2 < HK:
+            ahead.append(products(g + 2))
+        scores, dprob = ahead[g]
+        lse = eight(rows_ref[g : g + 1, :nq])
+        delta = eight(rows_ref[HK + g : HK + g + 1, :nq])
+        lse_rows = jnp.concatenate(
+            [jnp.broadcast_to((lse + f)[None], (PB // 8, 8, nq)) for f in far], axis=0
+        )
+        probs = probabilities(scores, lse_rows)
+        ds16 = score_grads(probs, dprob, delta[None])
+        if last:
+            use(*last)
+        last = (g, probs.reshape(ds16.shape).astype(jnp.bfloat16), ds16)
+    use(*last)
 
 
 def own_kernel(pieces, n_resp, q_ref, do_ref, rows_ref, kv_ref, ds_ref, part_ref):
     scale = 1.0 / DH**0.5
     far = block_rows(pieces, 0, n_resp, rows_ref, RATIO * q_ref.shape[0])
-    for g in range(HK):
-        q = head_rows(q_ref, g)
-        do = head_rows(do_ref, g)
-        probs, ds16 = prompt_terms(far, g, q, do, rows_ref, kv_ref)
+
+    def use(g, p16, ds16):
         ds_ref[g] = ds16
-        p16 = probs.reshape(ds16.shape).astype(jnp.bfloat16)
-        part_ref[:, head_cols(g)] = dot(ds16, q, NN) * scale
-        part_ref[:, head_cols(HK + g)] = dot(p16, do, NN)
+        part_ref[:, head_cols(g)] = dot(ds16, head_rows(q_ref, g), NN) * scale
+        part_ref[:, head_cols(HK + g)] = dot(p16, head_rows(do_ref, g), NN)
+
+    prompt_terms(far, q_ref, do_ref, rows_ref, kv_ref, use)
 
 
 def other_kernel(pieces, n_resp, cuts, q_ref, do_ref, rows_ref, kv_ref, part_ref, *outs):
@@ -158,13 +173,11 @@
         for out, low, high in zip(outs, cuts, cuts[1:]):
             out[:, cols] = sums[low:high].astype(out.dtype)
 
-    for g in range(HK):
-        q = head_rows(q_ref, g)
-        do = head_rows(do_ref, g)
-        probs, ds16 = prompt_terms(far, g, q, do, rows_ref, kv_ref)
-        p16 = probs.reshape(ds16.shape).astype(jnp.bfloat16)
-        put(dot(ds16, q, NN) * scale, head_cols(g))
-        put(dot(p16, do, NN), head_cols(HK + g))
+    def use(g, p16, ds16):
+        put(dot(ds16, head_rows(q_ref, g), NN) * scale, head_cols(g))
+        put(dot(p16, head_rows(do_ref, g), NN), head_cols(HK + g))
+
+    prompt_terms(far, q_ref, do_ref, rows_ref, kv_ref, use)
 
 
 def response_kernel(
@@ -172,13 +185,14 @@
 ):
     scale = 1.0 / DH**0.5
     far = block_rows(pieces, 1, n_resp, rows_ref, RATIO * q_ref.shape[0])
-    for g in range(HK):
-        q = head_rows(q_ref, g)
-        do = head_rows(do_ref, g)
+
+    def use(g, p16, ds16):
+        ds2_ref[g] = ds16
         cols = head_cols(g)
-        gv_ref[:, cols] = dot(p_ref[g], do, NN).astype(gv_ref.dtype)
-        gk_ref[:, cols] = (dot(ds_ref[g], q, NN) * scale).astype(gk_ref.dtype)
-        ds2_ref[g] = prompt_terms(far, g, q, do, rows_ref, kv_ref)[1]
+        gv_ref[:, cols] = dot(p_ref[g], head_rows(do_ref, g), NN).astype(gv_ref.dtype)
+        gk_ref[:, cols] = (dot(ds_ref[g], head_rows(q_ref, g), NN) * scale).astype(gk_ref.dtype)
+
+    prompt_terms(far, q_ref, do_ref, rows_ref, kv_ref, use)
 
 
 def query_kernel(ds0_ref, ds1_ref, ds2_ref, k0_ref, k1_ref, k2_ref, gq_ref):

time: 30.1 us -> 29.9 us (level)
  Pallas kernels: 9.01 us -> 8.43 us
  waiting for transfers between devices: 2.31 us -> 2.73 us
    pallas_call x6, Pallas kernels: 9.01 us -> 8.43 us  [call(): pl.pallas_call(kernel, name=name, out_shape=outs, in_specs=[SMEM] * len(s...]
    ppermute x5, waiting for transfers between devices: 1.86 us -> 2.28 us  [give(): lax.ppermute(array, ('dp', 'resp'), [(i, j) for j, i in pairs(*step)])]
  transfers between devices with their start and end apart: 14 -> 14, of which waited for: 5 -> 5; matrix products, arithmetic and copies ran while one was open for 0% -> 0% of each run, Pallas kernels for 30% -> 29%
where the time goes in v9:
time: 29.9 us; the launch traced here: 29.5 us
  starting transfers between devices  14.9 us (50%)
  Pallas kernels  8.43 us (28%)
  waiting for transfers between devices  2.73 us (9%)
  between operations  2.05 us (7%)
  other arithmetic  0.83 us (3%)
  local copies, waits for them, and re-layouts  0.64 us (2%)
    ppermute x9, starting transfers between devices, fetch(): return lax.ppermute(array, ('dp', 'resp'), pairs(*step))  9.43 us
    pallas_call x6, Pallas kernels, call(): pl.pallas_call(kernel, name=name, out_shape=outs, in_specs=[SMEM] * len(s...  8.43 us
    ppermute x5, starting transfers between devices, give(): lax.ppermute(array, ('dp', 'resp'), [(i, j) for j, i in pairs(*step)])  5.43 us
    ppermute x5, waiting for transfers between devices, give(): lax.ppermute(array, ('dp', 'resp'), [(i, j) for j, i in pairs(*step)])  2.28 us
    concatenate x1, other arithmetic, shards(): jnp.concatenate([prompt_keys[0], prompt_values[0]], axis=1)  0.74 us
    broadcast_in_dim x1, local copies, waits for them, and re-layouts, shards(): total[None, :, width:]  0.63 us
  transfers between devices with their start and end apart: 14, of which 5 were waited for; matrix products, arithmetic and copies ran while one was open for 0% of the time, Pallas kernels for 29%

profile of v9, /device:TPU:0, one launch (start us, length us, event | category | flops | bytes accessed | tf_op | source)
XLA Modules:
  0.0 29.5 jit_solution(12050309223775521796)
XLA Ops:
  0.6 0.7 %pad_maximum_fusion.2 = bf16[16,1024]{1,0:T(8,128)(2,1)S(1)} fusion(bf16[16,512]{1,0:T(8,128)(2,1)} %bitcast.23, bf16[16,512]{1,0:T(8,128)(2,1)} %bitcast.24), kind=kLoop, calls=%fused_computation.8 | loop fusion | flops 65536 | bytes 65536 | tf_op jit(solution)/shard_map/concatenate | solution.py:287
  1.4 3.5 %collective-permute-start = (bf16[16,1024]{1,0:T(8,128)(2,1)S(1)}, bf16[16,1024]{1,0:T(8,128)(2,1)S(1)}, u32[]{:S(2)}, u32[]{:S(2)}) collective-permute-start(bf16[16,1024]{1,0:T(8,128)(2,1)S(1)} %pad_maximum_fusion.2), channel_id=1, source_target_pairs={{6,0},{7,1},{4,2},{5,3},{2,4},{3,5},{0,6},{1,7},{14,8},{15,9},{12,... | collective-permute-start | bytes 98312 | tf_op jit(solution)/shard_map/ppermute | solution.py:249
  4.8 1.9 %collective-permute-start.1 = (bf16[16,1024]{1,0:T(8,128)(2,1)S(1)}, bf16[16,1024]{1,0:T(8,128)(2,1)S(1)}, u32[]{:S(2)}, u32[]{:S(2)}) collective-permute-start(bf16[16,1024]{1,0:T(8,128)(2,1)S(1)} %pad_maximum_fusion.2), channel_id=1, source_target_pairs={{5,0},{4,1},{7,2},{6,3},{1,4},{0,5},{3,6},{2,7},{13,8},{12,9},{15,... | collective-permute-start | bytes 98312 | tf_op jit(solution)/shard_map/ppermute | solution.py:249
  6.7 0.0 collective-permute-start.6
  6.7 0.5 %collective-permute-start.7 = (bf16[128,2560]{1,0:T(8,128)(2,1)}, bf16[128,2560]{1,0:T(8,128)(2,1)S(1)}, u32[]{:S(2)}, u32[]{:S(2)}) collective-permute-start(bf16[128,2560]{1,0:T(8,128)(2,1)} %bitcast.16), channel_id=1, source_target_pairs={{4,0},{5,1},{6,2},{7,3},{0,4},{1,5},{2,6},{3,7},{12,8},{13,9},{14,... | collective-permute-start | bytes 1966088 | tf_op jit(solution)/shard_map/ppermute | solution.py:249
  8.5 1.1 %load.1 = (bf16[128,2560]{1,0:T(8,128)(2,1)S(1)}, bf16[128,512]{1,0:T(8,128)(2,1)S(1)}, f32[20,1,128]{2,1,0:T(1,128)S(1)}, s32[8,256]{1,0:T(8,128)S(1)}) custom-call(s32[1]{0:T(128)S(6)} %copy.15.len_ref, s32[1]{0:T(128)S(6)} %copy.16.seen_ref, bf16[128,2560]{1,0:T(8,128)(2,1)} %bitcast.19, bf16[128,512]{1,0:T(8,128)(2,1)} %bitcast.21, f32[20,1,128]{2,1,0:T(1,128)} %bitcast.25), custom_call_target="tpu_custom_call" | custom-call | bytes 796672 | tf_op jit(solution)/shard_map/load/pallas_call | solution.py:219
  9.7 0.0 collective-permute-done
  9.7 0.0 collective-permute-done.1
  9.7 1.2 %collective-permute-start.3 = (bf16[48,1024]{1,0:T(8,128)(2,1)S(1)}, bf16[48,1024]{1,0:T(8,128)(2,1)S(1)}, u32[]{:S(2)}, u32[]{:S(2)}) collective-permute-start(bf16[48,1024]{1,0:T(8,128)(2,1)S(1)} %pad_maximum_fusion.1), channel_id=1, source_target_pairs={{12,0},{13,1},{14,2},{15,3},{8,4},{9,5},{10,6},{11,7},{4,8},{5,9},... | collective-permute-start | bytes 294920 | tf_op jit(solution)/shard_map/ppermute | solution.py:249
  10.9 0.5 %collective-permute-start.2 = (bf16[16,1024]{1,0:T(8,128)(2,1)S(1)}, bf16[16,1024]{1,0:T(8,128)(2,1)S(1)}, u32[]{:S(2)}, u32[]{:S(2)}) collective-permute-start(bf16[16,1024]{1,0:T(8,128)(2,1)S(1)} %slice.24), channel_id=1, source_target_pairs={{13,0},{12,1},{15,2},{14,3},{9,4},{8,5},{11,6},{10,7},{5,8},{4,9},... | collective-permute-start | bytes 98312 | tf_op jit(solution)/shard_map/ppermute | solution.py:249
  11.4 1.2 %collective-permute-start.4 = (bf16[16,1024]{1,0:T(8,128)(2,1)S(1)}, bf16[16,1024]{1,0:T(8,128)(2,1)S(1)}, u32[]{:S(2)}, u32[]{:S(2)}) collective-permute-start(bf16[16,1024]{1,0:T(8,128)(2,1)S(1)} %slice.24), channel_id=1, source_target_pairs={{5,0},{4,1},{7,2},{6,3},{1,4},{0,5},{3,6},{2,7},{13,8},{12,9},{15,... | collective-permute-start | bytes 98312 | tf_op jit(solution)/shard_map/ppermute | solution.py:249
  12.6 2.2 %self_pairs.1 = (bf16[128,2560]{1,0:T(8,128)(2,1)S(1)}, bf16[4,128,640]{2,1,0:T(8,128)(2,1)S(1)}, bf16[4,128,640]{2,1,0:T(8,128)(2,1)S(1)}, f32[8,768]{1,0:T(8,128)S(1)}) custom-call(s32[8,256]{1,0:T(8,128)S(1)} %get-tuple-element.61.scalars_ref, bf16[128,2560]{1,0:T(8,128)(2,1)S(1)} %get-tuple-element.57.q_ref, ...), custom_call_target="tpu_custom_call" | custom-call | flops 209715200 | bytes 2246656 | tf_op jit(solution)/shard_map/self_pairs/pallas_call | solution.py:219
  14.8 0.4 %collective-permute-done.2 = bf16[16,1024]{1,0:T(8,128)(2,1)S(1)} collective-permute-done((bf16[16,1024]{1,0:T(8,128)(2,1)S(1)}, bf16[16,1024]{1,0:T(8,128)(2,1)S(1)}, u32[]{:S(2)}, u32[]{:S(2)}) %collective-permute-start.2) | collective-permute-done | bytes 32800 | tf_op jit(solution)/shard_map/ppermute | solution.py:249
  15.2 0.6 %collective-permute-start.5 = (f32[8,768]{1,0:T(8,128)S(1)}, f32[8,768]{1,0:T(8,128)S(1)}, u32[]{:S(2)}, u32[]{:S(2)}) collective-permute-start(f32[8,768]{1,0:T(8,128)S(1)} %get-tuple-element.69.rows_ref), channel_id=1, source_target_pairs={{4,0},{5,1},{6,2},{7,3},{0,4},{1,5},{2,6},{3,7},{12,8},{13,9},{14,... | collective-permute-start | bytes 73736 | tf_op jit(solution)/shard_map/ppermute | solution.py:249
  15.8 0.0 collective-permute-done.4
  15.8 0.0 collective-permute-done.3
  15.9 0.1 collective-permute-start.11
  15.9 1.0 %own_pairs.1 = (bf16[4,128,640]{2,1,0:T(8,128)(2,1)S(1)}, f32[128,1024]{1,0:T(8,128)S(1)}) custom-call(bf16[128,2560]{1,0:T(8,128)(2,1)S(1)} %get-tuple-element.57.q_ref, bf16[128,2560]{1,0:T(8,128)(2,1)S(1)} %get-tuple-element.68.do_ref, f32[8,768]{1,0:T(8,128)S(1)} %get-tuple-element.69.rows_ref, bf16[128,1024]{1,0:T(8,128)(2,1)S(1)} %pad_maximum_fusion.kv_ref.k1_ref), custom_call_target="tpu_custom_call" | custom-call | flops 3690987520 | bytes 1597440 | tf_op jit(solution)/shard_map/own_pairs/pallas_call | solution.py:219
  16.9 0.0 collective-permute-done.5.rows_ref
  16.9 0.0 collective-permute-done.6.q_ref
  16.9 0.0 collective-permute-done.7.do_ref
  16.9 1.0 %other_pairs.1 = (f32[48,1024]{1,0:T(8,128)S(1)}, bf16[16,1024]{1,0:T(8,128)(2,1)S(1)}, bf16[48,1024]{1,0:T(8,128)(2,1)S(1)}, bf16[16,1024]{1,0:T(8,128)(2,1)S(1)}) custom-call(bf16[128,2560]{1,0:T(8,128)(2,1)S(1)} %collective-permute-done.6.q_ref, bf16[128,2560]{1,0:T(8,128)(2,1)S(1)} %collective-permute-done.7.do_ref, ...), custom_call_target="tpu_custom_call" | custom-call | flops 335544320 | bytes 2121728 | tf_op jit(solution)/shard_map/other_pairs/pallas_call | solution.py:219
  17.9 1.2 %collective-permute-start.8 = (bf16[48,1024]{1,0:T(8,128)(2,1)S(1)}, bf16[48,1024]{1,0:T(8,128)(2,1)S(1)}, u32[]{:S(2)}, u32[]{:S(2)}) collective-permute-start(bf16[48,1024]{1,0:T(8,128)(2,1)S(1)} %get-tuple-element.79), channel_id=1, source_target_pairs={{0,12},{1,13},{2,14},{3,15},{4,8},{5,9},{6,10},{7,11},{8,4},{9,5},... | collective-permute-start | bytes 294920 | tf_op jit(solution)/shard_map/ppermute | solution.py:253
  19.1 0.8 %collective-permute-start.10 = (bf16[16,1024]{1,0:T(8,128)(2,1)S(1)}, bf16[16,1024]{1,0:T(8,128)(2,1)S(1)}, u32[]{:S(2)}, u32[]{:S(2)}) collective-permute-start(bf16[16,1024]{1,0:T(8,128)(2,1)S(1)} %get-tuple-element.81), channel_id=1, source_target_pairs={{0,13},{1,12},{2,15},{3,14},{4,9},{5,8},{6,11},{7,10},{8,5},{9,4},... | collective-permute-start | bytes 98312 | tf_op jit(solution)/shard_map/ppermute | solution.py:253
  20.0 1.4 %collective-permute-start.9 = (bf16[16,1024]{1,0:T(8,128)(2,1)S(1)}, bf16[16,1024]{1,0:T(8,128)(2,1)S(1)}, u32[]{:S(2)}, u32[]{:S(2)}) collective-permute-start(bf16[16,1024]{1,0:T(8,128)(2,1)S(1)} %get-tuple-element.80), channel_id=1, source_target_pairs={{0,5},{1,4},{2,7},{3,6},{4,1},{5,0},{6,3},{7,2},{8,13},{9,12},{10,... | collective-permute-start | bytes 98312 | tf_op jit(solution)/shard_map/ppermute | solution.py:253
  21.3 0.0 collective-permute-done.11.kv_ref.k2_ref
  21.3 1.6 %response_grads.1 = (bf16[128,512]{1,0:T(8,128)(2,1)}, bf16[128,512]{1,0:T(8,128)(2,1)}, bf16[4,128,640]{2,1,0:T(8,128)(2,1)S(1)}) custom-call(bf16[128,2560]{1,0:T(8,128)(2,1)S(1)} %get-tuple-element.57.q_ref, bf16[128,2560]{1,0:T(8,128)(2,1)S(1)} %get-tuple-element.68.do_ref, f32[8,768]{1,0:T(8,128)S(1)} %get-tuple-element.69.rows_ref, ...), custom_call_target="tpu_custom_call" | custom-call | flops 335544320 | bytes 2908160 | tf_op jit(solution)/shard_map/response_grads/pallas_call | solution.py:219
  22.9 0.5 %collective-permute-done.10 = bf16[16,1024]{1,0:T(8,128)(2,1)S(1)} collective-permute-done((bf16[16,1024]{1,0:T(8,128)(2,1)S(1)}, bf16[16,1024]{1,0:T(8,128)(2,1)S(1)}, u32[]{:S(2)}, u32[]{:S(2)}) %collective-permute-start.10) | collective-permute-done | bytes 32800 | tf_op jit(solution)/shard_map/ppermute | solution.py:253
  23.5 0.3 collective-permute-done.9
  23.8 0.0 collective-permute-done.8
  23.8 1.3 %collective-permute-start.12 = (bf16[16,1024]{1,0:T(8,128)(2,1)S(1)}, bf16[16,1024]{1,0:T(8,128)(2,1)S(1)}, u32[]{:S(2)}, u32[]{:S(2)}) collective-permute-start(bf16[16,1024]{1,0:T(8,128)(2,1)S(1)} %get-tuple-element.91), channel_id=1, source_target_pairs={{0,6},{1,7},{2,4},{3,5},{4,2},{5,3},{6,0},{7,1},{8,14},{9,15},{10,... | collective-permute-start | bytes 98312 | tf_op jit(solution)/shard_map/ppermute | solution.py:253
  25.2 0.7 %collective-permute-start.13 = (bf16[16,1024]{1,0:T(8,128)(2,1)S(1)}, bf16[16,1024]{1,0:T(8,128)(2,1)S(1)}, u32[]{:S(2)}, u32[]{:S(2)}) collective-permute-start(bf16[16,1024]{1,0:T(8,128)(2,1)S(1)} %get-tuple-element.92), channel_id=1, source_target_pairs={{0,5},{1,4},{2,7},{3,6},{4,1},{5,0},{6,3},{7,2},{8,13},{9,12},{10,... | collective-permute-start | bytes 98312 | tf_op jit(solution)/shard_map/ppermute | solution.py:253
  25.9 1.5 %query_grads.1 = bf16[128,2560]{1,0:T(8,128)(2,1)} custom-call(bf16[4,128,640]{2,1,0:T(8,128)(2,1)S(1)} %get-tuple-element.83.ds_ref.ds0_ref, bf16[4,128,640]{2,1,0:T(8,128)(2,1)S(1)} %get-tuple-element.93.ds1_ref, bf16[4,128,640]{2,1,0:T(8,128)(2,1)S(1)} %get-tuple-element.94.ds2_ref, bf16[128,512]{1,0:T(8,128)(2,1)S(1)} %get-tuple-element.62.k_ref.k0_ref, ...), custom_call_target="tpu_custom_call" | custom-call | flops 251658240 | bytes 2621440 | tf_op jit(solution)/shard_map/query_grads/pallas_call | solution.py:219
  27.4 1.2 %collective-permute-done.12 = bf16[16,1024]{1,0:T(8,128)(2,1)S(1)} collective-permute-done((bf16[16,1024]{1,0:T(8,128)(2,1)S(1)}, bf16[16,1024]{1,0:T(8,128)(2,1)S(1)}, u32[]{:S(2)}, u32[]{:S(2)}) %collective-permute-start.12) | collective-permute-done | bytes 32800 | tf_op jit(solution)/shard_map/ppermute | solution.py:253
  28.6 0.2 collective-permute-done.13
  28.9 0.6 %slice_bitcast_fusion = (f32[1,16,512]{2,1,0:T(8,128)}, f32[1,16,512]{2,1,0:T(8,128)}) fusion(f32[16,1024]{1,0:T(8,128)S(1)} %convert_add_fusion.1), kind=kLoop, calls=%fused_computation.6 | loop fusion | bytes 131072 | tf_op jit(solution)/shard_map/broadcast_in_dim | solution.py:397
  (7 shorter events, 0.1 us)
Async XLA Ops:
  1.4 8.3 %collective-permute-start = (bf16[16,1024]{1,0:T(8,128)(2,1)S(1)}, bf16[16,1024]{1,0:T(8,128)(2,1)S(1)}, u32[]{:S(2)}, u32[]{:S(2)}) collective-permute-start(bf16[16,1024]{1,0:T(8,128)(2,1)S(1)} %pad_maximum_fusion.2), channel_id=1, source_target_pairs={{6,0},{7,1},{4,2},{5,3},{2,4},{3,5},{0,6},{1,7},{14,8},{15,9},{12,... | collective-permute-start | bytes 98312 | tf_op jit(solution)/shard_map/ppermute | solution.py:249
  4.8 4.8 %collective-permute-start.1 = (bf16[16,1024]{1,0:T(8,128)(2,1)S(1)}, bf16[16,1024]{1,0:T(8,128)(2,1)S(1)}, u32[]{:S(2)}, u32[]{:S(2)}) collective-permute-start(bf16[16,1024]{1,0:T(8,128)(2,1)S(1)} %pad_maximum_fusion.2), channel_id=1, source_target_pairs={{5,0},{4,1},{7,2},{6,3},{1,4},{0,5},{3,6},{2,7},{13,8},{12,9},{15,... | collective-permute-start | bytes 98312 | tf_op jit(solution)/shard_map/ppermute | solution.py:249
  6.7 10.2 %collective-permute-start.6 = (bf16[128,2560]{1,0:T(8,128)(2,1)}, bf16[128,2560]{1,0:T(8,128)(2,1)S(1)}, u32[]{:S(2)}, u32[]{:S(2)}) collective-permute-start(bf16[128,2560]{1,0:T(8,128)(2,1)} %bitcast.18), channel_id=1, source_target_pairs={{4,0},{5,1},{6,2},{7,3},{0,4},{1,5},{2,6},{3,7},{12,8},{13,9},{14,... | collective-permute-start | bytes 1966088 | tf_op jit(solution)/shard_map/ppermute | solution.py:249
  6.7 10.2 %collective-permute-start.7 = (bf16[128,2560]{1,0:T(8,128)(2,1)}, bf16[128,2560]{1,0:T(8,128)(2,1)S(1)}, u32[]{:S(2)}, u32[]{:S(2)}) collective-permute-start(bf16[128,2560]{1,0:T(8,128)(2,1)} %bitcast.16), channel_id=1, source_target_pairs={{4,0},{5,1},{6,2},{7,3},{0,4},{1,5},{2,6},{3,7},{12,8},{13,9},{14,... | collective-permute-start | bytes 1966088 | tf_op jit(solution)/shard_map/ppermute | solution.py:249
  9.7 6.1 %collective-permute-start.3 = (bf16[48,1024]{1,0:T(8,128)(2,1)S(1)}, bf16[48,1024]{1,0:T(8,128)(2,1)S(1)}, u32[]{:S(2)}, u32[]{:S(2)}) collective-permute-start(bf16[48,1024]{1,0:T(8,128)(2,1)S(1)} %pad_maximum_fusion.1), channel_id=1, source_target_pairs={{12,0},{13,1},{14,2},{15,3},{8,4},{9,5},{10,6},{11,7},{4,8},{5,9},... | collective-permute-start | bytes 294920 | tf_op jit(solution)/shard_map/ppermute | solution.py:249
  10.9 4.3 %collective-permute-start.2 = (bf16[16,1024]{1,0:T(8,128)(2,1)S(1)}, bf16[16,1024]{1,0:T(8,128)(2,1)S(1)}, u32[]{:S(2)}, u32[]{:S(2)}) collective-permute-start(bf16[16,1024]{1,0:T(8,128)(2,1)S(1)} %slice.24), channel_id=1, source_target_pairs={{13,0},{12,1},{15,2},{14,3},{9,4},{8,5},{11,6},{10,7},{5,8},{4,9},... | collective-permute-start | bytes 98312 | tf_op jit(solution)/shard_map/ppermute | solution.py:249
  11.4 4.4 %collective-permute-start.4 = (bf16[16,1024]{1,0:T(8,128)(2,1)S(1)}, bf16[16,1024]{1,0:T(8,128)(2,1)S(1)}, u32[]{:S(2)}, u32[]{:S(2)}) collective-permute-start(bf16[16,1024]{1,0:T(8,128)(2,1)S(1)} %slice.24), channel_id=1, source_target_pairs={{5,0},{4,1},{7,2},{6,3},{1,4},{0,5},{3,6},{2,7},{13,8},{12,9},{15,... | collective-permute-start | bytes 98312 | tf_op jit(solution)/shard_map/ppermute | solution.py:249
  15.2 1.7 %collective-permute-start.5 = (f32[8,768]{1,0:T(8,128)S(1)}, f32[8,768]{1,0:T(8,128)S(1)}, u32[]{:S(2)}, u32[]{:S(2)}) collective-permute-start(f32[8,768]{1,0:T(8,128)S(1)} %get-tuple-element.69.rows_ref), channel_id=1, source_target_pairs={{4,0},{5,1},{6,2},{7,3},{0,4},{1,5},{2,6},{3,7},{12,8},{13,9},{14,... | collective-permute-start | bytes 73736 | tf_op jit(solution)/shard_map/ppermute | solution.py:249
  15.9 5.5 %collective-permute-start.11 = (bf16[128,1024]{1,0:T(8,128)(2,1)S(1)}, bf16[128,1024]{1,0:T(8,128)(2,1)S(1)}, u32[]{:S(2)}, u32[]{:S(2)}) collective-permute-start(bf16[128,1024]{1,0:T(8,128)(2,1)S(1)} %pad_maximum_fusion.kv_ref.k1_ref), channel_id=1, source_target_pairs={{4,0},{5,1},{6,2},{7,3},{0,4},{1,5},{2,6},{3,7},{12,8},{13,9},{14,... | collective-permute-start | bytes 786440 | tf_op jit(solution)/shard_map/ppermute | solution.py:249
  17.9 5.8 %collective-permute-start.8 = (bf16[48,1024]{1,0:T(8,128)(2,1)S(1)}, bf16[48,1024]{1,0:T(8,128)(2,1)S(1)}, u32[]{:S(2)}, u32[]{:S(2)}) collective-permute-start(bf16[48,1024]{1,0:T(8,128)(2,1)S(1)} %get-tuple-element.79), channel_id=1, source_target_pairs={{0,12},{1,13},{2,14},{3,15},{4,8},{5,9},{6,10},{7,11},{8,4},{9,5},... | collective-permute-start | bytes 294920 | tf_op jit(solution)/shard_map/ppermute | solution.py:253
  19.1 4.4 %collective-permute-start.10 = (bf16[16,1024]{1,0:T(8,128)(2,1)S(1)}, bf16[16,1024]{1,0:T(8,128)(2,1)S(1)}, u32[]{:S(2)}, u32[]{:S(2)}) collective-permute-start(bf16[16,1024]{1,0:T(8,128)(2,1)S(1)} %get-tuple-element.81), channel_id=1, source_target_pairs={{0,13},{1,12},{2,15},{3,14},{4,9},{5,8},{6,11},{7,10},{8,5},{9,4},... | collective-permute-start | bytes 98312 | tf_op jit(solution)/shard_map/ppermute | solution.py:253
  20.0 3.8 %collective-permute-start.9 = (bf16[16,1024]{1,0:T(8,128)(2,1)S(1)}, bf16[16,1024]{1,0:T(8,128)(2,1)S(1)}, u32[]{:S(2)}, u32[]{:S(2)}) collective-permute-start(bf16[16,1024]{1,0:T(8,128)(2,1)S(1)} %get-tuple-element.80), channel_id=1, source_target_pairs={{0,5},{1,4},{2,7},{3,6},{4,1},{5,0},{6,3},{7,2},{8,13},{9,12},{10,... | collective-permute-start | bytes 98312 | tf_op jit(solution)/shard_map/ppermute | solution.py:253
  23.8 4.8 %collective-permute-start.12 = (bf16[16,1024]{1,0:T(8,128)(2,1)S(1)}, bf16[16,1024]{1,0:T(8,128)(2,1)S(1)}, u32[]{:S(2)}, u32[]{:S(2)}) collective-permute-start(bf16[16,1024]{1,0:T(8,128)(2,1)S(1)} %get-tuple-element.91), channel_id=1, source_target_pairs={{0,6},{1,7},{2,4},{3,5},{4,2},{5,3},{6,0},{7,1},{8,14},{9,15},{10,... | collective-permute-start | bytes 98312 | tf_op jit(solution)/shard_map/ppermute | solution.py:253
  25.2 3.7 %collective-permute-start.13 = (bf16[16,1024]{1,0:T(8,128)(2,1)S(1)}, bf16[16,1024]{1,0:T(8,128)(2,1)S(1)}, u32[]{:S(2)}, u32[]{:S(2)}) collective-permute-start(bf16[16,1024]{1,0:T(8,128)(2,1)S(1)} %get-tuple-element.92), channel_id=1, source_target_pairs={{0,5},{1,4},{2,7},{3,6},{4,1},{5,0},{6,3},{7,2},{8,13},{9,12},{10,... | collective-permute-start | bytes 98312 | tf_op jit(solution)/shard_map/ppermute | solution.py:253

commit v10 on v9

--- a/solution.py
+++ b/solution.py
@@ -273,13 +273,12 @@
     macs = HQ * rows * DH
 
     if n_resp == 4:
-        near, relay = (1, 2), (1, 2)
+        near, steps = (2,), [(1, 1, 0), (1, 0, 1), (1, 1, 1)]
     else:
-        near, relay = tuple(range(1, n_resp)), None
+        near, steps = tuple(range(1, n_resp)), [(1, 1, 0)]
     first = [(0, 0, 0)] + [(1, 0, k) for k in near]
-    extra = [(0, 0, relay[0] ^ relay[1])] if relay else []
-    pieces = first + extra + [(c ^ 1, 1, k) for c, _, k in first] + [(c, 1, k) for c, _, k in extra]
-    n_first, n_half = len(first) * PB, len(pieces) * PB // 2
+    pieces = first + [(c ^ i, i_row ^ row, j ^ k) for i, i_row, j in steps for c, row, k in first]
+    n_first = len(first) * PB
 
     array = jax.ShapeDtypeStruct
     full = array((rows, HQ * DH), b16)
@@ -305,11 +304,7 @@
     got = got[::-1]
 
     bundle = lax.optimization_barrier(jnp.concatenate(got, 0))
-    moved = [fetch(bundle, 1, 1, 0)]
-    if relay:
-        piece = bundle[relay[1] * PB :][:PB]
-        far = fetch(piece, 1, 1, relay[0])
-        moved = [fetch(piece, 1, 0, relay[0])] + moved + [far]
+    moved = [fetch(bundle, *step) for step in steps]
     pair_shape = array((HK, rows, RATIO * rows), b16)
     worked = call(
         self_kernel,
@@ -342,9 +337,9 @@
         88 * macs * nk,
     )
     part, terms2, q2, do2 = lax.optimization_barrier((part, terms2, q2, do2))
-    cuts = (0, n_first, n_half, n_half + n_first, nk) if relay else (0, n_half, nk)
-    kinds = (f32, b16, b16, b16) if relay else (f32, b16)
-    low, *sent = call(
+    cuts = (*range(0, n_first, PB), *range(n_first, nk + 1, n_first))
+    kinds = [f32] * len(first) + [b16] * len(steps)
+    parts = call(
         functools.partial(other_kernel, pieces, n_resp, cuts),
         "other_pairs",
         [array((j - i, 2 * width), t) for i, j, t in zip(cuts, cuts[1:], kinds)],
@@ -354,14 +349,8 @@
     )
 
     other = fetch(half, 1, 0, 0)
-    if relay:
-        moved = [
-            give(sent[1], 1, 1, 0),
-            give(sent[0], 1, 0, relay[0]),
-            give(sent[2], 1, 1, relay[0]),
-        ]
-    else:
-        moved = [give(sent[0], 1, 1, 0)]
+    low, sent = parts[: len(first)], parts[len(first) :]
+    moved = [give(part, *step) for part, step in zip(sent, steps)]
     late = call(
         functools.partial(response_kernel, pieces, n_resp),
         "response_grads",
@@ -370,13 +359,14 @@
         (q, do, terms, p_self, ds_self, other),
         4 * macs * rows + 4 * macs * nk,
     )
-    moved, (grad_rk, grad_rv, ds_other) = lax.optimization_barrier((moved, late))
-    total = low + moved[0].astype(f32)
-    sums = [total[i * PB : (i + 1) * PB] for i in range(len(first))]
-    for piece in moved[1:]:
-        sums[relay[1]] = sums[relay[1]] + piece.astype(f32)
+    moved, (grad_rk, grad_rv, ds_other) = lax.optimization_barrier((moved[::-1], late))
+    sums = []
+    for i, total in enumerate(low):
+        for part in moved:
+            total = total + part[i * PB : (i + 1) * PB].astype(f32)
+        sums.append(total)
     sums, ds_other = lax.optimization_barrier((sums, ds_other))
-    moved = [give(sums[k].astype(b16), 1, 0, k) for k in reversed(near)]
+    moved = [give(part.astype(b16), 1, 0, k) for part, k in zip(sums[1:], near)]
     grad_q = call(
         query_kernel,
         "query_grads",

time: 29.9 us -> 28.9 us (0.967)
  starting transfers between devices: 14.9 us -> 13.5 us
  waiting for transfers between devices: 2.73 us -> 3.1 us
    ppermute x9 -> x8, starting transfers between devices: 9.43 us -> 7.85 us  [fetch(): return lax.ppermute(array, ('dp', 'resp'), pairs(*step))]
    ppermute x9 -> x8, waiting for transfers between devices: 0.45 us -> 1.19 us  [fetch(): return lax.ppermute(array, ('dp', 'resp'), pairs(*step))]
    ppermute x5 -> x4, waiting for transfers between devices: 2.28 us -> 1.91 us  [give(): lax.ppermute(array, ('dp', 'resp'), [(i, j) for j, i in pairs(*step)])]
    ppermute x5 -> x4, starting transfers between devices: 5.43 us -> 5.7 us  [give(): lax.ppermute(array, ('dp', 'resp'), [(i, j) for j, i in pairs(*step)])]
  transfers between devices with their start and end apart: 14 -> 12, of which waited for: 5 -> 4; matrix products, arithmetic and copies ran while one was open for 0% -> 0% of each run, Pallas kernels for 29% -> 30%
where the time goes in v10:
time: 28.9 us; the launch traced here: 28.6 us
  starting transfers between devices  13.5 us (47%)
  Pallas kernels  8.45 us (29%)
  waiting for transfers between devices  3.1 us (11%)
  between operations  2.03 us (7%)
  other arithmetic  0.82 us (3%)
  local copies, waits for them, and re-layouts  0.63 us (2%)
    pallas_call x6, Pallas kernels, call(): pl.pallas_call(kernel, name=name, out_shape=outs, in_specs=[SMEM] * len(s...  8.45 us
    ppermute x8, starting transfers between devices, fetch(): return lax.ppermute(array, ('dp', 'resp'), pairs(*step))  7.85 us
    ppermute x4, starting transfers between devices, give(): lax.ppermute(array, ('dp', 'resp'), [(i, j) for j, i in pairs(*step)])  5.7 us
    ppermute x4, waiting for transfers between devices, give(): lax.ppermute(array, ('dp', 'resp'), [(i, j) for j, i in pairs(*step)])  1.91 us
    ppermute x8, waiting for transfers between devices, fetch(): return lax.ppermute(array, ('dp', 'resp'), pairs(*step))  1.19 us
    concatenate x1, other arithmetic, shards(): jnp.concatenate([prompt_keys[0], prompt_values[0]], axis=1)  0.74 us
    broadcast_in_dim x1, local copies, waits for them, and re-layouts, shards(): total[None, :, width:]  0.63 us
  transfers between devices with their start and end apart: 12, of which 4 were waited for; matrix products, arithmetic and copies ran while one was open for 0% of the time, Pallas kernels for 30%

profile of v10, /device:TPU:0, one launch (start us, length us, event | category | flops | bytes accessed | tf_op | source)
XLA Modules:
  0.0 28.6 jit_solution(4497138438132112669)
XLA Ops:
  0.6 0.7 %pad_maximum_fusion.2 = bf16[16,1024]{1,0:T(8,128)(2,1)S(1)} fusion(bf16[16,512]{1,0:T(8,128)(2,1)} %bitcast.23, bf16[16,512]{1,0:T(8,128)(2,1)} %bitcast.24), kind=kLoop, calls=%fused_computation.7 | loop fusion | flops 65536 | bytes 65536 | tf_op jit(solution)/shard_map/concatenate | solution.py:286
  1.4 3.5 %collective-permute-start = (bf16[16,1024]{1,0:T(8,128)(2,1)S(1)}, bf16[16,1024]{1,0:T(8,128)(2,1)S(1)}, u32[]{:S(2)}, u32[]{:S(2)}) collective-permute-start(bf16[16,1024]{1,0:T(8,128)(2,1)S(1)} %pad_maximum_fusion.2), channel_id=1, source_target_pairs={{6,0},{7,1},{4,2},{5,3},{2,4},{3,5},{0,6},{1,7},{14,8},{15,9},{12,... | collective-permute-start | bytes 98312 | tf_op jit(solution)/shard_map/ppermute | solution.py:249
  4.8 0.7 %collective-permute-start.5 = (bf16[128,2560]{1,0:T(8,128)(2,1)}, bf16[128,2560]{1,0:T(8,128)(2,1)S(1)}, u32[]{:S(2)}, u32[]{:S(2)}) collective-permute-start(bf16[128,2560]{1,0:T(8,128)(2,1)} %bitcast.18), channel_id=1, source_target_pairs={{4,0},{5,1},{6,2},{7,3},{0,4},{1,5},{2,6},{3,7},{12,8},{13,9},{14,... | collective-permute-start | bytes 1966088 | tf_op jit(solution)/shard_map/ppermute | solution.py:249
  5.5 0.0 collective-permute-start.6
  6.8 1.1 %load.1 = (bf16[128,2560]{1,0:T(8,128)(2,1)S(1)}, bf16[128,512]{1,0:T(8,128)(2,1)S(1)}, f32[20,1,128]{2,1,0:T(1,128)S(1)}, s32[8,256]{1,0:T(8,128)S(1)}) custom-call(s32[1]{0:T(128)S(6)} %copy.15.len_ref, s32[1]{0:T(128)S(6)} %copy.16.seen_ref, bf16[128,2560]{1,0:T(8,128)(2,1)} %bitcast.19, bf16[128,512]{1,0:T(8,128)(2,1)} %bitcast.21, f32[20,1,128]{2,1,0:T(1,128)} %bitcast.25), custom_call_target="tpu_custom_call" | custom-call | bytes 796672 | tf_op jit(solution)/shard_map/load/pallas_call | solution.py:219
  8.0 0.0 collective-permute-done
  8.0 2.7 %collective-permute-start.1 = (bf16[32,1024]{1,0:T(8,128)(2,1)S(1)}, bf16[32,1024]{1,0:T(8,128)(2,1)S(1)}, u32[]{:S(2)}, u32[]{:S(2)}) collective-permute-start(bf16[32,1024]{1,0:T(8,128)(2,1)S(1)} %pad_maximum_fusion.1), channel_id=1, source_target_pairs={{13,0},{12,1},{15,2},{14,3},{9,4},{8,5},{11,6},{10,7},{5,8},{4,9},... | collective-permute-start | bytes 196616 | tf_op jit(solution)/shard_map/ppermute | solution.py:249
  10.7 0.1 collective-permute-start.2
  10.7 0.6 %collective-permute-start.3 = (bf16[32,1024]{1,0:T(8,128)(2,1)S(1)}, bf16[32,1024]{1,0:T(8,128)(2,1)S(1)}, u32[]{:S(2)}, u32[]{:S(2)}) collective-permute-start(bf16[32,1024]{1,0:T(8,128)(2,1)S(1)} %pad_maximum_fusion.1), channel_id=1, source_target_pairs={{12,0},{13,1},{14,2},{15,3},{8,4},{9,5},{10,6},{11,7},{4,8},{5,9},... | collective-permute-start | bytes 196616 | tf_op jit(solution)/shard_map/ppermute | solution.py:249
  11.4 2.2 %self_pairs.1 = (bf16[128,2560]{1,0:T(8,128)(2,1)S(1)}, bf16[4,128,640]{2,1,0:T(8,128)(2,1)S(1)}, bf16[4,128,640]{2,1,0:T(8,128)(2,1)S(1)}, f32[8,768]{1,0:T(8,128)S(1)}) custom-call(s32[8,256]{1,0:T(8,128)S(1)} %get-tuple-element.58.scalars_ref, bf16[128,2560]{1,0:T(8,128)(2,1)S(1)} %get-tuple-element.55.q_ref, ...), custom_call_target="tpu_custom_call" | custom-call | flops 209715200 | bytes 2246656 | tf_op jit(solution)/shard_map/self_pairs/pallas_call | solution.py:219
  13.6 0.0 collective-permute-done.1
  13.6 0.1 collective-permute-start.4
  13.7 1.2 %collective-permute-done.2 = bf16[32,1024]{1,0:T(8,128)(2,1)S(1)} collective-permute-done((bf16[32,1024]{1,0:T(8,128)(2,1)S(1)}, bf16[32,1024]{1,0:T(8,128)(2,1)S(1)}, u32[]{:S(2)}, u32[]{:S(2)}) %collective-permute-start.2) | collective-permute-done | bytes 65568 | tf_op jit(solution)/shard_map/ppermute | solution.py:249
  14.9 0.0 collective-permute-done.3
  14.9 0.2 collective-permute-start.10
  15.1 1.0 %own_pairs.1 = (bf16[4,128,640]{2,1,0:T(8,128)(2,1)S(1)}, f32[128,1024]{1,0:T(8,128)S(1)}) custom-call(bf16[128,2560]{1,0:T(8,128)(2,1)S(1)} %get-tuple-element.55.q_ref, bf16[128,2560]{1,0:T(8,128)(2,1)S(1)} %get-tuple-element.65.do_ref, f32[8,768]{1,0:T(8,128)S(1)} %get-tuple-element.66.rows_ref, bf16[128,1024]{1,0:T(8,128)(2,1)S(1)} %pad_maximum_fusion.kv_ref.k1_ref), custom_call_target="tpu_custom_call" | custom-call | flops 3690987520 | bytes 1597440 | tf_op jit(solution)/shard_map/own_pairs/pallas_call | solution.py:219
  16.0 0.0 collective-permute-done.4.rows_ref
  16.1 0.0 collective-permute-done.5.q_ref
  16.1 0.0 collective-permute-done.6.do_ref
  16.1 1.0 %other_pairs.1 = (f32[16,1024]{1,0:T(8,128)S(1)}, f32[16,1024]{1,0:T(8,128)S(1)}, bf16[32,1024]{1,0:T(8,128)(2,1)S(1)}, bf16[32,1024]{1,0:T(8,128)(2,1)S(1)}, bf16[32,1024]{1,0:T(8,128)(2,1)S(1)}) custom-call(bf16[128,2560]{1,0:T(8,128)(2,1)S(1)} %collective-permute-done.5.q_ref, bf16[128,2560]{1,0:T(8,128)(2,1)S(1)} %collective-permute-done.6.do_ref, ...), custom_call_target="tpu_custom_call" | custom-call | flops 335544320 | bytes 2121728 | tf_op jit(solution)/shard_map/other_pairs/pallas_call | solution.py:219
  17.1 2.1 %collective-permute-start.7 = (bf16[32,1024]{1,0:T(8,128)(2,1)S(1)}, bf16[32,1024]{1,0:T(8,128)(2,1)S(1)}, u32[]{:S(2)}, u32[]{:S(2)}) collective-permute-start(bf16[32,1024]{1,0:T(8,128)(2,1)S(1)} %get-tuple-element.76), channel_id=1, source_target_pairs={{0,13},{1,12},{2,15},{3,14},{4,9},{5,8},{6,11},{7,10},{8,5},{9,4},... | collective-permute-start | bytes 196616 | tf_op jit(solution)/shard_map/ppermute | solution.py:253
  19.2 0.4 %collective-permute-start.8 = (bf16[32,1024]{1,0:T(8,128)(2,1)S(1)}, bf16[32,1024]{1,0:T(8,128)(2,1)S(1)}, u32[]{:S(2)}, u32[]{:S(2)}) collective-permute-start(bf16[32,1024]{1,0:T(8,128)(2,1)S(1)} %get-tuple-element.77), channel_id=1, source_target_pairs={{0,5},{1,4},{2,7},{3,6},{4,1},{5,0},{6,3},{7,2},{8,13},{9,12},{10,... | collective-permute-start | bytes 196616 | tf_op jit(solution)/shard_map/ppermute | solution.py:253
  19.6 0.7 %collective-permute-start.9 = (bf16[32,1024]{1,0:T(8,128)(2,1)S(1)}, bf16[32,1024]{1,0:T(8,128)(2,1)S(1)}, u32[]{:S(2)}, u32[]{:S(2)}) collective-permute-start(bf16[32,1024]{1,0:T(8,128)(2,1)S(1)} %get-tuple-element.78), channel_id=1, source_target_pairs={{0,12},{1,13},{2,14},{3,15},{4,8},{5,9},{6,10},{7,11},{8,4},{9,5},... | collective-permute-start | bytes 196616 | tf_op jit(solution)/shard_map/ppermute | solution.py:253
  20.4 0.0 collective-permute-done.10.kv_ref.k2_ref
  20.4 1.6 %response_grads.1 = (bf16[128,512]{1,0:T(8,128)(2,1)}, bf16[128,512]{1,0:T(8,128)(2,1)}, bf16[4,128,640]{2,1,0:T(8,128)(2,1)S(1)}) custom-call(bf16[128,2560]{1,0:T(8,128)(2,1)S(1)} %get-tuple-element.55.q_ref, bf16[128,2560]{1,0:T(8,128)(2,1)S(1)} %get-tuple-element.65.do_ref, f32[8,768]{1,0:T(8,128)S(1)} %get-tuple-element.66.rows_ref, ...), custom_call_target="tpu_custom_call" | custom-call | flops 335544320 | bytes 2908160 | tf_op jit(solution)/shard_map/response_grads/pallas_call | solution.py:219
  22.0 0.0 collective-permute-done.7
  22.0 1.4 %collective-permute-done.8 = bf16[32,1024]{1,0:T(8,128)(2,1)S(1)} collective-permute-done((bf16[32,1024]{1,0:T(8,128)(2,1)S(1)}, bf16[32,1024]{1,0:T(8,128)(2,1)S(1)}, u32[]{:S(2)}, u32[]{:S(2)}) %collective-permute-start.8) | collective-permute-done | bytes 65568 | tf_op jit(solution)/shard_map/ppermute | solution.py:253
  23.4 0.2 collective-permute-done.9
  23.6 2.4 %collective-permute-start.11 = (bf16[16,1024]{1,0:T(8,128)(2,1)S(1)}, bf16[16,1024]{1,0:T(8,128)(2,1)S(1)}, u32[]{:S(2)}, u32[]{:S(2)}) collective-permute-start(bf16[16,1024]{1,0:T(8,128)(2,1)S(1)} %convert_add_fusion.1), channel_id=1, source_target_pairs={{0,6},{1,7},{2,4},{3,5},{4,2},{5,3},{6,0},{7,1},{8,14},{9,15},{10,... | collective-permute-start | bytes 98312 | tf_op jit(solution)/shard_map/ppermute | solution.py:253
  26.1 1.5 %query_grads.1 = bf16[128,2560]{1,0:T(8,128)(2,1)} custom-call(bf16[4,128,640]{2,1,0:T(8,128)(2,1)S(1)} %get-tuple-element.80.ds_ref.ds0_ref, bf16[4,128,640]{2,1,0:T(8,128)(2,1)S(1)} %get-tuple-element.90.ds1_ref, bf16[4,128,640]{2,1,0:T(8,128)(2,1)S(1)} %get-tuple-element.91.ds2_ref, bf16[128,512]{1,0:T(8,128)(2,1)S(1)} %get-tuple-element.59.k_ref.k0_ref, ...), custom_call_target="tpu_custom_call" | custom-call | flops 251658240 | bytes 2621440 | tf_op jit(solution)/shard_map/query_grads/pallas_call | solution.py:219
  27.6 0.3 %collective-permute-done.11 = bf16[16,1024]{1,0:T(8,128)(2,1)S(1)} collective-permute-done((bf16[16,1024]{1,0:T(8,128)(2,1)S(1)}, bf16[16,1024]{1,0:T(8,128)(2,1)S(1)}, u32[]{:S(2)}, u32[]{:S(2)}) %collective-permute-start.11) | collective-permute-done | bytes 32800 | tf_op jit(solution)/shard_map/ppermute | solution.py:253
  27.9 0.6 %slice_bitcast_fusion = (f32[1,16,512]{2,1,0:T(8,128)}, f32[1,16,512]{2,1,0:T(8,128)}) fusion(f32[16,1024]{1,0:T(8,128)S(1)} %convert_add_fusion), kind=kLoop, calls=%fused_computation.5 | loop fusion | bytes 131072 | tf_op jit(solution)/shard_map/broadcast_in_dim | solution.py:387
  (5 shorter events, 0.1 us)
Async XLA Ops:
  1.4 6.6 %collective-permute-start = (bf16[16,1024]{1,0:T(8,128)(2,1)S(1)}, bf16[16,1024]{1,0:T(8,128)(2,1)S(1)}, u32[]{:S(2)}, u32[]{:S(2)}) collective-permute-start(bf16[16,1024]{1,0:T(8,128)(2,1)S(1)} %pad_maximum_fusion.2), channel_id=1, source_target_pairs={{6,0},{7,1},{4,2},{5,3},{2,4},{3,5},{0,6},{1,7},{14,8},{15,9},{12,... | collective-permute-start | bytes 98312 | tf_op jit(solution)/shard_map/ppermute | solution.py:249
  4.8 11.2 %collective-permute-start.5 = (bf16[128,2560]{1,0:T(8,128)(2,1)}, bf16[128,2560]{1,0:T(8,128)(2,1)S(1)}, u32[]{:S(2)}, u32[]{:S(2)}) collective-permute-start(bf16[128,2560]{1,0:T(8,128)(2,1)} %bitcast.18), channel_id=1, source_target_pairs={{4,0},{5,1},{6,2},{7,3},{0,4},{1,5},{2,6},{3,7},{12,8},{13,9},{14,... | collective-permute-start | bytes 1966088 | tf_op jit(solution)/shard_map/ppermute | solution.py:249
  5.5 10.5 %collective-permute-start.6 = (bf16[128,2560]{1,0:T(8,128)(2,1)}, bf16[128,2560]{1,0:T(8,128)(2,1)S(1)}, u32[]{:S(2)}, u32[]{:S(2)}) collective-permute-start(bf16[128,2560]{1,0:T(8,128)(2,1)} %bitcast.16), channel_id=1, source_target_pairs={{4,0},{5,1},{6,2},{7,3},{0,4},{1,5},{2,6},{3,7},{12,8},{13,9},{14,... | collective-permute-start | bytes 1966088 | tf_op jit(solution)/shard_map/ppermute | solution.py:249
  8.0 5.6 %collective-permute-start.1 = (bf16[32,1024]{1,0:T(8,128)(2,1)S(1)}, bf16[32,1024]{1,0:T(8,128)(2,1)S(1)}, u32[]{:S(2)}, u32[]{:S(2)}) collective-permute-start(bf16[32,1024]{1,0:T(8,128)(2,1)S(1)} %pad_maximum_fusion.1), channel_id=1, source_target_pairs={{13,0},{12,1},{15,2},{14,3},{9,4},{8,5},{11,6},{10,7},{5,8},{4,9},... | collective-permute-start | bytes 196616 | tf_op jit(solution)/shard_map/ppermute | solution.py:249
  10.7 4.2 %collective-permute-start.2 = (bf16[32,1024]{1,0:T(8,128)(2,1)S(1)}, bf16[32,1024]{1,0:T(8,128)(2,1)S(1)}, u32[]{:S(2)}, u32[]{:S(2)}) collective-permute-start(bf16[32,1024]{1,0:T(8,128)(2,1)S(1)} %pad_maximum_fusion.1), channel_id=1, source_target_pairs={{5,0},{4,1},{7,2},{6,3},{1,4},{0,5},{3,6},{2,7},{13,8},{12,9},{15,... | collective-permute-start | bytes 196616 | tf_op jit(solution)/shard_map/ppermute | solution.py:249
  10.7 4.2 %collective-permute-start.3 = (bf16[32,1024]{1,0:T(8,128)(2,1)S(1)}, bf16[32,1024]{1,0:T(8,128)(2,1)S(1)}, u32[]{:S(2)}, u32[]{:S(2)}) collective-permute-start(bf16[32,1024]{1,0:T(8,128)(2,1)S(1)} %pad_maximum_fusion.1), channel_id=1, source_target_pairs={{12,0},{13,1},{14,2},{15,3},{8,4},{9,5},{10,6},{11,7},{4,8},{5,9},... | collective-permute-start | bytes 196616 | tf_op jit(solution)/shard_map/ppermute | solution.py:249
  13.6 2.5 %collective-permute-start.4 = (f32[8,768]{1,0:T(8,128)S(1)}, f32[8,768]{1,0:T(8,128)S(1)}, u32[]{:S(2)}, u32[]{:S(2)}) collective-permute-start(f32[8,768]{1,0:T(8,128)S(1)} %get-tuple-element.66.rows_ref), channel_id=1, source_target_pairs={{4,0},{5,1},{6,2},{7,3},{0,4},{1,5},{2,6},{3,7},{12,8},{13,9},{14,... | collective-permute-start | bytes 73736 | tf_op jit(solution)/shard_map/ppermute | solution.py:249
  14.9 5.5 %collective-permute-start.10 = (bf16[128,1024]{1,0:T(8,128)(2,1)S(1)}, bf16[128,1024]{1,0:T(8,128)(2,1)S(1)}, u32[]{:S(2)}, u32[]{:S(2)}) collective-permute-start(bf16[128,1024]{1,0:T(8,128)(2,1)S(1)} %pad_maximum_fusion.kv_ref.k1_ref), channel_id=1, source_target_pairs={{4,0},{5,1},{6,2},{7,3},{0,4},{1,5},{2,6},{3,7},{12,8},{13,9},{14,... | collective-permute-start | bytes 786440 | tf_op jit(solution)/shard_map/ppermute | solution.py:249
  17.1 4.9 %collective-permute-start.7 = (bf16[32,1024]{1,0:T(8,128)(2,1)S(1)}, bf16[32,1024]{1,0:T(8,128)(2,1)S(1)}, u32[]{:S(2)}, u32[]{:S(2)}) collective-permute-start(bf16[32,1024]{1,0:T(8,128)(2,1)S(1)} %get-tuple-element.76), channel_id=1, source_target_pairs={{0,13},{1,12},{2,15},{3,14},{4,9},{5,8},{6,11},{7,10},{8,5},{9,4},... | collective-permute-start | bytes 196616 | tf_op jit(solution)/shard_map/ppermute | solution.py:253
  19.2 4.2 %collective-permute-start.8 = (bf16[32,1024]{1,0:T(8,128)(2,1)S(1)}, bf16[32,1024]{1,0:T(8,128)(2,1)S(1)}, u32[]{:S(2)}, u32[]{:S(2)}) collective-permute-start(bf16[32,1024]{1,0:T(8,128)(2,1)S(1)} %get-tuple-element.77), channel_id=1, source_target_pairs={{0,5},{1,4},{2,7},{3,6},{4,1},{5,0},{6,3},{7,2},{8,13},{9,12},{10,... | collective-permute-start | bytes 196616 | tf_op jit(solution)/shard_map/ppermute | solution.py:253
  19.6 3.9 %collective-permute-start.9 = (bf16[32,1024]{1,0:T(8,128)(2,1)S(1)}, bf16[32,1024]{1,0:T(8,128)(2,1)S(1)}, u32[]{:S(2)}, u32[]{:S(2)}) collective-permute-start(bf16[32,1024]{1,0:T(8,128)(2,1)S(1)} %get-tuple-element.78), channel_id=1, source_target_pairs={{0,12},{1,13},{2,14},{3,15},{4,8},{5,9},{6,10},{7,11},{8,4},{9,5},... | collective-permute-start | bytes 196616 | tf_op jit(solution)/shard_map/ppermute | solution.py:253
  23.6 4.3 %collective-permute-start.11 = (bf16[16,1024]{1,0:T(8,128)(2,1)S(1)}, bf16[16,1024]{1,0:T(8,128)(2,1)S(1)}, u32[]{:S(2)}, u32[]{:S(2)}) collective-permute-start(bf16[16,1024]{1,0:T(8,128)(2,1)S(1)} %convert_add_fusion.1), channel_id=1, source_target_pairs={{0,6},{1,7},{2,4},{3,5},{4,2},{5,3},{6,0},{7,1},{8,14},{9,15},{10,... | collective-permute-start | bytes 98312 | tf_op jit(solution)/shard_map/ppermute | solution.py:253

commit v11 on v10

--- a/solution.py
+++ b/solution.py
@@ -334,7 +334,7 @@
         (ds_shape, array((nk, 2 * width), f32)),
         (),
         (q, do, terms, half),
-        88 * macs * nk,
+        160 * macs * nk,
     )
     part, terms2, q2, do2 = lax.optimization_barrier((part, terms2, q2, do2))
     cuts = (*range(0, n_first, PB), *range(n_first, nk + 1, n_first))

time: 28.9 us -> 28.7 us (level)
  waiting for transfers between devices: 3.1 us -> 2.75 us
    ppermute x8, waiting for transfers between devices: 1.19 us -> 0.85 us  [fetch(): return lax.ppermute(array, ('dp', 'resp'), pairs(*step))]
where the time goes in v11:
time: 28.7 us; the launch traced here: 28.5 us
  starting transfers between devices  13.7 us (48%)
  Pallas kernels  8.44 us (29%)
  waiting for transfers between devices  2.75 us (10%)
  between operations  2.04 us (7%)
  other arithmetic  0.88 us (3%)
  local copies, waits for them, and re-layouts  0.64 us (2%)
    pallas_call x6, Pallas kernels, call(): pl.pallas_call(kernel, name=name, out_shape=outs, in_specs=[SMEM] * len(s...  8.44 us
    ppermute x8, starting transfers between devices, fetch(): return lax.ppermute(array, ('dp', 'resp'), pairs(*step))  7.84 us
    ppermute x4, starting transfers between devices, give(): lax.ppermute(array, ('dp', 'resp'), [(i, j) for j, i in pairs(*step)])  5.87 us
    ppermute x4, waiting for transfers between devices, give(): lax.ppermute(array, ('dp', 'resp'), [(i, j) for j, i in pairs(*step)])  1.9 us
    ppermute x8, waiting for transfers between devices, fetch(): return lax.ppermute(array, ('dp', 'resp'), pairs(*step))  0.85 us
    concatenate x1, other arithmetic, shards(): jnp.concatenate([prompt_keys[0], prompt_values[0]], axis=1)  0.8 us
    broadcast_in_dim x1, local copies, waits for them, and re-layouts, shards(): total[None, :, width:]  0.63 us
  transfers between devices with their start and end apart: 12, of which 4 were waited for; matrix products, arithmetic and copies ran while one was open for 0% of the time, Pallas kernels for 30%

profile of v11, /device:TPU:0, one launch (start us, length us, event | category | flops | bytes accessed | tf_op | source)
XLA Modules:
  0.0 28.5 jit_solution(2452023500679858920)
XLA Ops:
  0.6 0.0 copy-start
  0.6 0.8 %pad_maximum_fusion.2 = bf16[16,1024]{1,0:T(8,128)(2,1)S(1)} fusion(bf16[16,512]{1,0:T(8,128)(2,1)} %bitcast.23, bf16[16,512]{1,0:T(8,128)(2,1)} %bitcast.24), kind=kLoop, calls=%fused_computation.7 | loop fusion | flops 65536 | bytes 65536 | tf_op jit(solution)/shard_map/concatenate | solution.py:286
  1.4 3.5 %collective-permute-start = (bf16[16,1024]{1,0:T(8,128)(2,1)S(1)}, bf16[16,1024]{1,0:T(8,128)(2,1)S(1)}, u32[]{:S(2)}, u32[]{:S(2)}) collective-permute-start(bf16[16,1024]{1,0:T(8,128)(2,1)S(1)} %pad_maximum_fusion.2), channel_id=1, source_target_pairs={{6,0},{7,1},{4,2},{5,3},{2,4},{3,5},{0,6},{1,7},{14,8},{15,9},{12,... | collective-permute-start | bytes 98312 | tf_op jit(solution)/shard_map/ppermute | solution.py:249
  6.2 1.1 %load.1 = (bf16[128,2560]{1,0:T(8,128)(2,1)S(1)}, bf16[128,512]{1,0:T(8,128)(2,1)S(1)}, f32[20,1,128]{2,1,0:T(1,128)S(1)}, s32[8,256]{1,0:T(8,128)S(1)}) custom-call(s32[1]{0:T(128)S(6)} %copy.15.len_ref, s32[1]{0:T(128)S(6)} %copy.16.seen_ref, bf16[128,2560]{1,0:T(8,128)(2,1)} %bitcast.18, bf16[128,512]{1,0:T(8,128)(2,1)} %bitcast.21, f32[20,1,128]{2,1,0:T(1,128)} %bitcast.25), custom_call_target="tpu_custom_call" | custom-call | bytes 796672 | tf_op jit(solution)/shard_map/load/pallas_call | solution.py:219
  7.4 0.0 collective-permute-done
  7.4 2.8 %collective-permute-start.1 = (bf16[32,1024]{1,0:T(8,128)(2,1)S(1)}, bf16[32,1024]{1,0:T(8,128)(2,1)S(1)}, u32[]{:S(2)}, u32[]{:S(2)}) collective-permute-start(bf16[32,1024]{1,0:T(8,128)(2,1)S(1)} %pad_maximum_fusion.1), channel_id=1, source_target_pairs={{13,0},{12,1},{15,2},{14,3},{9,4},{8,5},{11,6},{10,7},{5,8},{4,9},... | collective-permute-start | bytes 196616 | tf_op jit(solution)/shard_map/ppermute | solution.py:249
  10.2 0.0 collective-permute-start.2
  10.2 0.7 %collective-permute-start.3 = (bf16[32,1024]{1,0:T(8,128)(2,1)S(1)}, bf16[32,1024]{1,0:T(8,128)(2,1)S(1)}, u32[]{:S(2)}, u32[]{:S(2)}) collective-permute-start(bf16[32,1024]{1,0:T(8,128)(2,1)S(1)} %pad_maximum_fusion.1), channel_id=1, source_target_pairs={{12,0},{13,1},{14,2},{15,3},{8,4},{9,5},{10,6},{11,7},{4,8},{5,9},... | collective-permute-start | bytes 196616 | tf_op jit(solution)/shard_map/ppermute | solution.py:249
  10.9 0.1 collective-permute-start.5
  11.0 0.0 copy-done
  11.0 0.5 %collective-permute-start.6 = (bf16[128,2560]{1,0:T(8,128)(2,1)S(1)}, bf16[128,2560]{1,0:T(8,128)(2,1)S(1)}, u32[]{:S(2)}, u32[]{:S(2)}) collective-permute-start(bf16[128,2560]{1,0:T(8,128)(2,1)S(1)} %bitcast.17), channel_id=1, source_target_pairs={{4,0},{5,1},{6,2},{7,3},{0,4},{1,5},{2,6},{3,7},{12,8},{13,9},{14,... | collective-permute-start | bytes 1966088 | tf_op jit(solution)/shard_map/ppermute | solution.py:249
  11.5 2.2 %self_pairs.1 = (bf16[128,2560]{1,0:T(8,128)(2,1)S(1)}, bf16[4,128,640]{2,1,0:T(8,128)(2,1)S(1)}, bf16[4,128,640]{2,1,0:T(8,128)(2,1)S(1)}, f32[8,768]{1,0:T(8,128)S(1)}) custom-call(s32[8,256]{1,0:T(8,128)S(1)} %get-tuple-element.58.scalars_ref, bf16[128,2560]{1,0:T(8,128)(2,1)S(1)} %get-tuple-element.55.q_ref, ...), custom_call_target="tpu_custom_call" | custom-call | flops 209715200 | bytes 2246656 | tf_op jit(solution)/shard_map/self_pairs/pallas_call | solution.py:219
  13.6 0.0 collective-permute-done.1
  13.7 0.1 collective-permute-start.4
  13.8 0.8 %collective-permute-done.2 = bf16[32,1024]{1,0:T(8,128)(2,1)S(1)} collective-permute-done((bf16[32,1024]{1,0:T(8,128)(2,1)S(1)}, bf16[32,1024]{1,0:T(8,128)(2,1)S(1)}, u32[]{:S(2)}, u32[]{:S(2)}) %collective-permute-start.2) | collective-permute-done | bytes 65568 | tf_op jit(solution)/shard_map/ppermute | solution.py:249
  14.6 0.0 collective-permute-done.3
  14.6 0.2 collective-permute-start.10
  14.8 1.0 %own_pairs.1 = (bf16[4,128,640]{2,1,0:T(8,128)(2,1)S(1)}, f32[128,1024]{1,0:T(8,128)S(1)}) custom-call(bf16[128,2560]{1,0:T(8,128)(2,1)S(1)} %get-tuple-element.55.q_ref, bf16[128,2560]{1,0:T(8,128)(2,1)S(1)} %get-tuple-element.65.do_ref, f32[8,768]{1,0:T(8,128)S(1)} %get-tuple-element.66.rows_ref, bf16[128,1024]{1,0:T(8,128)(2,1)S(1)} %pad_maximum_fusion.kv_ref.k1_ref), custom_call_target="tpu_custom_call" | custom-call | flops 6710886400 | bytes 1597440 | tf_op jit(solution)/shard_map/own_pairs/pallas_call | solution.py:219
  15.8 0.0 collective-permute-done.4.rows_ref
  15.8 0.0 collective-permute-done.5.q_ref
  15.8 0.0 collective-permute-done.6.do_ref
  15.8 1.0 %other_pairs.1 = (f32[16,1024]{1,0:T(8,128)S(1)}, f32[16,1024]{1,0:T(8,128)S(1)}, bf16[32,1024]{1,0:T(8,128)(2,1)S(1)}, bf16[32,1024]{1,0:T(8,128)(2,1)S(1)}, bf16[32,1024]{1,0:T(8,128)(2,1)S(1)}) custom-call(bf16[128,2560]{1,0:T(8,128)(2,1)S(1)} %collective-permute-done.5.q_ref, bf16[128,2560]{1,0:T(8,128)(2,1)S(1)} %collective-permute-done.6.do_ref, ...), custom_call_target="tpu_custom_call" | custom-call | flops 335544320 | bytes 2121728 | tf_op jit(solution)/shard_map/other_pairs/pallas_call | solution.py:219
  16.8 1.9 %collective-permute-start.7 = (bf16[32,1024]{1,0:T(8,128)(2,1)S(1)}, bf16[32,1024]{1,0:T(8,128)(2,1)S(1)}, u32[]{:S(2)}, u32[]{:S(2)}) collective-permute-start(bf16[32,1024]{1,0:T(8,128)(2,1)S(1)} %get-tuple-element.76), channel_id=1, source_target_pairs={{0,13},{1,12},{2,15},{3,14},{4,9},{5,8},{6,11},{7,10},{8,5},{9,4},... | collective-permute-start | bytes 196616 | tf_op jit(solution)/shard_map/ppermute | solution.py:253
  18.7 0.5 %collective-permute-start.8 = (bf16[32,1024]{1,0:T(8,128)(2,1)S(1)}, bf16[32,1024]{1,0:T(8,128)(2,1)S(1)}, u32[]{:S(2)}, u32[]{:S(2)}) collective-permute-start(bf16[32,1024]{1,0:T(8,128)(2,1)S(1)} %get-tuple-element.77), channel_id=1, source_target_pairs={{0,5},{1,4},{2,7},{3,6},{4,1},{5,0},{6,3},{7,2},{8,13},{9,12},{10,... | collective-permute-start | bytes 196616 | tf_op jit(solution)/shard_map/ppermute | solution.py:253
  19.2 1.0 %collective-permute-start.9 = (bf16[32,1024]{1,0:T(8,128)(2,1)S(1)}, bf16[32,1024]{1,0:T(8,128)(2,1)S(1)}, u32[]{:S(2)}, u32[]{:S(2)}) collective-permute-start(bf16[32,1024]{1,0:T(8,128)(2,1)S(1)} %get-tuple-element.78), channel_id=1, source_target_pairs={{0,12},{1,13},{2,14},{3,15},{4,8},{5,9},{6,10},{7,11},{8,4},{9,5},... | collective-permute-start | bytes 196616 | tf_op jit(solution)/shard_map/ppermute | solution.py:253
  20.2 0.0 collective-permute-done.10.kv_ref.k2_ref
  20.2 1.6 %response_grads.1 = (bf16[128,512]{1,0:T(8,128)(2,1)}, bf16[128,512]{1,0:T(8,128)(2,1)}, bf16[4,128,640]{2,1,0:T(8,128)(2,1)S(1)}) custom-call(bf16[128,2560]{1,0:T(8,128)(2,1)S(1)} %get-tuple-element.55.q_ref, bf16[128,2560]{1,0:T(8,128)(2,1)S(1)} %get-tuple-element.65.do_ref, f32[8,768]{1,0:T(8,128)S(1)} %get-tuple-element.66.rows_ref, ...), custom_call_target="tpu_custom_call" | custom-call | flops 335544320 | bytes 2908160 | tf_op jit(solution)/shard_map/response_grads/pallas_call | solution.py:219
  21.8 0.0 collective-permute-done.7
  21.8 1.1 %collective-permute-done.8 = bf16[32,1024]{1,0:T(8,128)(2,1)S(1)} collective-permute-done((bf16[32,1024]{1,0:T(8,128)(2,1)S(1)}, bf16[32,1024]{1,0:T(8,128)(2,1)S(1)}, u32[]{:S(2)}, u32[]{:S(2)}) %collective-permute-start.8) | collective-permute-done | bytes 65568 | tf_op jit(solution)/shard_map/ppermute | solution.py:253
  22.9 0.6 %collective-permute-done.9 = bf16[32,1024]{1,0:T(8,128)(2,1)S(1)} collective-permute-done((bf16[32,1024]{1,0:T(8,128)(2,1)S(1)}, bf16[32,1024]{1,0:T(8,128)(2,1)S(1)}, u32[]{:S(2)}, u32[]{:S(2)}) %collective-permute-start.9) | collective-permute-done | bytes 65568 | tf_op jit(solution)/shard_map/ppermute | solution.py:253
  23.5 2.5 %collective-permute-start.11 = (bf16[16,1024]{1,0:T(8,128)(2,1)S(1)}, bf16[16,1024]{1,0:T(8,128)(2,1)S(1)}, u32[]{:S(2)}, u32[]{:S(2)}) collective-permute-start(bf16[16,1024]{1,0:T(8,128)(2,1)S(1)} %convert_add_fusion.1), channel_id=1, source_target_pairs={{0,6},{1,7},{2,4},{3,5},{4,2},{5,3},{6,0},{7,1},{8,14},{9,15},{10,... | collective-permute-start | bytes 98312 | tf_op jit(solution)/shard_map/ppermute | solution.py:253
  26.1 1.5 %query_grads.1 = bf16[128,2560]{1,0:T(8,128)(2,1)} custom-call(bf16[4,128,640]{2,1,0:T(8,128)(2,1)S(1)} %get-tuple-element.80.ds_ref.ds0_ref, bf16[4,128,640]{2,1,0:T(8,128)(2,1)S(1)} %get-tuple-element.90.ds1_ref, bf16[4,128,640]{2,1,0:T(8,128)(2,1)S(1)} %get-tuple-element.91.ds2_ref, bf16[128,512]{1,0:T(8,128)(2,1)S(1)} %get-tuple-element.59.k_ref.k0_ref, ...), custom_call_target="tpu_custom_call" | custom-call | flops 251658240 | bytes 2621440 | tf_op jit(solution)/shard_map/query_grads/pallas_call | solution.py:219
  27.6 0.2 collective-permute-done.11
  27.8 0.6 %slice_bitcast_fusion = (f32[1,16,512]{2,1,0:T(8,128)}, f32[1,16,512]{2,1,0:T(8,128)}) fusion(f32[16,1024]{1,0:T(8,128)S(1)} %convert_add_fusion), kind=kLoop, calls=%fused_computation.5 | loop fusion | bytes 131072 | tf_op jit(solution)/shard_map/broadcast_in_dim | solution.py:387
  (5 shorter events, 0.1 us)
Async XLA Ops:
  0.6 10.4 %copy-start = (bf16[1,128,2560]{2,1,0:T(8,128)(2,1)S(1)}, bf16[1,128,2560]{2,1,0:T(8,128)(2,1)}, u32[]{:S(2)}) copy-start(bf16[1,128,2560]{2,1,0:T(8,128)(2,1)} %param.13) | copy-start | bytes 1966084
  1.4 5.9 %collective-permute-start = (bf16[16,1024]{1,0:T(8,128)(2,1)S(1)}, bf16[16,1024]{1,0:T(8,128)(2,1)S(1)}, u32[]{:S(2)}, u32[]{:S(2)}) collective-permute-start(bf16[16,1024]{1,0:T(8,128)(2,1)S(1)} %pad_maximum_fusion.2), channel_id=1, source_target_pairs={{6,0},{7,1},{4,2},{5,3},{2,4},{3,5},{0,6},{1,7},{14,8},{15,9},{12,... | collective-permute-start | bytes 98312 | tf_op jit(solution)/shard_map/ppermute | solution.py:249
  7.4 6.3 %collective-permute-start.1 = (bf16[32,1024]{1,0:T(8,128)(2,1)S(1)}, bf16[32,1024]{1,0:T(8,128)(2,1)S(1)}, u32[]{:S(2)}, u32[]{:S(2)}) collective-permute-start(bf16[32,1024]{1,0:T(8,128)(2,1)S(1)} %pad_maximum_fusion.1), channel_id=1, source_target_pairs={{13,0},{12,1},{15,2},{14,3},{9,4},{8,5},{11,6},{10,7},{5,8},{4,9},... | collective-permute-start | bytes 196616 | tf_op jit(solution)/shard_map/ppermute | solution.py:249
  10.2 4.4 %collective-permute-start.2 = (bf16[32,1024]{1,0:T(8,128)(2,1)S(1)}, bf16[32,1024]{1,0:T(8,128)(2,1)S(1)}, u32[]{:S(2)}, u32[]{:S(2)}) collective-permute-start(bf16[32,1024]{1,0:T(8,128)(2,1)S(1)} %pad_maximum_fusion.1), channel_id=1, source_target_pairs={{5,0},{4,1},{7,2},{6,3},{1,4},{0,5},{3,6},{2,7},{13,8},{12,9},{15,... | collective-permute-start | bytes 196616 | tf_op jit(solution)/shard_map/ppermute | solution.py:249
  10.2 4.4 %collective-permute-start.3 = (bf16[32,1024]{1,0:T(8,128)(2,1)S(1)}, bf16[32,1024]{1,0:T(8,128)(2,1)S(1)}, u32[]{:S(2)}, u32[]{:S(2)}) collective-permute-start(bf16[32,1024]{1,0:T(8,128)(2,1)S(1)} %pad_maximum_fusion.1), channel_id=1, source_target_pairs={{12,0},{13,1},{14,2},{15,3},{8,4},{9,5},{10,6},{11,7},{4,8},{5,9},... | collective-permute-start | bytes 196616 | tf_op jit(solution)/shard_map/ppermute | solution.py:249
  10.9 4.8 %collective-permute-start.5 = (bf16[128,2560]{1,0:T(8,128)(2,1)}, bf16[128,2560]{1,0:T(8,128)(2,1)S(1)}, u32[]{:S(2)}, u32[]{:S(2)}) collective-permute-start(bf16[128,2560]{1,0:T(8,128)(2,1)} %bitcast.19), channel_id=1, source_target_pairs={{4,0},{5,1},{6,2},{7,3},{0,4},{1,5},{2,6},{3,7},{12,8},{13,9},{14,... | collective-permute-start | bytes 1966088 | tf_op jit(solution)/shard_map/ppermute | solution.py:249
  11.0 4.8 %collective-permute-start.6 = (bf16[128,2560]{1,0:T(8,128)(2,1)S(1)}, bf16[128,2560]{1,0:T(8,128)(2,1)S(1)}, u32[]{:S(2)}, u32[]{:S(2)}) collective-permute-start(bf16[128,2560]{1,0:T(8,128)(2,1)S(1)} %bitcast.17), channel_id=1, source_target_pairs={{4,0},{5,1},{6,2},{7,3},{0,4},{1,5},{2,6},{3,7},{12,8},{13,9},{14,... | collective-permute-start | bytes 1966088 | tf_op jit(solution)/shard_map/ppermute | solution.py:249
  13.7 2.1 %collective-permute-start.4 = (f32[8,768]{1,0:T(8,128)S(1)}, f32[8,768]{1,0:T(8,128)S(1)}, u32[]{:S(2)}, u32[]{:S(2)}) collective-permute-start(f32[8,768]{1,0:T(8,128)S(1)} %get-tuple-element.66.rows_ref), channel_id=1, source_target_pairs={{4,0},{5,1},{6,2},{7,3},{0,4},{1,5},{2,6},{3,7},{12,8},{13,9},{14,... | collective-permute-start | bytes 73736 | tf_op jit(solution)/shard_map/ppermute | solution.py:249
  14.6 5.5 %collective-permute-start.10 = (bf16[128,1024]{1,0:T(8,128)(2,1)S(1)}, bf16[128,1024]{1,0:T(8,128)(2,1)S(1)}, u32[]{:S(2)}, u32[]{:S(2)}) collective-permute-start(bf16[128,1024]{1,0:T(8,128)(2,1)S(1)} %pad_maximum_fusion.kv_ref.k1_ref), channel_id=1, source_target_pairs={{4,0},{5,1},{6,2},{7,3},{0,4},{1,5},{2,6},{3,7},{12,8},{13,9},{14,... | collective-permute-start | bytes 786440 | tf_op jit(solution)/shard_map/ppermute | solution.py:249
  16.8 4.9 %collective-permute-start.7 = (bf16[32,1024]{1,0:T(8,128)(2,1)S(1)}, bf16[32,1024]{1,0:T(8,128)(2,1)S(1)}, u32[]{:S(2)}, u32[]{:S(2)}) collective-permute-start(bf16[32,1024]{1,0:T(8,128)(2,1)S(1)} %get-tuple-element.76), channel_id=1, source_target_pairs={{0,13},{1,12},{2,15},{3,14},{4,9},{5,8},{6,11},{7,10},{8,5},{9,4},... | collective-permute-start | bytes 196616 | tf_op jit(solution)/shard_map/ppermute | solution.py:253
  18.7 4.2 %collective-permute-start.8 = (bf16[32,1024]{1,0:T(8,128)(2,1)S(1)}, bf16[32,1024]{1,0:T(8,128)(2,1)S(1)}, u32[]{:S(2)}, u32[]{:S(2)}) collective-permute-start(bf16[32,1024]{1,0:T(8,128)(2,1)S(1)} %get-tuple-element.77), channel_id=1, source_target_pairs={{0,5},{1,4},{2,7},{3,6},{4,1},{5,0},{6,3},{7,2},{8,13},{9,12},{10,... | collective-permute-start | bytes 196616 | tf_op jit(solution)/shard_map/ppermute | solution.py:253
  19.2 4.3 %collective-permute-start.9 = (bf16[32,1024]{1,0:T(8,128)(2,1)S(1)}, bf16[32,1024]{1,0:T(8,128)(2,1)S(1)}, u32[]{:S(2)}, u32[]{:S(2)}) collective-permute-start(bf16[32,1024]{1,0:T(8,128)(2,1)S(1)} %get-tuple-element.78), channel_id=1, source_target_pairs={{0,12},{1,13},{2,14},{3,15},{4,8},{5,9},{6,10},{7,11},{8,4},{9,5},... | collective-permute-start | bytes 196616 | tf_op jit(solution)/shard_map/ppermute | solution.py:253
  23.5 4.3 %collective-permute-start.11 = (bf16[16,1024]{1,0:T(8,128)(2,1)S(1)}, bf16[16,1024]{1,0:T(8,128)(2,1)S(1)}, u32[]{:S(2)}, u32[]{:S(2)}) collective-permute-start(bf16[16,1024]{1,0:T(8,128)(2,1)S(1)} %convert_add_fusion.1), channel_id=1, source_target_pairs={{0,6},{1,7},{2,4},{3,5},{4,2},{5,3},{6,0},{7,1},{8,14},{9,15},{10,... | collective-permute-start | bytes 98312 | tf_op jit(solution)/shard_map/ppermute | solution.py:253

commit v12 on v11

--- a/solution.py
+++ b/solution.py
@@ -180,17 +180,19 @@
     prompt_terms(far, q_ref, do_ref, rows_ref, kv_ref, use)
 
 
-def response_kernel(
-    pieces, n_resp, q_ref, do_ref, rows_ref, p_ref, ds_ref, kv_ref, gk_ref, gv_ref, ds2_ref
-):
+def response_kernel(q_ref, do_ref, p_ref, ds_ref, gk_ref, gv_ref):
     scale = 1.0 / DH**0.5
-    far = block_rows(pieces, 1, n_resp, rows_ref, RATIO * q_ref.shape[0])
-
-    def use(g, p16, ds16):
-        ds2_ref[g] = ds16
+    for g in range(HK):
         cols = head_cols(g)
         gv_ref[:, cols] = dot(p_ref[g], head_rows(do_ref, g), NN).astype(gv_ref.dtype)
         gk_ref[:, cols] = (dot(ds_ref[g], head_rows(q_ref, g), NN) * scale).astype(gk_ref.dtype)
+
+
+def scores_kernel(pieces, n_resp, q_ref, do_ref, rows_ref, kv_ref, ds_ref):
+    far = block_rows(pieces, 1, n_resp, rows_ref, RATIO * q_ref.shape[0])
+
+    def use(g, p16, ds16):
+        ds_ref[g] = ds16
 
     prompt_terms(far, q_ref, do_ref, rows_ref, kv_ref, use)
 
@@ -322,8 +324,7 @@
         ),
     )
     terms2 = fetch(worked[3], 1, 0, 0)
-    moved, (do, p_self, ds_self, terms) = lax.optimization_barrier((moved[::-1], worked))
-    moved = moved[::-1]
+    moved, (do, p_self, ds_self, terms) = lax.optimization_barrier((moved, worked))
     half = jnp.concatenate([bundle] + moved, 0)
     nk = half.shape[0]
     ds_shape = array((HK, nk, RATIO * rows), b16)
@@ -348,18 +349,28 @@
         8 * macs * nk,
     )
 
-    other = fetch(half, 1, 0, 0)
+    after, parts = lax.optimization_barrier((half, parts))
+    other = fetch(after, 1, 0, 0)
     low, sent = parts[: len(first)], parts[len(first) :]
     moved = [give(part, *step) for part, step in zip(sent, steps)]
-    late = call(
-        functools.partial(response_kernel, pieces, n_resp),
+    grads = call(
+        response_kernel,
         "response_grads",
-        (array((rows, width), b16), array((rows, width), b16), ds_shape),
-        (),
-        (q, do, terms, p_self, ds_self, other),
-        4 * macs * rows + 4 * macs * nk,
-    )
-    moved, (grad_rk, grad_rv, ds_other) = lax.optimization_barrier((moved[::-1], late))
+        (array((rows, width), b16), array((rows, width), b16)),
+        (),
+        (q, do, p_self, ds_self),
+        160 * macs * rows,
+    )
+    other, grads = lax.optimization_barrier((other, grads))
+    ds_other = call(
+        functools.partial(scores_kernel, pieces, n_resp),
+        "other_scores",
+        ds_shape,
+        (),
+        (q, do, terms, other),
+        4 * macs * nk,
+    )
+    moved, (grad_rk, grad_rv), ds_other = lax.optimization_barrier((moved[::-1], grads, ds_other))
     sums = []
     for i, total in enumerate(low):
         for part in moved:

time: 28.7 us -> 28.8 us (level)
  starting transfers between devices: 13.7 us -> 13.3 us
  Pallas kernels: 8.44 us -> 8.8 us
    ppermute x4, starting transfers between devices: 5.87 us -> 5.17 us  [give(): lax.ppermute(array, ('dp', 'resp'), [(i, j) for j, i in pairs(*step)])]
    pallas_call x6 -> x7, Pallas kernels: 8.44 us -> 8.8 us  [call(): pl.pallas_call(kernel, name=name, out_shape=outs, in_specs=[SMEM] * len(s...]
  transfers between devices with their start and end apart: 12 -> 12, of which waited for: 4 -> 4; matrix products, arithmetic and copies ran while one was open for 0% -> 0% of each run, Pallas kernels for 30% -> 27%
where the time goes in v12:
time: 28.8 us; the launch traced here: 28.6 us
  starting transfers between devices  13.3 us (46%)
  Pallas kernels  8.8 us (31%)
  waiting for transfers between devices  2.92 us (10%)
  between operations  2.06 us (7%)
  other arithmetic  0.87 us (3%)
  local copies, waits for them, and re-layouts  0.64 us (2%)
    pallas_call x7, Pallas kernels, call(): pl.pallas_call(kernel, name=name, out_shape=outs, in_specs=[SMEM] * len(s...  8.8 us
    ppermute x8, starting transfers between devices, fetch(): return lax.ppermute(array, ('dp', 'resp'), pairs(*step))  8.09 us
    ppermute x4, starting transfers between devices, give(): lax.ppermute(array, ('dp', 'resp'), [(i, j) for j, i in pairs(*step)])  5.17 us
    ppermute x4, waiting for transfers between devices, give(): lax.ppermute(array, ('dp', 'resp'), [(i, j) for j, i in pairs(*step)])  2.12 us
    ppermute x8, waiting for transfers between devices, fetch(): return lax.ppermute(array, ('dp', 'resp'), pairs(*step))  0.81 us
    concatenate x1, other arithmetic, shards(): jnp.concatenate([prompt_keys[0], prompt_values[0]], axis=1)  0.8 us
    broadcast_in_dim x1, local copies, waits for them, and re-layouts, shards(): total[None, :, width:]  0.63 us
  transfers between devices with their start and end apart: 12, of which 4 were waited for; matrix products, arithmetic and copies ran while one was open for 0% of the time, Pallas kernels for 27%

profile of v12, /device:TPU:0, one launch (start us, length us, event | category | flops | bytes accessed | tf_op | source)
XLA Modules:
  0.0 28.6 jit_solution(10526567894622716092)
XLA Ops:
  0.6 0.0 copy-start
  0.6 0.8 %pad_maximum_fusion.2 = bf16[16,1024]{1,0:T(8,128)(2,1)S(1)} fusion(bf16[16,512]{1,0:T(8,128)(2,1)} %bitcast.23, bf16[16,512]{1,0:T(8,128)(2,1)} %bitcast.24), kind=kLoop, calls=%fused_computation.7 | loop fusion | flops 65536 | bytes 65536 | tf_op jit(solution)/shard_map/concatenate | solution.py:288
  1.4 3.5 %collective-permute-start = (bf16[16,1024]{1,0:T(8,128)(2,1)S(1)}, bf16[16,1024]{1,0:T(8,128)(2,1)S(1)}, u32[]{:S(2)}, u32[]{:S(2)}) collective-permute-start(bf16[16,1024]{1,0:T(8,128)(2,1)S(1)} %pad_maximum_fusion.2), channel_id=1, source_target_pairs={{6,0},{7,1},{4,2},{5,3},{2,4},{3,5},{0,6},{1,7},{14,8},{15,9},{12,... | collective-permute-start | bytes 98312 | tf_op jit(solution)/shard_map/ppermute | solution.py:251
  6.2 1.1 %load.1 = (bf16[128,2560]{1,0:T(8,128)(2,1)S(1)}, bf16[128,512]{1,0:T(8,128)(2,1)S(1)}, f32[20,1,128]{2,1,0:T(1,128)S(1)}, s32[8,256]{1,0:T(8,128)S(1)}) custom-call(s32[1]{0:T(128)S(6)} %copy.15.len_ref, s32[1]{0:T(128)S(6)} %copy.16.seen_ref, bf16[128,2560]{1,0:T(8,128)(2,1)} %bitcast.18, bf16[128,512]{1,0:T(8,128)(2,1)} %bitcast.21, f32[20,1,128]{2,1,0:T(1,128)} %bitcast.25), custom_call_target="tpu_custom_call" | custom-call | bytes 796672 | tf_op jit(solution)/shard_map/load/pallas_call | solution.py:221
  7.4 0.0 collective-permute-done
  7.4 2.8 %collective-permute-start.3 = (bf16[32,1024]{1,0:T(8,128)(2,1)S(1)}, bf16[32,1024]{1,0:T(8,128)(2,1)S(1)}, u32[]{:S(2)}, u32[]{:S(2)}) collective-permute-start(bf16[32,1024]{1,0:T(8,128)(2,1)S(1)} %pad_maximum_fusion.1), channel_id=1, source_target_pairs={{13,0},{12,1},{15,2},{14,3},{9,4},{8,5},{11,6},{10,7},{5,8},{4,9},... | collective-permute-start | bytes 196616 | tf_op jit(solution)/shard_map/ppermute | solution.py:251
  10.2 0.0 collective-permute-start.2
  10.2 0.7 %collective-permute-start.1 = (bf16[32,1024]{1,0:T(8,128)(2,1)S(1)}, bf16[32,1024]{1,0:T(8,128)(2,1)S(1)}, u32[]{:S(2)}, u32[]{:S(2)}) collective-permute-start(bf16[32,1024]{1,0:T(8,128)(2,1)S(1)} %pad_maximum_fusion.1), channel_id=1, source_target_pairs={{12,0},{13,1},{14,2},{15,3},{8,4},{9,5},{10,6},{11,7},{4,8},{5,9},... | collective-permute-start | bytes 196616 | tf_op jit(solution)/shard_map/ppermute | solution.py:251
  10.9 0.1 collective-permute-start.5
  11.0 0.0 copy-done
  11.0 0.5 %collective-permute-start.6 = (bf16[128,2560]{1,0:T(8,128)(2,1)S(1)}, bf16[128,2560]{1,0:T(8,128)(2,1)S(1)}, u32[]{:S(2)}, u32[]{:S(2)}) collective-permute-start(bf16[128,2560]{1,0:T(8,128)(2,1)S(1)} %bitcast.17), channel_id=1, source_target_pairs={{4,0},{5,1},{6,2},{7,3},{0,4},{1,5},{2,6},{3,7},{12,8},{13,9},{14,... | collective-permute-start | bytes 1966088 | tf_op jit(solution)/shard_map/ppermute | solution.py:251
  11.5 2.2 %self_pairs.1 = (bf16[128,2560]{1,0:T(8,128)(2,1)S(1)}, bf16[4,128,640]{2,1,0:T(8,128)(2,1)S(1)}, bf16[4,128,640]{2,1,0:T(8,128)(2,1)S(1)}, f32[8,768]{1,0:T(8,128)S(1)}) custom-call(s32[8,256]{1,0:T(8,128)S(1)} %get-tuple-element.65.scalars_ref, bf16[128,2560]{1,0:T(8,128)(2,1)S(1)} %get-tuple-element.66.q_ref, ...), custom_call_target="tpu_custom_call" | custom-call | flops 209715200 | bytes 2246656 | tf_op jit(solution)/shard_map/self_pairs/pallas_call | solution.py:221
  13.7 0.0 collective-permute-done.3
  13.7 0.1 collective-permute-start.4
  13.8 0.8 %collective-permute-done.2 = bf16[32,1024]{1,0:T(8,128)(2,1)S(1)} collective-permute-done((bf16[32,1024]{1,0:T(8,128)(2,1)S(1)}, bf16[32,1024]{1,0:T(8,128)(2,1)S(1)}, u32[]{:S(2)}, u32[]{:S(2)}) %collective-permute-start.2) | collective-permute-done | bytes 65568 | tf_op jit(solution)/shard_map/ppermute | solution.py:251
  14.6 0.0 collective-permute-done.1
  14.6 1.0 %own_pairs.1 = (bf16[4,128,640]{2,1,0:T(8,128)(2,1)S(1)}, f32[128,1024]{1,0:T(8,128)S(1)}) custom-call(bf16[128,2560]{1,0:T(8,128)(2,1)S(1)} %get-tuple-element.66.q_ref, bf16[128,2560]{1,0:T(8,128)(2,1)S(1)} %get-tuple-element.76.do_ref, f32[8,768]{1,0:T(8,128)S(1)} %get-tuple-element.77.rows_ref, bf16[128,1024]{1,0:T(8,128)(2,1)S(1)} %pad_maximum_fusion.kv_ref.k1_ref), custom_call_target="tpu_custom_call" | custom-call | flops 6710886400 | bytes 1597440 | tf_op jit(solution)/shard_map/own_pairs/pallas_call | solution.py:221
  15.7 0.0 collective-permute-done.4.rows_ref
  15.7 0.0 collective-permute-done.5.q_ref
  15.7 0.0 collective-permute-done.6.do_ref
  15.7 1.1 %other_pairs.1 = (f32[16,1024]{1,0:T(8,128)S(1)}, f32[16,1024]{1,0:T(8,128)S(1)}, bf16[32,1024]{1,0:T(8,128)(2,1)S(1)}, bf16[32,1024]{1,0:T(8,128)(2,1)S(1)}, bf16[32,1024]{1,0:T(8,128)(2,1)S(1)}) custom-call(bf16[128,2560]{1,0:T(8,128)(2,1)S(1)} %collective-permute-done.5.q_ref, bf16[128,2560]{1,0:T(8,128)(2,1)S(1)} %collective-permute-done.6.do_ref, ...), custom_call_target="tpu_custom_call" | custom-call | flops 335544320 | bytes 2121728 | tf_op jit(solution)/shard_map/other_pairs/pallas_call | solution.py:221
  16.8 1.8 %collective-permute-start.7 = (bf16[32,1024]{1,0:T(8,128)(2,1)S(1)}, bf16[32,1024]{1,0:T(8,128)(2,1)S(1)}, u32[]{:S(2)}, u32[]{:S(2)}) collective-permute-start(bf16[32,1024]{1,0:T(8,128)(2,1)S(1)} %get-tuple-element.89), channel_id=1, source_target_pairs={{0,13},{1,12},{2,15},{3,14},{4,9},{5,8},{6,11},{7,10},{8,5},{9,4},... | collective-permute-start | bytes 196616 | tf_op jit(solution)/shard_map/ppermute | solution.py:255
  18.6 0.5 %collective-permute-start.8 = (bf16[32,1024]{1,0:T(8,128)(2,1)S(1)}, bf16[32,1024]{1,0:T(8,128)(2,1)S(1)}, u32[]{:S(2)}, u32[]{:S(2)}) collective-permute-start(bf16[32,1024]{1,0:T(8,128)(2,1)S(1)} %get-tuple-element.90), channel_id=1, source_target_pairs={{0,5},{1,4},{2,7},{3,6},{4,1},{5,0},{6,3},{7,2},{8,13},{9,12},{10,... | collective-permute-start | bytes 196616 | tf_op jit(solution)/shard_map/ppermute | solution.py:255
  19.1 0.7 %collective-permute-start.9 = (bf16[32,1024]{1,0:T(8,128)(2,1)S(1)}, bf16[32,1024]{1,0:T(8,128)(2,1)S(1)}, u32[]{:S(2)}, u32[]{:S(2)}) collective-permute-start(bf16[32,1024]{1,0:T(8,128)(2,1)S(1)} %get-tuple-element.91), channel_id=1, source_target_pairs={{0,12},{1,13},{2,14},{3,15},{4,8},{5,9},{6,10},{7,11},{8,4},{9,5},... | collective-permute-start | bytes 196616 | tf_op jit(solution)/shard_map/ppermute | solution.py:255
  19.7 0.4 %collective-permute-start.10 = (bf16[128,1024]{1,0:T(8,128)(2,1)S(1)}, bf16[128,1024]{1,0:T(8,128)(2,1)S(1)}, u32[]{:S(2)}, u32[]{:S(2)}) collective-permute-start(bf16[128,1024]{1,0:T(8,128)(2,1)S(1)} %pad_maximum_fusion.kv_ref.k1_ref), channel_id=1, source_target_pairs={{4,0},{5,1},{6,2},{7,3},{0,4},{1,5},{2,6},{3,7},{12,8},{13,9},{14,... | collective-permute-start | bytes 786440 | tf_op jit(solution)/shard_map/ppermute | solution.py:251
  20.2 1.2 %response_grads.1 = (bf16[128,512]{1,0:T(8,128)(2,1)}, bf16[128,512]{1,0:T(8,128)(2,1)}) custom-call(bf16[128,2560]{1,0:T(8,128)(2,1)S(1)} %get-tuple-element.66.q_ref, bf16[128,2560]{1,0:T(8,128)(2,1)S(1)} %get-tuple-element.76.do_ref, bf16[4,128,640]{2,1,0:T(8,128)(2,1)S(1)} %get-tuple-element.93.p_ref, ...), custom_call_target="tpu_custom_call" | custom-call | flops 6710886400 | bytes 2621440 | tf_op jit(solution)/shard_map/response_grads/pallas_call | solution.py:221
  21.4 0.0 collective-permute-done.10.kv_ref.k2_ref
  21.4 0.6 %other_scores.1.ds2_ref = bf16[4,128,640]{2,1,0:T(8,128)(2,1)S(1)} custom-call(bf16[128,2560]{1,0:T(8,128)(2,1)S(1)} %get-tuple-element.66.q_ref, bf16[128,2560]{1,0:T(8,128)(2,1)S(1)} %get-tuple-element.76.do_ref, f32[8,768]{1,0:T(8,128)S(1)} %get-tuple-element.77.rows_ref, bf16[128,1024]{1,0:T(8,128)(2,1)S(1)} %collective-permute-done.10.kv_ref.k2_ref), custom_call_target="tpu_custom_call" | custom-call | flops 167772160 | bytes 1597440 | tf_op jit(solution)/shard_map/other_scores/pallas_call | solution.py:221
  22.0 0.0 collective-permute-done.7
  22.0 0.9 %collective-permute-done.8 = bf16[32,1024]{1,0:T(8,128)(2,1)S(1)} collective-permute-done((bf16[32,1024]{1,0:T(8,128)(2,1)S(1)}, bf16[32,1024]{1,0:T(8,128)(2,1)S(1)}, u32[]{:S(2)}, u32[]{:S(2)}) %collective-permute-start.8) | collective-permute-done | bytes 65568 | tf_op jit(solution)/shard_map/ppermute | solution.py:255
  22.9 0.6 %collective-permute-done.9 = bf16[32,1024]{1,0:T(8,128)(2,1)S(1)} collective-permute-done((bf16[32,1024]{1,0:T(8,128)(2,1)S(1)}, bf16[32,1024]{1,0:T(8,128)(2,1)S(1)}, u32[]{:S(2)}, u32[]{:S(2)}) %collective-permute-start.9) | collective-permute-done | bytes 65568 | tf_op jit(solution)/shard_map/ppermute | solution.py:255
  23.6 2.2 %collective-permute-start.11 = (bf16[16,1024]{1,0:T(8,128)(2,1)S(1)}, bf16[16,1024]{1,0:T(8,128)(2,1)S(1)}, u32[]{:S(2)}, u32[]{:S(2)}) collective-permute-start(bf16[16,1024]{1,0:T(8,128)(2,1)S(1)} %convert_add_fusion.1), channel_id=1, source_target_pairs={{0,6},{1,7},{2,4},{3,5},{4,2},{5,3},{6,0},{7,1},{8,14},{9,15},{10,... | collective-permute-start | bytes 98312 | tf_op jit(solution)/shard_map/ppermute | solution.py:255
  25.7 1.6 %query_grads.1 = bf16[128,2560]{1,0:T(8,128)(2,1)} custom-call(bf16[4,128,640]{2,1,0:T(8,128)(2,1)S(1)} %get-tuple-element.94.ds_ref.ds0_ref, bf16[4,128,640]{2,1,0:T(8,128)(2,1)S(1)} %get-tuple-element.106.ds1_ref, bf16[4,128,640]{2,1,0:T(8,128)(2,1)S(1)} %other_scores.1.ds2_ref, bf16[128,512]{1,0:T(8,128)(2,1)S(1)} %get-tuple-element.67.k_ref.k0_ref, ...), custom_call_target="tpu_custom_call" | custom-call | flops 251658240 | bytes 2621440 | tf_op jit(solution)/shard_map/query_grads/pallas_call | solution.py:221
  27.3 0.6 %collective-permute-done.11 = bf16[16,1024]{1,0:T(8,128)(2,1)S(1)} collective-permute-done((bf16[16,1024]{1,0:T(8,128)(2,1)S(1)}, bf16[16,1024]{1,0:T(8,128)(2,1)S(1)}, u32[]{:S(2)}, u32[]{:S(2)}) %collective-permute-start.11) | collective-permute-done | bytes 32800 | tf_op jit(solution)/shard_map/ppermute | solution.py:255
  27.9 0.6 %slice_bitcast_fusion = (f32[1,16,512]{2,1,0:T(8,128)}, f32[1,16,512]{2,1,0:T(8,128)}) fusion(f32[16,1024]{1,0:T(8,128)S(1)} %convert_add_fusion), kind=kLoop, calls=%fused_computation.5 | loop fusion | bytes 131072 | tf_op jit(solution)/shard_map/broadcast_in_dim | solution.py:398
  (5 shorter events, 0.1 us)
Async XLA Ops:
  0.6 10.4 %copy-start = (bf16[1,128,2560]{2,1,0:T(8,128)(2,1)S(1)}, bf16[1,128,2560]{2,1,0:T(8,128)(2,1)}, u32[]{:S(2)}) copy-start(bf16[1,128,2560]{2,1,0:T(8,128)(2,1)} %param.13) | copy-start | bytes 1966084
  1.4 5.9 %collective-permute-start = (bf16[16,1024]{1,0:T(8,128)(2,1)S(1)}, bf16[16,1024]{1,0:T(8,128)(2,1)S(1)}, u32[]{:S(2)}, u32[]{:S(2)}) collective-permute-start(bf16[16,1024]{1,0:T(8,128)(2,1)S(1)} %pad_maximum_fusion.2), channel_id=1, source_target_pairs={{6,0},{7,1},{4,2},{5,3},{2,4},{3,5},{0,6},{1,7},{14,8},{15,9},{12,... | collective-permute-start | bytes 98312 | tf_op jit(solution)/shard_map/ppermute | solution.py:251
  7.4 6.3 %collective-permute-start.3 = (bf16[32,1024]{1,0:T(8,128)(2,1)S(1)}, bf16[32,1024]{1,0:T(8,128)(2,1)S(1)}, u32[]{:S(2)}, u32[]{:S(2)}) collective-permute-start(bf16[32,1024]{1,0:T(8,128)(2,1)S(1)} %pad_maximum_fusion.1), channel_id=1, source_target_pairs={{13,0},{12,1},{15,2},{14,3},{9,4},{8,5},{11,6},{10,7},{5,8},{4,9},... | collective-permute-start | bytes 196616 | tf_op jit(solution)/shard_map/ppermute | solution.py:251
  10.2 4.4 %collective-permute-start.2 = (bf16[32,1024]{1,0:T(8,128)(2,1)S(1)}, bf16[32,1024]{1,0:T(8,128)(2,1)S(1)}, u32[]{:S(2)}, u32[]{:S(2)}) collective-permute-start(bf16[32,1024]{1,0:T(8,128)(2,1)S(1)} %pad_maximum_fusion.1), channel_id=1, source_target_pairs={{5,0},{4,1},{7,2},{6,3},{1,4},{0,5},{3,6},{2,7},{13,8},{12,9},{15,... | collective-permute-start | bytes 196616 | tf_op jit(solution)/shard_map/ppermute | solution.py:251
  10.2 4.4 %collective-permute-start.1 = (bf16[32,1024]{1,0:T(8,128)(2,1)S(1)}, bf16[32,1024]{1,0:T(8,128)(2,1)S(1)}, u32[]{:S(2)}, u32[]{:S(2)}) collective-permute-start(bf16[32,1024]{1,0:T(8,128)(2,1)S(1)} %pad_maximum_fusion.1), channel_id=1, source_target_pairs={{12,0},{13,1},{14,2},{15,3},{8,4},{9,5},{10,6},{11,7},{4,8},{5,9},... | collective-permute-start | bytes 196616 | tf_op jit(solution)/shard_map/ppermute | solution.py:251
  10.9 4.7 %collective-permute-start.5 = (bf16[128,2560]{1,0:T(8,128)(2,1)}, bf16[128,2560]{1,0:T(8,128)(2,1)S(1)}, u32[]{:S(2)}, u32[]{:S(2)}) collective-permute-start(bf16[128,2560]{1,0:T(8,128)(2,1)} %bitcast.19), channel_id=1, source_target_pairs={{4,0},{5,1},{6,2},{7,3},{0,4},{1,5},{2,6},{3,7},{12,8},{13,9},{14,... | collective-permute-start | bytes 1966088 | tf_op jit(solution)/shard_map/ppermute | solution.py:251
  11.0 4.7 %collective-permute-start.6 = (bf16[128,2560]{1,0:T(8,128)(2,1)S(1)}, bf16[128,2560]{1,0:T(8,128)(2,1)S(1)}, u32[]{:S(2)}, u32[]{:S(2)}) collective-permute-start(bf16[128,2560]{1,0:T(8,128)(2,1)S(1)} %bitcast.17), channel_id=1, source_target_pairs={{4,0},{5,1},{6,2},{7,3},{0,4},{1,5},{2,6},{3,7},{12,8},{13,9},{14,... | collective-permute-start | bytes 1966088 | tf_op jit(solution)/shard_map/ppermute | solution.py:251
  13.7 2.0 %collective-permute-start.4 = (f32[8,768]{1,0:T(8,128)S(1)}, f32[8,768]{1,0:T(8,128)S(1)}, u32[]{:S(2)}, u32[]{:S(2)}) collective-permute-start(f32[8,768]{1,0:T(8,128)S(1)} %get-tuple-element.77.rows_ref), channel_id=1, source_target_pairs={{4,0},{5,1},{6,2},{7,3},{0,4},{1,5},{2,6},{3,7},{12,8},{13,9},{14,... | collective-permute-start | bytes 73736 | tf_op jit(solution)/shard_map/ppermute | solution.py:251
  16.8 5.2 %collective-permute-start.7 = (bf16[32,1024]{1,0:T(8,128)(2,1)S(1)}, bf16[32,1024]{1,0:T(8,128)(2,1)S(1)}, u32[]{:S(2)}, u32[]{:S(2)}) collective-permute-start(bf16[32,1024]{1,0:T(8,128)(2,1)S(1)} %get-tuple-element.89), channel_id=1, source_target_pairs={{0,13},{1,12},{2,15},{3,14},{4,9},{5,8},{6,11},{7,10},{8,5},{9,4},... | collective-permute-start | bytes 196616 | tf_op jit(solution)/shard_map/ppermute | solution.py:255
  18.6 4.3 %collective-permute-start.8 = (bf16[32,1024]{1,0:T(8,128)(2,1)S(1)}, bf16[32,1024]{1,0:T(8,128)(2,1)S(1)}, u32[]{:S(2)}, u32[]{:S(2)}) collective-permute-start(bf16[32,1024]{1,0:T(8,128)(2,1)S(1)} %get-tuple-element.90), channel_id=1, source_target_pairs={{0,5},{1,4},{2,7},{3,6},{4,1},{5,0},{6,3},{7,2},{8,13},{9,12},{10,... | collective-permute-start | bytes 196616 | tf_op jit(solution)/shard_map/ppermute | solution.py:255
  19.1 4.4 %collective-permute-start.9 = (bf16[32,1024]{1,0:T(8,128)(2,1)S(1)}, bf16[32,1024]{1,0:T(8,128)(2,1)S(1)}, u32[]{:S(2)}, u32[]{:S(2)}) collective-permute-start(bf16[32,1024]{1,0:T(8,128)(2,1)S(1)} %get-tuple-element.91), channel_id=1, source_target_pairs={{0,12},{1,13},{2,14},{3,15},{4,8},{5,9},{6,10},{7,11},{8,4},{9,5},... | collective-permute-start | bytes 196616 | tf_op jit(solution)/shard_map/ppermute | solution.py:255
  19.7 1.6 %collective-permute-start.10 = (bf16[128,1024]{1,0:T(8,128)(2,1)S(1)}, bf16[128,1024]{1,0:T(8,128)(2,1)S(1)}, u32[]{:S(2)}, u32[]{:S(2)}) collective-permute-start(bf16[128,1024]{1,0:T(8,128)(2,1)S(1)} %pad_maximum_fusion.kv_ref.k1_ref), channel_id=1, source_target_pairs={{4,0},{5,1},{6,2},{7,3},{0,4},{1,5},{2,6},{3,7},{12,8},{13,9},{14,... | collective-permute-start | bytes 786440 | tf_op jit(solution)/shard_map/ppermute | solution.py:251
  23.6 4.4 %collective-permute-start.11 = (bf16[16,1024]{1,0:T(8,128)(2,1)S(1)}, bf16[16,1024]{1,0:T(8,128)(2,1)S(1)}, u32[]{:S(2)}, u32[]{:S(2)}) collective-permute-start(bf16[16,1024]{1,0:T(8,128)(2,1)S(1)} %convert_add_fusion.1), channel_id=1, source_target_pairs={{0,6},{1,7},{2,4},{3,5},{4,2},{5,3},{6,0},{7,1},{8,14},{9,15},{10,... | collective-permute-start | bytes 98312 | tf_op jit(solution)/shard_map/ppermute | solution.py:255

commit v13 on v11

--- a/solution.py
+++ b/solution.py
@@ -133,11 +133,11 @@
             dot(kv_ref[:, head_cols(HK + g)], head_rows(do_ref, g), NT),
         )
 
-    ahead = [products(g) for g in range(2)]
+    ahead = [products(g) for g in range(3)]
     last = None
     for g in range(HK):
-        if g + 2 < HK:
-            ahead.append(products(g + 2))
+        if g + 3 < HK:
+            ahead.append(products(g + 3))
         scores, dprob = ahead[g]
         lse = eight(rows_ref[g : g + 1, :nq])
         delta = eight(rows_ref[HK + g : HK + g + 1, :nq])

time: 28.7 us -> 28.7 us (level)
  no operation moved by 1% of the time
where the time goes in v13:
time: 28.7 us; the launch traced here: 28.5 us
  starting transfers between devices  13.7 us (48%)
  Pallas kernels  8.44 us (29%)
  waiting for transfers between devices  2.75 us (10%)
  between operations  2.04 us (7%)
  other arithmetic  0.88 us (3%)
  local copies, waits for them, and re-layouts  0.64 us (2%)
    pallas_call x6, Pallas kernels, call(): pl.pallas_call(kernel, name=name, out_shape=outs, in_specs=[SMEM] * len(s...  8.44 us
    ppermute x8, starting transfers between devices, fetch(): return lax.ppermute(array, ('dp', 'resp'), pairs(*step))  7.84 us
    ppermute x4, starting transfers between devices, give(): lax.ppermute(array, ('dp', 'resp'), [(i, j) for j, i in pairs(*step)])  5.87 us
    ppermute x4, waiting for transfers between devices, give(): lax.ppermute(array, ('dp', 'resp'), [(i, j) for j, i in pairs(*step)])  1.9 us
    ppermute x8, waiting for transfers between devices, fetch(): return lax.ppermute(array, ('dp', 'resp'), pairs(*step))  0.85 us
    concatenate x1, other arithmetic, shards(): jnp.concatenate([prompt_keys[0], prompt_values[0]], axis=1)  0.8 us
    broadcast_in_dim x1, local copies, waits for them, and re-layouts, shards(): total[None, :, width:]  0.63 us
  transfers between devices with their start and end apart: 12, of which 4 were waited for; matrix products, arithmetic and copies ran while one was open for 0% of the time, Pallas kernels for 30%

profile of v13, /device:TPU:0, one launch (start us, length us, event | category | flops | bytes accessed | tf_op | source)
XLA Modules:
  0.0 28.5 jit_solution(2452023500679858920)
XLA Ops:
  0.6 0.0 copy-start
  0.6 0.8 %pad_maximum_fusion.2 = bf16[16,1024]{1,0:T(8,128)(2,1)S(1)} fusion(bf16[16,512]{1,0:T(8,128)(2,1)} %bitcast.23, bf16[16,512]{1,0:T(8,128)(2,1)} %bitcast.24), kind=kLoop, calls=%fused_computation.7 | loop fusion | flops 65536 | bytes 65536 | tf_op jit(solution)/shard_map/concatenate | solution.py:286
  1.4 3.5 %collective-permute-start = (bf16[16,1024]{1,0:T(8,128)(2,1)S(1)}, bf16[16,1024]{1,0:T(8,128)(2,1)S(1)}, u32[]{:S(2)}, u32[]{:S(2)}) collective-permute-start(bf16[16,1024]{1,0:T(8,128)(2,1)S(1)} %pad_maximum_fusion.2), channel_id=1, source_target_pairs={{6,0},{7,1},{4,2},{5,3},{2,4},{3,5},{0,6},{1,7},{14,8},{15,9},{12,... | collective-permute-start | bytes 98312 | tf_op jit(solution)/shard_map/ppermute | solution.py:249
  6.2 1.1 %load.1 = (bf16[128,2560]{1,0:T(8,128)(2,1)S(1)}, bf16[128,512]{1,0:T(8,128)(2,1)S(1)}, f32[20,1,128]{2,1,0:T(1,128)S(1)}, s32[8,256]{1,0:T(8,128)S(1)}) custom-call(s32[1]{0:T(128)S(6)} %copy.15.len_ref, s32[1]{0:T(128)S(6)} %copy.16.seen_ref, bf16[128,2560]{1,0:T(8,128)(2,1)} %bitcast.18, bf16[128,512]{1,0:T(8,128)(2,1)} %bitcast.21, f32[20,1,128]{2,1,0:T(1,128)} %bitcast.25), custom_call_target="tpu_custom_call" | custom-call | bytes 796672 | tf_op jit(solution)/shard_map/load/pallas_call | solution.py:219
  7.4 0.0 collective-permute-done
  7.4 2.8 %collective-permute-start.1 = (bf16[32,1024]{1,0:T(8,128)(2,1)S(1)}, bf16[32,1024]{1,0:T(8,128)(2,1)S(1)}, u32[]{:S(2)}, u32[]{:S(2)}) collective-permute-start(bf16[32,1024]{1,0:T(8,128)(2,1)S(1)} %pad_maximum_fusion.1), channel_id=1, source_target_pairs={{13,0},{12,1},{15,2},{14,3},{9,4},{8,5},{11,6},{10,7},{5,8},{4,9},... | collective-permute-start | bytes 196616 | tf_op jit(solution)/shard_map/ppermute | solution.py:249
  10.2 0.0 collective-permute-start.2
  10.2 0.7 %collective-permute-start.3 = (bf16[32,1024]{1,0:T(8,128)(2,1)S(1)}, bf16[32,1024]{1,0:T(8,128)(2,1)S(1)}, u32[]{:S(2)}, u32[]{:S(2)}) collective-permute-start(bf16[32,1024]{1,0:T(8,128)(2,1)S(1)} %pad_maximum_fusion.1), channel_id=1, source_target_pairs={{12,0},{13,1},{14,2},{15,3},{8,4},{9,5},{10,6},{11,7},{4,8},{5,9},... | collective-permute-start | bytes 196616 | tf_op jit(solution)/shard_map/ppermute | solution.py:249
  10.9 0.1 collective-permute-start.5
  11.0 0.0 copy-done
  11.0 0.5 %collective-permute-start.6 = (bf16[128,2560]{1,0:T(8,128)(2,1)S(1)}, bf16[128,2560]{1,0:T(8,128)(2,1)S(1)}, u32[]{:S(2)}, u32[]{:S(2)}) collective-permute-start(bf16[128,2560]{1,0:T(8,128)(2,1)S(1)} %bitcast.17), channel_id=1, source_target_pairs={{4,0},{5,1},{6,2},{7,3},{0,4},{1,5},{2,6},{3,7},{12,8},{13,9},{14,... | collective-permute-start | bytes 1966088 | tf_op jit(solution)/shard_map/ppermute | solution.py:249
  11.5 2.2 %self_pairs.1 = (bf16[128,2560]{1,0:T(8,128)(2,1)S(1)}, bf16[4,128,640]{2,1,0:T(8,128)(2,1)S(1)}, bf16[4,128,640]{2,1,0:T(8,128)(2,1)S(1)}, f32[8,768]{1,0:T(8,128)S(1)}) custom-call(s32[8,256]{1,0:T(8,128)S(1)} %get-tuple-element.58.scalars_ref, bf16[128,2560]{1,0:T(8,128)(2,1)S(1)} %get-tuple-element.55.q_ref, ...), custom_call_target="tpu_custom_call" | custom-call | flops 209715200 | bytes 2246656 | tf_op jit(solution)/shard_map/self_pairs/pallas_call | solution.py:219
  13.6 0.0 collective-permute-done.1
  13.7 0.1 collective-permute-start.4
  13.8 0.8 %collective-permute-done.2 = bf16[32,1024]{1,0:T(8,128)(2,1)S(1)} collective-permute-done((bf16[32,1024]{1,0:T(8,128)(2,1)S(1)}, bf16[32,1024]{1,0:T(8,128)(2,1)S(1)}, u32[]{:S(2)}, u32[]{:S(2)}) %collective-permute-start.2) | collective-permute-done | bytes 65568 | tf_op jit(solution)/shard_map/ppermute | solution.py:249
  14.6 0.0 collective-permute-done.3
  14.6 0.2 collective-permute-start.10
  14.8 1.0 %own_pairs.1 = (bf16[4,128,640]{2,1,0:T(8,128)(2,1)S(1)}, f32[128,1024]{1,0:T(8,128)S(1)}) custom-call(bf16[128,2560]{1,0:T(8,128)(2,1)S(1)} %get-tuple-element.55.q_ref, bf16[128,2560]{1,0:T(8,128)(2,1)S(1)} %get-tuple-element.65.do_ref, f32[8,768]{1,0:T(8,128)S(1)} %get-tuple-element.66.rows_ref, bf16[128,1024]{1,0:T(8,128)(2,1)S(1)} %pad_maximum_fusion.kv_ref.k1_ref), custom_call_target="tpu_custom_call" | custom-call | flops 6710886400 | bytes 1597440 | tf_op jit(solution)/shard_map/own_pairs/pallas_call | solution.py:219
  15.8 0.0 collective-permute-done.4.rows_ref
  15.8 0.0 collective-permute-done.5.q_ref
  15.8 0.0 collective-permute-done.6.do_ref
  15.8 1.0 %other_pairs.1 = (f32[16,1024]{1,0:T(8,128)S(1)}, f32[16,1024]{1,0:T(8,128)S(1)}, bf16[32,1024]{1,0:T(8,128)(2,1)S(1)}, bf16[32,1024]{1,0:T(8,128)(2,1)S(1)}, bf16[32,1024]{1,0:T(8,128)(2,1)S(1)}) custom-call(bf16[128,2560]{1,0:T(8,128)(2,1)S(1)} %collective-permute-done.5.q_ref, bf16[128,2560]{1,0:T(8,128)(2,1)S(1)} %collective-permute-done.6.do_ref, ...), custom_call_target="tpu_custom_call" | custom-call | flops 335544320 | bytes 2121728 | tf_op jit(solution)/shard_map/other_pairs/pallas_call | solution.py:219
  16.8 1.9 %collective-permute-start.7 = (bf16[32,1024]{1,0:T(8,128)(2,1)S(1)}, bf16[32,1024]{1,0:T(8,128)(2,1)S(1)}, u32[]{:S(2)}, u32[]{:S(2)}) collective-permute-start(bf16[32,1024]{1,0:T(8,128)(2,1)S(1)} %get-tuple-element.76), channel_id=1, source_target_pairs={{0,13},{1,12},{2,15},{3,14},{4,9},{5,8},{6,11},{7,10},{8,5},{9,4},... | collective-permute-start | bytes 196616 | tf_op jit(solution)/shard_map/ppermute | solution.py:253
  18.7 0.5 %collective-permute-start.8 = (bf16[32,1024]{1,0:T(8,128)(2,1)S(1)}, bf16[32,1024]{1,0:T(8,128)(2,1)S(1)}, u32[]{:S(2)}, u32[]{:S(2)}) collective-permute-start(bf16[32,1024]{1,0:T(8,128)(2,1)S(1)} %get-tuple-element.77), channel_id=1, source_target_pairs={{0,5},{1,4},{2,7},{3,6},{4,1},{5,0},{6,3},{7,2},{8,13},{9,12},{10,... | collective-permute-start | bytes 196616 | tf_op jit(solution)/shard_map/ppermute | solution.py:253
  19.2 1.0 %collective-permute-start.9 = (bf16[32,1024]{1,0:T(8,128)(2,1)S(1)}, bf16[32,1024]{1,0:T(8,128)(2,1)S(1)}, u32[]{:S(2)}, u32[]{:S(2)}) collective-permute-start(bf16[32,1024]{1,0:T(8,128)(2,1)S(1)} %get-tuple-element.78), channel_id=1, source_target_pairs={{0,12},{1,13},{2,14},{3,15},{4,8},{5,9},{6,10},{7,11},{8,4},{9,5},... | collective-permute-start | bytes 196616 | tf_op jit(solution)/shard_map/ppermute | solution.py:253
  20.2 0.0 collective-permute-done.10.kv_ref.k2_ref
  20.2 1.6 %response_grads.1 = (bf16[128,512]{1,0:T(8,128)(2,1)}, bf16[128,512]{1,0:T(8,128)(2,1)}, bf16[4,128,640]{2,1,0:T(8,128)(2,1)S(1)}) custom-call(bf16[128,2560]{1,0:T(8,128)(2,1)S(1)} %get-tuple-element.55.q_ref, bf16[128,2560]{1,0:T(8,128)(2,1)S(1)} %get-tuple-element.65.do_ref, f32[8,768]{1,0:T(8,128)S(1)} %get-tuple-element.66.rows_ref, ...), custom_call_target="tpu_custom_call" | custom-call | flops 335544320 | bytes 2908160 | tf_op jit(solution)/shard_map/response_grads/pallas_call | solution.py:219
  21.8 0.0 collective-permute-done.7
  21.8 1.1 %collective-permute-done.8 = bf16[32,1024]{1,0:T(8,128)(2,1)S(1)} collective-permute-done((bf16[32,1024]{1,0:T(8,128)(2,1)S(1)}, bf16[32,1024]{1,0:T(8,128)(2,1)S(1)}, u32[]{:S(2)}, u32[]{:S(2)}) %collective-permute-start.8) | collective-permute-done | bytes 65568 | tf_op jit(solution)/shard_map/ppermute | solution.py:253
  22.9 0.6 %collective-permute-done.9 = bf16[32,1024]{1,0:T(8,128)(2,1)S(1)} collective-permute-done((bf16[32,1024]{1,0:T(8,128)(2,1)S(1)}, bf16[32,1024]{1,0:T(8,128)(2,1)S(1)}, u32[]{:S(2)}, u32[]{:S(2)}) %collective-permute-start.9) | collective-permute-done | bytes 65568 | tf_op jit(solution)/shard_map/ppermute | solution.py:253
  23.5 2.5 %collective-permute-start.11 = (bf16[16,1024]{1,0:T(8,128)(2,1)S(1)}, bf16[16,1024]{1,0:T(8,128)(2,1)S(1)}, u32[]{:S(2)}, u32[]{:S(2)}) collective-permute-start(bf16[16,1024]{1,0:T(8,128)(2,1)S(1)} %convert_add_fusion.1), channel_id=1, source_target_pairs={{0,6},{1,7},{2,4},{3,5},{4,2},{5,3},{6,0},{7,1},{8,14},{9,15},{10,... | collective-permute-start | bytes 98312 | tf_op jit(solution)/shard_map/ppermute | solution.py:253
  26.1 1.5 %query_grads.1 = bf16[128,2560]{1,0:T(8,128)(2,1)} custom-call(bf16[4,128,640]{2,1,0:T(8,128)(2,1)S(1)} %get-tuple-element.80.ds_ref.ds0_ref, bf16[4,128,640]{2,1,0:T(8,128)(2,1)S(1)} %get-tuple-element.90.ds1_ref, bf16[4,128,640]{2,1,0:T(8,128)(2,1)S(1)} %get-tuple-element.91.ds2_ref, bf16[128,512]{1,0:T(8,128)(2,1)S(1)} %get-tuple-element.59.k_ref.k0_ref, ...), custom_call_target="tpu_custom_call" | custom-call | flops 251658240 | bytes 2621440 | tf_op jit(solution)/shard_map/query_grads/pallas_call | solution.py:219
  27.6 0.2 collective-permute-done.11
  27.8 0.6 %slice_bitcast_fusion = (f32[1,16,512]{2,1,0:T(8,128)}, f32[1,16,512]{2,1,0:T(8,128)}) fusion(f32[16,1024]{1,0:T(8,128)S(1)} %convert_add_fusion), kind=kLoop, calls=%fused_computation.5 | loop fusion | bytes 131072 | tf_op jit(solution)/shard_map/broadcast_in_dim | solution.py:387
  (5 shorter events, 0.1 us)
Async XLA Ops:
  0.6 10.4 %copy-start = (bf16[1,128,2560]{2,1,0:T(8,128)(2,1)S(1)}, bf16[1,128,2560]{2,1,0:T(8,128)(2,1)}, u32[]{:S(2)}) copy-start(bf16[1,128,2560]{2,1,0:T(8,128)(2,1)} %param.13) | copy-start | bytes 1966084
  1.4 5.9 %collective-permute-start = (bf16[16,1024]{1,0:T(8,128)(2,1)S(1)}, bf16[16,1024]{1,0:T(8,128)(2,1)S(1)}, u32[]{:S(2)}, u32[]{:S(2)}) collective-permute-start(bf16[16,1024]{1,0:T(8,128)(2,1)S(1)} %pad_maximum_fusion.2), channel_id=1, source_target_pairs={{6,0},{7,1},{4,2},{5,3},{2,4},{3,5},{0,6},{1,7},{14,8},{15,9},{12,... | collective-permute-start | bytes 98312 | tf_op jit(solution)/shard_map/ppermute | solution.py:249
  7.4 6.3 %collective-permute-start.1 = (bf16[32,1024]{1,0:T(8,128)(2,1)S(1)}, bf16[32,1024]{1,0:T(8,128)(2,1)S(1)}, u32[]{:S(2)}, u32[]{:S(2)}) collective-permute-start(bf16[32,1024]{1,0:T(8,128)(2,1)S(1)} %pad_maximum_fusion.1), channel_id=1, source_target_pairs={{13,0},{12,1},{15,2},{14,3},{9,4},{8,5},{11,6},{10,7},{5,8},{4,9},... | collective-permute-start | bytes 196616 | tf_op jit(solution)/shard_map/ppermute | solution.py:249
  10.2 4.4 %collective-permute-start.2 = (bf16[32,1024]{1,0:T(8,128)(2,1)S(1)}, bf16[32,1024]{1,0:T(8,128)(2,1)S(1)}, u32[]{:S(2)}, u32[]{:S(2)}) collective-permute-start(bf16[32,1024]{1,0:T(8,128)(2,1)S(1)} %pad_maximum_fusion.1), channel_id=1, source_target_pairs={{5,0},{4,1},{7,2},{6,3},{1,4},{0,5},{3,6},{2,7},{13,8},{12,9},{15,... | collective-permute-start | bytes 196616 | tf_op jit(solution)/shard_map/ppermute | solution.py:249
  10.2 4.4 %collective-permute-start.3 = (bf16[32,1024]{1,0:T(8,128)(2,1)S(1)}, bf16[32,1024]{1,0:T(8,128)(2,1)S(1)}, u32[]{:S(2)}, u32[]{:S(2)}) collective-permute-start(bf16[32,1024]{1,0:T(8,128)(2,1)S(1)} %pad_maximum_fusion.1), channel_id=1, source_target_pairs={{12,0},{13,1},{14,2},{15,3},{8,4},{9,5},{10,6},{11,7},{4,8},{5,9},... | collective-permute-start | bytes 196616 | tf_op jit(solution)/shard_map/ppermute | solution.py:249
  10.9 4.8 %collective-permute-start.5 = (bf16[128,2560]{1,0:T(8,128)(2,1)}, bf16[128,2560]{1,0:T(8,128)(2,1)S(1)}, u32[]{:S(2)}, u32[]{:S(2)}) collective-permute-start(bf16[128,2560]{1,0:T(8,128)(2,1)} %bitcast.19), channel_id=1, source_target_pairs={{4,0},{5,1},{6,2},{7,3},{0,4},{1,5},{2,6},{3,7},{12,8},{13,9},{14,... | collective-permute-start | bytes 1966088 | tf_op jit(solution)/shard_map/ppermute | solution.py:249
  11.0 4.8 %collective-permute-start.6 = (bf16[128,2560]{1,0:T(8,128)(2,1)S(1)}, bf16[128,2560]{1,0:T(8,128)(2,1)S(1)}, u32[]{:S(2)}, u32[]{:S(2)}) collective-permute-start(bf16[128,2560]{1,0:T(8,128)(2,1)S(1)} %bitcast.17), channel_id=1, source_target_pairs={{4,0},{5,1},{6,2},{7,3},{0,4},{1,5},{2,6},{3,7},{12,8},{13,9},{14,... | collective-permute-start | bytes 1966088 | tf_op jit(solution)/shard_map/ppermute | solution.py:249
  13.7 2.1 %collective-permute-start.4 = (f32[8,768]{1,0:T(8,128)S(1)}, f32[8,768]{1,0:T(8,128)S(1)}, u32[]{:S(2)}, u32[]{:S(2)}) collective-permute-start(f32[8,768]{1,0:T(8,128)S(1)} %get-tuple-element.66.rows_ref), channel_id=1, source_target_pairs={{4,0},{5,1},{6,2},{7,3},{0,4},{1,5},{2,6},{3,7},{12,8},{13,9},{14,... | collective-permute-start | bytes 73736 | tf_op jit(solution)/shard_map/ppermute | solution.py:249
  14.6 5.5 %collective-permute-start.10 = (bf16[128,1024]{1,0:T(8,128)(2,1)S(1)}, bf16[128,1024]{1,0:T(8,128)(2,1)S(1)}, u32[]{:S(2)}, u32[]{:S(2)}) collective-permute-start(bf16[128,1024]{1,0:T(8,128)(2,1)S(1)} %pad_maximum_fusion.kv_ref.k1_ref), channel_id=1, source_target_pairs={{4,0},{5,1},{6,2},{7,3},{0,4},{1,5},{2,6},{3,7},{12,8},{13,9},{14,... | collective-permute-start | bytes 786440 | tf_op jit(solution)/shard_map/ppermute | solution.py:249
  16.8 4.9 %collective-permute-start.7 = (bf16[32,1024]{1,0:T(8,128)(2,1)S(1)}, bf16[32,1024]{1,0:T(8,128)(2,1)S(1)}, u32[]{:S(2)}, u32[]{:S(2)}) collective-permute-start(bf16[32,1024]{1,0:T(8,128)(2,1)S(1)} %get-tuple-element.76), channel_id=1, source_target_pairs={{0,13},{1,12},{2,15},{3,14},{4,9},{5,8},{6,11},{7,10},{8,5},{9,4},... | collective-permute-start | bytes 196616 | tf_op jit(solution)/shard_map/ppermute | solution.py:253
  18.7 4.2 %collective-permute-start.8 = (bf16[32,1024]{1,0:T(8,128)(2,1)S(1)}, bf16[32,1024]{1,0:T(8,128)(2,1)S(1)}, u32[]{:S(2)}, u32[]{:S(2)}) collective-permute-start(bf16[32,1024]{1,0:T(8,128)(2,1)S(1)} %get-tuple-element.77), channel_id=1, source_target_pairs={{0,5},{1,4},{2,7},{3,6},{4,1},{5,0},{6,3},{7,2},{8,13},{9,12},{10,... | collective-permute-start | bytes 196616 | tf_op jit(solution)/shard_map/ppermute | solution.py:253
  19.2 4.3 %collective-permute-start.9 = (bf16[32,1024]{1,0:T(8,128)(2,1)S(1)}, bf16[32,1024]{1,0:T(8,128)(2,1)S(1)}, u32[]{:S(2)}, u32[]{:S(2)}) collective-permute-start(bf16[32,1024]{1,0:T(8,128)(2,1)S(1)} %get-tuple-element.78), channel_id=1, source_target_pairs={{0,12},{1,13},{2,14},{3,15},{4,8},{5,9},{6,10},{7,11},{8,4},{9,5},... | collective-permute-start | bytes 196616 | tf_op jit(solution)/shard_map/ppermute | solution.py:253
  23.5 4.3 %collective-permute-start.11 = (bf16[16,1024]{1,0:T(8,128)(2,1)S(1)}, bf16[16,1024]{1,0:T(8,128)(2,1)S(1)}, u32[]{:S(2)}, u32[]{:S(2)}) collective-permute-start(bf16[16,1024]{1,0:T(8,128)(2,1)S(1)} %convert_add_fusion.1), channel_id=1, source_target_pairs={{0,6},{1,7},{2,4},{3,5},{4,2},{5,3},{6,0},{7,1},{8,14},{9,15},{10,... | collective-permute-start | bytes 98312 | tf_op jit(solution)/shard_map/ppermute | solution.py:253

commit v14 on v13

--- a/solution.py
+++ b/solution.py
@@ -133,11 +133,9 @@
             dot(kv_ref[:, head_cols(HK + g)], head_rows(do_ref, g), NT),
         )
 
-    ahead = [products(g) for g in range(3)]
+    ahead = [products(g) for g in range(HK)]
     last = None
     for g in range(HK):
-        if g + 3 < HK:
-            ahead.append(products(g + 3))
         scores, dprob = ahead[g]
         lse = eight(rows_ref[g : g + 1, :nq])
         delta = eight(rows_ref[HK + g : HK + g + 1, :nq])

time: 28.7 us -> 28.7 us (level)
  no operation moved by 1% of the time
where the time goes in v14:
time: 28.7 us; the launch traced here: 28.5 us
  starting transfers between devices  13.7 us (48%)
  Pallas kernels  8.44 us (29%)
  waiting for transfers between devices  2.75 us (10%)
  between operations  2.04 us (7%)
  other arithmetic  0.88 us (3%)
  local copies, waits for them, and re-layouts  0.64 us (2%)
    pallas_call x6, Pallas kernels, call(): pl.pallas_call(kernel, name=name, out_shape=outs, in_specs=[SMEM] * len(s...  8.44 us
    ppermute x8, starting transfers between devices, fetch(): return lax.ppermute(array, ('dp', 'resp'), pairs(*step))  7.84 us
    ppermute x4, starting transfers between devices, give(): lax.ppermute(array, ('dp', 'resp'), [(i, j) for j, i in pairs(*step)])  5.87 us
    ppermute x4, waiting for transfers between devices, give(): lax.ppermute(array, ('dp', 'resp'), [(i, j) for j, i in pairs(*step)])  1.9 us
    ppermute x8, waiting for transfers between devices, fetch(): return lax.ppermute(array, ('dp', 'resp'), pairs(*step))  0.85 us
    concatenate x1, other arithmetic, shards(): jnp.concatenate([prompt_keys[0], prompt_values[0]], axis=1)  0.8 us
    broadcast_in_dim x1, local copies, waits for them, and re-layouts, shards(): total[None, :, width:]  0.63 us
  transfers between devices with their start and end apart: 12, of which 4 were waited for; matrix products, arithmetic and copies ran while one was open for 0% of the time, Pallas kernels for 30%

profile of v14, /device:TPU:0, one launch (start us, length us, event | category | flops | bytes accessed | tf_op | source)
XLA Modules:
  0.0 28.5 jit_solution(2452023500679858920)
XLA Ops:
  0.6 0.0 copy-start
  0.6 0.8 %pad_maximum_fusion.2 = bf16[16,1024]{1,0:T(8,128)(2,1)S(1)} fusion(bf16[16,512]{1,0:T(8,128)(2,1)} %bitcast.23, bf16[16,512]{1,0:T(8,128)(2,1)} %bitcast.24), kind=kLoop, calls=%fused_computation.7 | loop fusion | flops 65536 | bytes 65536 | tf_op jit(solution)/shard_map/concatenate | solution.py:284
  1.4 3.5 %collective-permute-start = (bf16[16,1024]{1,0:T(8,128)(2,1)S(1)}, bf16[16,1024]{1,0:T(8,128)(2,1)S(1)}, u32[]{:S(2)}, u32[]{:S(2)}) collective-permute-start(bf16[16,1024]{1,0:T(8,128)(2,1)S(1)} %pad_maximum_fusion.2), channel_id=1, source_target_pairs={{6,0},{7,1},{4,2},{5,3},{2,4},{3,5},{0,6},{1,7},{14,8},{15,9},{12,... | collective-permute-start | bytes 98312 | tf_op jit(solution)/shard_map/ppermute | solution.py:247
  6.2 1.1 %load.1 = (bf16[128,2560]{1,0:T(8,128)(2,1)S(1)}, bf16[128,512]{1,0:T(8,128)(2,1)S(1)}, f32[20,1,128]{2,1,0:T(1,128)S(1)}, s32[8,256]{1,0:T(8,128)S(1)}) custom-call(s32[1]{0:T(128)S(6)} %copy.15.len_ref, s32[1]{0:T(128)S(6)} %copy.16.seen_ref, bf16[128,2560]{1,0:T(8,128)(2,1)} %bitcast.18, bf16[128,512]{1,0:T(8,128)(2,1)} %bitcast.21, f32[20,1,128]{2,1,0:T(1,128)} %bitcast.25), custom_call_target="tpu_custom_call" | custom-call | bytes 796672 | tf_op jit(solution)/shard_map/load/pallas_call | solution.py:217
  7.4 0.0 collective-permute-done
  7.4 2.8 %collective-permute-start.1 = (bf16[32,1024]{1,0:T(8,128)(2,1)S(1)}, bf16[32,1024]{1,0:T(8,128)(2,1)S(1)}, u32[]{:S(2)}, u32[]{:S(2)}) collective-permute-start(bf16[32,1024]{1,0:T(8,128)(2,1)S(1)} %pad_maximum_fusion.1), channel_id=1, source_target_pairs={{13,0},{12,1},{15,2},{14,3},{9,4},{8,5},{11,6},{10,7},{5,8},{4,9},... | collective-permute-start | bytes 196616 | tf_op jit(solution)/shard_map/ppermute | solution.py:247
  10.2 0.0 collective-permute-start.2
  10.2 0.7 %collective-permute-start.3 = (bf16[32,1024]{1,0:T(8,128)(2,1)S(1)}, bf16[32,1024]{1,0:T(8,128)(2,1)S(1)}, u32[]{:S(2)}, u32[]{:S(2)}) collective-permute-start(bf16[32,1024]{1,0:T(8,128)(2,1)S(1)} %pad_maximum_fusion.1), channel_id=1, source_target_pairs={{12,0},{13,1},{14,2},{15,3},{8,4},{9,5},{10,6},{11,7},{4,8},{5,9},... | collective-permute-start | bytes 196616 | tf_op jit(solution)/shard_map/ppermute | solution.py:247
  10.9 0.1 collective-permute-start.5
  11.0 0.0 copy-done
  11.0 0.5 %collective-permute-start.6 = (bf16[128,2560]{1,0:T(8,128)(2,1)S(1)}, bf16[128,2560]{1,0:T(8,128)(2,1)S(1)}, u32[]{:S(2)}, u32[]{:S(2)}) collective-permute-start(bf16[128,2560]{1,0:T(8,128)(2,1)S(1)} %bitcast.17), channel_id=1, source_target_pairs={{4,0},{5,1},{6,2},{7,3},{0,4},{1,5},{2,6},{3,7},{12,8},{13,9},{14,... | collective-permute-start | bytes 1966088 | tf_op jit(solution)/shard_map/ppermute | solution.py:247
  11.5 2.2 %self_pairs.1 = (bf16[128,2560]{1,0:T(8,128)(2,1)S(1)}, bf16[4,128,640]{2,1,0:T(8,128)(2,1)S(1)}, bf16[4,128,640]{2,1,0:T(8,128)(2,1)S(1)}, f32[8,768]{1,0:T(8,128)S(1)}) custom-call(s32[8,256]{1,0:T(8,128)S(1)} %get-tuple-element.58.scalars_ref, bf16[128,2560]{1,0:T(8,128)(2,1)S(1)} %get-tuple-element.55.q_ref, ...), custom_call_target="tpu_custom_call" | custom-call | flops 209715200 | bytes 2246656 | tf_op jit(solution)/shard_map/self_pairs/pallas_call | solution.py:217
  13.6 0.0 collective-permute-done.1
  13.7 0.1 collective-permute-start.4
  13.8 0.8 %collective-permute-done.2 = bf16[32,1024]{1,0:T(8,128)(2,1)S(1)} collective-permute-done((bf16[32,1024]{1,0:T(8,128)(2,1)S(1)}, bf16[32,1024]{1,0:T(8,128)(2,1)S(1)}, u32[]{:S(2)}, u32[]{:S(2)}) %collective-permute-start.2) | collective-permute-done | bytes 65568 | tf_op jit(solution)/shard_map/ppermute | solution.py:247
  14.6 0.0 collective-permute-done.3
  14.6 0.2 collective-permute-start.10
  14.8 1.0 %own_pairs.1 = (bf16[4,128,640]{2,1,0:T(8,128)(2,1)S(1)}, f32[128,1024]{1,0:T(8,128)S(1)}) custom-call(bf16[128,2560]{1,0:T(8,128)(2,1)S(1)} %get-tuple-element.55.q_ref, bf16[128,2560]{1,0:T(8,128)(2,1)S(1)} %get-tuple-element.65.do_ref, f32[8,768]{1,0:T(8,128)S(1)} %get-tuple-element.66.rows_ref, bf16[128,1024]{1,0:T(8,128)(2,1)S(1)} %pad_maximum_fusion.kv_ref.k1_ref), custom_call_target="tpu_custom_call" | custom-call | flops 6710886400 | bytes 1597440 | tf_op jit(solution)/shard_map/own_pairs/pallas_call | solution.py:217
  15.8 0.0 collective-permute-done.4.rows_ref
  15.8 0.0 collective-permute-done.5.q_ref
  15.8 0.0 collective-permute-done.6.do_ref
  15.8 1.0 %other_pairs.1 = (f32[16,1024]{1,0:T(8,128)S(1)}, f32[16,1024]{1,0:T(8,128)S(1)}, bf16[32,1024]{1,0:T(8,128)(2,1)S(1)}, bf16[32,1024]{1,0:T(8,128)(2,1)S(1)}, bf16[32,1024]{1,0:T(8,128)(2,1)S(1)}) custom-call(bf16[128,2560]{1,0:T(8,128)(2,1)S(1)} %collective-permute-done.5.q_ref, bf16[128,2560]{1,0:T(8,128)(2,1)S(1)} %collective-permute-done.6.do_ref, ...), custom_call_target="tpu_custom_call" | custom-call | flops 335544320 | bytes 2121728 | tf_op jit(solution)/shard_map/other_pairs/pallas_call | solution.py:217
  16.8 1.9 %collective-permute-start.7 = (bf16[32,1024]{1,0:T(8,128)(2,1)S(1)}, bf16[32,1024]{1,0:T(8,128)(2,1)S(1)}, u32[]{:S(2)}, u32[]{:S(2)}) collective-permute-start(bf16[32,1024]{1,0:T(8,128)(2,1)S(1)} %get-tuple-element.76), channel_id=1, source_target_pairs={{0,13},{1,12},{2,15},{3,14},{4,9},{5,8},{6,11},{7,10},{8,5},{9,4},... | collective-permute-start | bytes 196616 | tf_op jit(solution)/shard_map/ppermute | solution.py:251
  18.7 0.5 %collective-permute-start.8 = (bf16[32,1024]{1,0:T(8,128)(2,1)S(1)}, bf16[32,1024]{1,0:T(8,128)(2,1)S(1)}, u32[]{:S(2)}, u32[]{:S(2)}) collective-permute-start(bf16[32,1024]{1,0:T(8,128)(2,1)S(1)} %get-tuple-element.77), channel_id=1, source_target_pairs={{0,5},{1,4},{2,7},{3,6},{4,1},{5,0},{6,3},{7,2},{8,13},{9,12},{10,... | collective-permute-start | bytes 196616 | tf_op jit(solution)/shard_map/ppermute | solution.py:251
  19.2 1.0 %collective-permute-start.9 = (bf16[32,1024]{1,0:T(8,128)(2,1)S(1)}, bf16[32,1024]{1,0:T(8,128)(2,1)S(1)}, u32[]{:S(2)}, u32[]{:S(2)}) collective-permute-start(bf16[32,1024]{1,0:T(8,128)(2,1)S(1)} %get-tuple-element.78), channel_id=1, source_target_pairs={{0,12},{1,13},{2,14},{3,15},{4,8},{5,9},{6,10},{7,11},{8,4},{9,5},... | collective-permute-start | bytes 196616 | tf_op jit(solution)/shard_map/ppermute | solution.py:251
  20.2 0.0 collective-permute-done.10.kv_ref.k2_ref
  20.2 1.6 %response_grads.1 = (bf16[128,512]{1,0:T(8,128)(2,1)}, bf16[128,512]{1,0:T(8,128)(2,1)}, bf16[4,128,640]{2,1,0:T(8,128)(2,1)S(1)}) custom-call(bf16[128,2560]{1,0:T(8,128)(2,1)S(1)} %get-tuple-element.55.q_ref, bf16[128,2560]{1,0:T(8,128)(2,1)S(1)} %get-tuple-element.65.do_ref, f32[8,768]{1,0:T(8,128)S(1)} %get-tuple-element.66.rows_ref, ...), custom_call_target="tpu_custom_call" | custom-call | flops 335544320 | bytes 2908160 | tf_op jit(solution)/shard_map/response_grads/pallas_call | solution.py:217
  21.8 0.0 collective-permute-done.7
  21.8 1.1 %collective-permute-done.8 = bf16[32,1024]{1,0:T(8,128)(2,1)S(1)} collective-permute-done((bf16[32,1024]{1,0:T(8,128)(2,1)S(1)}, bf16[32,1024]{1,0:T(8,128)(2,1)S(1)}, u32[]{:S(2)}, u32[]{:S(2)}) %collective-permute-start.8) | collective-permute-done | bytes 65568 | tf_op jit(solution)/shard_map/ppermute | solution.py:251
  22.9 0.6 %collective-permute-done.9 = bf16[32,1024]{1,0:T(8,128)(2,1)S(1)} collective-permute-done((bf16[32,1024]{1,0:T(8,128)(2,1)S(1)}, bf16[32,1024]{1,0:T(8,128)(2,1)S(1)}, u32[]{:S(2)}, u32[]{:S(2)}) %collective-permute-start.9) | collective-permute-done | bytes 65568 | tf_op jit(solution)/shard_map/ppermute | solution.py:251
  23.5 2.5 %collective-permute-start.11 = (bf16[16,1024]{1,0:T(8,128)(2,1)S(1)}, bf16[16,1024]{1,0:T(8,128)(2,1)S(1)}, u32[]{:S(2)}, u32[]{:S(2)}) collective-permute-start(bf16[16,1024]{1,0:T(8,128)(2,1)S(1)} %convert_add_fusion.1), channel_id=1, source_target_pairs={{0,6},{1,7},{2,4},{3,5},{4,2},{5,3},{6,0},{7,1},{8,14},{9,15},{10,... | collective-permute-start | bytes 98312 | tf_op jit(solution)/shard_map/ppermute | solution.py:251
  26.1 1.5 %query_grads.1 = bf16[128,2560]{1,0:T(8,128)(2,1)} custom-call(bf16[4,128,640]{2,1,0:T(8,128)(2,1)S(1)} %get-tuple-element.80.ds_ref.ds0_ref, bf16[4,128,640]{2,1,0:T(8,128)(2,1)S(1)} %get-tuple-element.90.ds1_ref, bf16[4,128,640]{2,1,0:T(8,128)(2,1)S(1)} %get-tuple-element.91.ds2_ref, bf16[128,512]{1,0:T(8,128)(2,1)S(1)} %get-tuple-element.59.k_ref.k0_ref, ...), custom_call_target="tpu_custom_call" | custom-call | flops 251658240 | bytes 2621440 | tf_op jit(solution)/shard_map/query_grads/pallas_call | solution.py:217
  27.6 0.2 collective-permute-done.11
  27.8 0.6 %slice_bitcast_fusion = (f32[1,16,512]{2,1,0:T(8,128)}, f32[1,16,512]{2,1,0:T(8,128)}) fusion(f32[16,1024]{1,0:T(8,128)S(1)} %convert_add_fusion), kind=kLoop, calls=%fused_computation.5 | loop fusion | bytes 131072 | tf_op jit(solution)/shard_map/broadcast_in_dim | solution.py:385
  (5 shorter events, 0.1 us)
Async XLA Ops:
  0.6 10.4 %copy-start = (bf16[1,128,2560]{2,1,0:T(8,128)(2,1)S(1)}, bf16[1,128,2560]{2,1,0:T(8,128)(2,1)}, u32[]{:S(2)}) copy-start(bf16[1,128,2560]{2,1,0:T(8,128)(2,1)} %param.13) | copy-start | bytes 1966084
  1.4 5.9 %collective-permute-start = (bf16[16,1024]{1,0:T(8,128)(2,1)S(1)}, bf16[16,1024]{1,0:T(8,128)(2,1)S(1)}, u32[]{:S(2)}, u32[]{:S(2)}) collective-permute-start(bf16[16,1024]{1,0:T(8,128)(2,1)S(1)} %pad_maximum_fusion.2), channel_id=1, source_target_pairs={{6,0},{7,1},{4,2},{5,3},{2,4},{3,5},{0,6},{1,7},{14,8},{15,9},{12,... | collective-permute-start | bytes 98312 | tf_op jit(solution)/shard_map/ppermute | solution.py:247
  7.4 6.3 %collective-permute-start.1 = (bf16[32,1024]{1,0:T(8,128)(2,1)S(1)}, bf16[32,1024]{1,0:T(8,128)(2,1)S(1)}, u32[]{:S(2)}, u32[]{:S(2)}) collective-permute-start(bf16[32,1024]{1,0:T(8,128)(2,1)S(1)} %pad_maximum_fusion.1), channel_id=1, source_target_pairs={{13,0},{12,1},{15,2},{14,3},{9,4},{8,5},{11,6},{10,7},{5,8},{4,9},... | collective-permute-start | bytes 196616 | tf_op jit(solution)/shard_map/ppermute | solution.py:247
  10.2 4.4 %collective-permute-start.2 = (bf16[32,1024]{1,0:T(8,128)(2,1)S(1)}, bf16[32,1024]{1,0:T(8,128)(2,1)S(1)}, u32[]{:S(2)}, u32[]{:S(2)}) collective-permute-start(bf16[32,1024]{1,0:T(8,128)(2,1)S(1)} %pad_maximum_fusion.1), channel_id=1, source_target_pairs={{5,0},{4,1},{7,2},{6,3},{1,4},{0,5},{3,6},{2,7},{13,8},{12,9},{15,... | collective-permute-start | bytes 196616 | tf_op jit(solution)/shard_map/ppermute | solution.py:247
  10.2 4.4 %collective-permute-start.3 = (bf16[32,1024]{1,0:T(8,128)(2,1)S(1)}, bf16[32,1024]{1,0:T(8,128)(2,1)S(1)}, u32[]{:S(2)}, u32[]{:S(2)}) collective-permute-start(bf16[32,1024]{1,0:T(8,128)(2,1)S(1)} %pad_maximum_fusion.1), channel_id=1, source_target_pairs={{12,0},{13,1},{14,2},{15,3},{8,4},{9,5},{10,6},{11,7},{4,8},{5,9},... | collective-permute-start | bytes 196616 | tf_op jit(solution)/shard_map/ppermute | solution.py:247
  10.9 4.8 %collective-permute-start.5 = (bf16[128,2560]{1,0:T(8,128)(2,1)}, bf16[128,2560]{1,0:T(8,128)(2,1)S(1)}, u32[]{:S(2)}, u32[]{:S(2)}) collective-permute-start(bf16[128,2560]{1,0:T(8,128)(2,1)} %bitcast.19), channel_id=1, source_target_pairs={{4,0},{5,1},{6,2},{7,3},{0,4},{1,5},{2,6},{3,7},{12,8},{13,9},{14,... | collective-permute-start | bytes 1966088 | tf_op jit(solution)/shard_map/ppermute | solution.py:247
  11.0 4.8 %collective-permute-start.6 = (bf16[128,2560]{1,0:T(8,128)(2,1)S(1)}, bf16[128,2560]{1,0:T(8,128)(2,1)S(1)}, u32[]{:S(2)}, u32[]{:S(2)}) collective-permute-start(bf16[128,2560]{1,0:T(8,128)(2,1)S(1)} %bitcast.17), channel_id=1, source_target_pairs={{4,0},{5,1},{6,2},{7,3},{0,4},{1,5},{2,6},{3,7},{12,8},{13,9},{14,... | collective-permute-start | bytes 1966088 | tf_op jit(solution)/shard_map/ppermute | solution.py:247
  13.7 2.1 %collective-permute-start.4 = (f32[8,768]{1,0:T(8,128)S(1)}, f32[8,768]{1,0:T(8,128)S(1)}, u32[]{:S(2)}, u32[]{:S(2)}) collective-permute-start(f32[8,768]{1,0:T(8,128)S(1)} %get-tuple-element.66.rows_ref), channel_id=1, source_target_pairs={{4,0},{5,1},{6,2},{7,3},{0,4},{1,5},{2,6},{3,7},{12,8},{13,9},{14,... | collective-permute-start | bytes 73736 | tf_op jit(solution)/shard_map/ppermute | solution.py:247
  14.6 5.5 %collective-permute-start.10 = (bf16[128,1024]{1,0:T(8,128)(2,1)S(1)}, bf16[128,1024]{1,0:T(8,128)(2,1)S(1)}, u32[]{:S(2)}, u32[]{:S(2)}) collective-permute-start(bf16[128,1024]{1,0:T(8,128)(2,1)S(1)} %pad_maximum_fusion.kv_ref.k1_ref), channel_id=1, source_target_pairs={{4,0},{5,1},{6,2},{7,3},{0,4},{1,5},{2,6},{3,7},{12,8},{13,9},{14,... | collective-permute-start | bytes 786440 | tf_op jit(solution)/shard_map/ppermute | solution.py:247
  16.8 4.9 %collective-permute-start.7 = (bf16[32,1024]{1,0:T(8,128)(2,1)S(1)}, bf16[32,1024]{1,0:T(8,128)(2,1)S(1)}, u32[]{:S(2)}, u32[]{:S(2)}) collective-permute-start(bf16[32,1024]{1,0:T(8,128)(2,1)S(1)} %get-tuple-element.76), channel_id=1, source_target_pairs={{0,13},{1,12},{2,15},{3,14},{4,9},{5,8},{6,11},{7,10},{8,5},{9,4},... | collective-permute-start | bytes 196616 | tf_op jit(solution)/shard_map/ppermute | solution.py:251
  18.7 4.2 %collective-permute-start.8 = (bf16[32,1024]{1,0:T(8,128)(2,1)S(1)}, bf16[32,1024]{1,0:T(8,128)(2,1)S(1)}, u32[]{:S(2)}, u32[]{:S(2)}) collective-permute-start(bf16[32,1024]{1,0:T(8,128)(2,1)S(1)} %get-tuple-element.77), channel_id=1, source_target_pairs={{0,5},{1,4},{2,7},{3,6},{4,1},{5,0},{6,3},{7,2},{8,13},{9,12},{10,... | collective-permute-start | bytes 196616 | tf_op jit(solution)/shard_map/ppermute | solution.py:251
  19.2 4.3 %collective-permute-start.9 = (bf16[32,1024]{1,0:T(8,128)(2,1)S(1)}, bf16[32,1024]{1,0:T(8,128)(2,1)S(1)}, u32[]{:S(2)}, u32[]{:S(2)}) collective-permute-start(bf16[32,1024]{1,0:T(8,128)(2,1)S(1)} %get-tuple-element.78), channel_id=1, source_target_pairs={{0,12},{1,13},{2,14},{3,15},{4,8},{5,9},{6,10},{7,11},{8,4},{9,5},... | collective-permute-start | bytes 196616 | tf_op jit(solution)/shard_map/ppermute | solution.py:251
  23.5 4.3 %collective-permute-start.11 = (bf16[16,1024]{1,0:T(8,128)(2,1)S(1)}, bf16[16,1024]{1,0:T(8,128)(2,1)S(1)}, u32[]{:S(2)}, u32[]{:S(2)}) collective-permute-start(bf16[16,1024]{1,0:T(8,128)(2,1)S(1)} %convert_add_fusion.1), channel_id=1, source_target_pairs={{0,6},{1,7},{2,4},{3,5},{4,2},{5,3},{6,0},{7,1},{8,14},{9,15},{10,... | collective-permute-start | bytes 98312 | tf_op jit(solution)/shard_map/ppermute | solution.py:251
